TPU v7x, 32 devices: a whole 2x2x4 slice. The times are simulated.
32 devices in a mesh: grp: 4 (over y, x), shard: 8 (over z, core).
Axes of the slice: x: 2, y: 2, z: 4, core: 2. Of those that a mesh axis runs over, the one named last changes fastest.
Arguments:
- tokens: bfloat16 [32, 1024, 1024], P(('grp', 'shard')), may hold values from -6 to 6
- segment_ids: int32 [32, 1024], P(('grp', 'shard')), may hold values from 0 to 17, as said below
- keep_flag: int32 [32, 1024], P(('grp', 'shard')), may hold values from 0 to 1, as said below
- cotangent: bfloat16 [32, 1024, 1024], P(('grp', 'shard')), may hold values from -6 to 6
- w_qkv: bfloat16 [1024, 3072], P('shard', 'grp'), may hold values from -0.25 to 0.25
- b_query: bfloat16 [1024], P('shard'), may hold values from -3 to 3
- b_value: bfloat16 [1024], P('shard'), may hold values from -3 to 3
- w_attn_out: bfloat16 [1024, 1024], P('shard', 'grp'), may hold values from -0.75 to 0.75
- b_attn_out: bfloat16 [1024], P('shard'), may hold values from -3 to 3
- norm1_gain: bfloat16 [1024], P('shard'), may hold values from 0.5 to 1.5
- norm1_bias: bfloat16 [1024], P('shard'), may hold values from -3 to 3
- w_in: bfloat16 [1024, 4096], P('shard', 'grp'), may hold values from -0.1875 to 0.1875
- b_in: bfloat16 [4096], P('shard'), may hold values from -3 to 3
- w_out: bfloat16 [4096, 1024], P('shard', 'grp'), may hold values from -0.09375 to 0.09375
- b_out: bfloat16 [1024], P('shard'), may hold values from -3 to 3
- norm2_gain: bfloat16 [1024], P('shard'), may hold values from 0.5 to 1.5
- norm2_bias: bfloat16 [1024], P('shard'), may hold values from -3 to 3
Outputs:
- layer_out: bfloat16 [32, 1024, 1024], P(('grp', 'shard'))
- input_grad: float32 [32, 1024, 1024], P(('grp', 'shard'))
- grad_w_qkv: float32 [1024, 3072], P('shard')
- grad_b_query: float32 [1024], P('shard')
- grad_b_value: float32 [1024], P('shard')
- grad_w_attn_out: float32 [1024, 1024], P('shard')
- grad_b_attn_out: float32 [1024], P('shard')
- grad_norm1_gain: float32 [1024], P('shard')
- grad_norm1_bias: float32 [1024], P('shard')
- grad_w_in: float32 [1024, 4096], P('shard')
- grad_b_in: float32 [4096], P('shard')
- grad_w_out: float32 [4096, 1024], P('shard')
- grad_b_out: float32 [1024], P('shard')
- grad_norm2_gain: float32 [1024], P('shard')
- grad_norm2_bias: float32 [1024], P('shard')
Inputs may be any that keep to these rules, and one draw needn't show every extreme that they name: `segment_ids`: along each sequence the ids start at 0 and rise by one at the first token of each document; every document but the last of its sequence has 60 to 800 tokens, the last one is cut by the sequence's end. `keep_flag`: 0 exactly on the tokens of the last document of each sequence.
All inputs are finite; a program needn't handle non-finite values.
Results may differ from a plain program's by a relative error of at most 0.02.
Values may be sent and summed in bfloat16 or wider, within the bound.
No kernel may reach another device: no remote copies, remote signals or barrier semaphores. Data moves between devices by JAX's collectives and lax.ppermute only.
A program may use at most 256 MiB of HBM per device.

v0:
```python
import math

import jax
import jax.numpy as jnp
from jax import lax
from jax.sharding import PartitionSpec as P

H = 16
HD = 64


masked_score = -1e30
epsilon = 1e-05


def norm_layer(rows, gain_row, shift_row):
    row_mean = jnp.mean(rows, -1, keepdims=True)
    centered = rows - row_mean
    row_var = jnp.mean(centered * centered, -1, keepdims=True)
    return centered * lax.rsqrt(row_var + epsilon) * gain_row + shift_row


def gelu_exact(values):
    return 0.5 * values * (1.0 + lax.erf(values * (1.0 / math.sqrt(2.0))))


def contract_rows(left, right):
    return lax.dot_general(
        left, right, (((0,), (0,)), ((), ())), preferred_element_type=jnp.float32
    )


def contract_cols(left, right):
    return lax.dot_general(
        left, right, (((1,), (1,)), ((), ())), preferred_element_type=jnp.float32
    )


def attend_forward(queries, key_rows, value_rows, segment_row, block_rows):
    length, model_width = queries.shape
    scaling = 1.0 / math.sqrt(HD)
    key_heads = key_rows.reshape(length, H, HD)
    value_heads = value_rows.reshape(length, H, HD)
    query_blocks = queries.reshape(length // block_rows, block_rows, H, HD)
    segment_blocks = segment_row.reshape(length // block_rows, block_rows)

    def one_block(pieces):
        query_part, segment_part = pieces
        scores = (
            jnp.einsum("qhd,khd->hqk", query_part, key_heads, preferred_element_type=jnp.float32)
            * scaling
        )
        allowed = segment_part[:, None] == segment_row[None, :]
        scores = jnp.where(allowed[None], scores, masked_score)
        row_max = jnp.max(scores, -1, keepdims=True)
        powers = jnp.exp(scores - row_max)
        totals = jnp.sum(powers, -1, keepdims=True)
        attn_probs = (powers / totals).astype(jnp.bfloat16)
        context = jnp.einsum(
            "hqk,khd->qhd", attn_probs, value_heads, preferred_element_type=jnp.float32
        )
        return (
            context.reshape(block_rows, model_width).astype(jnp.bfloat16),
            (row_max + jnp.log(totals))[:, :, 0],
        )

    contexts, log_sums = lax.map(one_block, (query_blocks, segment_blocks))
    return (contexts.reshape(length, model_width), log_sums)


def attend_backward(queries, key_rows, value_rows, segment_row, log_sums, context_grad, block_rows):
    length, model_width = queries.shape
    scaling = 1.0 / math.sqrt(HD)
    key_heads = key_rows.reshape(length, H, HD)
    value_heads = value_rows.reshape(length, H, HD)
    query_blocks = queries.reshape(length // block_rows, block_rows, H, HD)
    segment_blocks = segment_row.reshape(length // block_rows, block_rows)
    grad_blocks = context_grad.reshape(length // block_rows, block_rows, H, HD)

    def one_block(running, pieces):
        key_acc, value_acc = running
        query_part, segment_part, lse_part, grad_part = pieces
        scores = (
            jnp.einsum("qhd,khd->hqk", query_part, key_heads, preferred_element_type=jnp.float32)
            * scaling
        )
        allowed = segment_part[:, None] == segment_row[None, :]
        scores = jnp.where(allowed[None], scores, masked_score)
        probs = jnp.exp(scores - lse_part[:, :, None])
        prob_low = probs.astype(jnp.bfloat16)
        prob_grad = jnp.einsum(
            "qhd,khd->hqk", grad_part, value_heads, preferred_element_type=jnp.float32
        )
        row_dot = jnp.sum(prob_grad * probs, -1, keepdims=True)
        score_grad = (probs * (prob_grad - row_dot)).astype(jnp.bfloat16)
        query_grad = (
            jnp.einsum("hqk,khd->qhd", score_grad, key_heads, preferred_element_type=jnp.float32)
            * scaling
        )
        key_acc = (
            key_acc
            + jnp.einsum("hqk,qhd->khd", score_grad, query_part, preferred_element_type=jnp.float32)
            * scaling
        )
        value_acc = value_acc + jnp.einsum(
            "hqk,qhd->khd", prob_low, grad_part, preferred_element_type=jnp.float32
        )
        return ((key_acc, value_acc), query_grad.reshape(block_rows, model_width))

    empty_acc = jnp.zeros((length, H, HD), jnp.float32)
    (key_grad, value_grad), query_grads = lax.scan(
        one_block, (empty_acc, empty_acc), (query_blocks, segment_blocks, log_sums, grad_blocks)
    )
    return (
        query_grads.reshape(length, model_width),
        key_grad.reshape(length, model_width),
        value_grad.reshape(length, model_width),
    )


def on_device(
    tokens,
    segment_ids,
    keep_flag,
    cotangent,
    w_qkv,
    b_query,
    b_value,
    w_attn_out,
    b_attn_out,
    norm1_gain,
    norm1_bias,
    w_in,
    b_in,
    w_out,
    b_out,
    norm2_gain,
    norm2_bias,
):
    seq_count, length, model_width = tokens.shape
    block_rows = min(512, length)
    within = (
        lax.all_gather(w_qkv, "shard", axis=0, tiled=True),
        lax.all_gather(w_attn_out, "shard", axis=0, tiled=True),
        lax.all_gather(w_in, "shard", axis=0, tiled=True),
        lax.all_gather(w_out, "shard", axis=0, tiled=True),
        lax.all_gather(b_query, "shard", axis=0, tiled=True),
        lax.all_gather(b_value, "shard", axis=0, tiled=True),
        lax.all_gather(b_attn_out, "shard", axis=0, tiled=True),
        lax.all_gather(norm1_gain, "shard", axis=0, tiled=True),
        lax.all_gather(norm1_bias, "shard", axis=0, tiled=True),
        lax.all_gather(b_in, "shard", axis=0, tiled=True),
        lax.all_gather(b_out, "shard", axis=0, tiled=True),
        lax.all_gather(norm2_gain, "shard", axis=0, tiled=True),
        lax.all_gather(norm2_bias, "shard", axis=0, tiled=True),
    )
    full_qkv, full_attn, full_in, full_out = (
        lax.all_gather(within[0], "grp", axis=1, tiled=True),
        lax.all_gather(within[1], "grp", axis=1, tiled=True),
        lax.all_gather(within[2], "grp", axis=1, tiled=True),
        lax.all_gather(within[3], "grp", axis=1, tiled=True),
    )
    (
        bias_query,
        bias_value,
        bias_attn,
        gain_one,
        shift_one,
        bias_in,
        bias_out,
        gain_two,
        shift_two,
    ) = [piece.astype(jnp.float32) for piece in within[4:]]
    flat_rows = tokens.reshape(seq_count * length, model_width)
    mixed_qkv = jnp.dot(flat_rows, full_qkv, preferred_element_type=jnp.float32)
    queries = (mixed_qkv[:, :model_width] + bias_query).astype(jnp.bfloat16)
    key_rows = mixed_qkv[:, model_width : 2 * model_width].astype(jnp.bfloat16)
    value_rows = (mixed_qkv[:, 2 * model_width :] + bias_value).astype(jnp.bfloat16)
    query_seqs = queries.reshape(seq_count, length, model_width)
    key_seqs = key_rows.reshape(seq_count, length, model_width)
    value_seqs = value_rows.reshape(seq_count, length, model_width)

    def forward_sequence(pieces):
        return attend_forward(pieces[0], pieces[1], pieces[2], pieces[3], block_rows)

    contexts, log_sums = lax.map(forward_sequence, (query_seqs, key_seqs, value_seqs, segment_ids))
    contexts = contexts.reshape(seq_count * length, model_width)
    attended = jnp.dot(contexts, full_attn, preferred_element_type=jnp.float32) + bias_attn
    first_sum = flat_rows.astype(jnp.float32) + attended
    normed_one, norm_one_back = jax.vjp(norm_layer, first_sum, gain_one, shift_one)
    normed_low = normed_one.astype(jnp.bfloat16)
    hidden_pre = jnp.dot(normed_low, full_in, preferred_element_type=jnp.float32) + bias_in
    hidden, gelu_back = jax.vjp(gelu_exact, hidden_pre)
    hidden_low = hidden.astype(jnp.bfloat16)
    second_sum = normed_one + (
        jnp.dot(hidden_low, full_out, preferred_element_type=jnp.float32) + bias_out
    )
    result, norm_two_back = jax.vjp(norm_layer, second_sum, gain_two, shift_two)
    layer_out = result.astype(jnp.bfloat16).reshape(seq_count, length, model_width)
    again = (
        lax.all_gather(w_qkv, "shard", axis=0, tiled=True),
        lax.all_gather(w_attn_out, "shard", axis=0, tiled=True),
        lax.all_gather(w_in, "shard", axis=0, tiled=True),
        lax.all_gather(w_out, "shard", axis=0, tiled=True),
    )
    back_qkv, back_attn, back_in, back_out = (
        lax.all_gather(again[0], "grp", axis=1, tiled=True),
        lax.all_gather(again[1], "grp", axis=1, tiled=True),
        lax.all_gather(again[2], "grp", axis=1, tiled=True),
        lax.all_gather(again[3], "grp", axis=1, tiled=True),
    )
    masked_cot = cotangent.astype(jnp.float32).reshape(
        seq_count * length, model_width
    ) * keep_flag.reshape(seq_count * length, 1).astype(jnp.float32)
    second_grad, gain_two_grad, shift_two_grad = norm_two_back(masked_cot)
    bias_out_grad = jnp.sum(second_grad, 0)
    out_low = second_grad.astype(jnp.bfloat16)
    w_out_grad = contract_rows(hidden_low, out_low)
    hidden_grad = contract_cols(out_low, back_out)
    (pre_grad,) = gelu_back(hidden_grad)
    bias_in_grad = jnp.sum(pre_grad, 0)
    pre_low = pre_grad.astype(jnp.bfloat16)
    w_in_grad = contract_rows(normed_low, pre_low)
    normed_grad = second_grad + contract_cols(pre_low, back_in)
    first_grad, gain_one_grad, shift_one_grad = norm_one_back(normed_grad)
    bias_attn_grad = jnp.sum(first_grad, 0)
    attn_low = first_grad.astype(jnp.bfloat16)
    w_attn_grad = contract_rows(contexts, attn_low)
    context_grad = contract_cols(attn_low, back_attn).astype(jnp.bfloat16)

    def backward_sequence(pieces):
        return attend_backward(
            pieces[0], pieces[1], pieces[2], pieces[3], pieces[4], pieces[5], block_rows
        )

    query_grad, key_grad, value_grad = lax.map(
        backward_sequence,
        (
            query_seqs,
            key_seqs,
            value_seqs,
            segment_ids,
            log_sums,
            context_grad.reshape(seq_count, length, model_width),
        ),
    )
    query_grad = query_grad.reshape(seq_count * length, model_width)
    key_grad = key_grad.reshape(seq_count * length, model_width)
    value_grad = value_grad.reshape(seq_count * length, model_width)
    bias_query_grad = jnp.sum(query_grad, 0)
    bias_value_grad = jnp.sum(value_grad, 0)
    qkv_low = jnp.concatenate([query_grad, key_grad, value_grad], 1).astype(jnp.bfloat16)
    w_qkv_grad = contract_rows(flat_rows, qkv_low)
    input_grad = first_grad + contract_cols(qkv_low, back_qkv)
    reduced = (
        lax.psum_scatter(
            w_qkv_grad.astype(jnp.bfloat16), "shard", scatter_dimension=0, tiled=True
        ).astype(jnp.float32),
        lax.psum_scatter(
            bias_query_grad.astype(jnp.bfloat16), "shard", scatter_dimension=0, tiled=True
        ).astype(jnp.float32),
        lax.psum_scatter(
            bias_value_grad.astype(jnp.bfloat16), "shard", scatter_dimension=0, tiled=True
        ).astype(jnp.float32),
        lax.psum_scatter(
            w_attn_grad.astype(jnp.bfloat16), "shard", scatter_dimension=0, tiled=True
        ).astype(jnp.float32),
        lax.psum_scatter(
            bias_attn_grad.astype(jnp.bfloat16), "shard", scatter_dimension=0, tiled=True
        ).astype(jnp.float32),
        lax.psum_scatter(
            gain_one_grad.astype(jnp.bfloat16), "shard", scatter_dimension=0, tiled=True
        ).astype(jnp.float32),
        lax.psum_scatter(
            shift_one_grad.astype(jnp.bfloat16), "shard", scatter_dimension=0, tiled=True
        ).astype(jnp.float32),
        lax.psum_scatter(
            w_in_grad.astype(jnp.bfloat16), "shard", scatter_dimension=0, tiled=True
        ).astype(jnp.float32),
        lax.psum_scatter(
            bias_in_grad.astype(jnp.bfloat16), "shard", scatter_dimension=0, tiled=True
        ).astype(jnp.float32),
        lax.psum_scatter(
            w_out_grad.astype(jnp.bfloat16), "shard", scatter_dimension=0, tiled=True
        ).astype(jnp.float32),
        lax.psum_scatter(
            bias_out_grad.astype(jnp.bfloat16), "shard", scatter_dimension=0, tiled=True
        ).astype(jnp.float32),
        lax.psum_scatter(
            gain_two_grad.astype(jnp.bfloat16), "shard", scatter_dimension=0, tiled=True
        ).astype(jnp.float32),
        lax.psum_scatter(
            shift_two_grad.astype(jnp.bfloat16), "shard", scatter_dimension=0, tiled=True
        ).astype(jnp.float32),
    )
    summed = (
        lax.psum(reduced[0].astype(jnp.bfloat16), "grp").astype(jnp.float32),
        lax.psum(reduced[1].astype(jnp.bfloat16), "grp").astype(jnp.float32),
        lax.psum(reduced[2].astype(jnp.bfloat16), "grp").astype(jnp.float32),
        lax.psum(reduced[3].astype(jnp.bfloat16), "grp").astype(jnp.float32),
        lax.psum(reduced[4].astype(jnp.bfloat16), "grp").astype(jnp.float32),
        lax.psum(reduced[5].astype(jnp.bfloat16), "grp").astype(jnp.float32),
        lax.psum(reduced[6].astype(jnp.bfloat16), "grp").astype(jnp.float32),
        lax.psum(reduced[7].astype(jnp.bfloat16), "grp").astype(jnp.float32),
        lax.psum(reduced[8].astype(jnp.bfloat16), "grp").astype(jnp.float32),
        lax.psum(reduced[9].astype(jnp.bfloat16), "grp").astype(jnp.float32),
        lax.psum(reduced[10].astype(jnp.bfloat16), "grp").astype(jnp.float32),
        lax.psum(reduced[11].astype(jnp.bfloat16), "grp").astype(jnp.float32),
        lax.psum(reduced[12].astype(jnp.bfloat16), "grp").astype(jnp.float32),
    )
    return (
        layer_out,
        input_grad.reshape(seq_count, length, model_width),
        summed[0],
        summed[1],
        summed[2],
        summed[3],
        summed[4],
        summed[5],
        summed[6],
        summed[7],
        summed[8],
        summed[9],
        summed[10],
        summed[11],
        summed[12],
    )


def solution(mesh):
    return jax.shard_map(
        on_device,
        mesh=mesh,
        in_specs=(
            P(("grp", "shard"), None, None),
            P(("grp", "shard"), None),
            P(("grp", "shard"), None),
            P(("grp", "shard"), None, None),
            P("shard", "grp"),
            P("shard"),
            P("shard"),
            P("shard", "grp"),
            P("shard"),
            P("shard"),
            P("shard"),
            P("shard", "grp"),
            P("shard"),
            P("shard", "grp"),
            P("shard"),
            P("shard"),
            P("shard"),
        ),
        out_specs=(
            P(("grp", "shard"), None, None),
            P(("grp", "shard"), None, None),
            P("shard", None),
            P("shard"),
            P("shard"),
            P("shard", None),
            P("shard"),
            P("shard"),
            P("shard"),
            P("shard", None),
            P("shard"),
            P("shard", None),
            P("shard"),
            P("shard"),
            P("shard"),
        ),
        check_vma=False,
    )
```

profile of v0, /device:TPU:0, one launch (start us, length us, event | category | flops | bytes accessed | tf_op | source)
XLA Modules:
  0.0 1117.7 jit_solution(2357451109760582016)
XLA Ops:
  9.6 28.0 %all-gather.17.cloned.1.call-done = bf16[1024,768]{1,0:T(8,128)(2,1)} async-done(((bf16[128,768]{1,0:T(8,128)(2,1)}), bf16[1024,768]{1,0:T(8,128)(2,1)}) %all-gather.17.cloned.1.call-update) | async-done | bytes 1572880 | tf_op jit(solution)/shard_map/all_gather | solution.py:143
  37.6 16.5 %all_gather.63 = bf16[1024,256]{1,0:T(8,128)(2,1)} all-gather(bf16[128,256]{1,0:T(8,128)(2,1)} %param.28), channel_id=1, replica_groups=mesh['grp'=4,'shard'=8] {'shard'}, dimensions={0}, use_global_device_ids=true | all-gather | bytes 589824 | tf_op jit(solution)/shard_map/all_gather | solution.py:144
  54.2 14.3 %all-gather.23.cloned.1.call-done = bf16[1024,1024]{1,0:T(8,128)(2,1)} async-done(((bf16[128,1024]{1,0:T(8,128)(2,1)}), bf16[1024,1024]{1,0:T(8,128)(2,1)}) %all-gather.23.cloned.1.call-update) | async-done | bytes 2097168 | tf_op jit(solution)/shard_map/all_gather | solution.py:145
  70.5 10.6 all-gather
  81.0 8.7 all-gather.1
  89.7 10.3 all-gather.2
  100.6 8.6 all-gather.3
  109.8 10.0 all-gather.4
  120.5 8.6 all-gather.6
  129.7 10.0 all-gather.7
  140.3 8.6 all-gather.8
  149.5 12.7 %all-gather.5 = bf16[8,1,512]{2,1,0:T(2,128)(2,1)S(1)} all-gather(bf16[1,1,512]{2,1,0:T(2,128)(2,1)S(1)} %reshape.329), channel_id=1, replica_groups=mesh['grp'=4,'shard'=8] {'shard'}, dimensions={0}, use_global_device_ids=true | all-gather | bytes 9216 | tf_op jit(solution)/shard_map/all_gather | solution.py:152
  165.5 4.1 copy.82
  170.5 8.7 fusion.48
  186.1 2.9 copy.84
  188.9 6.4 reshape.358
  195.3 5.5 copy.86
  200.8 99.6 %while.47 = (s32[]{:T(128)}, bf16[2,512,1024]{2,1,0:T(8,128)(2,1)}, f32[2,16,512]{2,1,0:T(8,128)S(1)}, s32[2,512]{1,0:T(2,128)S(1)}, s32[1024]{0:T(1024)S(1)}, /...) while((s32[]{:T(128)}, bf16[2,512,1024]{2,1,0:T(8,128)(2,1)}, ...), condition=%wide.region_3.4_spmd, body=%wide.region_0.3_spmd.sunk | while | flops 2249187328 | bytes 121907344 | solution.py:67
  201.6 16.4 %fusion.104 = (f32[16,512]{1,0:T(8,128)S(1)}, f32[16,512,1024]{2,1,0:T(8,128)}) fusion(pred[512,1024]{1,0:T(8,128)(4,1)S(1)} %broadcast_compare_fusion.4, bf16[1024,16,64]{0,2,1:T(8,128)(2,1)S(1)} %get-tuple-element.583, bf16[2,512,16,64]{1,3,2,0:T(8,128)(2,1)} %get-tuple-element.582, s32[]{:T(128)S(6)} %copy.118), kind=kOutput, calls=%fused_computation.3.clone.1 | convolution fusion | flops 1098899456 | bytes 37257220 | tf_op jit(solution)/shard_map/while/body/eval_jaxpr/while/body/eval_jaxpr/qhd,khd->hqk/dot_general | solution.py:50
  218.0 15.8 %fusion.105 = f32[16,512]{1,0:T(8,128)S(1)} fusion(f32[16,512,1024]{2,1,0:T(8,128)} %get-tuple-element.544, f32[16,512]{1,0:T(8,128)S(1)} %get-tuple-element.545, pred[512,1024]{1,0:T(8,128)(4,1)S(1)} %broadcast_compare_fusion.4), kind=kLoop, calls=%fused_computation.4.clone.1 | loop fusion | flops 33546240 | bytes 34144256 | tf_op jit(solution)/shard_map/while/body/eval_jaxpr/while/body/eval_jaxpr/reduce_sum | solution.py:57
  233.8 15.2 %fusion.106 = bf16[16,512,64]{1,2,0:T(8,128)(2,1)} fusion(bf16[1024,16,64]{0,2,1:T(8,128)(2,1)S(1)} %copy-done.4, f32[16,512,1024]{2,1,0:T(8,128)} %get-tuple-element.544, f32[16,512]{1,0:T(8,128)S(1)} %fusion.105, f32[16,512]{1,0:T(8,128)S(1)} %get-tuple-element.545, pred[512,1024]{1,0:T(8,128)(4,1)S(1)} %broadcast_compare_fusion.4), kind=kOutput, calls=%fused_computation.6.clone.1 | convolution fusion | flops 1116209152 | bytes 37289984 | tf_op jit(solution)/shard_map/while/body/eval_jaxpr/while/body/eval_jaxpr/hqk,khd->qhd/dot_general | solution.py:59
  252.2 15.3 %fusion.104 = (f32[16,512]{1,0:T(8,128)S(1)}, f32[16,512,1024]{2,1,0:T(8,128)}) fusion(pred[512,1024]{1,0:T(8,128)(4,1)S(1)} %broadcast_compare_fusion.4, bf16[1024,16,64]{0,2,1:T(8,128)(2,1)S(1)} %get-tuple-element.583, bf16[2,512,16,64]{1,3,2,0:T(8,128)(2,1)} %get-tuple-element.582, s32[]{:T(128)S(6)} %copy.118), kind=kOutput, calls=%fused_computation.3.clone.1 | convolution fusion | flops 1098899456 | bytes 37257220 | tf_op jit(solution)/shard_map/while/body/eval_jaxpr/while/body/eval_jaxpr/qhd,khd->hqk/dot_general | solution.py:50
  267.5 15.0 %fusion.105 = f32[16,512]{1,0:T(8,128)S(1)} fusion(f32[16,512,1024]{2,1,0:T(8,128)} %get-tuple-element.544, f32[16,512]{1,0:T(8,128)S(1)} %get-tuple-element.545, pred[512,1024]{1,0:T(8,128)(4,1)S(1)} %broadcast_compare_fusion.4), kind=kLoop, calls=%fused_computation.4.clone.1 | loop fusion | flops 33546240 | bytes 34144256 | tf_op jit(solution)/shard_map/while/body/eval_jaxpr/while/body/eval_jaxpr/reduce_sum | solution.py:57
  282.6 15.2 %fusion.106 = bf16[16,512,64]{1,2,0:T(8,128)(2,1)} fusion(bf16[1024,16,64]{0,2,1:T(8,128)(2,1)S(1)} %copy-done.4, f32[16,512,1024]{2,1,0:T(8,128)} %get-tuple-element.544, f32[16,512]{1,0:T(8,128)S(1)} %fusion.105, f32[16,512]{1,0:T(8,128)S(1)} %get-tuple-element.545, pred[512,1024]{1,0:T(8,128)(4,1)S(1)} %broadcast_compare_fusion.4), kind=kOutput, calls=%fused_computation.6.clone.1 | convolution fusion | flops 1116209152 | bytes 37289984 | tf_op jit(solution)/shard_map/while/body/eval_jaxpr/while/body/eval_jaxpr/hqk,khd->qhd/dot_general | solution.py:59
  300.4 5.7 fusion.63
  308.7 20.6 %multiply_convert_fusion.1 = (bf16[1024,4096]{1,0:T(8,128)(2,1)}, f32[1024,4096]{1,0:T(8,128)}) fusion(f32[4096]{0:T(1024)S(1)} %bitcast.167, bf16[1024,4096]{1,0:T(8,128)(2,1)} %all-gather.25.cloned.1.call-done, f32[1024,1024]{0,1:T(8,128)} %copy-done.9, f32[1024]{0:T(1024)S(1)} %bitcast.169, f32[1024]{0:T(1024)S(1)} %bitcast.160, f32[1024]{0:T(1024)S(1)} %fusion.53, ...), kind=kOutput, calls=%fused_computation.47 | convolution fusion | flops 8620343296 | bytes 37781504 | tf_op jit(solution)/shard_map/dot_general | solution.py:192
  329.2 56.8 %all-gather.29.cloned.1.call-done = bf16[4096,1024]{1,0:T(8,128)(2,1)} async-done(((bf16[4096,256]{1,0:T(8,128)(2,1)}), bf16[4096,1024]{1,0:T(8,128)(2,1)}) %all-gather.29.cloned.1.call-update) | async-done | bytes 8388624 | tf_op jit(solution)/shard_map/all_gather | solution.py:161
  386.1 16.2 %fusion.64 = (f32[1024]{0:T(1024)S(1)}, f32[1024,1024]{0,1:T(8,128)}) fusion(f32[1024]{0:T(1024)S(1)} %bitcast.172, bf16[1024,4096]{1,0:T(8,128)(2,1)} %get-tuple-element.426, bf16[4096,1024]{1,0:T(8,128)(2,1)} %all-gather.29.cloned.1.call-done, f32[1024]{0:T(1024)S(1)} %bitcast.170, f32[1024]{0:T(1024)S(1)} %bitcast.161, f32[1024]{0:T(1024)S(1)} %fusion.53, ...), kind=kOutput, calls=%fused_computation.111 | convolution fusion | flops 8597273600 | bytes 25190400 | tf_op jit(solution)/shard_map/dot_general | solution.py:196
  405.8 4.6 fusion.40
  410.4 3.2 fusion.61
  413.6 21.8 %fusion.65 = (bf16[4096]{0:T(1024)(128)(2,1)}, bf16[1024,4096]{1,0:T(8,128)(2,1)}) fusion(bf16[4096,1024]{1,0:T(8,128)(2,1)S(1)} %bitcast.183, f32[1024,1024]{0,1:T(8,128)S(1)} %get-tuple-element.414, f32[1024]{0:T(1024)S(1)} %negate_multiply_fusion.1, f32[1024,4096]{1,0:T(8,128)} %get-tuple-element.427, f32[4096]{0:T(1024)S(1)} %bitcast.168), kind=kOutput, calls=%fused_computation.112 | convolution fusion | flops 8654942208 | bytes 37777408 | tf_op jit(solution)/shard_map/dot_general | solution.py:34
  435.4 15.6 %multiply_reduce_fusion.1 = (bf16[1024]{0:T(1024)(128)(2,1)}, f32[1024]{0:T(1024)S(1)}, bf16[1024]{0:T(1024)(128)(2,1)}, f32[1024,1024]{0,1:T(8,128)S(1)}) fusion(f32[1024,1024]{0,1:T(8,128)S(1)} %copy-done.10, f32[1024]{0:T(1024)S(1)} %fusion.53, f32[1024]{0:T(1024)S(1)} %broadcast_multiply_fusion.1, f32[1024]{0:T(1024)S(1)} %bitcast.162, ...), kind=kOutput, calls=%fused_computation.68 | convolution fusion | flops 8600417280 | bytes 29384704 | tf_op jit(solution)/shard_map/dot_general | solution.py:34
  454.1 3.7 convolution_convert_fusion.3
  457.9 6.3 reshape.346
  464.2 5.4 copy.92
  469.7 217.7 %while.48 = (s32[]{:T(128)}, f32[1024,16,64]{0,2,1:T(8,128)}, f32[1024,16,64]{0,2,1:T(8,128)}, f32[2,512,1024]{1,2,0:T(8,128)}, bf16[2,512,16,64]{1,3,2,0:T(8,12...) while((s32[]{:T(128)}, f32[1024,16,64]{0,2,1:T(8,128)}, ...), condition=%wide.region_14.15_spmd.clone, body=%wide.region_12.14_spmd.clone.sunk | while | flops 5500821504 | bytes 413378912 | solution.py:111
  470.3 14.7 %fusion.116 = f32[16,512,1024]{2,1,0:T(8,128)} fusion(bf16[1024,16,64]{0,2,1:T(8,128)(2,1)S(1)} %get-tuple-element.619, bf16[2,512,16,64]{1,3,2,0:T(8,128)(2,1)} %get-tuple-element.616, s32[]{:T(128)S(6)} %copy.128), kind=kOutput, calls=%fused_computation.31.clone.1 | convolution fusion | flops 1073741824 | bytes 36700164 | tf_op jit(solution)/shard_map/while/body/eval_jaxpr/while/body/eval_jaxpr/qhd,khd->hqk/dot_general | solution.py:84
  485.0 17.5 %bitcast_add_fusion.5 = f32[1024,16,64]{0,2,1:T(8,128)} fusion(f32[1024,16,64]{0,2,1:T(8,128)} %get-tuple-element.601, f32[16,512,1024]{2,1,0:T(8,128)} %fusion.116, f32[16,512]{1,0:T(8,128)S(1)} %dynamic-slice_bitcast_fusion.2, pred[512,1024]{1,0:T(8,128)(4,1)S(1)} %broadcast_compare_fusion.5, pred[]{:T(512)S(6)} %compare.3, ...), kind=kOutput, calls=%fused_computation.23.clone.1 | convolution fusion | flops 1109393408 | bytes 43548676 | tf_op jit(solution)/shard_map/while/body/eval_jaxpr/while/body/eval_jaxpr/hqk,qhd->khd/dot_general | solution.py:105
  502.5 25.9 %multiply_reduce_fusion.6 = (f32[16,512]{1,0:T(8,128)S(1)}, f32[16,512,1024]{2,1,0:T(8,128)}) fusion(f32[16,512,1024]{2,1,0:T(8,128)} %fusion.116, f32[16,512]{1,0:T(8,128)S(1)} %dynamic-slice_bitcast_fusion.2, pred[512,1024]{1,0:T(8,128)(4,1)S(1)} %broadcast_compare_fusion.5, bf16[1024,16,64]{0,2,1:T(8,128)(2,1)} %get-tuple-element.622, ...), kind=kOutput, calls=%fused_computation.18.clone.1 | convolution fusion | flops 1115676672 | bytes 70844416 | tf_op jit(solution)/shard_map/while/body/eval_jaxpr/while/body/eval_jaxpr/qhd,khd->hqk/dot_general | solution.py:91
  528.4 27.8 %multiply_convert_fusion.3 = bf16[16,512,1024]{2,1,0:T(8,128)(2,1)} fusion(f32[16,512,1024]{2,1,0:T(8,128)} %get-tuple-element.557, f32[16,512,1024]{2,1,0:T(8,128)} %fusion.116, f32[16,512]{1,0:T(8,128)S(1)} %get-tuple-element.558, f32[16,512]{1,0:T(8,128)S(1)} %dynamic-slice_bitcast_fusion.2, pred[512,1024]{1,0:T(8,128)(4,1)S(1)} %broadcast_compare_fusion.5), kind=kLoop, calls=%fused_computation.17.clone.1 | loop fusion | flops 50331648 | bytes 84475904 | tf_op jit(solution)/shard_map/while/body/eval_jaxpr/while/body/eval_jaxpr/convert_element_type | solution.py:95
  556.2 10.6 convolution_multiply_fusion.2
  568.1 6.6 bitcast_add_fusion.4
  577.5 14.8 %fusion.116 = f32[16,512,1024]{2,1,0:T(8,128)} fusion(bf16[1024,16,64]{0,2,1:T(8,128)(2,1)S(1)} %get-tuple-element.619, bf16[2,512,16,64]{1,3,2,0:T(8,128)(2,1)} %get-tuple-element.616, s32[]{:T(128)S(6)} %copy.128), kind=kOutput, calls=%fused_computation.31.clone.1 | convolution fusion | flops 1073741824 | bytes 36700164 | tf_op jit(solution)/shard_map/while/body/eval_jaxpr/while/body/eval_jaxpr/qhd,khd->hqk/dot_general | solution.py:84
  592.3 18.8 %bitcast_add_fusion.5 = f32[1024,16,64]{0,2,1:T(8,128)} fusion(f32[1024,16,64]{0,2,1:T(8,128)} %get-tuple-element.601, f32[16,512,1024]{2,1,0:T(8,128)} %fusion.116, f32[16,512]{1,0:T(8,128)S(1)} %dynamic-slice_bitcast_fusion.2, pred[512,1024]{1,0:T(8,128)(4,1)S(1)} %broadcast_compare_fusion.5, pred[]{:T(512)S(6)} %compare.3, ...), kind=kOutput, calls=%fused_computation.23.clone.1 | convolution fusion | flops 1109393408 | bytes 43548676 | tf_op jit(solution)/shard_map/while/body/eval_jaxpr/while/body/eval_jaxpr/hqk,qhd->khd/dot_general | solution.py:105
  611.1 25.9 %multiply_reduce_fusion.6 = (f32[16,512]{1,0:T(8,128)S(1)}, f32[16,512,1024]{2,1,0:T(8,128)}) fusion(f32[16,512,1024]{2,1,0:T(8,128)} %fusion.116, f32[16,512]{1,0:T(8,128)S(1)} %dynamic-slice_bitcast_fusion.2, pred[512,1024]{1,0:T(8,128)(4,1)S(1)} %broadcast_compare_fusion.5, bf16[1024,16,64]{0,2,1:T(8,128)(2,1)} %get-tuple-element.622, ...), kind=kOutput, calls=%fused_computation.18.clone.1 | convolution fusion | flops 1115676672 | bytes 70844416 | tf_op jit(solution)/shard_map/while/body/eval_jaxpr/while/body/eval_jaxpr/qhd,khd->hqk/dot_general | solution.py:91
  637.0 27.8 %multiply_convert_fusion.3 = bf16[16,512,1024]{2,1,0:T(8,128)(2,1)} fusion(f32[16,512,1024]{2,1,0:T(8,128)} %get-tuple-element.557, f32[16,512,1024]{2,1,0:T(8,128)} %fusion.116, f32[16,512]{1,0:T(8,128)S(1)} %get-tuple-element.558, f32[16,512]{1,0:T(8,128)S(1)} %dynamic-slice_bitcast_fusion.2, pred[512,1024]{1,0:T(8,128)(4,1)S(1)} %broadcast_compare_fusion.5), kind=kLoop, calls=%fused_computation.17.clone.1 | loop fusion | flops 50331648 | bytes 84475904 | tf_op jit(solution)/shard_map/while/body/eval_jaxpr/while/body/eval_jaxpr/convert_element_type | solution.py:95
  664.7 10.6 convolution_multiply_fusion.2
  676.6 7.8 bitcast_add_fusion.4
  692.4 4.6 copy.93
  697.1 4.0 fusion.62
  703.7 11.9 %convert_bitcast_fusion = bf16[1024,3072]{0,1:T(8,128)(2,1)} fusion(bf16[1024,1024]{1,0:T(8,128)(2,1)} %copy.95, bf16[1024,1024]{1,0:T(8,128)(2,1)} %copy.94, bf16[1024,1024]{1,0:T(8,128)(2,1)} %bitcast.150, bf16[1,1024,1024]{2,1,0:T(8,128)(2,1)} %param.21), kind=kOutput, calls=%fused_computation.52 | convolution fusion | flops 6464471040 | bytes 14680064 | tf_op jit(solution)/shard_map/dot_general | solution.py:28
  715.6 8.7 copy.104
  724.9 6.5 convolution_convert_fusion.2
  731.5 15.4 %convolution_convert_fusion.1 = bf16[1024,4096]{1,0:T(8,128)(2,1)} fusion(bf16[1024,4096]{1,0:T(8,128)(2,1)} %get-tuple-element.432, f32[1024,1024]{0,1:T(8,128)} %copy-done.9, f32[1024]{0:T(1024)S(1)} %bitcast.171, f32[1024]{0:T(1024)S(1)} %bitcast.164, f32[1024]{0:T(1024)S(1)} %copy-done.31, f32[1024]{0:T(1024)S(1)} %copy-done.22), kind=kOutput, calls=%fused_computation.50 | convolution fusion | flops 8599371776 | bytes 20987904 | tf_op jit(solution)/shard_map/dot_general | solution.py:28
  747.7 15.5 %convolution_convert_fusion = bf16[4096,1024]{1,0:T(8,128)(2,1)} fusion(bf16[1024,4096]{1,0:T(8,128)(2,1)} %get-tuple-element.426, f32[1024,1024]{0,1:T(8,128)} %copy-done.11, f32[1024]{0:T(1024)S(1)} %copy-done.27), kind=kOutput, calls=%fused_computation.49 | convolution fusion | flops 8596226048 | bytes 20975616 | tf_op jit(solution)/shard_map/dot_general | solution.py:28
  763.3 31.0 %reduce-scatter.13.cloned.1.call-done = bf16[128,3072]{1,0:T(8,128)(2,1)} async-done(((bf16[1024,3072]{1,0:T(8,128)(2,1)}), bf16[128,3072]{1,0:T(8,128)(2,1)}) %reduce-scatter.13.cloned.1.call-update) | async-done | bytes 786448
  796.5 34.1 %reduce-scatter.7.cloned.1.call-done = bf16[128,1024]{1,0:T(8,128)(2,1)} async-done(((bf16[1024,1024]{1,0:T(8,128)(2,1)}), bf16[128,1024]{1,0:T(8,128)(2,1)}) %reduce-scatter.7.cloned.1.call-update) | async-done | bytes 262160 | tf_op jit(solution)/shard_map/reduce_scatter | solution.py:265
  830.7 90.5 %reduce-scatter.9.cloned.1.call-done = bf16[128,4096]{1,0:T(8,128)(2,1)} async-done(((bf16[1024,4096]{1,0:T(8,128)(2,1)}), bf16[128,4096]{1,0:T(8,128)(2,1)}) %reduce-scatter.9.cloned.1.call-update) | async-done | bytes 1048592 | tf_op jit(solution)/shard_map/reduce_scatter | solution.py:277
  921.2 90.3 %reduce-scatter.11.cloned.1.call-done = bf16[512,1024]{1,0:T(8,128)(2,1)} async-done(((bf16[4096,1024]{1,0:T(8,128)(2,1)}), bf16[512,1024]{1,0:T(8,128)(2,1)}) %reduce-scatter.11.cloned.1.call-update) | async-done | bytes 1048592 | tf_op jit(solution)/shard_map/reduce_scatter | solution.py:283
  1018.5 13.4 %add_bitcast_fusion = f32[1,1024,1024]{1,2,0:T(8,128)} fusion(f32[1024,1024]{0,1:T(8,128)} %copy-done.7, f32[1024]{0:T(1024)S(1)} %copy-done.29, bf16[1024,3072]{1,0:T(8,128)(2,1)} %all-gather.19.cloned.1.call-done, bf16[1024,1024]{1,0:T(8,128)(2,1)} %copy.95, bf16[1024,1024]{1,0:T(8,128)(2,1)} %copy.94, bf16[1024,1024]{1,0:T(8,128)(2,1)} %bitcast.151), kind=kOutput, calls=%fused_computation.69 | convolution fusion | flops 6463422464 | bytes 20975616 | tf_op jit(solution)/shard_map/dot_general | solution.py:34
  1031.9 5.4 copy.98
  1041.3 26.0 %all-reduce.9 = (bf16[1024]{0:T(1024)(128)(2,1)S(1)}, bf16[1024]{0:T(1024)(128)(2,1)S(1)}, bf16[1024]{0:T(1024)(128)(2,1)S(1)}, bf16[1024]{0:T(1024)(128)(2,1)S(...) all-reduce(bf16[1024]{0:T(1024)(128)(2,1)S(1)} %reduce_sum.183, ...), channel_id=3, replica_groups=mesh['grp'=4,'shard'=8] {'shard'}, use_global_device_ids=true, to_apply=%region_18.19.clone | all-reduce | flops 12288 | bytes 49152
  1067.9 10.2 all-reduce.10
  1082.8 19.1 %all-reduce.14.cloned.1.call-done = (bf16[128,3072]{0,1:T(8,128)(2,1)}, bf16[128,1024]{1,0:T(8,128)(2,1)}, bf16[128,4096]{1,0:T(8,128)(2,1)}, bf16[512,1024]{1,0:T(8,128)(2,1)}) async-done(((bf16[128,3072]{0,1:T(8,128)(2,1)}, bf16[128,1024]{1,0:T(8,128)(2,1)}, bf16[128,4096]{1,0:T(8,128)(2,1)}, bf16[512,1024]{1,0:T(8,128)(2,1)}), (bf16[128,3072]{0,1:T(8,128)(2,1)}, bf16[128,1024]{1,0:T(8,128)(2,1)}, ...) | async-done | bytes 3145744 | tf_op jit(solution)/shard_map/psum | solution.py:297
  (239 shorter events, 77.5 us)
Async XLA Ops:
  7.2 61.5 %copy-start.43 = (bf16[512]{0:T(512)(128)(2,1)S(1)}, bf16[512]{0:T(512)(128)(2,1)}, u32[]{:S(2)}) copy-start(bf16[512]{0:T(512)(128)(2,1)} %param.33) | copy-start | bytes 3076
  7.2 62.0 %copy-start.18 = (s32[1,1024]{1,0:T(1,128)S(1)}, s32[1,1024]{1,0:T(1,128)}, u32[]{:S(2)}) copy-start(s32[1,1024]{1,0:T(1,128)} %param.22) | copy-start | bytes 12292
  7.2 62.7 %copy-start.36 = (s32[1,1024]{1,0:T(1,128)S(1)}, s32[1,1024]{1,0:T(1,128)}, u32[]{:S(2)}) copy-start(s32[1,1024]{1,0:T(1,128)} %param.23) | copy-start | bytes 12292
  7.2 63.3 %copy-start.44 = (bf16[128]{0:T(256)(128)(2,1)S(1)}, bf16[128]{0:T(256)(128)(2,1)}, u32[]{:S(2)}) copy-start(bf16[128]{0:T(256)(128)(2,1)} %param.26) | copy-start | bytes 772
  7.2 73.8 %copy-start.45 = (bf16[128]{0:T(256)(128)(2,1)S(1)}, bf16[128]{0:T(256)(128)(2,1)}, u32[]{:S(2)}) copy-start(bf16[128]{0:T(256)(128)(2,1)} %param.27) | copy-start | bytes 772
  7.2 82.5 %copy-start.46 = (bf16[128]{0:T(256)(128)(2,1)S(1)}, bf16[128]{0:T(256)(128)(2,1)}, u32[]{:S(2)}) copy-start(bf16[128]{0:T(256)(128)(2,1)} %param.29) | copy-start | bytes 772
  7.2 93.4 %copy-start.47 = (bf16[128]{0:T(256)(128)(2,1)S(1)}, bf16[128]{0:T(256)(128)(2,1)}, u32[]{:S(2)}) copy-start(bf16[128]{0:T(256)(128)(2,1)} %param.30) | copy-start | bytes 772
  7.3 102.6 %copy-start.48 = (bf16[128]{0:T(256)(128)(2,1)S(1)}, bf16[128]{0:T(256)(128)(2,1)}, u32[]{:S(2)}) copy-start(bf16[128]{0:T(256)(128)(2,1)} %param.31) | copy-start | bytes 772
  7.3 113.2 %copy-start.49 = (bf16[128]{0:T(256)(128)(2,1)S(1)}, bf16[128]{0:T(256)(128)(2,1)}, u32[]{:S(2)}) copy-start(bf16[128]{0:T(256)(128)(2,1)} %param.35) | copy-start | bytes 772
  7.3 122.4 %copy-start.50 = (bf16[128]{0:T(256)(128)(2,1)S(1)}, bf16[128]{0:T(256)(128)(2,1)}, u32[]{:S(2)}) copy-start(bf16[128]{0:T(256)(128)(2,1)} %param.36) | copy-start | bytes 772
  7.3 133.0 %copy-start.51 = (bf16[128]{0:T(256)(128)(2,1)S(1)}, bf16[128]{0:T(256)(128)(2,1)}, u32[]{:S(2)}) copy-start(bf16[128]{0:T(256)(128)(2,1)} %param.37) | copy-start | bytes 772
  7.3 155.6 %copy-start.15 = (bf16[1,1024,1024]{2,1,0:T(8,128)(2,1)S(1)}, bf16[1,1024,1024]{2,1,0:T(8,128)(2,1)}, u32[]{:S(2)}) copy-start(bf16[1,1024,1024]{2,1,0:T(8,128)(2,1)} %param.24) | copy-start | bytes 6291460
  7.3 30.3 %all-gather.17.cloned.1.call-start = ((), (), s32[]{:S(2)}) async-start(), calls=%async_computation.4 | async-start | bytes 1769472 | tf_op jit(solution)/shard_map/all_gather | solution.py:143
  8.0 60.5 %all-gather.23.cloned.1.call-start = ((), (), s32[]{:S(2)}) async-start(), calls=%async_computation.7 | async-start | bytes 2359296 | tf_op jit(solution)/shard_map/all_gather | solution.py:145
  8.8 160.8 %all-gather.27.cloned.1.call-start = ((), (), s32[]{:S(2)}) async-start(), calls=%async_computation.9 | async-start | bytes 2359296 | tf_op jit(solution)/shard_map/all_gather | solution.py:146
  9.5 161.0 %all-gather.19.cloned.1.call-start = ((), (), s32[]{:S(2)}) async-start(), calls=%async_computation.5 | async-start | bytes 7864320 | tf_op jit(solution)/shard_map/all_gather | solution.py:158
  37.6 262.8 %all-gather.21.cloned.1.call-start = ((), (), s32[]{:S(2)}) async-start(), calls=%async_computation.6 | async-start | bytes 2621440 | tf_op jit(solution)/shard_map/all_gather | solution.py:159
  54.2 254.5 %all-gather.25.cloned.1.call-start = ((), (), s32[]{:S(2)}) async-start(), calls=%async_computation.8 | async-start | bytes 10485760 | tf_op jit(solution)/shard_map/all_gather | solution.py:160
  68.6 317.5 %all-gather.29.cloned.1.call-start = ((), (), s32[]{:S(2)}) async-start(), calls=%async_computation.10 | async-start | bytes 10485760 | tf_op jit(solution)/shard_map/all_gather | solution.py:161
  165.5 5.0 copy-start.16
  169.6 624.6 %reduce-scatter.13.cloned.1.call-start = ((), (), s32[]{:S(2)}) async-start(), calls=%async_computation.14 | async-start | bytes 7077888
  200.8 99.6 %copy-start.40 = (f32[8,1,128]{2,1,0:T(1,128)S(1)}, f32[8,1,128]{2,1,0:T(1,128)}, u32[]{:S(2)}) copy-start(f32[8,1,128]{2,1,0:T(1,128)} %convert_element_type.257) | copy-start | bytes 12292
  218.0 15.8 %copy-start.4 = (bf16[1024,16,64]{0,2,1:T(8,128)(2,1)S(1)}, bf16[1024,16,64]{0,2,1:T(8,128)(2,1)}, u32[]{:S(2)}) copy-start(bf16[1024,16,64]{0,2,1:T(8,128)(2,1)} %get-tuple-element.584) | copy-start | bytes 6291460 | tf_op jit(solution)/shard_map/while/body/eval_jaxpr/while
  267.5 15.1 %copy-start.4 = (bf16[1024,16,64]{0,2,1:T(8,128)(2,1)S(1)}, bf16[1024,16,64]{0,2,1:T(8,128)(2,1)}, u32[]{:S(2)}) copy-start(bf16[1024,16,64]{0,2,1:T(8,128)(2,1)} %get-tuple-element.584) | copy-start | bytes 6291460 | tf_op jit(solution)/shard_map/while/body/eval_jaxpr/while
  306.1 144.9 %copy-start.21 = (f32[1024]{0:T(1024)}, f32[1024]{0:T(1024)S(1)}, u32[]{:S(2)}) copy-start(f32[1024]{0:T(1024)S(1)} %broadcast_multiply_fusion.1) | copy-start | bytes 12292
  308.6 142.4 %copy-start.30 = (f32[1024]{0:T(1024)}, f32[1024]{0:T(1024)S(1)}, u32[]{:S(2)}) copy-start(f32[1024]{0:T(1024)S(1)} %fusion.53) | copy-start | bytes 12292
  308.7 77.4 %copy-start.39 = (f32[8,1,128]{2,1,0:T(1,128)S(1)}, f32[8,1,128]{2,1,0:T(1,128)}, u32[]{:S(2)}) copy-start(f32[8,1,128]{2,1,0:T(1,128)} %convert_element_type.261) | copy-start | bytes 12292
  402.3 3.4 copy-start.5
  402.3 3.4 copy-start.19
  402.3 3.5 copy-start.20
  405.1 5.2 copy-start.6
  405.2 5.2 copy-start.23
  405.8 7.8 slice-start
  410.4 3.2 slice-start.1
  413.5 21.8 %copy-start.11 = (f32[1024,1024]{0,1:T(8,128)}, f32[1024,1024]{0,1:T(8,128)S(1)}, u32[]{:S(2)}) copy-start(f32[1024,1024]{0,1:T(8,128)S(1)} %get-tuple-element.414) | copy-start | bytes 12582916
  413.6 21.8 %copy-start.26 = (f32[1024]{0:T(1024)}, f32[1024]{0:T(1024)S(1)}, u32[]{:S(2)}) copy-start(f32[1024]{0:T(1024)S(1)} %negate_multiply_fusion.1) | copy-start | bytes 12292
  413.6 21.8 %copy-start.10 = (f32[1024,1024]{0,1:T(8,128)S(1)}, f32[1024,1024]{0,1:T(8,128)}, u32[]{:S(2)}) copy-start(f32[1024,1024]{0,1:T(8,128)} %copy-done.9) | copy-start | bytes 12582916
  451.0 3.1 copy-start.52
  452.1 5.8 copy-start.28
  469.8 15.2 %copy-start.1 = (bf16[1024,16,64]{0,2,1:T(8,128)(2,1)}, bf16[1024,16,64]{0,2,1:T(8,128)(2,1)S(1)}, u32[]{:S(2)}) copy-start(bf16[1024,16,64]{0,2,1:T(8,128)(2,1)S(1)} %get-tuple-element.619) | copy-start | bytes 6291460 | tf_op jit(solution)/shard_map/while/body/eval_jaxpr/while
  556.2 11.9 %copy-start = (bf16[16,512,1024]{2,1,0:T(8,128)(2,1)S(1)}, bf16[16,512,1024]{2,1,0:T(8,128)(2,1)}, u32[]{:S(2)}) copy-start(bf16[16,512,1024]{2,1,0:T(8,128)(2,1)} %multiply_convert_fusion.3) | copy-start | bytes 50331652 | tf_op jit(solution)/shard_map/while/body/eval_jaxpr/while
  568.1 6.6 copy-start.3
  568.1 6.6 copy-start.12
  577.1 15.2 %copy-start.1 = (bf16[1024,16,64]{0,2,1:T(8,128)(2,1)}, bf16[1024,16,64]{0,2,1:T(8,128)(2,1)S(1)}, u32[]{:S(2)}) copy-start(bf16[1024,16,64]{0,2,1:T(8,128)(2,1)S(1)} %get-tuple-element.619) | copy-start | bytes 6291460 | tf_op jit(solution)/shard_map/while/body/eval_jaxpr/while
  664.7 11.9 %copy-start = (bf16[16,512,1024]{2,1,0:T(8,128)(2,1)S(1)}, bf16[16,512,1024]{2,1,0:T(8,128)(2,1)}, u32[]{:S(2)}) copy-start(bf16[16,512,1024]{2,1,0:T(8,128)(2,1)} %multiply_convert_fusion.3) | copy-start | bytes 50331652 | tf_op jit(solution)/shard_map/while/body/eval_jaxpr/while
  676.6 7.8 copy-start.3
  676.6 7.8 copy-start.12
  724.2 7.3 copy-start.22
  724.3 7.3 copy-start.25
  724.3 7.3 copy-start.31
  724.3 7.3 copy-start.38
  724.3 106.4 %reduce-scatter.7.cloned.1.call-start = ((), (), s32[]{:S(2)}) async-start(), calls=%async_computation.11 | async-start | bytes 2359296 | tf_op jit(solution)/shard_map/reduce_scatter | solution.py:265
  731.5 189.7 %reduce-scatter.9.cloned.1.call-start = ((), (), s32[]{:S(2)}) async-start(), calls=%async_computation.12 | async-start | bytes 9437184 | tf_op jit(solution)/shard_map/reduce_scatter | solution.py:277
  747.0 264.4 %reduce-scatter.11.cloned.1.call-start = ((), (), s32[]{:S(2)}) async-start(), calls=%async_computation.13 | async-start | bytes 9437184 | tf_op jit(solution)/shard_map/reduce_scatter | solution.py:283
  763.2 248.3 %copy-start.53 = (u32[32]{0:T(128)S(1)}, u32[32]{0:T(128)}, u32[]{:S(2)}) copy-start(u32[32]{0:T(128)} %constant.115) | copy-start | bytes 388
  763.2 252.6 %copy-start.14 = (bf16[1,1024,1024]{1,2,0:T(8,128)(2,1)S(1)}, bf16[1,1024,1024]{1,2,0:T(8,128)(2,1)}, u32[]{:S(2)}) copy-start(bf16[1,1024,1024]{1,2,0:T(8,128)(2,1)} %get-tuple-element.421) | copy-start | bytes 6291460
  763.2 338.7 %all-reduce.14.cloned.1.call-start = ((), (), s32[]{:S(2)}) async-start(), calls=%async_computation.15 | async-start | bytes 6291456 | tf_op jit(solution)/shard_map/psum | solution.py:297
  1037.3 3.6 copy-start.8
  1037.3 3.9 copy-start.33
  1037.3 3.9 copy-start.34
  1037.3 3.9 copy-start.35
  1037.3 4.0 copy-start.41
  1037.3 4.0 copy-start.42
  1101.9 7.2 copy-start.17
  (11 other events, 22.2 us)
Sparse Core Ops, SparseCore 0:
  9.8 27.7 all-gather.16
  39.2 29.3 all-gather.22
  70.1 28.9 all-gather.26
  100.8 69.6 all-gather.18
  172.2 35.1 all-gather.20
  209.1 87.6 all-gather.24
  298.6 87.4 all-gather.28
  724.4 69.8 reduce-scatter.12
  796.5 34.0 reduce-scatter.6
  832.8 88.3 reduce-scatter.8
  923.5 87.9 reduce-scatter.10
  1015.3 86.6 all-reduce.13
where the time goes:
time: 1130 us; the launch traced here: 1120 us
  matrix products  370 us (33%)
  waiting for transfers between devices  367 us (32%)
  blocking collectives  141 us (12%)
  other arithmetic  131 us (12%)
  local copies, waits for them, and re-layouts  90.5 us (8%)
  between operations  16.4 us (1%)
    reduce_scatter x1, waiting for transfers between devices, on_device(): lax.psum_scatter(w_in_grad.astype(jnp.bfloat16), 'shard', scatter_dimensi...  90.5 us
    reduce_scatter x1, waiting for transfers between devices, on_device(): lax.psum_scatter(w_out_grad.astype(jnp.bfloat16), 'shard', scatter_dimens...  90.3 us
    dot_general x4, matrix products, one_block(): jnp.einsum('qhd,khd->hqk', query_part, key_heads, preferred_element_type=...  61.2 us
    all_gather x1, waiting for transfers between devices, on_device(): lax.all_gather(within[3], 'grp', axis=1, tiled=True)  56.8 us
    convert_element_type x2, other arithmetic, one_block(): score_grad = (probs * (prob_grad - row_dot)).astype(jnp.bfloat16)  55.5 us
    dot_general x4, matrix products, contract_cols(): lax.dot_general(left, right, (((1,), (1,)), ((), ())), preferred_element_...  54.6 us
    dot_general x2, matrix products, one_block(): jnp.einsum('qhd,khd->hqk', grad_part, value_heads, preferred_element_type...  51.8 us
    dot_general x4, matrix products, contract_rows(): lax.dot_general(left, right, (((0,), (0,)), ((), ())), preferred_element_...  49.4 us
  transfers between devices with their start and end apart: 12, of which 9 were waited for; matrix products, arithmetic and copies ran while one was open for 22% of the time, Pallas kernels for 0%

commit v1 on v0

--- a/solution.py
+++ b/solution.py
@@ -1,8 +1,11 @@
+import functools
 import math
 
 import jax
 import jax.numpy as jnp
 from jax import lax
+from jax.experimental import pallas as pl
+from jax.experimental.pallas import tpu as pltpu
 from jax.sharding import PartitionSpec as P
 
 H = 16
@@ -327,9 +330,545 @@
     )
 
 
+NT = (((1,), (1,)), ((), ()))
+NN = (((1,), (0,)), ((), ()))
+TN = (((0,), (0,)), ((), ()))
+LANES = 128
+AXES = ("grp", "shard")
+
+
+def mxu(left, right, dims):
+    return lax.dot_general(left, right, dims, preferred_element_type=jnp.float32)
+
+
+def params(megabytes=60):
+    return pltpu.CompilerParams(vmem_limit_bytes=megabytes << 20)
+
+
+def attention_forward_kernel(q_ref, k_ref, v_ref, seg_col, seg_row, out_ref, lse_ref, *, rows):
+    length = q_ref.shape[0]
+    first = lax.broadcasted_iota(jnp.int32, (1, LANES), 1) < HD
+    keys = k_ref[...]
+    values = v_ref[...]
+    zero = jnp.zeros_like(keys)
+    head_keys = (jnp.where(first, keys, zero), jnp.where(first, zero, keys))
+    key_segments = seg_col[...]
+    for block in range(length // rows):
+        here = pl.ds(block * rows, rows)
+        q = q_ref[here, :]
+        allowed = key_segments == seg_row[:, here]
+        outs = []
+        for head in range(2):
+            scores = mxu(head_keys[head], q, NT)
+            scores = jnp.where(allowed, scores, masked_score)
+            top = jnp.max(scores, 0, keepdims=True)
+            powers = jnp.exp(scores - top)
+            total = jnp.sum(powers, 0, keepdims=True)
+            part = mxu(powers.astype(jnp.bfloat16), values, TN)
+            outs.append(part * jnp.transpose(jnp.broadcast_to(1.0 / total, (LANES, rows))))
+            lse_ref[0, head : head + 1, here] = top + jnp.log(total)
+        out_ref[here, :] = jnp.where(first, outs[0], outs[1]).astype(jnp.bfloat16)
+
+
+def attention_forward(q, k, v, seg_col, seg_row):
+    length, width = q.shape
+    pairs = width // LANES
+    rows = min(512, length)
+    pair = pl.BlockSpec((length, LANES), lambda j: (0, j))
+    return pl.pallas_call(
+        functools.partial(attention_forward_kernel, rows=rows),
+        grid=(pairs,),
+        in_specs=[
+            pair,
+            pair,
+            pair,
+            pl.BlockSpec((length, 1), lambda j: (0, 0)),
+            pl.BlockSpec((1, length), lambda j: (0, 0)),
+        ],
+        out_specs=[pair, pl.BlockSpec((1, 2, length), lambda j: (j, 0, 0))],
+        out_shape=[
+            jax.ShapeDtypeStruct((length, width), jnp.bfloat16),
+            jax.ShapeDtypeStruct((pairs, 2, length), jnp.float32),
+        ],
+        compiler_params=params(),
+        cost_estimate=pl.CostEstimate(
+            flops=16 * length * length * width, bytes_accessed=8 * length * width, transcendentals=0
+        ),
+        name="attn_fwd",
+    )(q, k, v, seg_col, seg_row)
+
+
+def attention_backward_kernel(
+    q_ref, k_ref, v_ref, o_ref, do_ref, seg_col, seg_row, lse_ref, grad_ref, sum_ref, *, rows
+):
+    length = q_ref.shape[0]
+    lane = lax.broadcasted_iota(jnp.int32, (1, LANES), 1)
+    first = lane < HD
+    pick = (
+        lax.broadcasted_iota(jnp.int32, (8, LANES), 0)
+        == lax.broadcasted_iota(jnp.int32, (8, LANES), 1) // HD
+    ).astype(jnp.float32)
+    keys = k_ref[...]
+    values = v_ref[...]
+    zero = jnp.zeros_like(keys)
+    head_keys = (jnp.where(first, keys, zero), jnp.where(first, zero, keys))
+    head_values = (jnp.where(first, values, zero), jnp.where(first, zero, values))
+    key_segments = seg_col[...]
+    key_sum = [None, None]
+    value_sum = [None, None]
+    query_total = jnp.zeros((1, LANES), jnp.float32)
+    for block in range(length // rows):
+        here = pl.ds(block * rows, rows)
+        q = q_ref[here, :]
+        do = do_ref[here, :]
+        allowed = key_segments == seg_row[:, here]
+        dots = lax.dot_general(
+            pick,
+            do.astype(jnp.float32) * o_ref[here, :].astype(jnp.float32),
+            NT,
+            precision=lax.Precision.HIGHEST,
+            preferred_element_type=jnp.float32,
+        )
+        parts = []
+        for head in range(2):
+            scores = mxu(head_keys[head], q, NT)
+            scores = jnp.where(allowed, scores, masked_score)
+            probs = jnp.exp(scores - lse_ref[0, head : head + 1, here])
+            prob_grad = mxu(head_values[head], do, NT)
+            score_grad = (probs * (prob_grad - dots[head : head + 1, :])).astype(jnp.bfloat16)
+            value_part = mxu(probs.astype(jnp.bfloat16), do, NN)
+            key_part = mxu(score_grad, q, NN)
+            value_sum[head] = value_part if block == 0 else value_sum[head] + value_part
+            key_sum[head] = key_part if block == 0 else key_sum[head] + key_part
+            parts.append(mxu(score_grad, keys, TN))
+        query_grad = jnp.where(first, parts[0], parts[1]) * (1.0 / math.sqrt(HD))
+        query_total = query_total + jnp.sum(query_grad, 0, keepdims=True)
+        grad_ref[0, here, :] = query_grad.astype(jnp.bfloat16)
+    grad_ref[1, :, :] = jnp.where(first, key_sum[0], key_sum[1]).astype(jnp.bfloat16)
+    value_grad = jnp.where(first, value_sum[0], value_sum[1])
+    grad_ref[2, :, :] = value_grad.astype(jnp.bfloat16)
+    sum_ref[0:1, :] = query_total
+    sum_ref[1:2, :] = jnp.sum(value_grad, 0, keepdims=True)
+
+
+def attention_backward(q, k, v, out, out_grad, seg_col, seg_row, lse, start, pairs):
+    length, width = q.shape
+    rows = min(256, length)
+    pair = pl.BlockSpec((length, LANES), lambda j: (0, j + start))
+    return pl.pallas_call(
+        functools.partial(attention_backward_kernel, rows=rows),
+        grid=(pairs,),
+        in_specs=[
+            pair,
+            pair,
+            pair,
+            pair,
+            pair,
+            pl.BlockSpec((length, 1), lambda j: (0, 0)),
+            pl.BlockSpec((1, length), lambda j: (0, 0)),
+            pl.BlockSpec((1, 2, length), lambda j: (j + start, 0, 0)),
+        ],
+        out_specs=[
+            pl.BlockSpec((3, length, LANES), lambda j: (0, 0, j)),
+            pl.BlockSpec((2, LANES), lambda j: (0, j)),
+        ],
+        out_shape=[
+            jax.ShapeDtypeStruct((3, length, pairs * LANES), jnp.bfloat16),
+            jax.ShapeDtypeStruct((2, pairs * LANES), jnp.float32),
+        ],
+        compiler_params=params(),
+        cost_estimate=pl.CostEstimate(
+            flops=40 * length * length * pairs * LANES,
+            bytes_accessed=16 * length * pairs * LANES,
+            transcendentals=0,
+        ),
+        name="attn_bwd",
+    )(q, k, v, out, out_grad, seg_col, seg_row, lse)
+
+
+class Place:
+    def __init__(self, groups, shards):
+        self.groups = groups
+        self.shards = shards
+        self.chips = shards // 2
+        grp = lax.axis_index("grp")
+        shard = lax.axis_index("shard")
+        self.grp = grp
+        self.shard = shard
+        self.core = shard % 2
+        self.chip = shard // 2
+        self.scalars = jnp.stack([self.core, self.chip, grp]).astype(jnp.int32)
+
+    def swap(self, array, grp=0, chip=0, core=0):
+        mask = grp * self.shards + chip * 2 + core
+        pairs = [(i, i ^ mask) for i in range(self.groups * self.shards)]
+        return lax.ppermute(array, AXES, pairs)
+
+
+def gather_pieces(place, piece):
+    rows = piece.shape[0]
+    half = rows // 2
+    along = [piece] + [place.swap(piece, chip=k) for k in range(1, place.chips)]
+    upper = [jnp.stack([p[:half] for p in along]), None, None, None]
+    lower = [jnp.stack([p[half:] for p in along]), None, None, None]
+    upper[1] = place.swap(upper[0], grp=1)
+    lower[2] = place.swap(lower[0], grp=2)
+    upper[2] = place.swap(upper[0], grp=2)
+    lower[1] = place.swap(lower[0], grp=1)
+    upper[3] = place.swap(upper[1], grp=2)
+    lower[3] = place.swap(lower[2], grp=1)
+    mine = upper + lower
+    return mine + [place.swap(p, core=1) for p in mine]
+
+
+def assemble_kernel(where, *refs, groups):
+    *pieces, whole = refs
+    _, half, cols = pieces[0].shape
+    core, grp = where[0], where[2]
+    for n, piece in enumerate(pieces):
+        other_core, lower, other_grp = n // (2 * groups), (n // groups) % 2, n % groups
+        col = pl.multiple_of((grp ^ other_grp) * cols, LANES)
+        row = pl.multiple_of(((core ^ other_core) * 2 + lower) * half, half)
+        whole[pl.ds(row, half), pl.ds(col, cols)] = piece[0]
+
+
+def assemble(place, pieces, name):
+    chips, half, cols = pieces[0].shape
+    shape = (chips * 4 * half, place.groups * cols)
+    return pl.pallas_call(
+        functools.partial(assemble_kernel, groups=place.groups),
+        grid_spec=pltpu.PrefetchScalarGridSpec(
+            num_scalar_prefetch=1,
+            grid=(chips,),
+            in_specs=[pl.BlockSpec((1, half, cols), lambda i, s: (i ^ s[1], 0, 0))] * len(pieces),
+            out_specs=pl.BlockSpec((4 * half, shape[1]), lambda i, s: (i, 0)),
+        ),
+        out_shape=jax.ShapeDtypeStruct(shape, jnp.bfloat16),
+        compiler_params=params(),
+        cost_estimate=pl.CostEstimate(
+            flops=0, bytes_accessed=4 * shape[0] * shape[1], transcendentals=0
+        ),
+        name="assemble_" + name,
+    )(place.scalars, *pieces)
+
+
+def weight_grad_kernel(where, left_ref, right_ref, *refs, own, rows, groups, split):
+    received = None
+    if own:
+        received, *outs = refs
+    else:
+        outs = refs
+    core, grp = where[0], where[2]
+    keep = core if own else 1 - core
+    chips = left_ref.shape[1] // (2 * rows)
+    lefts = []
+    for k in range(chips):
+        even = left_ref[:, 2 * k * rows : (2 * k + 1) * rows]
+        odd = left_ref[:, (2 * k + 1) * rows : (2 * k + 2) * rows]
+        lefts.append(jnp.where(keep == 0, even, odd))
+    left = lefts[0] if chips == 1 else jnp.concatenate(lefts, 1)
+    left = left.T
+    half = rows // 2
+
+    def emit(slot, result):
+        result = result.reshape(chips, 2, half, result.shape[-1])
+        if own:
+            pos = 0 if split else slot
+            result = result + received[pos].astype(jnp.float32)
+            result = result.astype(jnp.bfloat16)
+            for lower in range(2):
+                outs[slot + lower * groups][...] = result[:, lower]
+        else:
+            outs[0][0 if split else slot] = result.astype(jnp.bfloat16)
+
+    if split:
+        if len(right_ref.shape) == 3:
+            result = jnp.concatenate(
+                [mxu(left, right_ref[n], NN) for n in range(right_ref.shape[0])], 1
+            )
+        else:
+            result = mxu(left, right_ref[...], NN)
+        if own:
+            for slot in range(groups):
+                pl.when(pl.program_id(1) == slot)(functools.partial(emit, slot, result))
+        else:
+            emit(0, result)
+    else:
+        cols = right_ref.shape[1] // groups
+        for slot in range(groups):
+            at = pl.multiple_of((grp ^ slot) * cols, LANES)
+            emit(slot, mxu(left, right_ref[:, pl.ds(at, cols)], NN))
+
+
+def weight_grad(place, left, right, received, split, name):
+    tokens, height = left.shape
+    groups, chips = place.groups, place.chips
+    rows = height // place.shards
+    half = rows // 2
+    parts = right.shape[0] if right.ndim == 3 else 1
+    width = right.shape[-1] * parts
+    cols = width // groups
+    own = received is not None
+    step_chips = chips if split else max(1, 1024 // (2 * rows))
+    steps = chips // step_chips
+    if split:
+        grid = (steps, groups)
+        if parts > 1:
+            right_spec = pl.BlockSpec(
+                (parts, tokens, cols // parts), lambda i, j, s: (0, 0, j ^ s[2])
+            )
+        else:
+            right_spec = pl.BlockSpec((tokens, cols), lambda i, j, s: (0, j ^ s[2]))
+        passed = pl.BlockSpec((1, step_chips, 2, half, cols), lambda i, j, s: (j, i, 0, 0, 0))
+    else:
+        grid = (steps, 1)
+        right_spec = pl.BlockSpec((tokens, width), lambda i, j, s: (0, 0))
+        passed = pl.BlockSpec((groups, step_chips, 2, half, cols), lambda i, j, s: (0, i, 0, 0, 0))
+    in_specs = [pl.BlockSpec((tokens, step_chips * 2 * rows), lambda i, j, s: (0, i)), right_spec]
+    inputs = [left, right]
+    if own:
+        in_specs.append(passed)
+        inputs.append(received)
+        out_specs = [pl.BlockSpec((step_chips, half, cols), lambda i, j, s: (i, 0, 0))] * (2 * groups)
+        out_shape = [jax.ShapeDtypeStruct((chips, half, cols), jnp.bfloat16)] * (2 * groups)
+    else:
+        out_specs = passed
+        out_shape = jax.ShapeDtypeStruct((groups, chips, 2, half, cols), jnp.bfloat16)
+    return pl.pallas_call(
+        functools.partial(
+            weight_grad_kernel, own=own, rows=rows, groups=groups, split=split
+        ),
+        grid_spec=pltpu.PrefetchScalarGridSpec(
+            num_scalar_prefetch=1, grid=grid, in_specs=in_specs, out_specs=out_specs
+        ),
+        out_shape=out_shape,
+        compiler_params=params(),
+        cost_estimate=pl.CostEstimate(
+            flops=tokens * height * width,
+            bytes_accessed=2 * (tokens * (height + width) + height * width),
+            transcendentals=0,
+        ),
+        name="wgrad_" + name + ("_own" if own else "_sent"),
+    )(place.scalars, *inputs)
+
+
+def add(*terms):
+    total = terms[0].astype(jnp.float32)
+    for term in terms[1:]:
+        total = total + term.astype(jnp.float32)
+    return total.astype(jnp.bfloat16)
+
+
+def reduce_weight(place, left, right, split, name):
+    groups, chips = place.groups, place.chips
+    sent = weight_grad(place, left, right, None, split, name)
+    received = place.swap(sent, core=1)
+    own = weight_grad(place, left, right, received, split, name)
+    upper, lower = own[:groups], own[groups:]
+    upper_1, upper_3 = place.swap(upper[1], grp=1), place.swap(upper[3], grp=1)
+    lower_2, lower_3 = place.swap(lower[2], grp=2), place.swap(lower[3], grp=2)
+    upper_2 = place.swap(add(upper[2], upper_3), grp=2)
+    lower_1 = place.swap(add(lower[1], lower_3), grp=1)
+    mine = jnp.concatenate([add(upper[0], upper_1, upper_2), add(lower[0], lower_2, lower_1)], 1)
+    terms = [lax.dynamic_index_in_dim(mine, place.chip, 0, False)]
+    for k in range(1, chips):
+        outgoing = lax.dynamic_index_in_dim(mine, place.chip ^ k, 0, False)
+        terms.append(place.swap(outgoing, chip=k))
+    share = add(*terms)
+    return replicate(place, share)
+
+
+def replicate(place, share):
+    blocks = [share] + [place.swap(share, grp=k) for k in range(1, place.groups)]
+    blocks = [b.astype(jnp.float32) for b in blocks]
+    ordered = []
+    for g in range(place.groups):
+        block = blocks[0]
+        for k in range(1, place.groups):
+            block = jnp.where((place.grp ^ k) == g, blocks[k], block)
+        ordered.append(block)
+    return ordered
+
+
+def sum_everywhere(place, vector):
+    for how in ({"core": 1}, {"grp": 1}, {"grp": 2}):
+        vector = vector + place.swap(vector, **how)
+    step = 1
+    while step < place.chips:
+        vector = vector + place.swap(vector, chip=step)
+        step *= 2
+    return vector
+
+
+def own_part(place, vector):
+    size = vector.shape[0] // place.shards
+    return lax.dynamic_slice_in_dim(vector, place.shard * size, size)
+
+
+def on_device_permutes(
+    tokens,
+    segment_ids,
+    keep_flag,
+    cotangent,
+    w_qkv,
+    b_query,
+    b_value,
+    w_attn_out,
+    b_attn_out,
+    norm1_gain,
+    norm1_bias,
+    w_in,
+    b_in,
+    w_out,
+    b_out,
+    norm2_gain,
+    norm2_bias,
+    *,
+    groups,
+    shards,
+):
+    place = Place(groups, shards)
+    _, length, width = tokens.shape
+    vectors = (
+        b_query,
+        b_value,
+        b_attn_out,
+        norm1_gain,
+        norm1_bias,
+        b_in,
+        b_out,
+        norm2_gain,
+        norm2_bias,
+    )
+    packed = lax.all_gather(jnp.concatenate(vectors), "shard", axis=0)
+    unpacked = []
+    at = 0
+    for vector in vectors:
+        size = vector.shape[0]
+        unpacked.append(packed[:, at : at + size].reshape(1, -1).astype(jnp.float32))
+        at += size
+    (
+        bias_query,
+        bias_value,
+        bias_attn,
+        gain_one,
+        shift_one,
+        bias_in,
+        bias_out,
+        gain_two,
+        shift_two,
+    ) = unpacked
+    full_qkv = assemble(place, gather_pieces(place, w_qkv), "qkv")
+    full_attn = assemble(place, gather_pieces(place, w_attn_out), "attn")
+    full_in = assemble(place, gather_pieces(place, w_in), "in")
+    full_out = assemble(place, gather_pieces(place, w_out), "out")
+
+    rows = tokens[0]
+    seg_row = segment_ids.reshape(1, length)
+    seg_col = segment_ids.reshape(length, 1)
+    scaling = 1.0 / math.sqrt(HD)
+    mixed_qkv = jnp.dot(rows, full_qkv, preferred_element_type=jnp.float32)
+    queries = ((mixed_qkv[:, :width] + bias_query).astype(jnp.bfloat16) * scaling).astype(
+        jnp.bfloat16
+    )
+    key_rows = mixed_qkv[:, width : 2 * width].astype(jnp.bfloat16)
+    value_rows = (mixed_qkv[:, 2 * width :] + bias_value).astype(jnp.bfloat16)
+    contexts, lse = attention_forward(queries, key_rows, value_rows, seg_col, seg_row)
+    attended = jnp.dot(contexts, full_attn, preferred_element_type=jnp.float32) + bias_attn
+    first_sum = rows.astype(jnp.float32) + attended
+    normed_one, norm_one_back = jax.vjp(norm_layer, first_sum, gain_one, shift_one)
+    normed_low = normed_one.astype(jnp.bfloat16)
+    hidden_pre = jnp.dot(normed_low, full_in, preferred_element_type=jnp.float32) + bias_in
+    hidden, gelu_back = jax.vjp(gelu_exact, hidden_pre)
+    hidden_low = hidden.astype(jnp.bfloat16)
+    second_sum = normed_one + (
+        jnp.dot(hidden_low, full_out, preferred_element_type=jnp.float32) + bias_out
+    )
+    result, norm_two_back = jax.vjp(norm_layer, second_sum, gain_two, shift_two)
+    layer_out = result.astype(jnp.bfloat16)[None]
+
+    masked_cot = cotangent[0].astype(jnp.float32) * keep_flag.reshape(length, 1).astype(jnp.float32)
+    second_grad, gain_two_grad, shift_two_grad = norm_two_back(masked_cot)
+    bias_out_grad = jnp.sum(second_grad, 0)
+    out_low = second_grad.astype(jnp.bfloat16)
+    w_out_grad = reduce_weight(place, hidden_low, out_low, False, "out")
+    hidden_grad = contract_cols(out_low, full_out)
+    (pre_grad,) = gelu_back(hidden_grad)
+    bias_in_grad = jnp.sum(pre_grad, 0)
+    pre_low = pre_grad.astype(jnp.bfloat16)
+    w_in_grad = reduce_weight(place, normed_low, pre_low, True, "in")
+    normed_grad = second_grad + contract_cols(pre_low, full_in)
+    first_grad, gain_one_grad, shift_one_grad = norm_one_back(normed_grad)
+    bias_attn_grad = jnp.sum(first_grad, 0)
+    attn_low = first_grad.astype(jnp.bfloat16)
+    w_attn_grad = reduce_weight(place, contexts, attn_low, False, "attn")
+    context_grad = contract_cols(attn_low, full_attn).astype(jnp.bfloat16)
+    early = (
+        bias_attn_grad,
+        gain_one_grad[0],
+        shift_one_grad[0],
+        bias_in_grad,
+        bias_out_grad,
+        gain_two_grad[0],
+        shift_two_grad[0],
+    )
+    early_sum = sum_everywhere(place, jnp.concatenate(early).reshape(-1, LANES)).reshape(-1)
+    early_parts = []
+    at = 0
+    for vector in early:
+        early_parts.append(own_part(place, early_sum[at : at + vector.shape[0]]))
+        at += vector.shape[0]
+
+    qkv_low, late = attention_backward(
+        queries,
+        key_rows,
+        value_rows,
+        contexts,
+        context_grad,
+        seg_col,
+        seg_row,
+        lse,
+        0,
+        width // LANES,
+    )
+    late_sum = sum_everywhere(place, late)
+    w_qkv_grad = reduce_weight(place, rows, qkv_low, True, "qkv")
+    input_grad = first_grad
+    for n in range(3):
+        input_grad = input_grad + contract_cols(
+            qkv_low[n], full_qkv[:, n * width : (n + 1) * width]
+        )
+    heads = width // groups
+    w_qkv_grad = jnp.concatenate(
+        [block[:, n * heads : (n + 1) * heads] for n in range(3) for block in w_qkv_grad], 1
+    )
+    return (
+        layer_out,
+        input_grad[None],
+        w_qkv_grad,
+        own_part(place, late_sum[0]),
+        own_part(place, late_sum[1]),
+        jnp.concatenate(w_attn_grad, 1),
+        early_parts[0],
+        early_parts[1],
+        early_parts[2],
+        jnp.concatenate(w_in_grad, 1),
+        early_parts[3],
+        jnp.concatenate(w_out_grad, 1),
+        early_parts[4],
+        early_parts[5],
+        early_parts[6],
+    )
+
+
 def solution(mesh):
+    groups, shards = mesh.shape["grp"], mesh.shape["shard"]
+    if groups == 4 and shards == 8:
+        body = functools.partial(on_device_permutes, groups=groups, shards=shards)
+    else:
+        body = on_device
     return jax.shard_map(
-        on_device,
+        body,
         mesh=mesh,
         in_specs=(
             P(("grp", "shard"), None, None),

time: 1130 us -> 682 us (0.60)
  matrix products: 370 us -> 107 us
  Pallas kernels: 0 us -> 187 us
  waiting for transfers between devices: 367 us -> 184 us
  blocking collectives: 141 us -> 14.1 us
  starting transfers between devices: 0.48 us -> 118 us
  other arithmetic: 131 us -> 31 us
  local copies, waits for them, and re-layouts: 90.5 us -> 27.1 us
  between operations: 16.4 us -> 2.7 us
    dot_general x22 -> x4, matrix products: 316 us -> 44.3 us  [the longest x1 15.5 us: on_device_permutes(): jnp.dot(normed_low, full_in, preferred_element_type=jnp.float32) + bias_in]
    reduce_scatter x3 -> x0, waiting for transfers between devices: 215 us -> none  [the longest x1 90.5 us: on_device(): lax.psum_scatter(w_in_grad.astype(jnp.bfloat16), 'shard', scatter_dimensi...]
    pallas_call x0 -> x14, Pallas kernels: none -> 187 us  [the longest x8 72.2 us: weight_grad(): pl.pallas_call(functools.partial(weight_grad_kernel, own=own, rows=rows,...]
    ppermute x0 -> x130, waiting for transfers between devices: none -> 184 us  [swap(): return lax.ppermute(array, AXES, pairs)]
    ppermute x0 -> x130, starting transfers between devices: none -> 118 us  [swap(): return lax.ppermute(array, AXES, pairs)]
    all_gather x7 -> x0, waiting for transfers between devices: 100 us -> none  [the longest x1 56.8 us: on_device(): lax.all_gather(within[3], 'grp', axis=1, tiled=True)]
    all_gather x10 -> x1, blocking collectives: 105 us -> 14.1 us  [on_device_permutes(): packed = lax.all_gather(jnp.concatenate(vectors), 'shard', axis=0)]
    convert_element_type x25 -> x24, other arithmetic: 73.8 us -> 10.8 us  [the longest x20 7.38 us: add(): return total.astype(jnp.bfloat16)]
  transfers between devices with their start and end apart: 12 -> 130, of which waited for: 9 -> 44; matrix products, arithmetic and copies ran while one was open for 22% -> 11% of each run, Pallas kernels for 0% -> 17%
where the time goes in v1:
time: 682 us; the launch traced here: 671 us
  Pallas kernels  187 us (27%)
  waiting for transfers between devices  184 us (27%)
  starting transfers between devices  118 us (17%)
  matrix products  107 us (16%)
  other arithmetic  31 us (5%)
  local copies, waits for them, and re-layouts  27.1 us (4%)
  blocking collectives  14.1 us (2%)
    ppermute x130, waiting for transfers between devices, swap(): return lax.ppermute(array, AXES, pairs)  184 us
    ppermute x130, starting transfers between devices, swap(): return lax.ppermute(array, AXES, pairs)  118 us
    pallas_call x8, Pallas kernels, weight_grad(): pl.pallas_call(functools.partial(weight_grad_kernel, own=own, rows=rows,...  72.2 us
    dot_general x6, matrix products, contract_cols(): lax.dot_general(left, right, (((1,), (1,)), ((), ())), preferred_element_...  62.5 us
    pallas_call x1, Pallas kernels, attention_backward(): pl.pallas_call(functools.partial(attention_backward_kernel, rows=rows), g...  54.6 us
    pallas_call x1, Pallas kernels, attention_forward(): pl.pallas_call(functools.partial(attention_forward_kernel, rows=rows), gr...  33.3 us
    pallas_call x4, Pallas kernels, assemble(): pl.pallas_call(functools.partial(assemble_kernel, groups=place.groups), g...  27.1 us
    unnamed x170, local copies, waits for them, and re-layouts  16 us
  transfers between devices with their start and end apart: 130, of which 44 were waited for; matrix products, arithmetic and copies ran while one was open for 11% of the time, Pallas kernels for 17%

profile of v1, /device:TPU:0, one launch (start us, length us, event | category | flops | bytes accessed | tf_op | source)
XLA Modules:
  0.0 670.7 jit_solution(628201189756588480)
XLA Ops:
  0.7 3.1 collective-permute-start
  7.2 3.5 collective-permute-start.18
  20.0 14.1 %all-gather.1 = bf16[8,1,1536]{2,1,0:T(2,128)(2,1)S(1)} all-gather(bf16[1,1,1536]{2,1,0:T(2,128)(2,1)S(1)} %reshape.220), channel_id=2, replica_groups=mesh['grp'=4,'shard'=8] {'shard'}, dimensions={0}, use_global_device_ids=true | all-gather | bytes 27648 | tf_op jit(solution)/shard_map/all_gather | solution.py:743
  40.7 5.5 collective-permute-done.19
  51.3 3.5 collective-permute-done.24.refs_6_
  55.9 3.8 collective-permute-done.23.refs_5_
  61.1 3.0 collective-permute-start.52
  67.8 3.0 collective-permute-done.36
  70.8 3.9 collective-permute-done.51
  75.7 15.3 %collective-permute-done.52 = bf16[512,256]{1,0:T(8,128)(2,1)S(1)} collective-permute-done((bf16[512,256]{1,0:T(8,128)(2,1)S(1)}, bf16[512,256]{1,0:T(8,128)(2,1)S(1)}, u32[]{:S(2)}, u32[]{:S(2)}) %collective-permute-start.52) | collective-permute-done | bytes 262176 | tf_op jit(solution)/shard_map/ppermute | solution.py:505
  98.7 4.9 collective-permute-done.3.refs_1_
  103.6 9.3 %collective-permute-done.7.refs_6_ = bf16[4,64,768]{2,1,0:T(8,128)(2,1)} collective-permute-done((bf16[4,64,768]{2,1,0:T(8,128)(2,1)S(1)}, bf16[4,64,768]{2,1,0:T(8,128)(2,1)}, u32[]{:S(2)}, u32[]{:S(2)}) %collective-permute-start.7) | collective-permute-done | bytes 393248 | tf_op jit(solution)/shard_map/ppermute | solution.py:505
  115.7 7.7 %collective-permute-done.5.refs_3_ = bf16[4,64,768]{2,1,0:T(8,128)(2,1)} collective-permute-done((bf16[4,64,768]{2,1,0:T(8,128)(2,1)S(1)}, bf16[4,64,768]{2,1,0:T(8,128)(2,1)}, u32[]{:S(2)}, u32[]{:S(2)}) %collective-permute-start.5) | collective-permute-done | bytes 393248 | tf_op jit(solution)/shard_map/ppermute | solution.py:505
  123.4 2.9 collective-permute-done.8.refs_7_
  127.5 4.7 assemble_attn.1
  136.4 6.7 assemble_qkv.1
  143.1 9.4 %convolution_bitcast_fusion = f32[1024,3072]{1,0:T(8,128)S(1)} fusion(bf16[1024,3072]{1,0:T(8,128)(2,1)} %assemble_qkv.1, bf16[1,1024,1024]{2,1,0:T(8,128)(2,1)} %param.17), kind=kOutput, calls=%fused_computation.3 | convolution fusion | flops 6442450944 | bytes 20971520 | tf_op jit(solution)/shard_map/dot_general | solution.py:770
  153.1 5.2 collective-permute-done.41.refs_6_
  162.2 3.0 fusion.88
  167.8 5.3 collective-permute-done.54.refs_1_
  175.2 33.3 %attn_fwd.1 = (bf16[1024,1024]{1,0:T(8,128)(2,1)}, f32[8,2,1024]{2,1,0:T(2,128)}) custom-call(bf16[1024,1024]{1,0:T(8,128)(2,1)} %get-tuple-element.100.q_ref, bf16[1024,1024]{1,0:T(8,128)(2,1)} %get-tuple-element.99.k_ref, bf16[1024,1024]{1,0:T(8,128)(2,1)} %fusion.v_ref, s32[1024,1]{1,0:T(8,128)} %copy.41.seg_col, s32[1,1024]{1,0:T(1,128)} %seg_row.3), custom_call_target="tpu_custom_call" | custom-call | flops 17179869184 | bytes 8388608 | tf_op jit(solution)/shard_map/attn_fwd/pallas_call | solution.py:378
  209.8 4.7 fusion.90
  218.9 7.8 %assemble_in.1 = bf16[1024,4096]{1,0:T(8,128)(2,1)} custom-call(s32[3]{0:T(128)} %pad_add_fusion.where, bf16[4,64,1024]{2,1,0:T(8,128)(2,1)} %copy-done.10, bf16[4,64,1024]{2,1,0:T(8,128)(2,1)} %collective-permute-done.37.refs_1_, bf16[4,64,1024]{2,1,0:T(8,128)(2,1)} %collective-permute-done.38.refs_2_, ...), custom_call_target="tpu_custom_call" | custom-call | bytes 16777216 | tf_op jit(solution)/shard_map/assemble_in/pallas_call | solution.py:538
  227.2 3.0 collective-permute-done.56.refs_3_
  231.6 15.5 %multiply_convert_fusion = (bf16[1024,4096]{1,0:T(8,128)(2,1)}, f32[1024,4096]{1,0:T(8,128)}) fusion(f32[4096]{0:T(1024)S(1)} %bitcast.227, bf16[1024,1024]{1,0:T(8,128)(2,1)S(1)} %fusion.9.left_ref, bf16[1024,4096]{1,0:T(8,128)(2,1)} %assemble_in.1), kind=kOutput, calls=%fused_computation.1 | convolution fusion | flops 8615100416 | bytes 35667968 | tf_op jit(solution)/shard_map/dot_general | solution.py:781
  248.8 7.9 %assemble_out.1 = bf16[4096,1024]{1,0:T(8,128)(2,1)} custom-call(s32[3]{0:T(128)} %pad_add_fusion.where, bf16[4,256,256]{2,1,0:T(8,128)(2,1)} %copy-done.8, bf16[4,256,256]{2,1,0:T(8,128)(2,1)} %copy-done.18, bf16[4,256,256]{2,1,0:T(8,128)(2,1)} %collective-permute-done.55.refs_2_, bf16[4,256,256]{2,1,0:T(8,128)(2,1)} %collective-permute-done.56.refs_3_, ...), custom_call_target="tpu_custom_call" | custom-call | bytes 16777216 | tf_op jit(solution)/shard_map/assemble_out/pallas_call | solution.py:538
  256.7 14.8 %fusion.91 = (f32[1024]{0:T(1024)S(1)}, f32[1024,1024]{1,0:T(8,128)S(1)}) fusion(f32[1024]{0:T(1024)S(1)} %get-tuple-element.174, bf16[1024,4096]{1,0:T(8,128)(2,1)} %get-tuple-element.184.left_ref, bf16[4096,1024]{1,0:T(8,128)(2,1)} %assemble_out.1, f32[1024]{0:T(1024)S(1)} %get-tuple-element.175, f32[1024]{0:T(1024)S(1)} %get-tuple-element.176, ...), kind=kOutput, calls=%fused_computation.303 | convolution fusion | flops 8597273600 | bytes 25190400 | tf_op jit(solution)/shard_map/dot_general | solution.py:785
  275.7 3.4 fusion.87
  282.7 10.4 %wgrad_out_sent.1 = bf16[4,4,2,256,256]{4,3,2,1,0:T(8,128)(2,1)} custom-call(s32[3]{0:T(128)} %pad_add_fusion.where, bf16[1024,4096]{1,0:T(8,128)(2,1)} %get-tuple-element.184.left_ref, bf16[1024,1024]{1,0:T(8,128)(2,1)} %get-tuple-element.103.right_ref), custom_call_target="tpu_custom_call" | custom-call | flops 4294967296 | bytes 18874368 | tf_op jit(solution)/shard_map/wgrad_out_sent/pallas_call | solution.py:637
  293.2 20.3 %fusion.85 = (f32[4096]{0:T(1024)S(1)}, bf16[1024,4096]{1,0:T(8,128)(2,1)}) fusion(f32[1024,4096]{1,0:T(8,128)} %get-tuple-element.185, f32[4096]{0:T(1024)S(1)} %bitcast.228, bf16[1024,1024]{1,0:T(8,128)(2,1)S(1)} %copy-done.12, bf16[4096,1024]{1,0:T(8,128)(2,1)} %assemble_out.1), kind=kOutput, calls=%fused_computation.297 | convolution fusion | flops 8652845056 | bytes 35684352 | tf_op jit(solution)/shard_map/dot_general | solution.py:37
  313.5 14.9 %multiply_reduce_fusion = (f32[1024]{0:T(1024)S(1)}, f32[1024]{0:T(1024)S(1)}, f32[1024]{0:T(1024)S(1)}, f32[1024,1024]{1,0:T(8,128)S(1)}) fusion(f32[1024,1024]{1,0:T(8,128)S(1)} %copy-done.1, f32[1024]{0:T(1024)S(1)} %fusion.72, f32[1024]{0:T(1024)S(1)} %broadcast_multiply_fusion.1, f32[1024]{0:T(1024)S(1)} %get-tuple-element.176, ...), kind=kOutput, calls=%fused_computation.19 | convolution fusion | flops 8600417280 | bytes 29388800 | tf_op jit(solution)/shard_map/dot_general | solution.py:37
  330.8 2.7 copy-done.14
  333.5 3.7 convolution_convert_fusion.do_ref
  337.2 54.6 %attn_bwd.1 = (bf16[3,1024,1024]{2,1,0:T(8,128)(2,1)}, f32[2,1024]{1,0:T(2,128)}) custom-call(bf16[1024,1024]{1,0:T(8,128)(2,1)} %get-tuple-element.100.q_ref, bf16[1024,1024]{1,0:T(8,128)(2,1)} %get-tuple-element.99.k_ref, bf16[1024,1024]{1,0:T(8,128)(2,1)} %fusion.v_ref, bf16[1024,1024]{1,0:T(8,128)(2,1)} %get-tuple-element.51.o_ref.left_ref, ...), custom_call_target="tpu_custom_call" | custom-call | flops 42949672960 | bytes 16777216 | tf_op jit(solution)/shard_map/attn_bwd/pallas_call | solution.py:458
  391.8 6.6 fusion.16
  398.4 6.6 fusion.14
  407.6 8.7 %wgrad_qkv_sent.1 = bf16[4,4,2,64,768]{4,3,2,1,0:T(8,128)(2,1)} custom-call(s32[3]{0:T(128)} %pad_add_fusion.where, bf16[1024,1024]{1,0:T(8,128)(2,1)} %bitcast.230, bf16[3,1024,1024]{2,1,0:T(8,128)(2,1)} %get-tuple-element.53.right_ref), custom_call_target="tpu_custom_call" | custom-call | flops 3221225472 | bytes 14680064 | tf_op jit(solution)/shard_map/wgrad_qkv_sent/pallas_call | solution.py:637
  417.9 9.9 %wgrad_in_sent.1 = bf16[4,4,2,64,1024]{4,3,2,1,0:T(8,128)(2,1)} custom-call(s32[3]{0:T(128)} %pad_add_fusion.where, bf16[1024,1024]{1,0:T(8,128)(2,1)} %copy-done.7, bf16[1024,4096]{1,0:T(8,128)(2,1)} %get-tuple-element.94.right_ref), custom_call_target="tpu_custom_call" | custom-call | flops 4294967296 | bytes 18874368 | tf_op jit(solution)/shard_map/wgrad_in_sent/pallas_call | solution.py:637
  427.8 5.7 collective-permute-start.84
  434.2 5.2 wgrad_attn_sent.1
  441.6 10.4 %add_bitcast_fusion = f32[1,1024,1024]{2,1,0:T(8,128)} fusion(f32[1024,1024]{1,0:T(8,128)} %fusion.14, f32[1024,1024]{1,0:T(8,128)} %fusion.16, f32[1024,1024]{1,0:T(8,128)} %copy-done.3, f32[1024]{0:T(1024)S(1)} %negate_multiply_fusion, bf16[1024,3072]{1,0:T(8,128)(2,1)} %assemble_qkv.1, bf16[3,1024,1024]{2,1,0:T(8,128)(2,1)} %get-tuple-element.53.right_ref), kind=kOutput, calls=%fused_computation.20 | convolution fusion | flops 2151677952 | bytes 20975616 | tf_op jit(solution)/shard_map/dot_general | solution.py:37
  458.5 2.7 collective-permute-done.103
  462.2 5.3 wgrad_attn_own.1
  469.5 3.7 collective-permute-done.91
  475.6 4.0 collective-permute-done.88
  487.1 10.4 %wgrad_qkv_own.1 = (bf16[4,64,768]{2,1,0:T(8,128)(2,1)}, bf16[4,64,768]{2,1,0:T(8,128)(2,1)}, bf16[4,64,768]{2,1,0:T(8,128)(2,1)}, bf16[4,64,768]{2,1,0:T(8,128)...) custom-call(s32[3]{0:T(128)} %pad_add_fusion.where, ...), custom_call_target="tpu_custom_call" | custom-call | flops 3221225472 | bytes 14680064 | tf_op jit(solution)/shard_map/wgrad_qkv_own/pallas_call | solution.py:637
  505.7 3.1 collective-permute-done.73
  514.0 3.0 collective-permute-done.95
  517.9 3.8 collective-permute-done.72
  521.8 3.1 collective-permute-start.96
  527.3 2.9 collective-permute-done.71
  537.8 6.4 collective-permute-done.76
  547.8 10.4 %wgrad_out_own.1 = (bf16[4,256,256]{2,1,0:T(8,128)(2,1)}, bf16[4,256,256]{2,1,0:T(8,128)(2,1)}, bf16[4,256,256]{2,1,0:T(8,128)(2,1)}, bf16[4,256,256]{2,1,0:T(8,...) custom-call(s32[3]{0:T(128)} %pad_add_fusion.where, ...), custom_call_target="tpu_custom_call" | custom-call | flops 4294967296 | bytes 18874368 | tf_op jit(solution)/shard_map/wgrad_out_own/pallas_call | solution.py:637
  560.3 11.9 %wgrad_in_own.1 = (bf16[4,64,1024]{2,1,0:T(8,128)(2,1)}, bf16[4,64,1024]{2,1,0:T(8,128)(2,1)}, bf16[4,64,1024]{2,1,0:T(8,128)(2,1)}, bf16[4,64,1024]{2,1,0:T(8,1...) custom-call(s32[3]{0:T(128)} %pad_add_fusion.where, ...), custom_call_target="tpu_custom_call" | custom-call | flops 4294967296 | bytes 18874368 | tf_op jit(solution)/shard_map/wgrad_in_own/pallas_call | solution.py:637
  577.1 10.1 %collective-permute-done.119 = bf16[4,256,256]{2,1,0:T(8,128)(2,1)S(1)} collective-permute-done((bf16[4,256,256]{2,1,0:T(8,128)(2,1)S(1)}, bf16[4,256,256]{2,1,0:T(8,128)(2,1)S(1)}, u32[]{:S(2)}, u32[]{:S(2)}) %collective-permute-start.119) | collective-permute-done | bytes 524320 | tf_op jit(solution)/shard_map/ppermute | solution.py:505
  587.7 8.1 %collective-permute-done.109 = bf16[4,64,1024]{2,1,0:T(8,128)(2,1)S(1)} collective-permute-done((bf16[4,64,1024]{2,1,0:T(8,128)(2,1)}, bf16[4,64,1024]{2,1,0:T(8,128)(2,1)S(1)}, u32[]{:S(2)}, u32[]{:S(2)}) %collective-permute-start.109) | collective-permute-done | bytes 524320 | tf_op jit(solution)/shard_map/ppermute | solution.py:505
  596.4 13.4 %collective-permute-done.106 = bf16[4,64,1024]{2,1,0:T(8,128)(2,1)S(1)} collective-permute-done((bf16[4,64,1024]{2,1,0:T(8,128)(2,1)S(1)}, bf16[4,64,1024]{2,1,0:T(8,128)(2,1)S(1)}, u32[]{:S(2)}, u32[]{:S(2)}) %collective-permute-start.106) | collective-permute-done | bytes 524320 | tf_op jit(solution)/shard_map/ppermute | solution.py:505
  610.7 7.8 %collective-permute-done.123 = bf16[4,256,256]{2,1,0:T(8,128)(2,1)S(1)} collective-permute-done((bf16[4,256,256]{2,1,0:T(8,128)(2,1)S(1)}, bf16[4,256,256]{2,1,0:T(8,128)(2,1)S(1)}, u32[]{:S(2)}, u32[]{:S(2)}) %collective-permute-start.123) | collective-permute-done | bytes 524320 | tf_op jit(solution)/shard_map/ppermute | solution.py:505
  621.0 3.0 collective-permute-start.124
  624.0 7.4 %collective-permute-done.110 = bf16[4,64,1024]{2,1,0:T(8,128)(2,1)S(1)} collective-permute-done((bf16[4,64,1024]{2,1,0:T(8,128)(2,1)S(1)}, bf16[4,64,1024]{2,1,0:T(8,128)(2,1)S(1)}, u32[]{:S(2)}, u32[]{:S(2)}) %collective-permute-start.110) | collective-permute-done | bytes 524320 | tf_op jit(solution)/shard_map/ppermute | solution.py:505
  638.9 10.7 %collective-permute-done.125 = bf16[512,256]{1,0:T(8,128)(2,1)S(1)} collective-permute-done((bf16[512,256]{1,0:T(8,128)(2,1)S(1)}, bf16[512,256]{1,0:T(8,128)(2,1)S(1)}, u32[]{:S(2)}, u32[]{:S(2)}) %collective-permute-start.125) | collective-permute-done | bytes 262176 | tf_op jit(solution)/shard_map/ppermute | solution.py:505
  653.9 3.1 collective-permute-done.112
  657.3 2.6 collective-permute-start.114
  664.7 2.7 collective-permute-done.115
  (494 shorter events, 160.3 us)
Async XLA Ops:
  0.7 47.1 %collective-permute-start = (bf16[128,768]{1,0:T(8,128)(2,1)}, bf16[128,768]{1,0:T(8,128)(2,1)S(1)}, u32[]{:S(2)}, u32[]{:S(2)}) collective-permute-start(bf16[128,768]{1,0:T(8,128)(2,1)} %param.21), channel_id=1, source_target_pairs={{0,2},{1,3},{2,0},{3,1},{4,6},{5,7},{6,4},{7,5},{8,10},{9,11},{10,... | collective-permute-start | bytes 589832 | tf_op jit(solution)/shard_map/ppermute | solution.py:505
  3.8 45.7 %collective-permute-start.1 = (bf16[128,768]{1,0:T(8,128)(2,1)}, bf16[128,768]{1,0:T(8,128)(2,1)S(1)}, u32[]{:S(2)}, u32[]{:S(2)}) collective-permute-start(bf16[128,768]{1,0:T(8,128)(2,1)} %param.21), channel_id=1, source_target_pairs={{0,4},{1,5},{2,6},{3,7},{4,0},{5,1},{6,2},{7,3},{8,12},{9,13},{10,... | collective-permute-start | bytes 589832 | tf_op jit(solution)/shard_map/ppermute | solution.py:505
  6.3 48.9 %collective-permute-start.2 = (bf16[128,768]{1,0:T(8,128)(2,1)}, bf16[128,768]{1,0:T(8,128)(2,1)S(1)}, u32[]{:S(2)}, u32[]{:S(2)}) collective-permute-start(bf16[128,768]{1,0:T(8,128)(2,1)} %param.21), channel_id=1, source_target_pairs={{0,6},{1,7},{2,4},{3,5},{4,2},{5,3},{6,0},{7,1},{8,14},{9,15},{10,... | collective-permute-start | bytes 589832 | tf_op jit(solution)/shard_map/ppermute | solution.py:505
  6.4 32.9 %collective-permute-start.17 = (bf16[128,256]{1,0:T(8,128)(2,1)}, bf16[128,256]{1,0:T(8,128)(2,1)S(1)}, u32[]{:S(2)}, u32[]{:S(2)}) collective-permute-start(bf16[128,256]{1,0:T(8,128)(2,1)} %param.24), channel_id=1, source_target_pairs={{0,2},{1,3},{2,0},{3,1},{4,6},{5,7},{6,4},{7,5},{8,10},{9,11},{10,... | collective-permute-start | bytes 196616 | tf_op jit(solution)/shard_map/ppermute | solution.py:505
  7.2 33.4 %collective-permute-start.18 = (bf16[128,256]{1,0:T(8,128)(2,1)}, bf16[128,256]{1,0:T(8,128)(2,1)S(1)}, u32[]{:S(2)}, u32[]{:S(2)}) collective-permute-start(bf16[128,256]{1,0:T(8,128)(2,1)} %param.24), channel_id=1, source_target_pairs={{0,4},{1,5},{2,6},{3,7},{4,0},{5,1},{6,2},{7,3},{8,12},{9,13},{10,... | collective-permute-start | bytes 196616 | tf_op jit(solution)/shard_map/ppermute | solution.py:505
  40.6 23.5 %collective-permute-start.34 = (bf16[128,1024]{1,0:T(8,128)(2,1)}, bf16[128,1024]{1,0:T(8,128)(2,1)S(1)}, u32[]{:S(2)}, u32[]{:S(2)}) collective-permute-start(bf16[128,1024]{1,0:T(8,128)(2,1)} %param.28), channel_id=1, source_target_pairs={{0,2},{1,3},{2,0},{3,1},{4,6},{5,7},{6,4},{7,5},{8,10},{9,11},{10,... | collective-permute-start | bytes 786440 | tf_op jit(solution)/shard_map/ppermute | solution.py:505
  51.2 15.0 %collective-permute-start.35 = (bf16[128,1024]{1,0:T(8,128)(2,1)S(1)}, bf16[128,1024]{1,0:T(8,128)(2,1)S(1)}, u32[]{:S(2)}, u32[]{:S(2)}) collective-permute-start(bf16[128,1024]{1,0:T(8,128)(2,1)S(1)} %copy-done.48), channel_id=1, source_target_pairs={{0,4},{1,5},{2,6},{3,7},{4,0},{5,1},{6,2},{7,3},{8,12},{9,13},{10,... | collective-permute-start | bytes 786440 | tf_op jit(solution)/shard_map/ppermute | solution.py:505
  61.1 29.8 %collective-permute-start.52 = (bf16[512,256]{1,0:T(8,128)(2,1)S(1)}, bf16[512,256]{1,0:T(8,128)(2,1)S(1)}, u32[]{:S(2)}, u32[]{:S(2)}) collective-permute-start(bf16[512,256]{1,0:T(8,128)(2,1)S(1)} %copy-done.49), channel_id=1, source_target_pairs={{0,4},{1,5},{2,6},{3,7},{4,0},{5,1},{6,2},{7,3},{8,12},{9,13},{10,... | collective-permute-start | bytes 786440 | tf_op jit(solution)/shard_map/ppermute | solution.py:505
  64.2 26.8 %collective-permute-start.53 = (bf16[512,256]{1,0:T(8,128)(2,1)S(1)}, bf16[512,256]{1,0:T(8,128)(2,1)S(1)}, u32[]{:S(2)}, u32[]{:S(2)}) collective-permute-start(bf16[512,256]{1,0:T(8,128)(2,1)S(1)} %copy-done.49), channel_id=1, source_target_pairs={{0,6},{1,7},{2,4},{3,5},{4,2},{5,3},{6,0},{7,1},{8,14},{9,15},{10,... | collective-permute-start | bytes 786440 | tf_op jit(solution)/shard_map/ppermute | solution.py:505
  66.3 25.2 %collective-permute-start.22 = (bf16[4,64,256]{2,1,0:T(8,128)(2,1)S(1)}, bf16[4,64,256]{2,1,0:T(8,128)(2,1)S(1)}, u32[]{:S(2)}, u32[]{:S(2)}) collective-permute-start(bf16[4,64,256]{2,1,0:T(8,128)(2,1)S(1)} %collective-permute-done.20.refs_1_), channel_id=1, source_target_pairs={{0,16},{1,17},{2,18},{3,19},{4,20},{5,21},{6,22},{7,23},{8,24},{9,... | collective-permute-start | bytes 393224 | tf_op jit(solution)/shard_map/ppermute | solution.py:505
  70.8 22.3 %collective-permute-start.27 = (bf16[4,64,256]{2,1,0:T(8,128)(2,1)S(1)}, bf16[4,64,256]{2,1,0:T(8,128)(2,1)S(1)}, u32[]{:S(2)}, u32[]{:S(2)}) collective-permute-start(bf16[4,64,256]{2,1,0:T(8,128)(2,1)S(1)} %collective-permute-done.20.refs_1_), channel_id=1, source_target_pairs={{0,1},{1,0},{2,3},{3,2},{4,5},{5,4},{6,7},{7,6},{8,9},{9,8},{10,11... | collective-permute-start | bytes 393224 | tf_op jit(solution)/shard_map/ppermute | solution.py:505
  74.7 16.9 %collective-permute-start.25 = (bf16[4,64,256]{2,1,0:T(8,128)(2,1)S(1)}, bf16[4,64,256]{2,1,0:T(8,128)(2,1)S(1)}, u32[]{:S(2)}, u32[]{:S(2)}) collective-permute-start(bf16[4,64,256]{2,1,0:T(8,128)(2,1)S(1)} %collective-permute-done.24.refs_6_), channel_id=1, source_target_pairs={{0,8},{1,9},{2,10},{3,11},{4,12},{5,13},{6,14},{7,15},{8,0},{9,1},... | collective-permute-start | bytes 393224 | tf_op jit(solution)/shard_map/ppermute | solution.py:505
  93.2 21.2 %collective-permute-start.4 = (bf16[4,64,768]{2,1,0:T(8,128)(2,1)S(1)}, bf16[4,64,768]{2,1,0:T(8,128)(2,1)}, u32[]{:S(2)}, u32[]{:S(2)}) collective-permute-start(bf16[4,64,768]{2,1,0:T(8,128)(2,1)S(1)} %pad_maximum_fusion.7.refs_0_), channel_id=1, source_target_pairs={{0,16},{1,17},{2,18},{3,19},{4,20},{5,21},{6,22},{7,23},{8,24},{9,... | collective-permute-start | bytes 1179656 | tf_op jit(solution)/shard_map/ppermute | solution.py:505
  94.7 18.2 %collective-permute-start.7 = (bf16[4,64,768]{2,1,0:T(8,128)(2,1)S(1)}, bf16[4,64,768]{2,1,0:T(8,128)(2,1)}, u32[]{:S(2)}, u32[]{:S(2)}) collective-permute-start(bf16[4,64,768]{2,1,0:T(8,128)(2,1)S(1)} %pad_maximum_fusion.8.refs_4_), channel_id=1, source_target_pairs={{0,16},{1,17},{2,18},{3,19},{4,20},{5,21},{6,22},{7,23},{8,24},{9,... | collective-permute-start | bytes 1179656 | tf_op jit(solution)/shard_map/ppermute | solution.py:505
  95.2 19.2 %collective-permute-start.6 = (bf16[4,64,768]{2,1,0:T(8,128)(2,1)S(1)}, bf16[4,64,768]{2,1,0:T(8,128)(2,1)}, u32[]{:S(2)}, u32[]{:S(2)}) collective-permute-start(bf16[4,64,768]{2,1,0:T(8,128)(2,1)S(1)} %pad_maximum_fusion.8.refs_4_), channel_id=1, source_target_pairs={{0,8},{1,9},{2,10},{3,11},{4,12},{5,13},{6,14},{7,15},{8,0},{9,1},... | collective-permute-start | bytes 1179656 | tf_op jit(solution)/shard_map/ppermute | solution.py:505
  98.6 16.5 %collective-permute-start.13 = (bf16[4,64,768]{2,1,0:T(8,128)(2,1)S(1)}, bf16[4,64,768]{2,1,0:T(8,128)(2,1)S(1)}, u32[]{:S(2)}, u32[]{:S(2)}) collective-permute-start(bf16[4,64,768]{2,1,0:T(8,128)(2,1)S(1)} %pad_maximum_fusion.8.refs_4_), channel_id=1, source_target_pairs={{0,1},{1,0},{2,3},{3,2},{4,5},{5,4},{6,7},{7,6},{8,9},{9,8},{10,11... | collective-permute-start | bytes 1179656 | tf_op jit(solution)/shard_map/ppermute | solution.py:505
  115.1 17.1 %collective-permute-start.15 = (bf16[4,64,768]{2,1,0:T(8,128)(2,1)}, bf16[4,64,768]{2,1,0:T(8,128)(2,1)}, u32[]{:S(2)}, u32[]{:S(2)}) collective-permute-start(bf16[4,64,768]{2,1,0:T(8,128)(2,1)} %collective-permute-done.7.refs_6_), channel_id=1, source_target_pairs={{0,1},{1,0},{2,3},{3,2},{4,5},{5,4},{6,7},{7,6},{8,9},{9,8},{10,11... | collective-permute-start | bytes 1179656 | tf_op jit(solution)/shard_map/ppermute | solution.py:505
  115.3 17.5 %collective-permute-start.11 = (bf16[4,64,768]{2,1,0:T(8,128)(2,1)}, bf16[4,64,768]{2,1,0:T(8,128)(2,1)}, u32[]{:S(2)}, u32[]{:S(2)}) collective-permute-start(bf16[4,64,768]{2,1,0:T(8,128)(2,1)} %collective-permute-done.4.refs_2_), channel_id=1, source_target_pairs={{0,1},{1,0},{2,3},{3,2},{4,5},{5,4},{6,7},{7,6},{8,9},{9,8},{10,11... | collective-permute-start | bytes 1179656 | tf_op jit(solution)/shard_map/ppermute | solution.py:505
  132.2 20.2 %collective-permute-start.37 = (bf16[4,64,1024]{2,1,0:T(8,128)(2,1)S(1)}, bf16[4,64,1024]{2,1,0:T(8,128)(2,1)}, u32[]{:S(2)}, u32[]{:S(2)}) collective-permute-start(bf16[4,64,1024]{2,1,0:T(8,128)(2,1)S(1)} %pad_maximum_fusion.2.refs_0_), channel_id=1, source_target_pairs={{0,8},{1,9},{2,10},{3,11},{4,12},{5,13},{6,14},{7,15},{8,0},{9,1},... | collective-permute-start | bytes 1572872 | tf_op jit(solution)/shard_map/ppermute | solution.py:505
  132.8 26.9 %collective-permute-start.38 = (bf16[4,64,1024]{2,1,0:T(8,128)(2,1)S(1)}, bf16[4,64,1024]{2,1,0:T(8,128)(2,1)}, u32[]{:S(2)}, u32[]{:S(2)}) collective-permute-start(bf16[4,64,1024]{2,1,0:T(8,128)(2,1)S(1)} %pad_maximum_fusion.2.refs_0_), channel_id=1, source_target_pairs={{0,16},{1,17},{2,18},{3,19},{4,20},{5,21},{6,22},{7,23},{8,24},{9,... | collective-permute-start | bytes 1572872 | tf_op jit(solution)/shard_map/ppermute | solution.py:505
  133.3 24.9 %collective-permute-start.41 = (bf16[4,64,1024]{2,1,0:T(8,128)(2,1)S(1)}, bf16[4,64,1024]{2,1,0:T(8,128)(2,1)}, u32[]{:S(2)}, u32[]{:S(2)}) collective-permute-start(bf16[4,64,1024]{2,1,0:T(8,128)(2,1)S(1)} %pad_maximum_fusion.3.refs_4_), channel_id=1, source_target_pairs={{0,16},{1,17},{2,18},{3,19},{4,20},{5,21},{6,22},{7,23},{8,24},{9,... | collective-permute-start | bytes 1572872 | tf_op jit(solution)/shard_map/ppermute | solution.py:505
  134.9 30.3 %collective-permute-start.40 = (bf16[4,64,1024]{2,1,0:T(8,128)(2,1)S(1)}, bf16[4,64,1024]{2,1,0:T(8,128)(2,1)S(1)}, u32[]{:S(2)}, u32[]{:S(2)}) collective-permute-start(bf16[4,64,1024]{2,1,0:T(8,128)(2,1)S(1)} %pad_maximum_fusion.3.refs_4_), channel_id=1, source_target_pairs={{0,8},{1,9},{2,10},{3,11},{4,12},{5,13},{6,14},{7,15},{8,0},{9,1},... | collective-permute-start | bytes 1572872 | tf_op jit(solution)/shard_map/ppermute | solution.py:505
  136.4 30.4 %collective-permute-start.43 = (bf16[4,64,1024]{2,1,0:T(8,128)(2,1)S(1)}, bf16[4,64,1024]{2,1,0:T(8,128)(2,1)S(1)}, u32[]{:S(2)}, u32[]{:S(2)}) collective-permute-start(bf16[4,64,1024]{2,1,0:T(8,128)(2,1)S(1)} %pad_maximum_fusion.2.refs_0_), channel_id=1, source_target_pairs={{0,1},{1,0},{2,3},{3,2},{4,5},{5,4},{6,7},{7,6},{8,9},{9,8},{10,11... | collective-permute-start | bytes 1572872 | tf_op jit(solution)/shard_map/ppermute | solution.py:505
  152.5 14.8 %collective-permute-start.47 = (bf16[4,64,1024]{2,1,0:T(8,128)(2,1)S(1)}, bf16[4,64,1024]{2,1,0:T(8,128)(2,1)S(1)}, u32[]{:S(2)}, u32[]{:S(2)}) collective-permute-start(bf16[4,64,1024]{2,1,0:T(8,128)(2,1)S(1)} %pad_maximum_fusion.3.refs_4_), channel_id=1, source_target_pairs={{0,1},{1,0},{2,3},{3,2},{4,5},{5,4},{6,7},{7,6},{8,9},{9,8},{10,11... | collective-permute-start | bytes 1572872 | tf_op jit(solution)/shard_map/ppermute | solution.py:505
  158.2 14.9 %collective-permute-start.54 = (bf16[4,256,256]{2,1,0:T(8,128)(2,1)S(1)}, bf16[4,256,256]{2,1,0:T(8,128)(2,1)S(1)}, u32[]{:S(2)}, u32[]{:S(2)}) collective-permute-start(bf16[4,256,256]{2,1,0:T(8,128)(2,1)S(1)} %pad_maximum_fusion.4.refs_0_), channel_id=1, source_target_pairs={{0,8},{1,9},{2,10},{3,11},{4,12},{5,13},{6,14},{7,15},{8,0},{9,1},... | collective-permute-start | bytes 1572872 | tf_op jit(solution)/shard_map/ppermute | solution.py:505
  159.7 15.0 %collective-permute-start.58 = (bf16[4,256,256]{2,1,0:T(8,128)(2,1)S(1)}, bf16[4,256,256]{2,1,0:T(8,128)(2,1)}, u32[]{:S(2)}, u32[]{:S(2)}) collective-permute-start(bf16[4,256,256]{2,1,0:T(8,128)(2,1)S(1)} %pad_maximum_fusion.5.refs_4_), channel_id=1, source_target_pairs={{0,16},{1,17},{2,18},{3,19},{4,20},{5,21},{6,22},{7,23},{8,24},{9,... | collective-permute-start | bytes 1572872 | tf_op jit(solution)/shard_map/ppermute | solution.py:505
  165.2 43.4 %collective-permute-start.55 = (bf16[4,256,256]{2,1,0:T(8,128)(2,1)S(1)}, bf16[4,256,256]{2,1,0:T(8,128)(2,1)}, u32[]{:S(2)}, u32[]{:S(2)}) collective-permute-start(bf16[4,256,256]{2,1,0:T(8,128)(2,1)S(1)} %pad_maximum_fusion.4.refs_0_), channel_id=1, source_target_pairs={{0,16},{1,17},{2,18},{3,19},{4,20},{5,21},{6,22},{7,23},{8,24},{9,... | collective-permute-start | bytes 1572872 | tf_op jit(solution)/shard_map/ppermute | solution.py:505
  166.7 42.0 %collective-permute-start.57 = (bf16[4,256,256]{2,1,0:T(8,128)(2,1)S(1)}, bf16[4,256,256]{2,1,0:T(8,128)(2,1)S(1)}, u32[]{:S(2)}, u32[]{:S(2)}) collective-permute-start(bf16[4,256,256]{2,1,0:T(8,128)(2,1)S(1)} %pad_maximum_fusion.5.refs_4_), channel_id=1, source_target_pairs={{0,8},{1,9},{2,10},{3,11},{4,12},{5,13},{6,14},{7,15},{8,0},{9,1},... | collective-permute-start | bytes 1572872 | tf_op jit(solution)/shard_map/ppermute | solution.py:505
  167.3 41.9 %collective-permute-start.39 = (bf16[4,64,1024]{2,1,0:T(8,128)(2,1)}, bf16[4,64,1024]{2,1,0:T(8,128)(2,1)}, u32[]{:S(2)}, u32[]{:S(2)}) collective-permute-start(bf16[4,64,1024]{2,1,0:T(8,128)(2,1)} %collective-permute-done.37.refs_1_), channel_id=1, source_target_pairs={{0,16},{1,17},{2,18},{3,19},{4,20},{5,21},{6,22},{7,23},{8,24},{9,... | collective-permute-start | bytes 1572872 | tf_op jit(solution)/shard_map/ppermute | solution.py:505
  173.1 36.6 %collective-permute-start.44 = (bf16[4,64,1024]{2,1,0:T(8,128)(2,1)}, bf16[4,64,1024]{2,1,0:T(8,128)(2,1)}, u32[]{:S(2)}, u32[]{:S(2)}) collective-permute-start(bf16[4,64,1024]{2,1,0:T(8,128)(2,1)} %collective-permute-done.37.refs_1_), channel_id=1, source_target_pairs={{0,1},{1,0},{2,3},{3,2},{4,5},{5,4},{6,7},{7,6},{8,9},{9,8},{10,11... | collective-permute-start | bytes 1572872 | tf_op jit(solution)/shard_map/ppermute | solution.py:505
  174.7 34.6 %collective-permute-start.42 = (bf16[4,64,1024]{2,1,0:T(8,128)(2,1)}, bf16[4,64,1024]{2,1,0:T(8,128)(2,1)}, u32[]{:S(2)}, u32[]{:S(2)}) collective-permute-start(bf16[4,64,1024]{2,1,0:T(8,128)(2,1)} %collective-permute-done.41.refs_6_), channel_id=1, source_target_pairs={{0,8},{1,9},{2,10},{3,11},{4,12},{5,13},{6,14},{7,15},{8,0},{9,1},... | collective-permute-start | bytes 1572872 | tf_op jit(solution)/shard_map/ppermute | solution.py:505
  215.9 14.4 %collective-permute-start.56 = (bf16[4,256,256]{2,1,0:T(8,128)(2,1)S(1)}, bf16[4,256,256]{2,1,0:T(8,128)(2,1)}, u32[]{:S(2)}, u32[]{:S(2)}) collective-permute-start(bf16[4,256,256]{2,1,0:T(8,128)(2,1)S(1)} %copy-done.19), channel_id=1, source_target_pairs={{0,16},{1,17},{2,18},{3,19},{4,20},{5,21},{6,22},{7,23},{8,24},{9,... | collective-permute-start | bytes 1572872 | tf_op jit(solution)/shard_map/ppermute | solution.py:505
  216.4 14.7 %collective-permute-start.61 = (bf16[4,256,256]{2,1,0:T(8,128)(2,1)S(1)}, bf16[4,256,256]{2,1,0:T(8,128)(2,1)}, u32[]{:S(2)}, u32[]{:S(2)}) collective-permute-start(bf16[4,256,256]{2,1,0:T(8,128)(2,1)S(1)} %copy-done.19), channel_id=1, source_target_pairs={{0,1},{1,0},{2,3},{3,2},{4,5},{5,4},{6,7},{7,6},{8,9},{9,8},{10,11... | collective-permute-start | bytes 1572872 | tf_op jit(solution)/shard_map/ppermute | solution.py:505
  216.6 14.5 %collective-permute-start.59 = (bf16[4,256,256]{2,1,0:T(8,128)(2,1)}, bf16[4,256,256]{2,1,0:T(8,128)(2,1)}, u32[]{:S(2)}, u32[]{:S(2)}) collective-permute-start(bf16[4,256,256]{2,1,0:T(8,128)(2,1)} %collective-permute-done.58.refs_6_), channel_id=1, source_target_pairs={{0,8},{1,9},{2,10},{3,11},{4,12},{5,13},{6,14},{7,15},{8,0},{9,1},... | collective-permute-start | bytes 1572872 | tf_op jit(solution)/shard_map/ppermute | solution.py:505
  226.7 20.4 %collective-permute-start.66 = (bf16[4,256,256]{2,1,0:T(8,128)(2,1)}, bf16[4,256,256]{2,1,0:T(8,128)(2,1)S(1)}, u32[]{:S(2)}, u32[]{:S(2)}) collective-permute-start(bf16[4,256,256]{2,1,0:T(8,128)(2,1)} %collective-permute-done.58.refs_6_), channel_id=1, source_target_pairs={{0,1},{1,0},{2,3},{3,2},{4,5},{5,4},{6,7},{7,6},{8,9},{9,8},{10,11... | collective-permute-start | bytes 1572872 | tf_op jit(solution)/shard_map/ppermute | solution.py:505
  226.8 20.2 %collective-permute-start.62 = (bf16[4,256,256]{2,1,0:T(8,128)(2,1)}, bf16[4,256,256]{2,1,0:T(8,128)(2,1)S(1)}, u32[]{:S(2)}, u32[]{:S(2)}) collective-permute-start(bf16[4,256,256]{2,1,0:T(8,128)(2,1)} %collective-permute-done.55.refs_2_), channel_id=1, source_target_pairs={{0,1},{1,0},{2,3},{3,2},{4,5},{5,4},{6,7},{7,6},{8,9},{9,8},{10,11... | collective-permute-start | bytes 1572872 | tf_op jit(solution)/shard_map/ppermute | solution.py:505
  230.3 16.8 %collective-permute-start.65 = (bf16[4,256,256]{2,1,0:T(8,128)(2,1)}, bf16[4,256,256]{2,1,0:T(8,128)(2,1)}, u32[]{:S(2)}, u32[]{:S(2)}) collective-permute-start(bf16[4,256,256]{2,1,0:T(8,128)(2,1)} %copy-done.20), channel_id=1, source_target_pairs={{0,1},{1,0},{2,3},{3,2},{4,5},{5,4},{6,7},{7,6},{8,9},{9,8},{10,11... | collective-permute-start | bytes 1572872 | tf_op jit(solution)/shard_map/ppermute | solution.py:505
  231.1 16.0 %collective-permute-start.63 = (bf16[4,256,256]{2,1,0:T(8,128)(2,1)}, bf16[4,256,256]{2,1,0:T(8,128)(2,1)}, u32[]{:S(2)}, u32[]{:S(2)}) collective-permute-start(bf16[4,256,256]{2,1,0:T(8,128)(2,1)} %collective-permute-done.56.refs_3_), channel_id=1, source_target_pairs={{0,1},{1,0},{2,3},{3,2},{4,5},{5,4},{6,7},{7,6},{8,9},{9,8},{10,11... | collective-permute-start | bytes 1572872 | tf_op jit(solution)/shard_map/ppermute | solution.py:505
  231.1 16.0 %collective-permute-start.67 = (bf16[4,256,256]{2,1,0:T(8,128)(2,1)}, bf16[4,256,256]{2,1,0:T(8,128)(2,1)S(1)}, u32[]{:S(2)}, u32[]{:S(2)}) collective-permute-start(bf16[4,256,256]{2,1,0:T(8,128)(2,1)} %collective-permute-done.59.refs_7_), channel_id=1, source_target_pairs={{0,1},{1,0},{2,3},{3,2},{4,5},{5,4},{6,7},{7,6},{8,9},{9,8},{10,11... | collective-permute-start | bytes 1572872 | tf_op jit(solution)/shard_map/ppermute | solution.py:505
  405.0 28.5 %collective-permute-start.99 = (f32[80,128]{1,0:T(8,128)S(1)}, f32[80,128]{1,0:T(8,128)S(1)}, u32[]{:S(2)}, u32[]{:S(2)}) collective-permute-start(f32[80,128]{1,0:T(8,128)S(1)} %bitcast.222), channel_id=1, source_target_pairs={{0,1},{1,0},{2,3},{3,2},{4,5},{5,4},{6,7},{7,6},{8,9},{9,8},{10,11... | collective-permute-start | bytes 122888 | tf_op jit(solution)/shard_map/ppermute | solution.py:505
  416.3 70.8 %collective-permute-start.68 = (bf16[4,4,2,64,768]{4,3,2,1,0:T(8,128)(2,1)}, bf16[4,4,2,64,768]{4,3,2,1,0:T(8,128)(2,1)}, u32[]{:S(2)}, u32[]{:S(2)}) collective-permute-start(bf16[4,4,2,64,768]{4,3,2,1,0:T(8,128)(2,1)} %wgrad_qkv_sent.1), channel_id=1, source_target_pairs={{0,1},{1,0},{2,3},{3,2},{4,5},{5,4},{6,7},{7,6},{8,9},{9,8},{10,11... | collective-permute-start | bytes 9437192 | tf_op jit(solution)/shard_map/ppermute | solution.py:505
  439.3 108.5 %collective-permute-start.117 = (bf16[4,4,2,256,256]{4,3,2,1,0:T(8,128)(2,1)}, bf16[4,4,2,256,256]{4,3,2,1,0:T(8,128)(2,1)}, u32[]{:S(2)}, u32[]{:S(2)}) collective-permute-start(bf16[4,4,2,256,256]{4,3,2,1,0:T(8,128)(2,1)} %wgrad_out_sent.1), channel_id=1, source_target_pairs={{0,1},{1,0},{2,3},{3,2},{4,5},{5,4},{6,7},{7,6},{8,9},{9,8},{10,11... | collective-permute-start | bytes 12582920 | tf_op jit(solution)/shard_map/ppermute | solution.py:505
  439.4 21.9 %collective-permute-start.86 = (bf16[4,4,2,64,256]{4,3,2,1,0:T(8,128)(2,1)}, bf16[4,4,2,64,256]{4,3,2,1,0:T(8,128)(2,1)S(1)}, u32[]{:S(2)}, u32[]{:S(2)}) collective-permute-start(bf16[4,4,2,64,256]{4,3,2,1,0:T(8,128)(2,1)} %wgrad_attn_sent.1), channel_id=1, source_target_pairs={{0,1},{1,0},{2,3},{3,2},{4,5},{5,4},{6,7},{7,6},{8,9},{9,8},{10,11... | collective-permute-start | bytes 3145736 | tf_op jit(solution)/shard_map/ppermute | solution.py:505
  451.9 106.5 %collective-permute-start.104 = (bf16[4,4,2,64,1024]{4,3,2,1,0:T(8,128)(2,1)}, bf16[4,4,2,64,1024]{4,3,2,1,0:T(8,128)(2,1)}, u32[]{:S(2)}, u32[]{:S(2)}) collective-permute-start(bf16[4,4,2,64,1024]{4,3,2,1,0:T(8,128)(2,1)} %wgrad_in_sent.1), channel_id=1, source_target_pairs={{0,1},{1,0},{2,3},{3,2},{4,5},{5,4},{6,7},{7,6},{8,9},{9,8},{10,11... | collective-permute-start | bytes 12582920 | tf_op jit(solution)/shard_map/ppermute | solution.py:505
  482.0 16.0 %collective-permute-start.87 = (bf16[4,64,256]{2,1,0:T(8,128)(2,1)}, bf16[4,64,256]{2,1,0:T(8,128)(2,1)S(1)}, u32[]{:S(2)}, u32[]{:S(2)}) collective-permute-start(bf16[4,64,256]{2,1,0:T(8,128)(2,1)} %get-tuple-element.64), channel_id=1, source_target_pairs={{0,8},{1,9},{2,10},{3,11},{4,12},{5,13},{6,14},{7,15},{8,0},{9,1},... | collective-permute-start | bytes 393224 | tf_op jit(solution)/shard_map/ppermute | solution.py:505
  544.2 28.1 %collective-permute-start.78 = (bf16[128,768]{1,0:T(8,128)(2,1)S(1)}, bf16[128,768]{1,0:T(8,128)(2,1)S(1)}, u32[]{:S(2)}, u32[]{:S(2)}) collective-permute-start(bf16[128,768]{1,0:T(8,128)(2,1)S(1)} %fusion.36), channel_id=1, source_target_pairs={{0,24},{1,25},{2,26},{3,27},{4,28},{5,29},{6,30},{7,31},{8,16},{9,... | collective-permute-start | bytes 589832 | tf_op jit(solution)/shard_map/ppermute | solution.py:505
  544.3 28.4 %collective-permute-start.79 = (bf16[128,768]{1,0:T(8,128)(2,1)S(1)}, bf16[128,768]{1,0:T(8,128)(2,1)S(1)}, u32[]{:S(2)}, u32[]{:S(2)}) collective-permute-start(bf16[128,768]{1,0:T(8,128)(2,1)S(1)} %fusion.36), channel_id=1, source_target_pairs={{0,16},{1,17},{2,18},{3,19},{4,20},{5,21},{6,22},{7,23},{8,24},{9,... | collective-permute-start | bytes 589832 | tf_op jit(solution)/shard_map/ppermute | solution.py:505
  546.1 28.4 %collective-permute-start.80 = (bf16[128,768]{1,0:T(8,128)(2,1)S(1)}, bf16[128,768]{1,0:T(8,128)(2,1)S(1)}, u32[]{:S(2)}, u32[]{:S(2)}) collective-permute-start(bf16[128,768]{1,0:T(8,128)(2,1)S(1)} %fusion.36), channel_id=1, source_target_pairs={{0,8},{1,9},{2,10},{3,11},{4,12},{5,13},{6,14},{7,15},{8,0},{9,1},... | collective-permute-start | bytes 589832 | tf_op jit(solution)/shard_map/ppermute | solution.py:505
  558.2 16.9 %collective-permute-start.122 = (bf16[4,256,256]{2,1,0:T(8,128)(2,1)}, bf16[4,256,256]{2,1,0:T(8,128)(2,1)S(1)}, u32[]{:S(2)}, u32[]{:S(2)}) collective-permute-start(bf16[4,256,256]{2,1,0:T(8,128)(2,1)} %get-tuple-element.86), channel_id=1, source_target_pairs={{0,16},{1,17},{2,18},{3,19},{4,20},{5,21},{6,22},{7,23},{8,24},{9,... | collective-permute-start | bytes 1572872 | tf_op jit(solution)/shard_map/ppermute | solution.py:505
  558.4 51.8 %collective-permute-start.121 = (bf16[4,256,256]{2,1,0:T(8,128)(2,1)}, bf16[4,256,256]{2,1,0:T(8,128)(2,1)S(1)}, u32[]{:S(2)}, u32[]{:S(2)}) collective-permute-start(bf16[4,256,256]{2,1,0:T(8,128)(2,1)} %get-tuple-element.84), channel_id=1, source_target_pairs={{0,16},{1,17},{2,18},{3,19},{4,20},{5,21},{6,22},{7,23},{8,24},{9,... | collective-permute-start | bytes 1572872 | tf_op jit(solution)/shard_map/ppermute | solution.py:505
  572.3 14.9 %collective-permute-start.119 = (bf16[4,256,256]{2,1,0:T(8,128)(2,1)S(1)}, bf16[4,256,256]{2,1,0:T(8,128)(2,1)S(1)}, u32[]{:S(2)}, u32[]{:S(2)}) collective-permute-start(bf16[4,256,256]{2,1,0:T(8,128)(2,1)S(1)} %copy-done.69), channel_id=1, source_target_pairs={{0,8},{1,9},{2,10},{3,11},{4,12},{5,13},{6,14},{7,15},{8,0},{9,1},... | collective-permute-start | bytes 1572872 | tf_op jit(solution)/shard_map/ppermute | solution.py:505
  572.7 47.4 %collective-permute-start.118 = (bf16[4,256,256]{2,1,0:T(8,128)(2,1)S(1)}, bf16[4,256,256]{2,1,0:T(8,128)(2,1)S(1)}, u32[]{:S(2)}, u32[]{:S(2)}) collective-permute-start(bf16[4,256,256]{2,1,0:T(8,128)(2,1)S(1)} %copy-done.68), channel_id=1, source_target_pairs={{0,8},{1,9},{2,10},{3,11},{4,12},{5,13},{6,14},{7,15},{8,0},{9,1},... | collective-permute-start | bytes 1572872 | tf_op jit(solution)/shard_map/ppermute | solution.py:505
  574.5 21.4 %collective-permute-start.109 = (bf16[4,64,1024]{2,1,0:T(8,128)(2,1)}, bf16[4,64,1024]{2,1,0:T(8,128)(2,1)S(1)}, u32[]{:S(2)}, u32[]{:S(2)}) collective-permute-start(bf16[4,64,1024]{2,1,0:T(8,128)(2,1)} %get-tuple-element.78), channel_id=1, source_target_pairs={{0,16},{1,17},{2,18},{3,19},{4,20},{5,21},{6,22},{7,23},{8,24},{9,... | collective-permute-start | bytes 1572872 | tf_op jit(solution)/shard_map/ppermute | solution.py:505
  575.2 48.8 %collective-permute-start.108 = (bf16[4,64,1024]{2,1,0:T(8,128)(2,1)S(1)}, bf16[4,64,1024]{2,1,0:T(8,128)(2,1)S(1)}, u32[]{:S(2)}, u32[]{:S(2)}) collective-permute-start(bf16[4,64,1024]{2,1,0:T(8,128)(2,1)S(1)} %copy-done.67), channel_id=1, source_target_pairs={{0,16},{1,17},{2,18},{3,19},{4,20},{5,21},{6,22},{7,23},{8,24},{9,... | collective-permute-start | bytes 1572872 | tf_op jit(solution)/shard_map/ppermute | solution.py:505
  587.3 22.5 %collective-permute-start.106 = (bf16[4,64,1024]{2,1,0:T(8,128)(2,1)S(1)}, bf16[4,64,1024]{2,1,0:T(8,128)(2,1)S(1)}, u32[]{:S(2)}, u32[]{:S(2)}) collective-permute-start(bf16[4,64,1024]{2,1,0:T(8,128)(2,1)S(1)} %copy-done.70), channel_id=1, source_target_pairs={{0,8},{1,9},{2,10},{3,11},{4,12},{5,13},{6,14},{7,15},{8,0},{9,1},... | collective-permute-start | bytes 1572872 | tf_op jit(solution)/shard_map/ppermute | solution.py:505
  595.8 22.7 %collective-permute-start.123 = (bf16[4,256,256]{2,1,0:T(8,128)(2,1)S(1)}, bf16[4,256,256]{2,1,0:T(8,128)(2,1)S(1)}, u32[]{:S(2)}, u32[]{:S(2)}) collective-permute-start(bf16[4,256,256]{2,1,0:T(8,128)(2,1)S(1)} %add_convert_fusion.4), channel_id=1, source_target_pairs={{0,8},{1,9},{2,10},{3,11},{4,12},{5,13},{6,14},{7,15},{8,0},{9,1},... | collective-permute-start | bytes 1572872 | tf_op jit(solution)/shard_map/ppermute | solution.py:505
  610.2 23.6 %collective-permute-start.105 = (bf16[4,64,1024]{2,1,0:T(8,128)(2,1)S(1)}, bf16[4,64,1024]{2,1,0:T(8,128)(2,1)S(1)}, u32[]{:S(2)}, u32[]{:S(2)}) collective-permute-start(bf16[4,64,1024]{2,1,0:T(8,128)(2,1)S(1)} %copy-done.66), channel_id=1, source_target_pairs={{0,8},{1,9},{2,10},{3,11},{4,12},{5,13},{6,14},{7,15},{8,0},{9,1},... | collective-permute-start | bytes 1572872 | tf_op jit(solution)/shard_map/ppermute | solution.py:505
  620.1 13.7 %collective-permute-start.107 = (bf16[4,64,1024]{2,1,0:T(8,128)(2,1)S(1)}, bf16[4,64,1024]{2,1,0:T(8,128)(2,1)S(1)}, u32[]{:S(2)}, u32[]{:S(2)}) collective-permute-start(bf16[4,64,1024]{2,1,0:T(8,128)(2,1)S(1)} %add_convert_fusion.10), channel_id=1, source_target_pairs={{0,16},{1,17},{2,18},{3,19},{4,20},{5,21},{6,22},{7,23},{8,24},{9,... | collective-permute-start | bytes 1572872 | tf_op jit(solution)/shard_map/ppermute | solution.py:505
  621.0 15.7 %collective-permute-start.124 = (bf16[512,256]{1,0:T(8,128)(2,1)S(1)}, bf16[512,256]{1,0:T(8,128)(2,1)S(1)}, u32[]{:S(2)}, u32[]{:S(2)}) collective-permute-start(bf16[512,256]{1,0:T(8,128)(2,1)S(1)} %get-tuple-element.110), channel_id=1, source_target_pairs={{0,2},{1,3},{2,0},{3,1},{4,6},{5,7},{6,4},{7,5},{8,10},{9,11},{10,... | collective-permute-start | bytes 786440 | tf_op jit(solution)/shard_map/ppermute | solution.py:505
  624.0 25.6 %collective-permute-start.125 = (bf16[512,256]{1,0:T(8,128)(2,1)S(1)}, bf16[512,256]{1,0:T(8,128)(2,1)S(1)}, u32[]{:S(2)}, u32[]{:S(2)}) collective-permute-start(bf16[512,256]{1,0:T(8,128)(2,1)S(1)} %get-tuple-element.111), channel_id=1, source_target_pairs={{0,4},{1,5},{2,6},{3,7},{4,0},{5,1},{6,2},{7,3},{8,12},{9,13},{10,... | collective-permute-start | bytes 786440 | tf_op jit(solution)/shard_map/ppermute | solution.py:505
  631.4 18.2 %collective-permute-start.126 = (bf16[512,256]{1,0:T(8,128)(2,1)S(1)}, bf16[512,256]{1,0:T(8,128)(2,1)S(1)}, u32[]{:S(2)}, u32[]{:S(2)}) collective-permute-start(bf16[512,256]{1,0:T(8,128)(2,1)S(1)} %get-tuple-element.112), channel_id=1, source_target_pairs={{0,6},{1,7},{2,4},{3,5},{4,2},{5,3},{6,0},{7,1},{8,14},{9,15},{10,... | collective-permute-start | bytes 786440 | tf_op jit(solution)/shard_map/ppermute | solution.py:505
  634.2 19.7 %collective-permute-start.111 = (bf16[128,1024]{1,0:T(8,128)(2,1)S(1)}, bf16[128,1024]{1,0:T(8,128)(2,1)S(1)}, u32[]{:S(2)}, u32[]{:S(2)}) collective-permute-start(bf16[128,1024]{1,0:T(8,128)(2,1)S(1)} %get-tuple-element.117), channel_id=1, source_target_pairs={{0,2},{1,3},{2,0},{3,1},{4,6},{5,7},{6,4},{7,5},{8,10},{9,11},{10,... | collective-permute-start | bytes 786440 | tf_op jit(solution)/shard_map/ppermute | solution.py:505
  636.5 20.6 %collective-permute-start.112 = (bf16[128,1024]{1,0:T(8,128)(2,1)S(1)}, bf16[128,1024]{1,0:T(8,128)(2,1)S(1)}, u32[]{:S(2)}, u32[]{:S(2)}) collective-permute-start(bf16[128,1024]{1,0:T(8,128)(2,1)S(1)} %get-tuple-element.118), channel_id=1, source_target_pairs={{0,4},{1,5},{2,6},{3,7},{4,0},{5,1},{6,2},{7,3},{8,12},{9,13},{10,... | collective-permute-start | bytes 786440 | tf_op jit(solution)/shard_map/ppermute | solution.py:505
  636.6 20.5 %collective-permute-start.113 = (bf16[128,1024]{1,0:T(8,128)(2,1)S(1)}, bf16[128,1024]{1,0:T(8,128)(2,1)S(1)}, u32[]{:S(2)}, u32[]{:S(2)}) collective-permute-start(bf16[128,1024]{1,0:T(8,128)(2,1)S(1)} %get-tuple-element.119), channel_id=1, source_target_pairs={{0,6},{1,7},{2,4},{3,5},{4,2},{5,3},{6,0},{7,1},{8,14},{9,15},{10,... | collective-permute-start | bytes 786440 | tf_op jit(solution)/shard_map/ppermute | solution.py:505
  (137 other events, 2201.2 us)

commit v2 on v1

--- a/solution.py
+++ b/solution.py
@@ -370,32 +370,46 @@
         out_ref[here, :] = jnp.where(first, outs[0], outs[1]).astype(jnp.bfloat16)
 
 
-def attention_forward(q, k, v, seg_col, seg_row):
-    length, width = q.shape
-    pairs = width // LANES
+def attention_forward(qkv, seg_col, seg_row, start, pairs, before=None):
+    length, width = qkv.shape[0], qkv.shape[1] // 3
+    total = width // LANES
     rows = min(512, length)
-    pair = pl.BlockSpec((length, LANES), lambda j: (0, j))
+    anywhere = pl.BlockSpec(memory_space=pl.ANY)
+
+    def pair(part):
+        return pl.BlockSpec((length, LANES), lambda j: (0, part * total + start + j))
+
+    def body(q_ref, k_ref, v_ref, seg_c, seg_r, *refs):
+        attention_forward_kernel(q_ref, k_ref, v_ref, seg_c, seg_r, *refs[-2:], rows=rows)
+
     return pl.pallas_call(
-        functools.partial(attention_forward_kernel, rows=rows),
+        body,
         grid=(pairs,),
         in_specs=[
-            pair,
-            pair,
-            pair,
+            pair(0),
+            pair(1),
+            pair(2),
             pl.BlockSpec((length, 1), lambda j: (0, 0)),
             pl.BlockSpec((1, length), lambda j: (0, 0)),
+        ]
+        + [anywhere] * (0 if before is None else 2),
+        out_specs=[
+            pl.BlockSpec((length, LANES), lambda j: (0, start + j)),
+            pl.BlockSpec((1, 2, length), lambda j: (start + j, 0, 0)),
         ],
-        out_specs=[pair, pl.BlockSpec((1, 2, length), lambda j: (j, 0, 0))],
         out_shape=[
             jax.ShapeDtypeStruct((length, width), jnp.bfloat16),
-            jax.ShapeDtypeStruct((pairs, 2, length), jnp.float32),
+            jax.ShapeDtypeStruct((total, 2, length), jnp.float32),
         ],
-        compiler_params=params(),
+        input_output_aliases={} if before is None else {5: 0, 6: 1},
+        compiler_params=params(40),
         cost_estimate=pl.CostEstimate(
-            flops=16 * length * length * width, bytes_accessed=8 * length * width, transcendentals=0
+            flops=16 * length * length * pairs * LANES,
+            bytes_accessed=8 * length * pairs * LANES,
+            transcendentals=0,
         ),
         name="attn_fwd",
-    )(q, k, v, seg_col, seg_row)
+    )(qkv, qkv, qkv, seg_col, seg_row, *(() if before is None else before))
 
 
 def attention_backward_kernel(
@@ -451,39 +465,49 @@
     sum_ref[1:2, :] = jnp.sum(value_grad, 0, keepdims=True)
 
 
-def attention_backward(q, k, v, out, out_grad, seg_col, seg_row, lse, start, pairs):
-    length, width = q.shape
+def attention_backward(qkv, out, out_grad, seg_col, seg_row, lse, start, pairs, at, size, before=None):
+    length, width = out.shape
+    total = width // LANES
     rows = min(256, length)
-    pair = pl.BlockSpec((length, LANES), lambda j: (0, j + start))
+    anywhere = pl.BlockSpec(memory_space=pl.ANY)
+
+    def pair(part):
+        return pl.BlockSpec((length, LANES), lambda j: (0, part * total + start + j))
+
+    def body(*refs):
+        attention_backward_kernel(*refs[:8], *refs[-2:], rows=rows)
+
     return pl.pallas_call(
-        functools.partial(attention_backward_kernel, rows=rows),
+        body,
         grid=(pairs,),
         in_specs=[
-            pair,
-            pair,
-            pair,
-            pair,
-            pair,
+            pair(0),
+            pair(1),
+            pair(2),
+            pair(0),
+            pair(0),
             pl.BlockSpec((length, 1), lambda j: (0, 0)),
             pl.BlockSpec((1, length), lambda j: (0, 0)),
             pl.BlockSpec((1, 2, length), lambda j: (j + start, 0, 0)),
-        ],
+        ]
+        + [anywhere] * (0 if before is None else 2),
         out_specs=[
-            pl.BlockSpec((3, length, LANES), lambda j: (0, 0, j)),
-            pl.BlockSpec((2, LANES), lambda j: (0, j)),
+            pl.BlockSpec((3, length, LANES), lambda j: (0, 0, j + at)),
+            pl.BlockSpec((2, LANES), lambda j: (0, j + at)),
         ],
         out_shape=[
-            jax.ShapeDtypeStruct((3, length, pairs * LANES), jnp.bfloat16),
-            jax.ShapeDtypeStruct((2, pairs * LANES), jnp.float32),
+            jax.ShapeDtypeStruct((3, length, size * LANES), jnp.bfloat16),
+            jax.ShapeDtypeStruct((2, size * LANES), jnp.float32),
         ],
-        compiler_params=params(),
+        input_output_aliases={} if before is None else {8: 0, 9: 1},
+        compiler_params=params(40),
         cost_estimate=pl.CostEstimate(
             flops=40 * length * length * pairs * LANES,
             bytes_accessed=16 * length * pairs * LANES,
             transcendentals=0,
         ),
         name="attn_bwd",
-    )(q, k, v, out, out_grad, seg_col, seg_row, lse)
+    )(qkv, qkv, qkv, out, out_grad, seg_col, seg_row, lse, *(() if before is None else before))
 
 
 class Place:
@@ -505,54 +529,400 @@
         return lax.ppermute(array, AXES, pairs)
 
 
-def gather_pieces(place, piece):
-    rows = piece.shape[0]
-    half = rows // 2
-    along = [piece] + [place.swap(piece, chip=k) for k in range(1, place.chips)]
-    upper = [jnp.stack([p[:half] for p in along]), None, None, None]
-    lower = [jnp.stack([p[half:] for p in along]), None, None, None]
-    upper[1] = place.swap(upper[0], grp=1)
-    lower[2] = place.swap(lower[0], grp=2)
-    upper[2] = place.swap(upper[0], grp=2)
-    lower[1] = place.swap(lower[0], grp=1)
-    upper[3] = place.swap(upper[1], grp=2)
-    lower[3] = place.swap(lower[2], grp=1)
-    mine = upper + lower
-    return mine + [place.swap(p, core=1) for p in mine]
-
-
-def assemble_kernel(where, *refs, groups):
-    *pieces, whole = refs
-    _, half, cols = pieces[0].shape
-    core, grp = where[0], where[2]
-    for n, piece in enumerate(pieces):
-        other_core, lower, other_grp = n // (2 * groups), (n // groups) % 2, n % groups
-        col = pl.multiple_of((grp ^ other_grp) * cols, LANES)
-        row = pl.multiple_of(((core ^ other_core) * 2 + lower) * half, half)
-        whole[pl.ds(row, half), pl.ds(col, cols)] = piece[0]
-
-
-def assemble(place, pieces, name):
+def after(value, *others):
+    return lax.optimization_barrier((value, *others))[0]
+
+
+class Gather:
+    def __init__(self, place, piece):
+        self.place = place
+        half = piece.shape[0] // 2
+        self.halves = [piece[:half], piece[half:]]
+        self.mine = [[None] * place.groups for _ in range(2)]
+        self.theirs = [[None] * place.groups for _ in range(2)]
+
+    def chips(self, half, *wait):
+        piece = after(self.halves[half], *wait) if wait else self.halves[half]
+        place = self.place
+        along = [piece] + [place.swap(piece, chip=k) for k in range(1, place.chips)]
+        self.mine[half][0] = jnp.stack(along)
+        return self.mine[half][0]
+
+    def near(self, half, *wait):
+        slots = self.mine[half]
+        piece = after(slots[0], *wait) if wait else slots[0]
+        order = (1, 2) if half == 0 else (2, 1)
+        for k in order:
+            slots[k] = self.place.swap(piece, grp=k)
+        return slots[order[0]]
+
+    def far(self, half, *wait):
+        slots = self.mine[half]
+        first, second = (1, 2) if half == 0 else (2, 1)
+        piece = after(slots[first], *wait) if wait else slots[first]
+        slots[3] = self.place.swap(piece, grp=second)
+        return slots[3]
+
+    def cross(self, half, slot, *wait):
+        piece = self.mine[half][slot]
+        piece = after(piece, *wait) if wait else piece
+        self.theirs[half][slot] = self.place.swap(piece, core=1)
+
+    def pieces(self):
+        return [p for side in (self.mine, self.theirs) for half in side for p in half]
+
+
+def fetch(where, pieces, whole, sem, groups, by):
     chips, half, cols = pieces[0].shape
-    shape = (chips * 4 * half, place.groups * cols)
+    core, chip, grp = where[0], where[1], where[2]
+    for k in range(chips):
+        for n, piece in enumerate(pieces):
+            other_core, lower, other_grp = n // (2 * groups), (n // groups) % 2, n % groups
+            col = pl.multiple_of((grp ^ other_grp) * cols, LANES)
+            row = pl.multiple_of((((chip ^ k) * 2 + (core ^ other_core)) * 2 + lower) * half, half)
+            slot = {"grp": other_grp, "chip": k, "all": 0}[by]
+            pltpu.make_async_copy(
+                piece.at[k], whole.at[pl.ds(row, half), pl.ds(col, cols)], sem.at[slot]
+            ).start()
+
+
+def fetched(view, sem):
+    pltpu.make_async_copy(view, view, sem).wait()
+
+
+def weight_call(place, kernel, pieces, inputs, in_specs, outs, out_specs, steps, by, name, flops, mb=40):
+    chips, half, cols = pieces[0].shape
+    groups = place.groups
+    shape = (chips * 4 * half, groups * cols)
+    slots = {"grp": groups, "chip": chips, "all": 1}[by]
+    anywhere = pl.BlockSpec(memory_space=pl.ANY)
+
+    def body(where, *refs):
+        taken, refs = refs[: len(pieces)], refs[len(pieces) :]
+        *refs, weight, sem = refs
+        step = pl.program_id(0)
+
+        @pl.when(step == 0)
+        def _():
+            fetch(where, taken, weight, sem, groups, by)
+
+        def ready():
+            if by == "all":
+
+                @pl.when(step == 0)
+                def _():
+                    fetched(weight, sem.at[0])
+
+            elif by == "grp":
+                at = pl.multiple_of((where[2] ^ step) * cols, LANES)
+                fetched(weight.at[:, pl.ds(at, cols)], sem.at[step])
+            else:
+                at = pl.multiple_of((where[1] ^ step) * 4 * half, 4 * half)
+                fetched(weight.at[pl.ds(at, 4 * half), :], sem.at[step])
+
+        kernel(where, ready, weight, *refs)
+
+    total = sum(math.prod(x.shape) * x.dtype.itemsize for x in list(inputs) + list(outs))
     return pl.pallas_call(
-        functools.partial(assemble_kernel, groups=place.groups),
+        body,
         grid_spec=pltpu.PrefetchScalarGridSpec(
             num_scalar_prefetch=1,
-            grid=(chips,),
-            in_specs=[pl.BlockSpec((1, half, cols), lambda i, s: (i ^ s[1], 0, 0))] * len(pieces),
-            out_specs=pl.BlockSpec((4 * half, shape[1]), lambda i, s: (i, 0)),
+            grid=(steps,),
+            in_specs=[anywhere] * len(pieces) + in_specs,
+            out_specs=out_specs,
+            scratch_shapes=[pltpu.VMEM(shape, jnp.bfloat16), pltpu.SemaphoreType.DMA((slots,))],
         ),
-        out_shape=jax.ShapeDtypeStruct(shape, jnp.bfloat16),
-        compiler_params=params(),
+        out_shape=outs,
+        compiler_params=params(mb),
         cost_estimate=pl.CostEstimate(
-            flops=0, bytes_accessed=4 * shape[0] * shape[1], transcendentals=0
+            flops=flops, bytes_accessed=2 * shape[0] * shape[1] + total, transcendentals=0
         ),
-        name="assemble_" + name,
-    )(place.scalars, *pieces)
+        name=name,
+    )(place.scalars, *pieces, *inputs)
+
+
+TILE = 256
+
+
+def row_tiles(width):
+    return pl.BlockSpec((TILE, width), lambda i, s: (i, 0))
+
+
+def fixed(*shape):
+    return pl.BlockSpec(shape, lambda i, s: (0,) * len(shape))
+
+
+def shaped(shape, dtype):
+    return jax.ShapeDtypeStruct(shape, dtype)
+
+
+def project_qkv(place, rows, pieces, bias, scale):
+    length, width = rows.shape
+    cols = pieces[0].shape[2]
+
+    def kernel(where, ready, weight, x_ref, bias_ref, scale_ref, out_ref):
+        ready()
+        at = pl.ds(pl.multiple_of((where[2] ^ pl.program_id(0)) * cols, LANES), cols)
+        for tile in range(length // TILE):
+            here = pl.ds(tile * TILE, TILE)
+            mixed = mxu(x_ref[here, :], weight[:, at], NN) + bias_ref[:, at]
+            mixed = mixed.astype(jnp.bfloat16).astype(jnp.float32) * scale_ref[:, at]
+            out_ref[here, :] = mixed.astype(jnp.bfloat16)
+
+    total = cols * place.groups
+    return weight_call(
+        place,
+        kernel,
+        pieces,
+        (rows, bias, scale),
+        [fixed(length, width), fixed(1, total), fixed(1, total)],
+        [shaped((length, total), jnp.bfloat16)],
+        [pl.BlockSpec((length, cols), lambda i, s: (0, i ^ s[2]))],
+        place.groups,
+        "grp",
+        "qkv",
+        2 * length * width * total,
+    )[0]
+
+
+def norm_parts(rows):
+    centered = rows - jnp.mean(rows, -1, keepdims=True)
+    scale = lax.rsqrt(jnp.mean(centered * centered, -1, keepdims=True) + epsilon)
+    return centered * scale, scale
+
+
+def norm_back(grad, normed, scale):
+    return scale * (
+        grad
+        - jnp.mean(grad, -1, keepdims=True)
+        - normed * jnp.mean(grad * normed, -1, keepdims=True)
+    )
+
+
+def add_rows(sum_ref, *terms):
+    @pl.when(pl.program_id(0) == 0)
+    def _():
+        sum_ref[...] = jnp.zeros_like(sum_ref)
+
+    for n, term in enumerate(terms):
+        sum_ref[n : n + 1, :] += jnp.sum(term, 0, keepdims=True)
+
+
+def project_out(place, contexts, pieces, rows, bias, gain, shift):
+    length, width = rows.shape
+
+    def kernel(where, ready, weight, c_ref, x_ref, b_ref, g_ref, s_ref, n_ref, r_ref, low_ref):
+        ready()
+        first_sum = mxu(c_ref[...], weight[...], NN) + b_ref[...] + x_ref[...].astype(jnp.float32)
+        normed, scale = norm_parts(first_sum)
+        n_ref[...] = normed
+        r_ref[...] = jnp.broadcast_to(scale, r_ref.shape)
+        low_ref[...] = (normed * g_ref[...] + s_ref[...]).astype(jnp.bfloat16)
+
+    return weight_call(
+        place,
+        kernel,
+        pieces,
+        (contexts, rows, bias, gain, shift),
+        [row_tiles(width), row_tiles(width)] + [fixed(1, width)] * 3,
+        [
+            shaped((length, width), jnp.float32),
+            shaped((length, LANES), jnp.float32),
+            shaped((length, width), jnp.bfloat16),
+        ],
+        [row_tiles(width), row_tiles(LANES), row_tiles(width)],
+        length // TILE,
+        "all",
+        "attn_out",
+        2 * length * width * width,
+    )
+
+
+def feed_in(place, normed_low, pieces, bias):
+    length, width = normed_low.shape
+    cols = pieces[0].shape[2]
+
+    def kernel(where, ready, weight, x_ref, bias_ref, hid_ref, slope_ref):
+        ready()
+        at = pl.ds(pl.multiple_of((where[2] ^ pl.program_id(0)) * cols, LANES), cols)
+        for tile in range(length // TILE):
+            here = pl.ds(tile * TILE, TILE)
+            pre = mxu(x_ref[here, :], weight[:, at], NN) + bias_ref[:, at]
+            share = 0.5 + 0.5 * lax.erf(pre * (1.0 / math.sqrt(2.0)))
+            bell = jnp.exp(-0.5 * pre * pre) * (1.0 / math.sqrt(2.0 * math.pi))
+            hid_ref[here, :] = (pre * share).astype(jnp.bfloat16)
+            slope_ref[here, :] = (share + pre * bell).astype(jnp.bfloat16)
+
+    total = cols * place.groups
+    block = pl.BlockSpec((length, cols), lambda i, s: (0, i ^ s[2]))
+    return weight_call(
+        place,
+        kernel,
+        pieces,
+        (normed_low, bias),
+        [fixed(length, width), fixed(1, total)],
+        [shaped((length, total), jnp.bfloat16)] * 2,
+        [block, block],
+        place.groups,
+        "grp",
+        "feed_in",
+        2 * length * width * total,
+    )
+
+
+def feed_out(place, hidden, pieces, normed, cot, keep, vectors):
+    length, inner = hidden.shape
+    width = normed.shape[1]
+
+    def kernel(where, ready, weight, h_ref, n_ref, cot_ref, keep_ref, g1, s1, b2, g2, s2, *outs):
+        out_ref, grad_ref, low_ref, sum_ref = outs
+        ready()
+        fed = mxu(h_ref[...], weight[...], NN)
+        second_sum = n_ref[...] * g1[...] + s1[...] + (fed + b2[...])
+        second, scale = norm_parts(second_sum)
+        out_ref[...] = (second * g2[...] + s2[...]).astype(jnp.bfloat16)
+        masked = cot_ref[...].astype(jnp.float32) * keep_ref[...]
+        grad = norm_back(masked * g2[...], second, scale)
+        grad_ref[...] = grad
+        low_ref[...] = grad.astype(jnp.bfloat16)
+        add_rows(sum_ref, masked * second, masked, grad)
+
+    return weight_call(
+        place,
+        kernel,
+        pieces,
+        (hidden, normed, cot, keep, *vectors),
+        [row_tiles(inner), row_tiles(width), row_tiles(width), row_tiles(1)] + [fixed(1, width)] * 5,
+        [
+            shaped((length, width), jnp.bfloat16),
+            shaped((length, width), jnp.float32),
+            shaped((length, width), jnp.bfloat16),
+            shaped((8, width), jnp.float32),
+        ],
+        [row_tiles(width), row_tiles(width), row_tiles(width), fixed(8, width)],
+        length // TILE,
+        "all",
+        "feed_out",
+        2 * length * width * inner,
+    )
+
+
+def feed_out_back(place, out_low, pieces, slope):
+    length, width = out_low.shape
+    inner = slope.shape[1]
+    cols = inner // place.chips
+
+    def kernel(where, ready, weight, g_ref, slope_ref, pre_ref, sum_ref):
+        ready_rows = pl.ds(pl.multiple_of((where[1] ^ pl.program_id(0)) * cols, cols), cols)
+        ready()
+        total = jnp.zeros((1, cols), jnp.float32)
+        for tile in range(length // TILE):
+            here = pl.ds(tile * TILE, TILE)
+            grad = mxu(g_ref[here, :], weight[ready_rows, :], NT) * slope_ref[here, :].astype(jnp.float32)
+            pre_ref[here, :] = grad.astype(jnp.bfloat16)
+            total = total + jnp.sum(grad, 0, keepdims=True)
+        sum_ref[...] = total
+
+    block = pl.BlockSpec((length, cols), lambda i, s: (0, i ^ s[1]))
+    return weight_call(
+        place,
+        kernel,
+        pieces,
+        (out_low, slope),
+        [fixed(length, width), block],
+        [shaped((length, inner), jnp.bfloat16), shaped((1, inner), jnp.float32)],
+        [block, pl.BlockSpec((1, cols), lambda i, s: (0, i ^ s[1]))],
+        place.chips,
+        "chip",
+        "feed_out_back",
+        2 * length * width * inner,
+    )
+
+
+def feed_in_back(place, pre_low, pieces, second_grad, normed, scale, gain):
+    length, inner = pre_low.shape
+    width = normed.shape[1]
+
+    def kernel(where, ready, weight, p_ref, g_ref, n_ref, r_ref, gain_ref, first_ref, low_ref, sum_ref):
+        ready()
+        grad = g_ref[...] + mxu(p_ref[...], weight[...], NT)
+        first = norm_back(grad * gain_ref[...], n_ref[...], r_ref[:, :1])
+        first_ref[...] = first
+        low_ref[...] = first.astype(jnp.bfloat16)
+        add_rows(sum_ref, grad * n_ref[...], grad, first)
+
+    return weight_call(
+        place,
+        kernel,
+        pieces,
+        (pre_low, second_grad, normed, scale, gain),
+        [row_tiles(inner), row_tiles(width), row_tiles(width), row_tiles(LANES), fixed(1, width)],
+        [
+            shaped((length, width), jnp.float32),
+            shaped((length, width), jnp.bfloat16),
+            shaped((8, width), jnp.float32),
+        ],
+        [row_tiles(width), row_tiles(width), fixed(8, width)],
+        length // TILE,
+        "all",
+        "feed_in_back",
+        2 * length * width * inner,
+    )
+
+
+def project_out_back(place, attn_low, pieces):
+    length, width = attn_low.shape
+
+    def kernel(where, ready, weight, g_ref, out_ref):
+        ready()
+        out_ref[...] = mxu(g_ref[...], weight[...], NT).astype(jnp.bfloat16)
+
+    return weight_call(
+        place,
+        kernel,
+        pieces,
+        (attn_low,),
+        [row_tiles(width)],
+        [shaped((length, width), jnp.bfloat16)],
+        [row_tiles(width)],
+        length // TILE,
+        "all",
+        "attn_out_back",
+        2 * length * width * width,
+    )[0]
+
+
+def project_qkv_back(place, grads, pieces, first_grad):
+    length, width = first_grad.shape
+    part = width // len(grads)
+
+    def kernel(where, ready, weight, *refs):
+        *grad_refs, first_ref, out_ref = refs
+        ready()
+        total = first_ref[...]
+        for n in range(3):
+            for m, grad_ref in enumerate(grad_refs):
+                at = n * width + m * part
+                total = total + mxu(grad_ref[n], weight[:, at : at + part], NT)
+        out_ref[...] = total
+
+    return weight_call(
+        place,
+        kernel,
+        pieces,
+        (*grads, first_grad),
+        [pl.BlockSpec((3, TILE, part), lambda i, s: (0, i, 0))] * len(grads) + [row_tiles(width)],
+        [shaped((length, width), jnp.float32)],
+        [row_tiles(width)],
+        length // TILE,
+        "all",
+        "qkv_back",
+        6 * length * width * width,
+    )[0]
 
 
 def weight_grad_kernel(where, left_ref, right_ref, *refs, own, rows, groups, split):
+    *refs, kept = refs
     received = None
     if own:
         received, *outs = refs
@@ -561,43 +931,51 @@
     core, grp = where[0], where[2]
     keep = core if own else 1 - core
     chips = left_ref.shape[1] // (2 * rows)
-    lefts = []
-    for k in range(chips):
-        even = left_ref[:, 2 * k * rows : (2 * k + 1) * rows]
-        odd = left_ref[:, (2 * k + 1) * rows : (2 * k + 2) * rows]
-        lefts.append(jnp.where(keep == 0, even, odd))
-    left = lefts[0] if chips == 1 else jnp.concatenate(lefts, 1)
-    left = left.T
     half = rows // 2
 
-    def emit(slot, result):
-        result = result.reshape(chips, 2, half, result.shape[-1])
+    @pl.when(pl.program_id(1) == 0)
+    def _():
+        lefts = []
+        for k in range(chips):
+            even = left_ref[:, 2 * k * rows : (2 * k + 1) * rows]
+            odd = left_ref[:, (2 * k + 1) * rows : (2 * k + 2) * rows]
+            lefts.append(jnp.where(keep == 0, even, odd))
+        left = lefts[0] if chips == 1 else jnp.concatenate(lefts, 1)
+        kept[...] = left.T
+
+    def emit(slot, part, at):
+        part = part.reshape(chips, 2, half, part.shape[-1])
+        pos = 0 if split else slot
         if own:
-            pos = 0 if split else slot
-            result = result + received[pos].astype(jnp.float32)
-            result = result.astype(jnp.bfloat16)
-            for lower in range(2):
-                outs[slot + lower * groups][...] = result[:, lower]
+            part = part + received[pos, :, :, :, at].astype(jnp.float32)
+            part = part.astype(jnp.bfloat16)
+
+            def store(slot):
+                for lower in range(2):
+                    outs[slot + lower * groups][:, :, at] = part[:, lower]
+
+            if split:
+                for n in range(groups):
+                    pl.when(pl.program_id(1) == n)(functools.partial(store, n))
+            else:
+                store(slot)
         else:
-            outs[0][0 if split else slot] = result.astype(jnp.bfloat16)
-
-    if split:
-        if len(right_ref.shape) == 3:
-            result = jnp.concatenate(
-                [mxu(left, right_ref[n], NN) for n in range(right_ref.shape[0])], 1
-            )
-        else:
-            result = mxu(left, right_ref[...], NN)
-        if own:
-            for slot in range(groups):
-                pl.when(pl.program_id(1) == slot)(functools.partial(emit, slot, result))
-        else:
-            emit(0, result)
+            outs[0][pos, :, :, :, at] = part.astype(jnp.bfloat16)
+
+    if split and len(right_ref.shape) == 3:
+        size = right_ref.shape[2]
+        for n in range(right_ref.shape[0]):
+            emit(0, mxu(kept[...], right_ref[n], NN), slice(n * size, (n + 1) * size))
+    elif split:
+        size = min(512, right_ref.shape[1])
+        for n in range(right_ref.shape[1] // size):
+            at = slice(n * size, (n + 1) * size)
+            emit(0, mxu(kept[...], right_ref[:, at], NN), at)
     else:
         cols = right_ref.shape[1] // groups
         for slot in range(groups):
             at = pl.multiple_of((grp ^ slot) * cols, LANES)
-            emit(slot, mxu(left, right_ref[:, pl.ds(at, cols)], NN))
+            emit(slot, mxu(kept[...], right_ref[:, pl.ds(at, cols)], NN), slice(0, cols))
 
 
 def weight_grad(place, left, right, received, split, name):
@@ -630,19 +1008,21 @@
         in_specs.append(passed)
         inputs.append(received)
         out_specs = [pl.BlockSpec((step_chips, half, cols), lambda i, j, s: (i, 0, 0))] * (2 * groups)
-        out_shape = [jax.ShapeDtypeStruct((chips, half, cols), jnp.bfloat16)] * (2 * groups)
+        out_shape = [shaped((chips, half, cols), jnp.bfloat16)] * (2 * groups)
     else:
         out_specs = passed
-        out_shape = jax.ShapeDtypeStruct((groups, chips, 2, half, cols), jnp.bfloat16)
+        out_shape = shaped((groups, chips, 2, half, cols), jnp.bfloat16)
     return pl.pallas_call(
-        functools.partial(
-            weight_grad_kernel, own=own, rows=rows, groups=groups, split=split
-        ),
+        functools.partial(weight_grad_kernel, own=own, rows=rows, groups=groups, split=split),
         grid_spec=pltpu.PrefetchScalarGridSpec(
-            num_scalar_prefetch=1, grid=grid, in_specs=in_specs, out_specs=out_specs
+            num_scalar_prefetch=1,
+            grid=grid,
+            in_specs=in_specs,
+            out_specs=out_specs,
+            scratch_shapes=[pltpu.VMEM((step_chips * rows, tokens), jnp.bfloat16)],
         ),
         out_shape=out_shape,
-        compiler_params=params(),
+        compiler_params=params(40),
         cost_estimate=pl.CostEstimate(
             flops=tokens * height * width,
             bytes_accessed=2 * (tokens * (height + width) + height * width),
@@ -659,27 +1039,58 @@
     return total.astype(jnp.bfloat16)
 
 
-def reduce_weight(place, left, right, split, name):
-    groups, chips = place.groups, place.chips
-    sent = weight_grad(place, left, right, None, split, name)
-    received = place.swap(sent, core=1)
-    own = weight_grad(place, left, right, received, split, name)
-    upper, lower = own[:groups], own[groups:]
-    upper_1, upper_3 = place.swap(upper[1], grp=1), place.swap(upper[3], grp=1)
-    lower_2, lower_3 = place.swap(lower[2], grp=2), place.swap(lower[3], grp=2)
-    upper_2 = place.swap(add(upper[2], upper_3), grp=2)
-    lower_1 = place.swap(add(lower[1], lower_3), grp=1)
-    mine = jnp.concatenate([add(upper[0], upper_1, upper_2), add(lower[0], lower_2, lower_1)], 1)
-    terms = [lax.dynamic_index_in_dim(mine, place.chip, 0, False)]
-    for k in range(1, chips):
-        outgoing = lax.dynamic_index_in_dim(mine, place.chip ^ k, 0, False)
-        terms.append(place.swap(outgoing, chip=k))
-    share = add(*terms)
-    return replicate(place, share)
-
-
-def replicate(place, share):
-    blocks = [share] + [place.swap(share, grp=k) for k in range(1, place.groups)]
+class Reduction:
+    def __init__(self, place, left, right, split, name, *wait):
+        self.place = place
+        left = after(left, *wait) if wait else left
+        self.call = (left, right, split, name)
+        self.sent = weight_grad(place, left, right, None, split, name)
+        self.received = place.swap(self.sent, core=1)
+
+    def own(self, *wait):
+        left, right, split, name = self.call
+        received = after(self.received, *wait) if wait else self.received
+        out = weight_grad(self.place, left, right, received, split, name)
+        swap, groups = self.place.swap, self.place.groups
+        self.upper, self.lower = out[:groups], out[groups:]
+        self.near = [
+            swap(self.upper[3], grp=1),
+            swap(self.lower[3], grp=2),
+            swap(self.upper[1], grp=1),
+            swap(self.lower[2], grp=2),
+        ]
+        return out[0]
+
+    def middle(self, *wait):
+        near = after(self.near[0], *wait) if wait else self.near[0]
+        upper = add(self.upper[2], near)
+        lower = add(self.lower[1], self.near[1])
+        self.far = [self.place.swap(upper, grp=2), self.place.swap(lower, grp=1)]
+        return upper
+
+    def along(self, *wait):
+        place = self.place
+        far = after(self.far[0], *wait) if wait else self.far[0]
+        mine = jnp.concatenate(
+            [add(self.upper[0], self.near[2], far), add(self.lower[0], self.near[3], self.far[1])], 1
+        )
+        self.terms = [lax.dynamic_index_in_dim(mine, place.chip, 0, False)]
+        for k in range(1, place.chips):
+            outgoing = lax.dynamic_index_in_dim(mine, place.chip ^ k, 0, False)
+            self.terms.append(place.swap(outgoing, chip=k))
+        return self.terms[0]
+
+    def share(self, *wait):
+        last = after(self.terms[-1], *wait) if wait else self.terms[-1]
+        share = add(*self.terms[:-1], last)
+        self.blocks = [share] + [self.place.swap(share, grp=k) for k in range(1, self.place.groups)]
+        return share
+
+    def result(self):
+        return in_order(self.place, self.blocks)
+
+
+def in_order(place, blocks):
     blocks = [b.astype(jnp.float32) for b in blocks]
     ordered = []
     for g in range(place.groups):
@@ -758,106 +1169,168 @@
         gain_two,
         shift_two,
     ) = unpacked
-    full_qkv = assemble(place, gather_pieces(place, w_qkv), "qkv")
-    full_attn = assemble(place, gather_pieces(place, w_attn_out), "attn")
-    full_in = assemble(place, gather_pieces(place, w_in), "in")
-    full_out = assemble(place, gather_pieces(place, w_out), "out")
-
     rows = tokens[0]
     seg_row = segment_ids.reshape(1, length)
     seg_col = segment_ids.reshape(length, 1)
-    scaling = 1.0 / math.sqrt(HD)
-    mixed_qkv = jnp.dot(rows, full_qkv, preferred_element_type=jnp.float32)
-    queries = ((mixed_qkv[:, :width] + bias_query).astype(jnp.bfloat16) * scaling).astype(
-        jnp.bfloat16
-    )
-    key_rows = mixed_qkv[:, width : 2 * width].astype(jnp.bfloat16)
-    value_rows = (mixed_qkv[:, 2 * width :] + bias_value).astype(jnp.bfloat16)
-    contexts, lse = attention_forward(queries, key_rows, value_rows, seg_col, seg_row)
-    attended = jnp.dot(contexts, full_attn, preferred_element_type=jnp.float32) + bias_attn
-    first_sum = rows.astype(jnp.float32) + attended
-    normed_one, norm_one_back = jax.vjp(norm_layer, first_sum, gain_one, shift_one)
-    normed_low = normed_one.astype(jnp.bfloat16)
-    hidden_pre = jnp.dot(normed_low, full_in, preferred_element_type=jnp.float32) + bias_in
-    hidden, gelu_back = jax.vjp(gelu_exact, hidden_pre)
-    hidden_low = hidden.astype(jnp.bfloat16)
-    second_sum = normed_one + (
-        jnp.dot(hidden_low, full_out, preferred_element_type=jnp.float32) + bias_out
-    )
-    result, norm_two_back = jax.vjp(norm_layer, second_sum, gain_two, shift_two)
-    layer_out = result.astype(jnp.bfloat16)[None]
-
-    masked_cot = cotangent[0].astype(jnp.float32) * keep_flag.reshape(length, 1).astype(jnp.float32)
-    second_grad, gain_two_grad, shift_two_grad = norm_two_back(masked_cot)
-    bias_out_grad = jnp.sum(second_grad, 0)
-    out_low = second_grad.astype(jnp.bfloat16)
-    w_out_grad = reduce_weight(place, hidden_low, out_low, False, "out")
-    hidden_grad = contract_cols(out_low, full_out)
-    (pre_grad,) = gelu_back(hidden_grad)
-    bias_in_grad = jnp.sum(pre_grad, 0)
-    pre_low = pre_grad.astype(jnp.bfloat16)
-    w_in_grad = reduce_weight(place, normed_low, pre_low, True, "in")
-    normed_grad = second_grad + contract_cols(pre_low, full_in)
-    first_grad, gain_one_grad, shift_one_grad = norm_one_back(normed_grad)
-    bias_attn_grad = jnp.sum(first_grad, 0)
-    attn_low = first_grad.astype(jnp.bfloat16)
-    w_attn_grad = reduce_weight(place, contexts, attn_low, False, "attn")
-    context_grad = contract_cols(attn_low, full_attn).astype(jnp.bfloat16)
-    early = (
-        bias_attn_grad,
-        gain_one_grad[0],
-        shift_one_grad[0],
-        bias_in_grad,
-        bias_out_grad,
-        gain_two_grad[0],
-        shift_two_grad[0],
-    )
-    early_sum = sum_everywhere(place, jnp.concatenate(early).reshape(-1, LANES)).reshape(-1)
-    early_parts = []
+    keep = keep_flag.reshape(length, 1).astype(jnp.float32)
+    pairs = width // LANES
+    blank = jnp.zeros_like(bias_query)
+    qkv_bias = jnp.concatenate([bias_query, blank, bias_value], 1)
+    qkv_scale = jnp.concatenate([blank + 1.0 / math.sqrt(HD), blank + 1.0, blank + 1.0], 1)
+
+    qkv, attn = Gather(place, w_qkv), Gather(place, w_attn_out)
+    fin, fout = Gather(place, w_in), Gather(place, w_out)
+    t0 = qkv.chips(0)
+    t1 = qkv.chips(1, t0)
+    qkv.near(0)
+    qkv.near(1, qkv.mine[0][1], qkv.mine[0][2])
+    qkv.far(0)
+    qkv.far(1)
+    tz = [g.chips(half, t1) for g in (attn, fin) for half in range(2)]
+    for half, slot in ((0, 0), (0, 1), (0, 2), (1, 0), (1, 1), (1, 2), (0, 3), (1, 3)):
+        qkv.cross(half, slot)
+    last = (qkv.mine[0][1], qkv.mine[1][2], qkv.mine[1][1])
+    for g in (attn, fin):
+        for half in range(2):
+            g.near(half, *last)
+    for half in range(2):
+        fout.chips(half, *tz)
+    mixed = project_qkv(place, rows, qkv.pieces(), qkv_bias, qkv_scale)
+
+    forward = attention_forward(mixed, seg_col, seg_row, 0, pairs // 2)
+    forward_gate = forward[1]
+    for g in (attn, fin):
+        for half in range(2):
+            g.far(half, mixed)
+    for half in range(2):
+        fout.near(half, attn.mine[0][2], attn.mine[1][1], fin.mine[0][2], fin.mine[1][1])
+    for g in (attn, fin):
+        for half in range(2):
+            for slot in range(3):
+                g.cross(half, slot)
+    contexts, lse = attention_forward(
+        after(mixed, fin.mine[0][1], fin.mine[1][2]), seg_col, seg_row, pairs // 2, pairs // 2, forward
+    )
+    for g in (attn, fin):
+        for half in range(2):
+            g.cross(half, 3)
+    for half in range(2):
+        fout.far(half, forward_gate)
+    normed, scale_one, normed_low = project_out(
+        place, contexts, attn.pieces(), rows, bias_attn, gain_one, shift_one
+    )
+    for half in range(2):
+        for slot in range(4):
+            fout.cross(half, slot)
+    hidden, slope = feed_in(place, normed_low, fin.pieces(), bias_in)
+    layer_out, second_grad, out_low, second_sums = feed_out(
+        place,
+        hidden,
+        fout.pieces(),
+        normed,
+        cotangent[0],
+        keep,
+        (gain_one, shift_one, bias_out, gain_two, shift_two),
+    )
+
+    r_out = Reduction(place, hidden, out_low, False, "out")
+    pre_low, bias_in_grad = feed_out_back(place, after(out_low, r_out.sent), fout.pieces(), slope)
+    own_out = r_out.own(pre_low)
+    r_in = Reduction(place, normed_low, pre_low, True, "in", own_out)
+    first_grad, attn_low, first_sums = feed_in_back(
+        place, after(pre_low, r_in.sent), fin.pieces(), second_grad, normed, scale_one, gain_one
+    )
+    own_in = r_in.own(first_grad)
+    r_attn = Reduction(place, contexts, attn_low, False, "attn", own_in)
+    context_grad = project_out_back(place, after(attn_low, r_attn.sent), attn.pieces())
+    own_attn = r_attn.own(context_grad)
+    quarter = pairs // 4
+
+    def back(start, at, before=None, *wait):
+        return attention_backward(
+            mixed,
+            contexts,
+            after(context_grad, *wait),
+            seg_col,
+            seg_row,
+            lse,
+            start,
+            quarter,
+            at,
+            2 * quarter,
+            before,
+        )
+
+    mid_out = r_out.middle(own_attn)
+    part = back(0, 0, None, mid_out)
+    mid_in = r_in.middle(part[1])
+    low_a, late_a = back(quarter, quarter, part, mid_in)
+    along_out = r_out.along(late_a)
+    mid_attn = r_attn.middle(late_a)
+    r_qkv_a = Reduction(place, rows, low_a, True, "qkv_a", along_out, mid_attn)
+    part = back(2 * quarter, 0, None, r_qkv_a.sent)
+    along_in = r_in.along(part[1])
+    along_attn = r_attn.along(part[1])
+    share_out = r_out.share(part[1])
+    own_a = r_qkv_a.own(part[1], along_in, along_attn, share_out)
+    low_b, late_b = back(3 * quarter, quarter, part, own_a)
+    mid_a = r_qkv_a.middle(late_b)
+    share_in = r_in.share(late_b)
+    share_attn = r_attn.share(late_b)
+    r_qkv_b = Reduction(place, rows, low_b, True, "qkv_b", mid_a, share_in, share_attn)
+    input_grad = project_qkv_back(place, (low_a, after(low_b, r_qkv_b.sent)), qkv.pieces(), first_grad)
+    own_b = r_qkv_b.own(input_grad)
+    r_qkv_a.along(own_b)
+    r_qkv_b.middle()
+    r_qkv_a.share()
+    r_qkv_b.along()
+    r_qkv_b.share()
+
+    sums = (
+        jnp.concatenate([late_a[0], late_b[0]]),
+        jnp.concatenate([late_a[1], late_b[1]]),
+        first_sums[2],
+        first_sums[0],
+        first_sums[1],
+        bias_in_grad[0],
+        second_sums[2],
+        second_sums[0],
+        second_sums[1],
+    )
+    summed = sum_everywhere(place, jnp.concatenate(sums).reshape(-1, LANES)).reshape(-1)
+    vectors = []
     at = 0
-    for vector in early:
-        early_parts.append(own_part(place, early_sum[at : at + vector.shape[0]]))
+    for vector in sums:
+        vectors.append(own_part(place, summed[at : at + vector.shape[0]]))
         at += vector.shape[0]
 
-    qkv_low, late = attention_backward(
-        queries,
-        key_rows,
-        value_rows,
-        contexts,
-        context_grad,
-        seg_col,
-        seg_row,
-        lse,
-        0,
-        width // LANES,
-    )
-    late_sum = sum_everywhere(place, late)
-    w_qkv_grad = reduce_weight(place, rows, qkv_low, True, "qkv")
-    input_grad = first_grad
-    for n in range(3):
-        input_grad = input_grad + contract_cols(
-            qkv_low[n], full_qkv[:, n * width : (n + 1) * width]
-        )
-    heads = width // groups
+    parts_a, parts_b = r_qkv_a.result(), r_qkv_b.result()
+    heads = parts_a[0].shape[1] // 3
     w_qkv_grad = jnp.concatenate(
-        [block[:, n * heads : (n + 1) * heads] for n in range(3) for block in w_qkv_grad], 1
+        [
+            block[:, n * heads : (n + 1) * heads]
+            for n in range(3)
+            for half in (parts_a, parts_b)
+            for block in half
+        ],
+        1,
     )
     return (
-        layer_out,
+        layer_out[None],
         input_grad[None],
         w_qkv_grad,
-        own_part(place, late_sum[0]),
-        own_part(place, late_sum[1]),
-        jnp.concatenate(w_attn_grad, 1),
-        early_parts[0],
-        early_parts[1],
-        early_parts[2],
-        jnp.concatenate(w_in_grad, 1),
-        early_parts[3],
-        jnp.concatenate(w_out_grad, 1),
-        early_parts[4],
-        early_parts[5],
-        early_parts[6],
+        vectors[0],
+        vectors[1],
+        jnp.concatenate(r_attn.result(), 1),
+        vectors[2],
+        vectors[3],
+        vectors[4],
+        jnp.concatenate(r_in.result(), 1),
+        vectors[5],
+        jnp.concatenate(r_out.result(), 1),
+        vectors[6],
+        vectors[7],
+        vectors[8],
     )
 
 

time: 682 us -> 687 us (level)
  matrix products: 107 us -> 0 us
  Pallas kernels: 187 us -> 260 us
  local copies, waits for them, and re-layouts: 27.1 us -> 73.6 us
  starting transfers between devices: 118 us -> 141 us
  waiting for transfers between devices: 184 us -> 165 us
  other arithmetic: 31 us -> 21.9 us
    dot_general x10 -> x0, matrix products: 107 us -> none  [the longest x6 62.5 us: contract_cols(): lax.dot_general(left, right, (((1,), (1,)), ((), ())), preferred_element_...]
    pallas_call x6 -> x14, Pallas kernels: 115 us -> 196 us  [the longest x8 106 us: weight_call(): pl.pallas_call(body, grid_spec=pltpu.PrefetchScalarGridSpec(num_scalar_pr...]
    unnamed x170 -> x336, local copies, waits for them, and re-layouts: 16 us -> 61.9 us
    ppermute x130 -> x150, starting transfers between devices: 118 us -> 141 us  [swap(): return lax.ppermute(array, AXES, pairs)]
    ppermute x130 -> x150, waiting for transfers between devices: 184 us -> 165 us  [swap(): return lax.ppermute(array, AXES, pairs)]
    reduce_sum x7 -> x0, other arithmetic: 11 us -> none  [the longest x2 5.26 us: norm_layer(): centered = rows - row_mean]
    pallas_call x8 -> x10, Pallas kernels: 72.2 us -> 63.9 us  [weight_grad(): pl.pallas_call(functools.partial(weight_grad_kernel, own=own, rows=rows,...]
  transfers between devices with their start and end apart: 130 -> 150, of which waited for: 44 -> 48; matrix products, arithmetic and copies ran while one was open for 11% -> 6% of each run, Pallas kernels for 17% -> 32%
where the time goes in v2:
time: 687 us; the launch traced here: 678 us
  Pallas kernels  260 us (38%)
  waiting for transfers between devices  165 us (24%)
  starting transfers between devices  141 us (21%)
  local copies, waits for them, and re-layouts  73.6 us (11%)
  other arithmetic  21.9 us (3%)
  blocking collectives  14 us (2%)
    ppermute x150, waiting for transfers between devices, swap(): return lax.ppermute(array, AXES, pairs)  165 us
    ppermute x150, starting transfers between devices, swap(): return lax.ppermute(array, AXES, pairs)  141 us
    pallas_call x8, Pallas kernels, weight_call(): pl.pallas_call(body, grid_spec=pltpu.PrefetchScalarGridSpec(num_scalar_pr...  106 us
    pallas_call x10, Pallas kernels, weight_grad(): pl.pallas_call(functools.partial(weight_grad_kernel, own=own, rows=rows,...  63.9 us
    unnamed x336, local copies, waits for them, and re-layouts  61.9 us
    pallas_call x4, Pallas kernels, attention_backward(): pl.pallas_call(body, grid=(pairs,), in_specs=[pair(0), pair(1), pair(2),...  56.4 us
    pallas_call x2, Pallas kernels, attention_forward(): pl.pallas_call(body, grid=(pairs,), in_specs=[pair(0), pair(1), pair(2),...  33.4 us
    all_gather x1, blocking collectives, on_device_permutes(): packed = lax.all_gather(jnp.concatenate(vectors), 'shard', axis=0)  14 us
  transfers between devices with their start and end apart: 150, of which 48 were waited for; matrix products, arithmetic and copies ran while one was open for 6% of the time, Pallas kernels for 32%

profile of v2, /device:TPU:0, one launch (start us, length us, event | category | flops | bytes accessed | tf_op | source)
XLA Modules:
  0.0 678.5 jit_solution(11129933527784255023)
XLA Ops:
  1.7 3.1 collective-permute-start
  4.8 2.6 collective-permute-start.1
  8.4 6.8 %collective-permute-done.1 = bf16[64,768]{1,0:T(8,128)(2,1)S(1)} collective-permute-done((bf16[64,768]{1,0:T(8,128)(2,1)S(1)}, bf16[64,768]{1,0:T(8,128)(2,1)S(1)}, u32[]{:S(2)}, u32[]{:S(2)}) %collective-permute-start.1) | collective-permute-done | bytes 98336 | tf_op jit(solution)/shard_map/ppermute | solution.py:529
  15.2 2.5 collective-permute-start.5
  19.7 2.4 collective-permute-done.5
  36.5 2.6 collective-permute-done.6
  39.8 7.6 %collective-permute-done.7 = bf16[64,256]{1,0:T(8,128)(2,1)S(1)} collective-permute-done((bf16[64,256]{1,0:T(8,128)(2,1)S(1)}, bf16[64,256]{1,0:T(8,128)(2,1)S(1)}, u32[]{:S(2)}, u32[]{:S(2)}) %collective-permute-start.7) | collective-permute-done | bytes 32800 | tf_op jit(solution)/shard_map/ppermute | solution.py:529
  49.1 2.7 collective-permute-start.14
  55.7 3.2 collective-permute-done.13
  62.3 2.4 collective-permute-start.44
  66.3 7.3 %collective-permute-done.43 = bf16[256,256]{1,0:T(8,128)(2,1)S(1)} collective-permute-done((bf16[256,256]{1,0:T(8,128)(2,1)S(1)}, bf16[256,256]{1,0:T(8,128)(2,1)S(1)}, u32[]{:S(2)}, u32[]{:S(2)}) %collective-permute-start.43) | collective-permute-done | bytes 131104 | tf_op jit(solution)/shard_map/ppermute | solution.py:529
  75.7 3.4 collective-permute-done.18
  79.1 2.5 collective-permute-done.19
  83.0 6.4 collective-permute-done.20
  97.0 3.9 collective-permute-done.23.refs_6_
  102.0 6.4 collective-permute-done.31.refs_3_
  117.1 8.9 %collective-permute-done.26.refs_5_ = bf16[4,64,256]{2,1,0:T(8,128)(2,1)S(1)} collective-permute-done((bf16[4,64,256]{2,1,0:T(8,128)(2,1)}, bf16[4,64,256]{2,1,0:T(8,128)(2,1)S(1)}, u32[]{:S(2)}, u32[]{:S(2)}) %collective-permute-start.26) | collective-permute-done | bytes 131104 | tf_op jit(solution)/shard_map/ppermute | solution.py:529
  135.4 14.0 %all-gather.1 = bf16[8,1,1536]{2,1,0:T(2,128)(2,1)S(1)} all-gather(bf16[1,1,1536]{2,1,0:T(2,128)(2,1)S(1)} %reshape.213), channel_id=2, replica_groups=mesh['grp'=4,'shard'=8] {'shard'}, dimensions={0}, use_global_device_ids=true | all-gather | bytes 27648 | tf_op jit(solution)/shard_map/all_gather | solution.py:1154
  169.3 10.4 %qkv.1.q_ref.k_ref.v_ref.refs_0_.refs_1_.refs_2_ = bf16[1024,3072]{1,0:T(8,128)(2,1)} custom-call(s32[3]{0:T(128)S(1)} %pad_add_fusion.where, bf16[4,64,768]{2,1,0:T(8,128)(2,1)S(1)} %pad_maximum_fusion.7.refs_0_, bf16[4,64,768]{2,1,0:T(8,128)(2,1)S(1)} %copy-done.62, bf16[4,64,768]{2,1,0:T(8,128)(2,1)S(1)} %copy-done.65, ...), custom_call_target="tpu_custom_call" | custom-call | flops 6442450944 | bytes 14704640 | tf_op jit(solution)/shard_map/qkv/pallas_call | solution.py:626
  182.0 3.9 collective-permute-done.71.refs_7_
  196.2 2.8 copy-done.125
  199.0 16.7 %attn_fwd.2 = (bf16[1024,1024]{1,0:T(8,128)(2,1)S(1)}, f32[8,2,1024]{2,1,0:T(2,128)S(1)}) custom-call(bf16[1024,3072]{1,0:T(8,128)(2,1)S(1)} %copy-done.125, bf16[1024,3072]{1,0:T(8,128)(2,1)S(1)} %copy-done.125, bf16[1024,3072]{1,0:T(8,128)(2,1)S(1)} %copy-done.125, s32[1024,1]{1,0:T(8,128)S(1)} %copy.52.seg_c.refs_5_, s32[1,1024]{1,0:T(1,128)S(1)} %copy-done.26), custom_call_target="tpu_custom_call" | custom-call | flops 8589934592 | bytes 4194304 | tf_op jit(solution)/shard_map/attn_fwd/pallas_call | solution.py:385
  218.4 2.9 copy-done.126
  221.4 16.7 %attn_fwd.3 = (bf16[1024,1024]{1,0:T(8,128)(2,1)S(1)}, f32[8,2,1024]{2,1,0:T(2,128)S(1)}) custom-call(bf16[1024,3072]{1,0:T(8,128)(2,1)S(1)} %copy-done.126, bf16[1024,3072]{1,0:T(8,128)(2,1)S(1)} %copy-done.126, bf16[1024,3072]{1,0:T(8,128)(2,1)S(1)} %copy-done.126, ...), custom_call_target="tpu_custom_call", output_to_operand_aliasing={{0}: (5, {}), {1}: (6, {})} | custom-call | flops 8589934592 | bytes 4194304 | tf_op jit(solution)/shard_map/attn_fwd/pallas_call | solution.py:385
  238.9 6.4 attn_out.1
  252.6 19.9 %feed_in.1 = (bf16[1024,4096]{1,0:T(8,128)(2,1)}, bf16[1024,4096]{1,0:T(8,128)(2,1)}) custom-call(s32[3]{0:T(128)S(1)} %pad_add_fusion.where, bf16[4,64,1024]{2,1,0:T(8,128)(2,1)S(1)} %copy-done.8, bf16[4,64,1024]{2,1,0:T(8,128)(2,1)} %collective-permute-done.56.refs_1_, bf16[4,64,1024]{2,1,0:T(8,128)(2,1)} %collective-permute-done.27.refs_2_, ...), custom_call_target="tpu_custom_call" | custom-call | flops 8589934592 | bytes 27279360 | tf_op jit(solution)/shard_map/feed_in/pallas_call | solution.py:626
  272.7 18.8 %feed_out.1 = (bf16[1024,1024]{1,0:T(8,128)(2,1)}, f32[1024,1024]{1,0:T(8,128)}, bf16[1024,1024]{1,0:T(8,128)(2,1)S(1)}, f32[8,1024]{1,0:T(8,128)S(1)}) custom-call(s32[3]{0:T(128)S(1)} %pad_add_fusion.where, bf16[4,256,256]{2,1,0:T(8,128)(2,1)S(1)} %copy-done.13, bf16[4,256,256]{2,1,0:T(8,128)(2,1)} %collective-permute-done.29.refs_1_, ...), custom_call_target="tpu_custom_call" | custom-call | flops 8589934592 | bytes 31514624 | tf_op jit(solution)/shard_map/feed_out/pallas_call | solution.py:626
  291.5 8.1 %wgrad_out_sent.1 = bf16[4,4,2,256,256]{4,3,2,1,0:T(8,128)(2,1)S(1)} custom-call(s32[3]{0:T(128)S(1)} %pad_add_fusion.where, bf16[1024,4096]{1,0:T(8,128)(2,1)} %get-tuple-element.155.refs_16_.left_ref, bf16[1024,1024]{1,0:T(8,128)(2,1)S(1)} %get-tuple-element.159.right_ref.refs_16_), custom_call_target="tpu_custom_call" | custom-call | flops 4294967296 | bytes 18874368 | tf_op jit(solution)/shard_map/wgrad_out_sent/pallas_call | solution.py:1015
  301.5 14.9 %feed_out_back.1 = (bf16[1024,4096]{1,0:T(8,128)(2,1)}, f32[1,4096]{1,0:T(1,128)S(1)}) custom-call(s32[3]{0:T(128)S(1)} %pad_add_fusion.where, bf16[4,256,256]{2,1,0:T(8,128)(2,1)S(1)} %copy-done.13, bf16[4,256,256]{2,1,0:T(8,128)(2,1)} %collective-permute-done.29.refs_1_, bf16[4,256,256]{2,1,0:T(8,128)(2,1)S(1)} %collective-permute-done.30.refs_2_, ...), custom_call_target="tpu_custom_call" | custom-call | flops 8589934592 | bytes 27279360 | tf_op jit(solution)/shard_map/feed_out_back/pallas_call | solution.py:626
  318.0 7.9 %wgrad_out_own.1 = (bf16[4,256,256]{2,1,0:T(8,128)(2,1)S(1)}, bf16[4,256,256]{2,1,0:T(8,128)(2,1)S(1)}, bf16[4,256,256]{2,1,0:T(8,128)(2,1)S(1)}, bf16[4,256,256...) custom-call(s32[3]{0:T(128)S(1)} %pad_add_fusion.where, ...), custom_call_target="tpu_custom_call" | custom-call | flops 4294967296 | bytes 18874368 | tf_op jit(solution)/shard_map/wgrad_out_own/pallas_call | solution.py:1015
  328.4 9.5 %wgrad_in_sent.1 = bf16[4,4,2,64,1024]{4,3,2,1,0:T(8,128)(2,1)} custom-call(s32[3]{0:T(128)S(1)} %pad_add_fusion.where, bf16[1024,1024]{1,0:T(8,128)(2,1)S(1)} %copy-done.116, bf16[1024,4096]{1,0:T(8,128)(2,1)} %get-tuple-element.165.right_ref.refs_16_), custom_call_target="tpu_custom_call" | custom-call | flops 4294967296 | bytes 18874368 | tf_op jit(solution)/shard_map/wgrad_in_sent/pallas_call | solution.py:1015
  350.7 17.9 %feed_in_back.1 = (f32[1024,1024]{1,0:T(8,128)}, bf16[1024,1024]{1,0:T(8,128)(2,1)S(1)}, f32[8,1024]{1,0:T(8,128)S(1)}) custom-call(s32[3]{0:T(128)S(1)} %pad_add_fusion.where, bf16[4,64,1024]{2,1,0:T(8,128)(2,1)S(1)} %copy-done.9, bf16[4,64,1024]{2,1,0:T(8,128)(2,1)} %collective-permute-done.56.refs_1_, ...), custom_call_target="tpu_custom_call" | custom-call | flops 8589934592 | bytes 32018432 | tf_op jit(solution)/shard_map/feed_in_back/pallas_call | solution.py:626
  369.8 9.6 %wgrad_in_own.1 = (bf16[4,64,1024]{2,1,0:T(8,128)(2,1)S(1)}, bf16[4,64,1024]{2,1,0:T(8,128)(2,1)S(1)}, bf16[4,64,1024]{2,1,0:T(8,128)(2,1)S(1)}, bf16[4,64,1024]...) custom-call(s32[3]{0:T(128)S(1)} %pad_add_fusion.where, ...), custom_call_target="tpu_custom_call" | custom-call | flops 4294967296 | bytes 18874368 | tf_op jit(solution)/shard_map/wgrad_in_own/pallas_call | solution.py:1015
  388.0 4.9 attn_out_back.1.refs_4_
  392.9 4.7 collective-permute-done.95
  405.2 13.9 %attn_bwd.4 = (bf16[3,1024,512]{2,1,0:T(8,128)(2,1)S(1)}, f32[2,512]{1,0:T(2,128)S(1)}) custom-call(bf16[1024,3072]{1,0:T(8,128)(2,1)S(1)} %bitcast.158, bf16[1024,3072]{1,0:T(8,128)(2,1)S(1)} %bitcast.158, bf16[1024,3072]{1,0:T(8,128)(2,1)S(1)} %bitcast.158, bf16[1024,1024]{1,0:T(8,128)(2,1)S(1)} %copy-done.2, bf16[1024,1024]{1,0:T(8,128)(2,1)S(1)} %attn_out_back.1.refs_4_, ...), custom_call_target="tpu_custom_call" | custom-call | flops 10737418240 | bytes 4194304 | tf_op jit(solution)/shard_map/attn_bwd/pallas_call | solution.py:480
  422.9 14.1 %attn_bwd.5 = (bf16[3,1024,512]{2,1,0:T(8,128)(2,1)S(1)}, f32[2,512]{1,0:T(2,128)S(1)}) custom-call(bf16[1024,3072]{1,0:T(8,128)(2,1)S(1)} %bitcast.158, bf16[1024,3072]{1,0:T(8,128)(2,1)S(1)} %bitcast.158, bf16[1024,3072]{1,0:T(8,128)(2,1)S(1)} %bitcast.158, bf16[1024,1024]{1,0:T(8,128)(2,1)S(1)} %copy-done.2, ...), custom_call_target="tpu_custom_call", output_to_operand_aliasing={{0}: (8, {}), {1}: (9, {})} | custom-call | flops 10737418240 | bytes 4194304 | tf_op jit(solution)/shard_map/attn_bwd/pallas_call | solution.py:480
  438.6 3.6 collective-permute-done.96
  456.7 5.5 wgrad_qkv_a_sent.1
  462.3 2.8 copy-done.127
  465.0 14.3 %attn_bwd.6 = (bf16[3,1024,512]{2,1,0:T(8,128)(2,1)S(1)}, f32[2,512]{1,0:T(2,128)S(1)}) custom-call(bf16[1024,3072]{1,0:T(8,128)(2,1)S(1)} %copy-done.127, bf16[1024,3072]{1,0:T(8,128)(2,1)S(1)} %copy-done.127, bf16[1024,3072]{1,0:T(8,128)(2,1)S(1)} %copy-done.127, bf16[1024,1024]{1,0:T(8,128)(2,1)S(1)} %copy-done.2, bf16[1024,1024]{1,0:T(8,128)(2,1)S(1)} %copy-done.122, ...), custom_call_target="tpu_custom_call" | custom-call | flops 10737418240 | bytes 4194304 | tf_op jit(solution)/shard_map/attn_bwd/pallas_call | solution.py:480
  480.7 3.1 collective-permute-start.103
  486.5 4.1 collective-permute-done.104
  491.9 6.0 collective-permute-done.102
  497.9 12.2 %collective-permute-done.103 = bf16[512,256]{1,0:T(8,128)(2,1)S(1)} collective-permute-done((bf16[512,256]{1,0:T(8,128)(2,1)S(1)}, bf16[512,256]{1,0:T(8,128)(2,1)S(1)}, u32[]{:S(2)}, u32[]{:S(2)}) %collective-permute-start.103) | collective-permute-done | bytes 262176 | tf_op jit(solution)/shard_map/ppermute | solution.py:529
  514.9 5.7 collective-permute-done.147
  520.6 3.8 collective-permute-done.148
  524.4 2.5 collective-permute-start.111
  529.8 7.1 %wgrad_qkv_a_own.1 = (bf16[4,64,384]{2,1,0:T(8,128)(2,1)S(1)}, bf16[4,64,384]{2,1,0:T(8,128)(2,1)S(1)}, bf16[4,64,384]{2,1,0:T(8,128)(2,1)S(1)}, bf16[4,64,384]{...) custom-call(s32[3]{0:T(128)S(1)} %pad_add_fusion.where, ...), custom_call_target="tpu_custom_call" | custom-call | flops 1610612736 | bytes 8388608 | tf_op jit(solution)/shard_map/wgrad_qkv_a_own/pallas_call | solution.py:1015
  536.9 2.8 copy-done.128
  539.7 14.1 %attn_bwd.7 = (bf16[3,1024,512]{2,1,0:T(8,128)(2,1)S(1)}, f32[2,512]{1,0:T(2,128)S(1)}) custom-call(bf16[1024,3072]{1,0:T(8,128)(2,1)S(1)} %copy-done.128, bf16[1024,3072]{1,0:T(8,128)(2,1)S(1)} %copy-done.128, bf16[1024,3072]{1,0:T(8,128)(2,1)S(1)} %copy-done.128, bf16[1024,1024]{1,0:T(8,128)(2,1)S(1)} %copy-done.2, ...), custom_call_target="tpu_custom_call", output_to_operand_aliasing={{0}: (8, {}), {1}: (9, {})} | custom-call | flops 10737418240 | bytes 4194304 | tf_op jit(solution)/shard_map/attn_bwd/pallas_call | solution.py:480
  563.3 2.3 collective-permute-done.141
  566.7 5.2 collective-permute-done.142
  574.1 2.9 collective-permute-done.137
  583.2 5.5 wgrad_qkv_b_sent.1
  588.8 12.6 %qkv_back.1 = f32[1024,1024]{1,0:T(8,128)} custom-call(s32[3]{0:T(128)S(1)} %pad_add_fusion.where, bf16[4,64,768]{2,1,0:T(8,128)(2,1)S(1)} %pad_maximum_fusion.7.refs_0_, bf16[4,64,768]{2,1,0:T(8,128)(2,1)S(1)} %copy-done.63, bf16[4,64,768]{2,1,0:T(8,128)(2,1)S(1)} %copy-done.66, bf16[4,64,768]{2,1,0:T(8,128)(2,1)S(1)} %copy-done.78, ...), custom_call_target="tpu_custom_call" | custom-call | flops 6442450944 | bytes 20971520 | tf_op jit(solution)/shard_map/qkv_back/pallas_call | solution.py:626
  603.9 4.3 collective-permute-done.140
  618.0 7.2 %collective-permute-done.117 = bf16[4,64,384]{2,1,0:T(8,128)(2,1)S(1)} collective-permute-done((bf16[4,64,384]{2,1,0:T(8,128)(2,1)S(1)}, bf16[4,64,384]{2,1,0:T(8,128)(2,1)S(1)}, u32[]{:S(2)}, u32[]{:S(2)}) %collective-permute-start.117) | collective-permute-done | bytes 196640 | tf_op jit(solution)/shard_map/ppermute | solution.py:529
  625.2 7.1 %wgrad_qkv_b_own.1 = (bf16[4,64,384]{2,1,0:T(8,128)(2,1)S(1)}, bf16[4,64,384]{2,1,0:T(8,128)(2,1)S(1)}, bf16[4,64,384]{2,1,0:T(8,128)(2,1)S(1)}, bf16[4,64,384]{...) custom-call(s32[3]{0:T(128)S(1)} %pad_add_fusion.where, ...), custom_call_target="tpu_custom_call" | custom-call | flops 1610612736 | bytes 8388608 | tf_op jit(solution)/shard_map/wgrad_qkv_b_own/pallas_call | solution.py:1015
  633.0 3.9 collective-permute-start.120
  649.3 5.1 collective-permute-done.121
  656.3 4.6 collective-permute-done.126
  661.8 3.8 collective-permute-start.132
  666.9 2.5 collective-permute-done.132
  (682 shorter events, 228.0 us)
Async XLA Ops:
  30.7 18.4 %collective-permute-start.15 = (bf16[64,1024]{1,0:T(8,128)(2,1)S(1)}, bf16[64,1024]{1,0:T(8,128)(2,1)S(1)}, u32[]{:S(2)}, u32[]{:S(2)}) collective-permute-start(bf16[64,1024]{1,0:T(8,128)(2,1)S(1)} %get-tuple-element.134), channel_id=1, source_target_pairs={{0,2},{1,3},{2,0},{3,1},{4,6},{5,7},{6,4},{7,5},{8,10},{9,11},{10,... | collective-permute-start | bytes 393224 | tf_op jit(solution)/shard_map/ppermute | solution.py:529
  32.8 19.7 %collective-permute-start.16 = (bf16[64,1024]{1,0:T(8,128)(2,1)S(1)}, bf16[64,1024]{1,0:T(8,128)(2,1)S(1)}, u32[]{:S(2)}, u32[]{:S(2)}) collective-permute-start(bf16[64,1024]{1,0:T(8,128)(2,1)S(1)} %get-tuple-element.134), channel_id=1, source_target_pairs={{0,4},{1,5},{2,6},{3,7},{4,0},{5,1},{6,2},{7,3},{8,12},{9,13},{10,... | collective-permute-start | bytes 393224 | tf_op jit(solution)/shard_map/ppermute | solution.py:529
  33.1 20.9 %collective-permute-start.17 = (bf16[64,1024]{1,0:T(8,128)(2,1)S(1)}, bf16[64,1024]{1,0:T(8,128)(2,1)S(1)}, u32[]{:S(2)}, u32[]{:S(2)}) collective-permute-start(bf16[64,1024]{1,0:T(8,128)(2,1)S(1)} %get-tuple-element.134), channel_id=1, source_target_pairs={{0,6},{1,7},{2,4},{3,5},{4,2},{5,3},{6,0},{7,1},{8,14},{9,15},{10,... | collective-permute-start | bytes 393224 | tf_op jit(solution)/shard_map/ppermute | solution.py:529
  52.5 29.1 %collective-permute-start.21 = (bf16[4,64,768]{2,1,0:T(8,128)(2,1)S(1)}, bf16[4,64,768]{2,1,0:T(8,128)(2,1)S(1)}, u32[]{:S(2)}, u32[]{:S(2)}) collective-permute-start(bf16[4,64,768]{2,1,0:T(8,128)(2,1)S(1)} %pad_maximum_fusion.7.refs_0_), channel_id=1, source_target_pairs={{0,8},{1,9},{2,10},{3,11},{4,12},{5,13},{6,14},{7,15},{8,0},{9,1},... | collective-permute-start | bytes 1179656 | tf_op jit(solution)/shard_map/ppermute | solution.py:529
  54.0 28.8 %collective-permute-start.22 = (bf16[4,64,768]{2,1,0:T(8,128)(2,1)S(1)}, bf16[4,64,768]{2,1,0:T(8,128)(2,1)S(1)}, u32[]{:S(2)}, u32[]{:S(2)}) collective-permute-start(bf16[4,64,768]{2,1,0:T(8,128)(2,1)S(1)} %pad_maximum_fusion.7.refs_0_), channel_id=1, source_target_pairs={{0,16},{1,17},{2,18},{3,19},{4,20},{5,21},{6,22},{7,23},{8,24},{9,... | collective-permute-start | bytes 1179656 | tf_op jit(solution)/shard_map/ppermute | solution.py:529
  66.3 24.5 %collective-permute-start.33 = (bf16[4,64,768]{2,1,0:T(8,128)(2,1)S(1)}, bf16[4,64,768]{2,1,0:T(8,128)(2,1)S(1)}, u32[]{:S(2)}, u32[]{:S(2)}) collective-permute-start(bf16[4,64,768]{2,1,0:T(8,128)(2,1)S(1)} %pad_maximum_fusion.7.refs_0_), channel_id=1, source_target_pairs={{0,1},{1,0},{2,3},{3,2},{4,5},{5,4},{6,7},{7,6},{8,9},{9,8},{10,11... | collective-permute-start | bytes 1179656 | tf_op jit(solution)/shard_map/ppermute | solution.py:529
  94.1 19.4 %collective-permute-start.52 = (bf16[4,256,256]{2,1,0:T(8,128)(2,1)S(1)}, bf16[4,256,256]{2,1,0:T(8,128)(2,1)S(1)}, u32[]{:S(2)}, u32[]{:S(2)}) collective-permute-start(bf16[4,256,256]{2,1,0:T(8,128)(2,1)S(1)} %pad_maximum_fusion.5.refs_4_), channel_id=1, source_target_pairs={{0,1},{1,0},{2,3},{3,2},{4,5},{5,4},{6,7},{7,6},{8,9},{9,8},{10,11... | collective-permute-start | bytes 1572872 | tf_op jit(solution)/shard_map/ppermute | solution.py:529
  95.2 19.7 %collective-permute-start.48 = (bf16[4,256,256]{2,1,0:T(8,128)(2,1)S(1)}, bf16[4,256,256]{2,1,0:T(8,128)(2,1)S(1)}, u32[]{:S(2)}, u32[]{:S(2)}) collective-permute-start(bf16[4,256,256]{2,1,0:T(8,128)(2,1)S(1)} %pad_maximum_fusion.4.refs_0_), channel_id=1, source_target_pairs={{0,1},{1,0},{2,3},{3,2},{4,5},{5,4},{6,7},{7,6},{8,9},{9,8},{10,11... | collective-permute-start | bytes 1572872 | tf_op jit(solution)/shard_map/ppermute | solution.py:529
  108.4 44.8 %collective-permute-start.28 = (bf16[4,64,1024]{2,1,0:T(8,128)(2,1)S(1)}, bf16[4,64,1024]{2,1,0:T(8,128)(2,1)}, u32[]{:S(2)}, u32[]{:S(2)}) collective-permute-start(bf16[4,64,1024]{2,1,0:T(8,128)(2,1)S(1)} %pad_maximum_fusion.3.refs_4_), channel_id=1, source_target_pairs={{0,8},{1,9},{2,10},{3,11},{4,12},{5,13},{6,14},{7,15},{8,0},{9,1},... | collective-permute-start | bytes 1572872 | tf_op jit(solution)/shard_map/ppermute | solution.py:529
  110.7 42.7 %collective-permute-start.27 = (bf16[4,64,1024]{2,1,0:T(8,128)(2,1)S(1)}, bf16[4,64,1024]{2,1,0:T(8,128)(2,1)}, u32[]{:S(2)}, u32[]{:S(2)}) collective-permute-start(bf16[4,64,1024]{2,1,0:T(8,128)(2,1)S(1)} %pad_maximum_fusion.2.refs_0_), channel_id=1, source_target_pairs={{0,16},{1,17},{2,18},{3,19},{4,20},{5,21},{6,22},{7,23},{8,24},{9,... | collective-permute-start | bytes 1572872 | tf_op jit(solution)/shard_map/ppermute | solution.py:529
  115.6 37.2 %collective-permute-start.32 = (bf16[4,64,768]{2,1,0:T(8,128)(2,1)}, bf16[4,64,768]{2,1,0:T(8,128)(2,1)}, u32[]{:S(2)}, u32[]{:S(2)}) collective-permute-start(bf16[4,64,768]{2,1,0:T(8,128)(2,1)} %collective-permute-done.23.refs_6_), channel_id=1, source_target_pairs={{0,8},{1,9},{2,10},{3,11},{4,12},{5,13},{6,14},{7,15},{8,0},{9,1},... | collective-permute-start | bytes 1179656 | tf_op jit(solution)/shard_map/ppermute | solution.py:529
  126.1 23.3 %collective-permute-start.70 = (bf16[4,64,256]{2,1,0:T(8,128)(2,1)}, bf16[4,64,256]{2,1,0:T(8,128)(2,1)}, u32[]{:S(2)}, u32[]{:S(2)}) collective-permute-start(bf16[4,64,256]{2,1,0:T(8,128)(2,1)} %pad_maximum_fusion.10.refs_4_), channel_id=1, source_target_pairs={{0,16},{1,17},{2,18},{3,19},{4,20},{5,21},{6,22},{7,23},{8,24},{9,... | collective-permute-start | bytes 393224 | tf_op jit(solution)/shard_map/ppermute | solution.py:529
  128.3 21.5 %collective-permute-start.68 = (bf16[4,64,256]{2,1,0:T(8,128)(2,1)}, bf16[4,64,256]{2,1,0:T(8,128)(2,1)}, u32[]{:S(2)}, u32[]{:S(2)}) collective-permute-start(bf16[4,64,256]{2,1,0:T(8,128)(2,1)} %pad_maximum_fusion.9.refs_0_), channel_id=1, source_target_pairs={{0,8},{1,9},{2,10},{3,11},{4,12},{5,13},{6,14},{7,15},{8,0},{9,1},... | collective-permute-start | bytes 393224 | tf_op jit(solution)/shard_map/ppermute | solution.py:529
  155.5 25.5 %collective-permute-start.58 = (bf16[4,64,1024]{2,1,0:T(8,128)(2,1)S(1)}, bf16[4,64,1024]{2,1,0:T(8,128)(2,1)}, u32[]{:S(2)}, u32[]{:S(2)}) collective-permute-start(bf16[4,64,1024]{2,1,0:T(8,128)(2,1)S(1)} %pad_maximum_fusion.3.refs_4_), channel_id=1, source_target_pairs={{0,16},{1,17},{2,18},{3,19},{4,20},{5,21},{6,22},{7,23},{8,24},{9,... | collective-permute-start | bytes 1572872 | tf_op jit(solution)/shard_map/ppermute | solution.py:529
  156.1 25.9 %collective-permute-start.56 = (bf16[4,64,1024]{2,1,0:T(8,128)(2,1)S(1)}, bf16[4,64,1024]{2,1,0:T(8,128)(2,1)}, u32[]{:S(2)}, u32[]{:S(2)}) collective-permute-start(bf16[4,64,1024]{2,1,0:T(8,128)(2,1)S(1)} %pad_maximum_fusion.2.refs_0_), channel_id=1, source_target_pairs={{0,8},{1,9},{2,10},{3,11},{4,12},{5,13},{6,14},{7,15},{8,0},{9,1},... | collective-permute-start | bytes 1572872 | tf_op jit(solution)/shard_map/ppermute | solution.py:529
  156.9 22.8 %collective-permute-start.73 = (bf16[4,64,256]{2,1,0:T(8,128)(2,1)}, bf16[4,64,256]{2,1,0:T(8,128)(2,1)S(1)}, u32[]{:S(2)}, u32[]{:S(2)}) collective-permute-start(bf16[4,64,256]{2,1,0:T(8,128)(2,1)} %collective-permute-done.68.refs_1_), channel_id=1, source_target_pairs={{0,1},{1,0},{2,3},{3,2},{4,5},{5,4},{6,7},{7,6},{8,9},{9,8},{10,11... | collective-permute-start | bytes 393224 | tf_op jit(solution)/shard_map/ppermute | solution.py:529
  156.9 32.2 %collective-permute-start.46 = (bf16[4,256,256]{2,1,0:T(8,128)(2,1)}, bf16[4,256,256]{2,1,0:T(8,128)(2,1)}, u32[]{:S(2)}, u32[]{:S(2)}) collective-permute-start(bf16[4,256,256]{2,1,0:T(8,128)(2,1)} %copy-done.10), channel_id=1, source_target_pairs={{0,16},{1,17},{2,18},{3,19},{4,20},{5,21},{6,22},{7,23},{8,24},{9,... | collective-permute-start | bytes 1572872 | tf_op jit(solution)/shard_map/ppermute | solution.py:529
  158.1 31.2 %collective-permute-start.29 = (bf16[4,256,256]{2,1,0:T(8,128)(2,1)}, bf16[4,256,256]{2,1,0:T(8,128)(2,1)}, u32[]{:S(2)}, u32[]{:S(2)}) collective-permute-start(bf16[4,256,256]{2,1,0:T(8,128)(2,1)} %copy-done.12), channel_id=1, source_target_pairs={{0,8},{1,9},{2,10},{3,11},{4,12},{5,13},{6,14},{7,15},{8,0},{9,1},... | collective-permute-start | bytes 1572872 | tf_op jit(solution)/shard_map/ppermute | solution.py:529
  191.4 25.8 %collective-permute-start.45 = (bf16[4,256,256]{2,1,0:T(8,128)(2,1)}, bf16[4,256,256]{2,1,0:T(8,128)(2,1)S(1)}, u32[]{:S(2)}, u32[]{:S(2)}) collective-permute-start(bf16[4,256,256]{2,1,0:T(8,128)(2,1)} %copy-done.10), channel_id=1, source_target_pairs={{0,8},{1,9},{2,10},{3,11},{4,12},{5,13},{6,14},{7,15},{8,0},{9,1},... | collective-permute-start | bytes 1572872 | tf_op jit(solution)/shard_map/ppermute | solution.py:529
  192.8 25.0 %collective-permute-start.30 = (bf16[4,256,256]{2,1,0:T(8,128)(2,1)}, bf16[4,256,256]{2,1,0:T(8,128)(2,1)S(1)}, u32[]{:S(2)}, u32[]{:S(2)}) collective-permute-start(bf16[4,256,256]{2,1,0:T(8,128)(2,1)} %copy-done.12), channel_id=1, source_target_pairs={{0,16},{1,17},{2,18},{3,19},{4,20},{5,21},{6,22},{7,23},{8,24},{9,... | collective-permute-start | bytes 1572872 | tf_op jit(solution)/shard_map/ppermute | solution.py:529
  193.4 22.2 %collective-permute-start.62 = (bf16[4,64,1024]{2,1,0:T(8,128)(2,1)}, bf16[4,64,1024]{2,1,0:T(8,128)(2,1)S(1)}, u32[]{:S(2)}, u32[]{:S(2)}) collective-permute-start(bf16[4,64,1024]{2,1,0:T(8,128)(2,1)} %collective-permute-done.27.refs_2_), channel_id=1, source_target_pairs={{0,1},{1,0},{2,3},{3,2},{4,5},{5,4},{6,7},{7,6},{8,9},{9,8},{10,11... | collective-permute-start | bytes 1572872 | tf_op jit(solution)/shard_map/ppermute | solution.py:529
  193.4 24.4 %collective-permute-start.59 = (bf16[4,64,1024]{2,1,0:T(8,128)(2,1)}, bf16[4,64,1024]{2,1,0:T(8,128)(2,1)S(1)}, u32[]{:S(2)}, u32[]{:S(2)}) collective-permute-start(bf16[4,64,1024]{2,1,0:T(8,128)(2,1)} %collective-permute-done.58.refs_6_), channel_id=1, source_target_pairs={{0,8},{1,9},{2,10},{3,11},{4,12},{5,13},{6,14},{7,15},{8,0},{9,1},... | collective-permute-start | bytes 1572872 | tf_op jit(solution)/shard_map/ppermute | solution.py:529
  194.4 23.9 %collective-permute-start.57 = (bf16[4,64,1024]{2,1,0:T(8,128)(2,1)}, bf16[4,64,1024]{2,1,0:T(8,128)(2,1)S(1)}, u32[]{:S(2)}, u32[]{:S(2)}) collective-permute-start(bf16[4,64,1024]{2,1,0:T(8,128)(2,1)} %collective-permute-done.56.refs_1_), channel_id=1, source_target_pairs={{0,16},{1,17},{2,18},{3,19},{4,20},{5,21},{6,22},{7,23},{8,24},{9,... | collective-permute-start | bytes 1572872 | tf_op jit(solution)/shard_map/ppermute | solution.py:529
  215.7 33.9 %collective-permute-start.47 = (bf16[4,256,256]{2,1,0:T(8,128)(2,1)}, bf16[4,256,256]{2,1,0:T(8,128)(2,1)S(1)}, u32[]{:S(2)}, u32[]{:S(2)}) collective-permute-start(bf16[4,256,256]{2,1,0:T(8,128)(2,1)} %collective-permute-done.46.refs_6_), channel_id=1, source_target_pairs={{0,8},{1,9},{2,10},{3,11},{4,12},{5,13},{6,14},{7,15},{8,0},{9,1},... | collective-permute-start | bytes 1572872 | tf_op jit(solution)/shard_map/ppermute | solution.py:529
  217.2 32.9 %collective-permute-start.41 = (bf16[4,256,256]{2,1,0:T(8,128)(2,1)}, bf16[4,256,256]{2,1,0:T(8,128)(2,1)S(1)}, u32[]{:S(2)}, u32[]{:S(2)}) collective-permute-start(bf16[4,256,256]{2,1,0:T(8,128)(2,1)} %collective-permute-done.29.refs_1_), channel_id=1, source_target_pairs={{0,16},{1,17},{2,18},{3,19},{4,20},{5,21},{6,22},{7,23},{8,24},{9,... | collective-permute-start | bytes 1572872 | tf_op jit(solution)/shard_map/ppermute | solution.py:529
  217.8 32.0 %collective-permute-start.53 = (bf16[4,256,256]{2,1,0:T(8,128)(2,1)S(1)}, bf16[4,256,256]{2,1,0:T(8,128)(2,1)S(1)}, u32[]{:S(2)}, u32[]{:S(2)}) collective-permute-start(bf16[4,256,256]{2,1,0:T(8,128)(2,1)S(1)} %collective-permute-done.45.refs_5_), channel_id=1, source_target_pairs={{0,1},{1,0},{2,3},{3,2},{4,5},{5,4},{6,7},{7,6},{8,9},{9,8},{10,11... | collective-permute-start | bytes 1572872 | tf_op jit(solution)/shard_map/ppermute | solution.py:529
  217.8 32.5 %collective-permute-start.67 = (bf16[4,64,1024]{2,1,0:T(8,128)(2,1)S(1)}, bf16[4,64,1024]{2,1,0:T(8,128)(2,1)S(1)}, u32[]{:S(2)}, u32[]{:S(2)}) collective-permute-start(bf16[4,64,1024]{2,1,0:T(8,128)(2,1)S(1)} %collective-permute-done.59.refs_7_), channel_id=1, source_target_pairs={{0,1},{1,0},{2,3},{3,2},{4,5},{5,4},{6,7},{7,6},{8,9},{9,8},{10,11... | collective-permute-start | bytes 1572872 | tf_op jit(solution)/shard_map/ppermute | solution.py:529
  218.4 32.2 %collective-permute-start.63 = (bf16[4,64,1024]{2,1,0:T(8,128)(2,1)S(1)}, bf16[4,64,1024]{2,1,0:T(8,128)(2,1)S(1)}, u32[]{:S(2)}, u32[]{:S(2)}) collective-permute-start(bf16[4,64,1024]{2,1,0:T(8,128)(2,1)S(1)} %collective-permute-done.57.refs_3_), channel_id=1, source_target_pairs={{0,1},{1,0},{2,3},{3,2},{4,5},{5,4},{6,7},{7,6},{8,9},{9,8},{10,11... | collective-permute-start | bytes 1572872 | tf_op jit(solution)/shard_map/ppermute | solution.py:529
  249.5 23.0 %collective-permute-start.54 = (bf16[4,256,256]{2,1,0:T(8,128)(2,1)}, bf16[4,256,256]{2,1,0:T(8,128)(2,1)S(1)}, u32[]{:S(2)}, u32[]{:S(2)}) collective-permute-start(bf16[4,256,256]{2,1,0:T(8,128)(2,1)} %collective-permute-done.46.refs_6_), channel_id=1, source_target_pairs={{0,1},{1,0},{2,3},{3,2},{4,5},{5,4},{6,7},{7,6},{8,9},{9,8},{10,11... | collective-permute-start | bytes 1572872 | tf_op jit(solution)/shard_map/ppermute | solution.py:529
  249.9 22.7 %collective-permute-start.49 = (bf16[4,256,256]{2,1,0:T(8,128)(2,1)}, bf16[4,256,256]{2,1,0:T(8,128)(2,1)S(1)}, u32[]{:S(2)}, u32[]{:S(2)}) collective-permute-start(bf16[4,256,256]{2,1,0:T(8,128)(2,1)} %collective-permute-done.29.refs_1_), channel_id=1, source_target_pairs={{0,1},{1,0},{2,3},{3,2},{4,5},{5,4},{6,7},{7,6},{8,9},{9,8},{10,11... | collective-permute-start | bytes 1572872 | tf_op jit(solution)/shard_map/ppermute | solution.py:529
  250.1 22.6 %collective-permute-start.50 = (bf16[4,256,256]{2,1,0:T(8,128)(2,1)S(1)}, bf16[4,256,256]{2,1,0:T(8,128)(2,1)S(1)}, u32[]{:S(2)}, u32[]{:S(2)}) collective-permute-start(bf16[4,256,256]{2,1,0:T(8,128)(2,1)S(1)} %collective-permute-done.30.refs_2_), channel_id=1, source_target_pairs={{0,1},{1,0},{2,3},{3,2},{4,5},{5,4},{6,7},{7,6},{8,9},{9,8},{10,11... | collective-permute-start | bytes 1572872 | tf_op jit(solution)/shard_map/ppermute | solution.py:529
  250.4 22.2 %collective-permute-start.55 = (bf16[4,256,256]{2,1,0:T(8,128)(2,1)S(1)}, bf16[4,256,256]{2,1,0:T(8,128)(2,1)S(1)}, u32[]{:S(2)}, u32[]{:S(2)}) collective-permute-start(bf16[4,256,256]{2,1,0:T(8,128)(2,1)S(1)} %collective-permute-done.47.refs_7_), channel_id=1, source_target_pairs={{0,1},{1,0},{2,3},{3,2},{4,5},{5,4},{6,7},{7,6},{8,9},{9,8},{10,11... | collective-permute-start | bytes 1572872 | tf_op jit(solution)/shard_map/ppermute | solution.py:529
  250.6 22.0 %collective-permute-start.51 = (bf16[4,256,256]{2,1,0:T(8,128)(2,1)S(1)}, bf16[4,256,256]{2,1,0:T(8,128)(2,1)S(1)}, u32[]{:S(2)}, u32[]{:S(2)}) collective-permute-start(bf16[4,256,256]{2,1,0:T(8,128)(2,1)S(1)} %collective-permute-done.41.refs_3_), channel_id=1, source_target_pairs={{0,1},{1,0},{2,3},{3,2},{4,5},{5,4},{6,7},{7,6},{8,9},{9,8},{10,11... | collective-permute-start | bytes 1572872 | tf_op jit(solution)/shard_map/ppermute | solution.py:529
  337.9 31.9 %collective-permute-start.81 = (bf16[4,4,2,64,1024]{4,3,2,1,0:T(8,128)(2,1)}, bf16[4,4,2,64,1024]{4,3,2,1,0:T(8,128)(2,1)}, u32[]{:S(2)}, u32[]{:S(2)}) collective-permute-start(bf16[4,4,2,64,1024]{4,3,2,1,0:T(8,128)(2,1)} %wgrad_in_sent.1), channel_id=1, source_target_pairs={{0,1},{1,0},{2,3},{3,2},{4,5},{5,4},{6,7},{7,6},{8,9},{9,8},{10,11... | collective-permute-start | bytes 12582920 | tf_op jit(solution)/shard_map/ppermute | solution.py:529
  338.3 30.3 %collective-permute-start.88 = (bf16[4,256,256]{2,1,0:T(8,128)(2,1)}, bf16[4,256,256]{2,1,0:T(8,128)(2,1)S(1)}, u32[]{:S(2)}, u32[]{:S(2)}) collective-permute-start(bf16[4,256,256]{2,1,0:T(8,128)(2,1)} %copy-done.60), channel_id=1, source_target_pairs={{0,16},{1,17},{2,18},{3,19},{4,20},{5,21},{6,22},{7,23},{8,24},{9,... | collective-permute-start | bytes 1572872 | tf_op jit(solution)/shard_map/ppermute | solution.py:529
  339.7 45.9 %collective-permute-start.87 = (bf16[4,256,256]{2,1,0:T(8,128)(2,1)}, bf16[4,256,256]{2,1,0:T(8,128)(2,1)S(1)}, u32[]{:S(2)}, u32[]{:S(2)}) collective-permute-start(bf16[4,256,256]{2,1,0:T(8,128)(2,1)} %copy-done.59), channel_id=1, source_target_pairs={{0,16},{1,17},{2,18},{3,19},{4,20},{5,21},{6,22},{7,23},{8,24},{9,... | collective-permute-start | bytes 1572872 | tf_op jit(solution)/shard_map/ppermute | solution.py:529
  368.8 17.5 %collective-permute-start.89 = (bf16[4,256,256]{2,1,0:T(8,128)(2,1)S(1)}, bf16[4,256,256]{2,1,0:T(8,128)(2,1)S(1)}, u32[]{:S(2)}, u32[]{:S(2)}) collective-permute-start(bf16[4,256,256]{2,1,0:T(8,128)(2,1)S(1)} %add_convert_fusion.4), channel_id=1, source_target_pairs={{0,8},{1,9},{2,10},{3,11},{4,12},{5,13},{6,14},{7,15},{8,0},{9,1},... | collective-permute-start | bytes 1572872 | tf_op jit(solution)/shard_map/ppermute | solution.py:529
  381.4 18.6 %collective-permute-start.84 = (bf16[4,4,2,64,256]{4,3,2,1,0:T(8,128)(2,1)S(1)}, bf16[4,4,2,64,256]{4,3,2,1,0:T(8,128)(2,1)S(1)}, u32[]{:S(2)}, u32[]{:S(2)}) collective-permute-start(bf16[4,4,2,64,256]{4,3,2,1,0:T(8,128)(2,1)S(1)} %wgrad_attn_sent.1), channel_id=1, source_target_pairs={{0,1},{1,0},{2,3},{3,2},{4,5},{5,4},{6,7},{7,6},{8,9},{9,8},{10,11... | collective-permute-start | bytes 3145736 | tf_op jit(solution)/shard_map/ppermute | solution.py:529
  382.5 20.0 %collective-permute-start.83 = (bf16[4,256,256]{2,1,0:T(8,128)(2,1)S(1)}, bf16[4,256,256]{2,1,0:T(8,128)(2,1)S(1)}, u32[]{:S(2)}, u32[]{:S(2)}) collective-permute-start(bf16[4,256,256]{2,1,0:T(8,128)(2,1)S(1)} %copy-done.54), channel_id=1, source_target_pairs={{0,8},{1,9},{2,10},{3,11},{4,12},{5,13},{6,14},{7,15},{8,0},{9,1},... | collective-permute-start | bytes 1572872 | tf_op jit(solution)/shard_map/ppermute | solution.py:529
  385.6 69.0 %collective-permute-start.85 = (bf16[4,256,256]{2,1,0:T(8,128)(2,1)S(1)}, bf16[4,256,256]{2,1,0:T(8,128)(2,1)}, u32[]{:S(2)}, u32[]{:S(2)}) collective-permute-start(bf16[4,256,256]{2,1,0:T(8,128)(2,1)S(1)} %copy-done.46), channel_id=1, source_target_pairs={{0,8},{1,9},{2,10},{3,11},{4,12},{5,13},{6,14},{7,15},{8,0},{9,1},... | collective-permute-start | bytes 1572872 | tf_op jit(solution)/shard_map/ppermute | solution.py:529
  386.4 33.4 %collective-permute-start.82 = (bf16[4,64,1024]{2,1,0:T(8,128)(2,1)S(1)}, bf16[4,64,1024]{2,1,0:T(8,128)(2,1)}, u32[]{:S(2)}, u32[]{:S(2)}) collective-permute-start(bf16[4,64,1024]{2,1,0:T(8,128)(2,1)S(1)} %get-tuple-element.175), channel_id=1, source_target_pairs={{0,8},{1,9},{2,10},{3,11},{4,12},{5,13},{6,14},{7,15},{8,0},{9,1},... | collective-permute-start | bytes 1572872 | tf_op jit(solution)/shard_map/ppermute | solution.py:529
  397.6 39.5 %collective-permute-start.94 = (bf16[4,64,1024]{2,1,0:T(8,128)(2,1)S(1)}, bf16[4,64,1024]{2,1,0:T(8,128)(2,1)}, u32[]{:S(2)}, u32[]{:S(2)}) collective-permute-start(bf16[4,64,1024]{2,1,0:T(8,128)(2,1)S(1)} %get-tuple-element.204), channel_id=1, source_target_pairs={{0,16},{1,17},{2,18},{3,19},{4,20},{5,21},{6,22},{7,23},{8,24},{9,... | collective-permute-start | bytes 1572872 | tf_op jit(solution)/shard_map/ppermute | solution.py:529
  400.0 80.7 %collective-permute-start.92 = (bf16[4,64,1024]{2,1,0:T(8,128)(2,1)S(1)}, bf16[4,64,1024]{2,1,0:T(8,128)(2,1)}, u32[]{:S(2)}, u32[]{:S(2)}) collective-permute-start(bf16[4,64,1024]{2,1,0:T(8,128)(2,1)S(1)} %get-tuple-element.201), channel_id=1, source_target_pairs={{0,8},{1,9},{2,10},{3,11},{4,12},{5,13},{6,14},{7,15},{8,0},{9,1},... | collective-permute-start | bytes 1572872 | tf_op jit(solution)/shard_map/ppermute | solution.py:529
  402.5 39.7 %collective-permute-start.96 = (bf16[4,64,1024]{2,1,0:T(8,128)(2,1)}, bf16[4,64,1024]{2,1,0:T(8,128)(2,1)S(1)}, u32[]{:S(2)}, u32[]{:S(2)}) collective-permute-start(bf16[4,64,1024]{2,1,0:T(8,128)(2,1)} %add_convert_fusion.1), channel_id=1, source_target_pairs={{0,8},{1,9},{2,10},{3,11},{4,12},{5,13},{6,14},{7,15},{8,0},{9,1},... | collective-permute-start | bytes 1572872 | tf_op jit(solution)/shard_map/ppermute | solution.py:529
  419.8 34.7 %collective-permute-start.86 = (bf16[4,256,256]{2,1,0:T(8,128)(2,1)S(1)}, bf16[4,256,256]{2,1,0:T(8,128)(2,1)S(1)}, u32[]{:S(2)}, u32[]{:S(2)}) collective-permute-start(bf16[4,256,256]{2,1,0:T(8,128)(2,1)S(1)} %add_convert_fusion.7), channel_id=1, source_target_pairs={{0,16},{1,17},{2,18},{3,19},{4,20},{5,21},{6,22},{7,23},{8,24},{9,... | collective-permute-start | bytes 1572872 | tf_op jit(solution)/shard_map/ppermute | solution.py:529
  452.5 28.2 %collective-permute-start.93 = (bf16[4,64,1024]{2,1,0:T(8,128)(2,1)}, bf16[4,64,1024]{2,1,0:T(8,128)(2,1)}, u32[]{:S(2)}, u32[]{:S(2)}) collective-permute-start(bf16[4,64,1024]{2,1,0:T(8,128)(2,1)} %add_convert_fusion.6), channel_id=1, source_target_pairs={{0,16},{1,17},{2,18},{3,19},{4,20},{5,21},{6,22},{7,23},{8,24},{9,... | collective-permute-start | bytes 1572872 | tf_op jit(solution)/shard_map/ppermute | solution.py:529
  453.5 31.7 %collective-permute-start.98 = (bf16[4,64,256]{2,1,0:T(8,128)(2,1)}, bf16[4,64,256]{2,1,0:T(8,128)(2,1)}, u32[]{:S(2)}, u32[]{:S(2)}) collective-permute-start(bf16[4,64,256]{2,1,0:T(8,128)(2,1)} %add_convert_fusion.21), channel_id=1, source_target_pairs={{0,16},{1,17},{2,18},{3,19},{4,20},{5,21},{6,22},{7,23},{8,24},{9,... | collective-permute-start | bytes 393224 | tf_op jit(solution)/shard_map/ppermute | solution.py:529
  462.2 66.7 %collective-permute-start.91 = (bf16[4,4,2,64,384]{4,3,2,1,0:T(8,128)(2,1)S(1)}, bf16[4,4,2,64,384]{4,3,2,1,0:T(8,128)(2,1)S(1)}, u32[]{:S(2)}, u32[]{:S(2)}) collective-permute-start(bf16[4,4,2,64,384]{4,3,2,1,0:T(8,128)(2,1)S(1)} %wgrad_qkv_a_sent.1), channel_id=1, source_target_pairs={{0,1},{1,0},{2,3},{3,2},{4,5},{5,4},{6,7},{7,6},{8,9},{9,8},{10,11... | collective-permute-start | bytes 4718600 | tf_op jit(solution)/shard_map/ppermute | solution.py:529
  480.7 17.2 %collective-permute-start.102 = (bf16[512,256]{1,0:T(8,128)(2,1)}, bf16[512,256]{1,0:T(8,128)(2,1)S(1)}, u32[]{:S(2)}, u32[]{:S(2)}) collective-permute-start(bf16[512,256]{1,0:T(8,128)(2,1)} %get-tuple-element.257), channel_id=1, source_target_pairs={{0,2},{1,3},{2,0},{3,1},{4,6},{5,7},{6,4},{7,5},{8,10},{9,11},{10,... | collective-permute-start | bytes 786440 | tf_op jit(solution)/shard_map/ppermute | solution.py:529
  480.7 29.5 %collective-permute-start.103 = (bf16[512,256]{1,0:T(8,128)(2,1)S(1)}, bf16[512,256]{1,0:T(8,128)(2,1)S(1)}, u32[]{:S(2)}, u32[]{:S(2)}) collective-permute-start(bf16[512,256]{1,0:T(8,128)(2,1)S(1)} %get-tuple-element.259), channel_id=1, source_target_pairs={{0,4},{1,5},{2,6},{3,7},{4,0},{5,1},{6,2},{7,3},{8,12},{9,13},{10,... | collective-permute-start | bytes 786440 | tf_op jit(solution)/shard_map/ppermute | solution.py:529
  485.2 27.7 %collective-permute-start.97 = (bf16[4,64,256]{2,1,0:T(8,128)(2,1)S(1)}, bf16[4,64,256]{2,1,0:T(8,128)(2,1)S(1)}, u32[]{:S(2)}, u32[]{:S(2)}) collective-permute-start(bf16[4,64,256]{2,1,0:T(8,128)(2,1)S(1)} %get-tuple-element.207), channel_id=1, source_target_pairs={{0,8},{1,9},{2,10},{3,11},{4,12},{5,13},{6,14},{7,15},{8,0},{9,1},... | collective-permute-start | bytes 393224 | tf_op jit(solution)/shard_map/ppermute | solution.py:529
  490.6 63.2 %collective-permute-start.108 = (bf16[128,1024]{1,0:T(8,128)(2,1)S(1)}, bf16[128,1024]{1,0:T(8,128)(2,1)S(1)}, u32[]{:S(2)}, u32[]{:S(2)}) collective-permute-start(bf16[128,1024]{1,0:T(8,128)(2,1)S(1)} %get-tuple-element.256), channel_id=1, source_target_pairs={{0,6},{1,7},{2,4},{3,5},{4,2},{5,3},{6,0},{7,1},{8,14},{9,15},{10,... | collective-permute-start | bytes 786440 | tf_op jit(solution)/shard_map/ppermute | solution.py:529
  520.6 34.4 %collective-permute-start.106 = (bf16[128,1024]{1,0:T(8,128)(2,1)S(1)}, bf16[128,1024]{1,0:T(8,128)(2,1)S(1)}, u32[]{:S(2)}, u32[]{:S(2)}) collective-permute-start(bf16[128,1024]{1,0:T(8,128)(2,1)S(1)} %get-tuple-element.253), channel_id=1, source_target_pairs={{0,2},{1,3},{2,0},{3,1},{4,6},{5,7},{6,4},{7,5},{8,10},{9,11},{10,... | collective-permute-start | bytes 786440 | tf_op jit(solution)/shard_map/ppermute | solution.py:529
  524.4 30.5 %collective-permute-start.107 = (bf16[128,1024]{1,0:T(8,128)(2,1)S(1)}, bf16[128,1024]{1,0:T(8,128)(2,1)S(1)}, u32[]{:S(2)}, u32[]{:S(2)}) collective-permute-start(bf16[128,1024]{1,0:T(8,128)(2,1)S(1)} %get-tuple-element.255), channel_id=1, source_target_pairs={{0,4},{1,5},{2,6},{3,7},{4,0},{5,1},{6,2},{7,3},{8,12},{9,13},{10,... | collective-permute-start | bytes 786440 | tf_op jit(solution)/shard_map/ppermute | solution.py:529
  524.4 33.3 %collective-permute-start.111 = (bf16[128,256]{1,0:T(8,128)(2,1)S(1)}, bf16[128,256]{1,0:T(8,128)(2,1)S(1)}, u32[]{:S(2)}, u32[]{:S(2)}) collective-permute-start(bf16[128,256]{1,0:T(8,128)(2,1)S(1)} %get-tuple-element.282), channel_id=1, source_target_pairs={{0,6},{1,7},{2,4},{3,5},{4,2},{5,3},{6,0},{7,1},{8,14},{9,15},{10,... | collective-permute-start | bytes 196616 | tf_op jit(solution)/shard_map/ppermute | solution.py:529
  528.8 29.1 %collective-permute-start.109 = (bf16[128,256]{1,0:T(8,128)(2,1)S(1)}, bf16[128,256]{1,0:T(8,128)(2,1)S(1)}, u32[]{:S(2)}, u32[]{:S(2)}) collective-permute-start(bf16[128,256]{1,0:T(8,128)(2,1)S(1)} %get-tuple-element.279), channel_id=1, source_target_pairs={{0,2},{1,3},{2,0},{3,1},{4,6},{5,7},{6,4},{7,5},{8,10},{9,11},{10,... | collective-permute-start | bytes 196616 | tf_op jit(solution)/shard_map/ppermute | solution.py:529
  555.1 59.4 %collective-permute-start.144 = (bf16[128,1024]{1,0:T(8,128)(2,1)S(1)}, bf16[128,1024]{1,0:T(8,128)(2,1)S(1)}, u32[]{:S(2)}, u32[]{:S(2)}) collective-permute-start(bf16[128,1024]{1,0:T(8,128)(2,1)S(1)} %add_convert_fusion.8), channel_id=1, source_target_pairs={{0,24},{1,25},{2,26},{3,27},{4,28},{5,29},{6,30},{7,31},{8,16},{9,... | collective-permute-start | bytes 786440 | tf_op jit(solution)/shard_map/ppermute | solution.py:529
  556.9 58.5 %collective-permute-start.145 = (bf16[128,1024]{1,0:T(8,128)(2,1)S(1)}, bf16[128,1024]{1,0:T(8,128)(2,1)S(1)}, u32[]{:S(2)}, u32[]{:S(2)}) collective-permute-start(bf16[128,1024]{1,0:T(8,128)(2,1)S(1)} %add_convert_fusion.8), channel_id=1, source_target_pairs={{0,16},{1,17},{2,18},{3,19},{4,20},{5,21},{6,22},{7,23},{8,24},{9,... | collective-permute-start | bytes 786440 | tf_op jit(solution)/shard_map/ppermute | solution.py:529
  565.7 17.3 %collective-permute-start.105 = (bf16[4,64,384]{2,1,0:T(8,128)(2,1)S(1)}, bf16[4,64,384]{2,1,0:T(8,128)(2,1)S(1)}, u32[]{:S(2)}, u32[]{:S(2)}) collective-permute-start(bf16[4,64,384]{2,1,0:T(8,128)(2,1)S(1)} %get-tuple-element.220), channel_id=1, source_target_pairs={{0,8},{1,9},{2,10},{3,11},{4,12},{5,13},{6,14},{7,15},{8,0},{9,1},... | collective-permute-start | bytes 589832 | tf_op jit(solution)/shard_map/ppermute | solution.py:529
  571.9 30.8 %collective-permute-start.116 = (bf16[4,64,384]{2,1,0:T(8,128)(2,1)S(1)}, bf16[4,64,384]{2,1,0:T(8,128)(2,1)S(1)}, u32[]{:S(2)}, u32[]{:S(2)}) collective-permute-start(bf16[4,64,384]{2,1,0:T(8,128)(2,1)S(1)} %get-tuple-element.234), channel_id=1, source_target_pairs={{0,16},{1,17},{2,18},{3,19},{4,20},{5,21},{6,22},{7,23},{8,24},{9,... | collective-permute-start | bytes 589832 | tf_op jit(solution)/shard_map/ppermute | solution.py:529
  581.2 20.2 %collective-permute-start.139 = (f32[96,128]{1,0:T(8,128)S(1)}, f32[96,128]{1,0:T(8,128)S(1)}, u32[]{:S(2)}, u32[]{:S(2)}) collective-permute-start(f32[96,128]{1,0:T(8,128)S(1)} %add.252), channel_id=1, source_target_pairs={{0,2},{1,3},{2,0},{3,1},{4,6},{5,7},{6,4},{7,5},{8,10},{9,11},{10,... | collective-permute-start | bytes 147464 | tf_op jit(solution)/shard_map/ppermute | solution.py:529
  588.6 36.6 %collective-permute-start.114 = (bf16[4,4,2,64,384]{4,3,2,1,0:T(8,128)(2,1)S(1)}, bf16[4,4,2,64,384]{4,3,2,1,0:T(8,128)(2,1)S(1)}, u32[]{:S(2)}, u32[]{:S(2)}) collective-permute-start(bf16[4,4,2,64,384]{4,3,2,1,0:T(8,128)(2,1)S(1)} %wgrad_qkv_b_sent.1), channel_id=1, source_target_pairs={{0,1},{1,0},{2,3},{3,2},{4,5},{5,4},{6,7},{7,6},{8,9},{9,8},{10,11... | collective-permute-start | bytes 4718600 | tf_op jit(solution)/shard_map/ppermute | solution.py:529
  614.5 17.8 %collective-permute-start.112 = (bf16[4,64,384]{2,1,0:T(8,128)(2,1)S(1)}, bf16[4,64,384]{2,1,0:T(8,128)(2,1)S(1)}, u32[]{:S(2)}, u32[]{:S(2)}) collective-permute-start(bf16[4,64,384]{2,1,0:T(8,128)(2,1)S(1)} %get-tuple-element.227), channel_id=1, source_target_pairs={{0,8},{1,9},{2,10},{3,11},{4,12},{5,13},{6,14},{7,15},{8,0},{9,1},... | collective-permute-start | bytes 589832 | tf_op jit(solution)/shard_map/ppermute | solution.py:529
  639.5 21.5 %collective-permute-start.127 = (bf16[4,64,384]{2,1,0:T(8,128)(2,1)S(1)}, bf16[4,64,384]{2,1,0:T(8,128)(2,1)S(1)}, u32[]{:S(2)}, u32[]{:S(2)}) collective-permute-start(bf16[4,64,384]{2,1,0:T(8,128)(2,1)S(1)} %get-tuple-element.239), channel_id=1, source_target_pairs={{0,16},{1,17},{2,18},{3,19},{4,20},{5,21},{6,22},{7,23},{8,24},{9,... | collective-permute-start | bytes 589832 | tf_op jit(solution)/shard_map/ppermute | solution.py:529
  (232 other events, 2676.2 us)

commit v3 on v2

--- a/solution.py
+++ b/solution.py
@@ -536,91 +536,107 @@
 class Gather:
     def __init__(self, place, piece):
         self.place = place
-        half = piece.shape[0] // 2
-        self.halves = [piece[:half], piece[half:]]
-        self.mine = [[None] * place.groups for _ in range(2)]
-        self.theirs = [[None] * place.groups for _ in range(2)]
-
-    def chips(self, half, *wait):
-        piece = after(self.halves[half], *wait) if wait else self.halves[half]
+        self.piece = piece
+        self.held = [None] * 5
+        self.crossed = [None] * 5
+
+    def chips(self, *wait):
         place = self.place
+        piece = after(self.piece, *wait) if wait else self.piece
         along = [piece] + [place.swap(piece, chip=k) for k in range(1, place.chips)]
-        self.mine[half][0] = jnp.stack(along)
-        return self.mine[half][0]
-
-    def near(self, half, *wait):
-        slots = self.mine[half]
-        piece = after(slots[0], *wait) if wait else slots[0]
-        order = (1, 2) if half == 0 else (2, 1)
-        for k in order:
-            slots[k] = self.place.swap(piece, grp=k)
-        return slots[order[0]]
-
-    def far(self, half, *wait):
-        slots = self.mine[half]
-        first, second = (1, 2) if half == 0 else (2, 1)
-        piece = after(slots[first], *wait) if wait else slots[first]
-        slots[3] = self.place.swap(piece, grp=second)
-        return slots[3]
-
-    def cross(self, half, slot, *wait):
-        piece = self.mine[half][slot]
-        piece = after(piece, *wait) if wait else piece
-        self.theirs[half][slot] = self.place.swap(piece, core=1)
+        self.along = along
+        self.held[0] = jnp.stack(along)
+        return along[-1]
+
+    def near(self, *wait):
+        piece = after(self.held[0], *wait) if wait else self.held[0]
+        self.held[1] = self.place.swap(piece, grp=1)
+        self.held[2] = self.place.swap(piece, grp=2)
+        return self.held[2]
+
+    def far(self, *wait):
+        half = self.held[0].shape[1] // 2
+        first = after(self.held[1], *wait) if wait else self.held[1]
+        second = after(self.held[2], *wait) if wait else self.held[2]
+        self.held[3] = self.place.swap(first[:, :half], grp=2)
+        self.held[4] = self.place.swap(second[:, half:], grp=1)
+        return self.held[4]
+
+    def cross(self, *which, wait=()):
+        for n in which:
+            piece = after(self.held[n], *wait) if wait else self.held[n]
+            self.crossed[n] = self.place.swap(piece, core=1)
 
     def pieces(self):
-        return [p for side in (self.mine, self.theirs) for half in side for p in half]
-
-
-def fetch(where, pieces, whole, sem, groups, by):
-    chips, half, cols = pieces[0].shape
+        return self.held + self.crossed
+
+
+class Window:
+    def __init__(self, gather, start, cols):
+        self.arrays = gather.pieces()
+        self.start, self.cols = start, cols
+        chips, rows, _ = self.arrays[0].shape
+        self.chips, self.rows = chips, rows
+
+
+def fetch(where, window, refs, whole, sem, groups, by):
+    rows, cols = window.rows, window.cols
     core, chip, grp = where[0], where[1], where[2]
-    for k in range(chips):
-        for n, piece in enumerate(pieces):
-            other_core, lower, other_grp = n // (2 * groups), (n // groups) % 2, n % groups
-            col = pl.multiple_of((grp ^ other_grp) * cols, LANES)
-            row = pl.multiple_of((((chip ^ k) * 2 + (core ^ other_core)) * 2 + lower) * half, half)
-            slot = {"grp": other_grp, "chip": k, "all": 0}[by]
-            pltpu.make_async_copy(
-                piece.at[k], whole.at[pl.ds(row, half), pl.ds(col, cols)], sem.at[slot]
-            ).start()
-
-
-def fetched(view, sem):
-    pltpu.make_async_copy(view, view, sem).wait()
-
-
-def weight_call(place, kernel, pieces, inputs, in_specs, outs, out_specs, steps, by, name, flops, mb=40):
-    chips, half, cols = pieces[0].shape
-    groups = place.groups
-    shape = (chips * 4 * half, groups * cols)
-    slots = {"grp": groups, "chip": chips, "all": 1}[by]
+    for other_grp in range(groups):
+        for k in range(window.chips):
+            for n, ref in enumerate(refs):
+                other_core, kind = n // 5, n % 5
+                if min(kind, 3) != other_grp:
+                    continue
+                size = rows if kind < 3 else rows // 2
+                col = pl.multiple_of((grp ^ other_grp) * cols, LANES)
+                row = ((chip ^ k) * 2 + (core ^ other_core)) * rows + max(kind - 3, 0) * size
+                slot = {"grp": other_grp, "all": 0}[by]
+                pltpu.make_async_copy(
+                    ref.at[k, :, pl.ds(window.start, cols)],
+                    whole.at[pl.ds(pl.multiple_of(row, size), size), pl.ds(col, cols)],
+                    sem.at[slot],
+                ).start()
+
+
+def weight_call(place, kernel, window, inputs, in_specs, outs, out_specs, steps, by, name, flops, mb=40):
+    cols, groups = window.cols, place.groups
+    pieces = window.arrays
+    shape = (window.chips * 2 * window.rows, groups * cols)
+    slots = {"grp": groups, "all": 1}[by]
     anywhere = pl.BlockSpec(memory_space=pl.ANY)
 
     def body(where, *refs):
         taken, refs = refs[: len(pieces)], refs[len(pieces) :]
-        *refs, weight, sem = refs
+        *refs, written, weight, sem, out_sem = refs
         step = pl.program_id(0)
 
         @pl.when(step == 0)
         def _():
-            fetch(where, taken, weight, sem, groups, by)
+            fetch(where, window, taken, weight, sem, groups, by)
 
         def ready():
             if by == "all":
 
                 @pl.when(step == 0)
                 def _():
-                    fetched(weight, sem.at[0])
-
-            elif by == "grp":
-                at = pl.multiple_of((where[2] ^ step) * cols, LANES)
-                fetched(weight.at[:, pl.ds(at, cols)], sem.at[step])
+                    pltpu.make_async_copy(weight, weight, sem.at[0]).wait()
+                    pltpu.make_async_copy(weight, written, out_sem.at[0]).start()
+
             else:
-                at = pl.multiple_of((where[1] ^ step) * 4 * half, 4 * half)
-                fetched(weight.at[pl.ds(at, 4 * half), :], sem.at[step])
+                at = pl.ds(pl.multiple_of((where[2] ^ step) * cols, LANES), cols)
+                view = weight.at[:, at]
+                pltpu.make_async_copy(view, view, sem.at[step]).wait()
+                pltpu.make_async_copy(view, written.at[:, at], out_sem.at[step]).start()
 
         kernel(where, ready, weight, *refs)
+
+        @pl.when(step == steps - 1)
+        def _():
+            for slot in range(slots):
+                width = shape[1] // slots
+                view = weight.at[:, pl.ds(slot * width, width)]
+                pltpu.make_async_copy(view, view, out_sem.at[slot]).wait()
 
     total = sum(math.prod(x.shape) * x.dtype.itemsize for x in list(inputs) + list(outs))
     return pl.pallas_call(
@@ -629,36 +645,58 @@
             num_scalar_prefetch=1,
             grid=(steps,),
             in_specs=[anywhere] * len(pieces) + in_specs,
-            out_specs=out_specs,
-            scratch_shapes=[pltpu.VMEM(shape, jnp.bfloat16), pltpu.SemaphoreType.DMA((slots,))],
+            out_specs=out_specs + [anywhere],
+            scratch_shapes=[
+                pltpu.VMEM(shape, jnp.bfloat16),
+                pltpu.SemaphoreType.DMA((slots,)),
+                pltpu.SemaphoreType.DMA((slots,)),
+            ],
         ),
-        out_shape=outs,
+        out_shape=outs + [shaped(shape, jnp.bfloat16)],
         compiler_params=params(mb),
         cost_estimate=pl.CostEstimate(
-            flops=flops, bytes_accessed=2 * shape[0] * shape[1] + total, transcendentals=0
+            flops=flops, bytes_accessed=4 * shape[0] * shape[1] + total, transcendentals=0
         ),
         name=name,
     )(place.scalars, *pieces, *inputs)
 
 
+def plain_call(kernel, inputs, in_specs, outs, out_specs, steps, name, flops, mb=40):
+    total = sum(math.prod(x.shape) * x.dtype.itemsize for x in list(inputs) + list(outs))
+    return pl.pallas_call(
+        kernel,
+        grid=(steps,),
+        in_specs=in_specs,
+        out_specs=out_specs,
+        out_shape=outs,
+        compiler_params=params(mb),
+        cost_estimate=pl.CostEstimate(flops=flops, bytes_accessed=total, transcendentals=0),
+        name=name,
+    )(*inputs)
+
+
 TILE = 256
 
 
 def row_tiles(width):
-    return pl.BlockSpec((TILE, width), lambda i, s: (i, 0))
+    return pl.BlockSpec((TILE, width), lambda i, *s: (i, 0))
 
 
 def fixed(*shape):
-    return pl.BlockSpec(shape, lambda i, s: (0,) * len(shape))
+    return pl.BlockSpec(shape, lambda i, *s: (0,) * len(shape))
+
+
+def whole_once(shape):
+    return pl.BlockSpec(shape, lambda i: (0,) * len(shape), pipeline_mode=pl.Buffered(1))
 
 
 def shaped(shape, dtype):
     return jax.ShapeDtypeStruct(shape, dtype)
 
 
-def project_qkv(place, rows, pieces, bias, scale):
+def project_qkv(place, rows, window, bias, scale):
     length, width = rows.shape
-    cols = pieces[0].shape[2]
+    cols = window.cols
 
     def kernel(where, ready, weight, x_ref, bias_ref, scale_ref, out_ref):
         ready()
@@ -673,7 +711,7 @@
     return weight_call(
         place,
         kernel,
-        pieces,
+        window,
         (rows, bias, scale),
         [fixed(length, width), fixed(1, total), fixed(1, total)],
         [shaped((length, total), jnp.bfloat16)],
@@ -682,7 +720,7 @@
         "grp",
         "qkv",
         2 * length * width * total,
-    )[0]
+    )
 
 
 def norm_parts(rows):
@@ -708,7 +746,7 @@
         sum_ref[n : n + 1, :] += jnp.sum(term, 0, keepdims=True)
 
 
-def project_out(place, contexts, pieces, rows, bias, gain, shift):
+def project_out(place, contexts, window, rows, bias, gain, shift):
     length, width = rows.shape
 
     def kernel(where, ready, weight, c_ref, x_ref, b_ref, g_ref, s_ref, n_ref, r_ref, low_ref):
@@ -722,7 +760,7 @@
     return weight_call(
         place,
         kernel,
-        pieces,
+        window,
         (contexts, rows, bias, gain, shift),
         [row_tiles(width), row_tiles(width)] + [fixed(1, width)] * 3,
         [
@@ -738,9 +776,9 @@
     )
 
 
-def feed_in(place, normed_low, pieces, bias):
+def feed_in(place, normed_low, window, bias):
     length, width = normed_low.shape
-    cols = pieces[0].shape[2]
+    cols = window.cols
 
     def kernel(where, ready, weight, x_ref, bias_ref, hid_ref, slope_ref):
         ready()
@@ -758,7 +796,7 @@
     return weight_call(
         place,
         kernel,
-        pieces,
+        window,
         (normed_low, bias),
         [fixed(length, width), fixed(1, total)],
         [shaped((length, total), jnp.bfloat16)] * 2,
@@ -770,7 +808,7 @@
     )
 
 
-def feed_out(place, hidden, pieces, normed, cot, keep, vectors):
+def feed_out(place, hidden, window, normed, cot, keep, vectors):
     length, inner = hidden.shape
     width = normed.shape[1]
 
@@ -790,7 +828,7 @@
     return weight_call(
         place,
         kernel,
-        pieces,
+        window,
         (hidden, normed, cot, keep, *vectors),
         [row_tiles(inner), row_tiles(width), row_tiles(width), row_tiles(1)] + [fixed(1, width)] * 5,
         [
@@ -807,56 +845,55 @@
     )
 
 
-def feed_out_back(place, out_low, pieces, slope):
+def feed_out_back(out_low, weight, slope):
     length, width = out_low.shape
     inner = slope.shape[1]
-    cols = inner // place.chips
-
-    def kernel(where, ready, weight, g_ref, slope_ref, pre_ref, sum_ref):
-        ready_rows = pl.ds(pl.multiple_of((where[1] ^ pl.program_id(0)) * cols, cols), cols)
-        ready()
+    cols = min(1024, inner)
+
+    def kernel(g_ref, w_ref, slope_ref, pre_ref, sum_ref):
         total = jnp.zeros((1, cols), jnp.float32)
         for tile in range(length // TILE):
             here = pl.ds(tile * TILE, TILE)
-            grad = mxu(g_ref[here, :], weight[ready_rows, :], NT) * slope_ref[here, :].astype(jnp.float32)
+            grad = mxu(g_ref[here, :], w_ref[...], NT) * slope_ref[here, :].astype(jnp.float32)
             pre_ref[here, :] = grad.astype(jnp.bfloat16)
             total = total + jnp.sum(grad, 0, keepdims=True)
         sum_ref[...] = total
 
-    block = pl.BlockSpec((length, cols), lambda i, s: (0, i ^ s[1]))
-    return weight_call(
-        place,
+    block = pl.BlockSpec((length, cols), lambda i: (0, i))
+    return plain_call(
         kernel,
-        pieces,
-        (out_low, slope),
-        [fixed(length, width), block],
+        (out_low, weight, slope),
+        [fixed(length, width), pl.BlockSpec((cols, width), lambda i: (i, 0)), block],
         [shaped((length, inner), jnp.bfloat16), shaped((1, inner), jnp.float32)],
-        [block, pl.BlockSpec((1, cols), lambda i, s: (0, i ^ s[1]))],
-        place.chips,
-        "chip",
+        [block, pl.BlockSpec((1, cols), lambda i: (0, i))],
+        inner // cols,
         "feed_out_back",
         2 * length * width * inner,
     )
 
 
-def feed_in_back(place, pre_low, pieces, second_grad, normed, scale, gain):
+def feed_in_back(pre_low, weight, second_grad, normed, scale, gain):
     length, inner = pre_low.shape
     width = normed.shape[1]
 
-    def kernel(where, ready, weight, p_ref, g_ref, n_ref, r_ref, gain_ref, first_ref, low_ref, sum_ref):
-        ready()
-        grad = g_ref[...] + mxu(p_ref[...], weight[...], NT)
+    def kernel(p_ref, w_ref, g_ref, n_ref, r_ref, gain_ref, first_ref, low_ref, sum_ref):
+        grad = g_ref[...] + mxu(p_ref[...], w_ref[...], NT)
         first = norm_back(grad * gain_ref[...], n_ref[...], r_ref[:, :1])
         first_ref[...] = first
         low_ref[...] = first.astype(jnp.bfloat16)
         add_rows(sum_ref, grad * n_ref[...], grad, first)
 
-    return weight_call(
-        place,
+    return plain_call(
         kernel,
-        pieces,
-        (pre_low, second_grad, normed, scale, gain),
-        [row_tiles(inner), row_tiles(width), row_tiles(width), row_tiles(LANES), fixed(1, width)],
+        (pre_low, weight, second_grad, normed, scale, gain),
+        [
+            row_tiles(inner),
+            whole_once(weight.shape),
+            row_tiles(width),
+            row_tiles(width),
+            row_tiles(LANES),
+            fixed(1, width),
+        ],
         [
             shaped((length, width), jnp.float32),
             shaped((length, width), jnp.bfloat16),
@@ -864,58 +901,51 @@
         ],
         [row_tiles(width), row_tiles(width), fixed(8, width)],
         length // TILE,
-        "all",
         "feed_in_back",
         2 * length * width * inner,
     )
 
 
-def project_out_back(place, attn_low, pieces):
+def project_out_back(attn_low, weight):
     length, width = attn_low.shape
 
-    def kernel(where, ready, weight, g_ref, out_ref):
-        ready()
-        out_ref[...] = mxu(g_ref[...], weight[...], NT).astype(jnp.bfloat16)
-
-    return weight_call(
-        place,
+    def kernel(g_ref, w_ref, out_ref):
+        out_ref[...] = mxu(g_ref[...], w_ref[...], NT).astype(jnp.bfloat16)
+
+    return plain_call(
         kernel,
-        pieces,
-        (attn_low,),
-        [row_tiles(width)],
+        (attn_low, weight),
+        [row_tiles(width), whole_once(weight.shape)],
         [shaped((length, width), jnp.bfloat16)],
         [row_tiles(width)],
         length // TILE,
-        "all",
         "attn_out_back",
         2 * length * width * width,
     )[0]
 
 
-def project_qkv_back(place, grads, pieces, first_grad):
+def project_qkv_back(grads, weight, first_grad):
     length, width = first_grad.shape
     part = width // len(grads)
 
-    def kernel(where, ready, weight, *refs):
+    def kernel(w_ref, *refs):
         *grad_refs, first_ref, out_ref = refs
-        ready()
         total = first_ref[...]
         for n in range(3):
             for m, grad_ref in enumerate(grad_refs):
                 at = n * width + m * part
-                total = total + mxu(grad_ref[n], weight[:, at : at + part], NT)
+                total = total + mxu(grad_ref[n], w_ref[:, at : at + part], NT)
         out_ref[...] = total
 
-    return weight_call(
-        place,
+    return plain_call(
         kernel,
-        pieces,
-        (*grads, first_grad),
-        [pl.BlockSpec((3, TILE, part), lambda i, s: (0, i, 0))] * len(grads) + [row_tiles(width)],
+        (weight, *grads, first_grad),
+        [whole_once(weight.shape)]
+        + [pl.BlockSpec((3, TILE, part), lambda i: (0, i, 0))] * len(grads)
+        + [row_tiles(width)],
         [shaped((length, width), jnp.float32)],
         [row_tiles(width)],
         length // TILE,
-        "all",
         "qkv_back",
         6 * length * width * width,
     )[0]
@@ -952,7 +982,12 @@
 
             def store(slot):
                 for lower in range(2):
-                    outs[slot + lower * groups][:, :, at] = part[:, lower]
+                    near, far = ((1, 2), (2, 1))[lower]
+                    block = part[:, lower]
+                    if slot in (near, 3):
+                        outs[3 * lower + 2][0 if slot == near else 1, :, :, at] = block
+                    else:
+                        outs[3 * lower + (1 if slot == far else 0)][:, :, at] = block
 
             if split:
                 for n in range(groups):
@@ -1007,8 +1042,15 @@
     if own:
         in_specs.append(passed)
         inputs.append(received)
-        out_specs = [pl.BlockSpec((step_chips, half, cols), lambda i, j, s: (i, 0, 0))] * (2 * groups)
-        out_shape = [shaped((chips, half, cols), jnp.bfloat16)] * (2 * groups)
+        one = pl.BlockSpec((step_chips, half, cols), lambda i, j, s: (i, 0, 0))
+        two = pl.BlockSpec((2, step_chips, half, cols), lambda i, j, s: (0, i, 0, 0))
+        out_specs = [one, one, two] * 2
+        shape = (chips, half, cols)
+        out_shape = [
+            shaped(shape, jnp.bfloat16),
+            shaped(shape, jnp.bfloat16),
+            shaped((2, *shape), jnp.bfloat16),
+        ] * 2
     else:
         out_specs = passed
         out_shape = shaped((groups, chips, 2, half, cols), jnp.bfloat16)
@@ -1051,20 +1093,15 @@
         left, right, split, name = self.call
         received = after(self.received, *wait) if wait else self.received
         out = weight_grad(self.place, left, right, received, split, name)
-        swap, groups = self.place.swap, self.place.groups
-        self.upper, self.lower = out[:groups], out[groups:]
-        self.near = [
-            swap(self.upper[3], grp=1),
-            swap(self.lower[3], grp=2),
-            swap(self.upper[1], grp=1),
-            swap(self.lower[2], grp=2),
-        ]
+        self.kept = out
+        self.near = [self.place.swap(out[2], grp=1), self.place.swap(out[5], grp=2)]
         return out[0]
 
     def middle(self, *wait):
         near = after(self.near[0], *wait) if wait else self.near[0]
-        upper = add(self.upper[2], near)
-        lower = add(self.lower[1], self.near[1])
+        self.near[0] = near
+        upper = add(self.kept[1], near[1])
+        lower = add(self.kept[4], self.near[1][1])
         self.far = [self.place.swap(upper, grp=2), self.place.swap(lower, grp=1)]
         return upper
 
@@ -1072,7 +1109,11 @@
         place = self.place
         far = after(self.far[0], *wait) if wait else self.far[0]
         mine = jnp.concatenate(
-            [add(self.upper[0], self.near[2], far), add(self.lower[0], self.near[3], self.far[1])], 1
+            [
+                add(self.kept[0], self.near[0][0], far),
+                add(self.kept[3], self.near[1][0], self.far[1]),
+            ],
+            1,
         )
         self.terms = [lax.dynamic_index_in_dim(mine, place.chip, 0, False)]
         for k in range(1, place.chips):
@@ -1151,12 +1192,45 @@
         norm2_gain,
         norm2_bias,
     )
-    packed = lax.all_gather(jnp.concatenate(vectors), "shard", axis=0)
+    rows = tokens[0]
+    seg_row = segment_ids.reshape(1, length)
+    seg_col = segment_ids.reshape(length, 1)
+    keep = keep_flag.reshape(length, 1).astype(jnp.float32)
+    pairs = width // LANES
+
+    flat = jnp.concatenate(vectors)
+    extra = 16
+    flat = jnp.pad(flat, (0, extra * w_qkv.shape[1] - flat.shape[0])).reshape(extra, -1)
+    c1 = Gather(place, jnp.concatenate([w_qkv, flat], 0))
+    c2 = Gather(place, jnp.concatenate([w_in, w_attn_out], 1))
+    c3 = Gather(place, w_out)
+    wait = c1.chips()
+    rider = jnp.stack([p[-extra:] for p in c1.along])
+    c1.held[0] = jnp.stack([p[:-extra] for p in c1.along])
+    near = c1.near()
+    both = [rider, place.swap(rider, core=1)]
+    wait = c2.chips(wait)
+    c1.cross(0)
+    c1.far()
+    c1.cross(1, 2)
+    c2.near(near)
+    c3.chips(near, wait)
+    c1.cross(3, 4)
+
+    def owner(shard):
+        found = both[0][0]
+        for other in range(1, shards):
+            found = jnp.where(
+                (place.shard ^ other) == shard, both[other % 2][other // 2], found
+            )
+        return found.reshape(-1)
+
+    parts = [owner(shard).astype(jnp.float32) for shard in range(shards)]
     unpacked = []
     at = 0
     for vector in vectors:
         size = vector.shape[0]
-        unpacked.append(packed[:, at : at + size].reshape(1, -1).astype(jnp.float32))
+        unpacked.append(jnp.concatenate([p[at : at + size] for p in parts]).reshape(1, -1))
         at += size
     (
         bias_query,
@@ -1169,64 +1243,33 @@
         gain_two,
         shift_two,
     ) = unpacked
-    rows = tokens[0]
-    seg_row = segment_ids.reshape(1, length)
-    seg_col = segment_ids.reshape(length, 1)
-    keep = keep_flag.reshape(length, 1).astype(jnp.float32)
-    pairs = width // LANES
     blank = jnp.zeros_like(bias_query)
     qkv_bias = jnp.concatenate([bias_query, blank, bias_value], 1)
     qkv_scale = jnp.concatenate([blank + 1.0 / math.sqrt(HD), blank + 1.0, blank + 1.0], 1)
 
-    qkv, attn = Gather(place, w_qkv), Gather(place, w_attn_out)
-    fin, fout = Gather(place, w_in), Gather(place, w_out)
-    t0 = qkv.chips(0)
-    t1 = qkv.chips(1, t0)
-    qkv.near(0)
-    qkv.near(1, qkv.mine[0][1], qkv.mine[0][2])
-    qkv.far(0)
-    qkv.far(1)
-    tz = [g.chips(half, t1) for g in (attn, fin) for half in range(2)]
-    for half, slot in ((0, 0), (0, 1), (0, 2), (1, 0), (1, 1), (1, 2), (0, 3), (1, 3)):
-        qkv.cross(half, slot)
-    last = (qkv.mine[0][1], qkv.mine[1][2], qkv.mine[1][1])
-    for g in (attn, fin):
-        for half in range(2):
-            g.near(half, *last)
-    for half in range(2):
-        fout.chips(half, *tz)
-    mixed = project_qkv(place, rows, qkv.pieces(), qkv_bias, qkv_scale)
-
+    mixed, full_qkv = project_qkv(place, rows, Window(c1, 0, w_qkv.shape[1]), qkv_bias, qkv_scale)
+    c2.far(mixed)
+    c2.cross(0, 1, 2, wait=(mixed,))
     forward = attention_forward(mixed, seg_col, seg_row, 0, pairs // 2)
-    forward_gate = forward[1]
-    for g in (attn, fin):
-        for half in range(2):
-            g.far(half, mixed)
-    for half in range(2):
-        fout.near(half, attn.mine[0][2], attn.mine[1][1], fin.mine[0][2], fin.mine[1][1])
-    for g in (attn, fin):
-        for half in range(2):
-            for slot in range(3):
-                g.cross(half, slot)
+    done = forward[1]
+    c2.cross(3, 4, wait=(done,))
+    c3.near(done, c2.held[3], c2.held[4])
     contexts, lse = attention_forward(
-        after(mixed, fin.mine[0][1], fin.mine[1][2]), seg_col, seg_row, pairs // 2, pairs // 2, forward
-    )
-    for g in (attn, fin):
-        for half in range(2):
-            g.cross(half, 3)
-    for half in range(2):
-        fout.far(half, forward_gate)
-    normed, scale_one, normed_low = project_out(
-        place, contexts, attn.pieces(), rows, bias_attn, gain_one, shift_one
-    )
-    for half in range(2):
-        for slot in range(4):
-            fout.cross(half, slot)
-    hidden, slope = feed_in(place, normed_low, fin.pieces(), bias_in)
-    layer_out, second_grad, out_low, second_sums = feed_out(
+        after(mixed, c2.held[3], c2.held[4]), seg_col, seg_row, pairs // 2, pairs // 2, forward
+    )
+    normed, scale_one, normed_low, full_attn = project_out(
+        place, contexts, Window(c2, w_in.shape[1], w_attn_out.shape[1]), rows, bias_attn, gain_one, shift_one
+    )
+    c3.far(normed_low)
+    c3.cross(0, 1, 2, wait=(normed_low,))
+    hidden, slope, full_in = feed_in(
+        place, after(normed_low, c3.held[1], c3.held[2]), Window(c2, 0, w_in.shape[1]), bias_in
+    )
+    c3.cross(3, 4, wait=(hidden,))
+    layer_out, second_grad, out_low, second_sums, full_out = feed_out(
         place,
         hidden,
-        fout.pieces(),
+        Window(c3, 0, w_out.shape[1]),
         normed,
         cotangent[0],
         keep,
@@ -1234,15 +1277,15 @@
     )
 
     r_out = Reduction(place, hidden, out_low, False, "out")
-    pre_low, bias_in_grad = feed_out_back(place, after(out_low, r_out.sent), fout.pieces(), slope)
+    pre_low, bias_in_grad = feed_out_back(after(out_low, r_out.sent), full_out, slope)
     own_out = r_out.own(pre_low)
     r_in = Reduction(place, normed_low, pre_low, True, "in", own_out)
     first_grad, attn_low, first_sums = feed_in_back(
-        place, after(pre_low, r_in.sent), fin.pieces(), second_grad, normed, scale_one, gain_one
+        after(pre_low, r_in.sent), full_in, second_grad, normed, scale_one, gain_one
     )
     own_in = r_in.own(first_grad)
     r_attn = Reduction(place, contexts, attn_low, False, "attn", own_in)
-    context_grad = project_out_back(place, after(attn_low, r_attn.sent), attn.pieces())
+    context_grad = project_out_back(after(attn_low, r_attn.sent), full_attn)
     own_attn = r_attn.own(context_grad)
     quarter = pairs // 4
 
@@ -1278,7 +1321,7 @@
     share_in = r_in.share(late_b)
     share_attn = r_attn.share(late_b)
     r_qkv_b = Reduction(place, rows, low_b, True, "qkv_b", mid_a, share_in, share_attn)
-    input_grad = project_qkv_back(place, (low_a, after(low_b, r_qkv_b.sent)), qkv.pieces(), first_grad)
+    input_grad = project_qkv_back((low_a, after(low_b, r_qkv_b.sent)), full_qkv, first_grad)
     own_b = r_qkv_b.own(input_grad)
     r_qkv_a.along(own_b)
     r_qkv_b.middle()

time: 687 us -> 628 us (0.914)
  starting transfers between devices: 141 us -> 102 us
  local copies, waits for them, and re-layouts: 73.6 us -> 53.6 us
  blocking collectives: 14 us -> 0 us
  other arithmetic: 21.9 us -> 29.7 us
    pallas_call x8 -> x4, Pallas kernels: 106 us -> 60.5 us  [weight_call(): pl.pallas_call(body, grid_spec=pltpu.PrefetchScalarGridSpec(num_scalar_pr...]
    pallas_call x0 -> x4, Pallas kernels: none -> 43.5 us  [plain_call(): pl.pallas_call(kernel, grid=(steps,), in_specs=in_specs, out_specs=out_sp...]
    ppermute x150 -> x97, starting transfers between devices: 141 us -> 102 us  [swap(): return lax.ppermute(array, AXES, pairs)]
    unnamed x336 -> x178, local copies, waits for them, and re-layouts: 61.9 us -> 43.5 us
    all_gather x1 -> x0, blocking collectives: 14 us -> none  [on_device_permutes(): packed = lax.all_gather(jnp.concatenate(vectors), 'shard', axis=0)]
    ppermute x150 -> x97, waiting for transfers between devices: 165 us -> 171 us  [swap(): return lax.ppermute(array, AXES, pairs)]
  transfers between devices with their start and end apart: 150 -> 97, of which waited for: 48 -> 36; matrix products, arithmetic and copies ran while one was open for 6% -> 7% of each run, Pallas kernels for 32% -> 34%
where the time goes in v3:
time: 628 us; the launch traced here: 617 us
  Pallas kernels  258 us (41%)
  waiting for transfers between devices  171 us (27%)
  starting transfers between devices  102 us (16%)
  local copies, waits for them, and re-layouts  53.6 us (9%)
  other arithmetic  29.7 us (5%)
    ppermute x97, waiting for transfers between devices, swap(): return lax.ppermute(array, AXES, pairs)  171 us
    ppermute x97, starting transfers between devices, swap(): return lax.ppermute(array, AXES, pairs)  102 us
    pallas_call x10, Pallas kernels, weight_grad(): pl.pallas_call(functools.partial(weight_grad_kernel, own=own, rows=rows,...  64.5 us
    pallas_call x4, Pallas kernels, weight_call(): pl.pallas_call(body, grid_spec=pltpu.PrefetchScalarGridSpec(num_scalar_pr...  60.5 us
    pallas_call x4, Pallas kernels, attention_backward(): pl.pallas_call(body, grid=(pairs,), in_specs=[pair(0), pair(1), pair(2),...  56.2 us
    unnamed x178, local copies, waits for them, and re-layouts  43.5 us
    pallas_call x4, Pallas kernels, plain_call(): pl.pallas_call(kernel, grid=(steps,), in_specs=in_specs, out_specs=out_sp...  43.5 us
    pallas_call x2, Pallas kernels, attention_forward(): pl.pallas_call(body, grid=(pairs,), in_specs=[pair(0), pair(1), pair(2),...  33.5 us
  transfers between devices with their start and end apart: 97, of which 36 were waited for; matrix products, arithmetic and copies ran while one was open for 7% of the time, Pallas kernels for 34%

profile of v3, /device:TPU:0, one launch (start us, length us, event | category | flops | bytes accessed | tf_op | source)
XLA Modules:
  0.0 617.3 jit_solution(5852063951601758715)
XLA Ops:
  9.2 5.1 collective-permute-start.2
  18.1 2.6 collective-permute-done.2
  20.8 12.4 %collective-permute-done.1 = bf16[144,768]{1,0:T(8,128)(2,1)S(1)} collective-permute-done((bf16[144,768]{1,0:T(8,128)(2,1)S(1)}, bf16[144,768]{1,0:T(8,128)(2,1)S(1)}, u32[]{:S(2)}, u32[]{:S(2)}) %collective-permute-start.1) | collective-permute-done | bytes 221216 | tf_op jit(solution)/shard_map/ppermute | solution.py:529
  37.1 2.5 collective-permute-start.4
  49.8 11.8 %collective-permute-start.17 = (bf16[128,1280]{1,0:T(8,128)(2,1)}, bf16[128,1280]{1,0:T(8,128)(2,1)}, u32[]{:S(2)}, u32[]{:S(2)}) collective-permute-start(bf16[128,1280]{1,0:T(8,128)(2,1)} %pad_maximum_fusion.6), channel_id=1, source_target_pairs={{0,2},{1,3},{2,0},{3,1},{4,6},{5,7},{6,4},{7,5},{8,10},{9,11},{10,... | collective-permute-start | bytes 983048 | tf_op jit(solution)/shard_map/ppermute | solution.py:529
  61.7 6.1 collective-permute-done.18
  67.8 6.9 %collective-permute-done.17 = bf16[128,1280]{1,0:T(8,128)(2,1)} collective-permute-done((bf16[128,1280]{1,0:T(8,128)(2,1)}, bf16[128,1280]{1,0:T(8,128)(2,1)}, u32[]{:S(2)}, u32[]{:S(2)}) %collective-permute-start.17) | collective-permute-done | bytes 327712 | tf_op jit(solution)/shard_map/ppermute | solution.py:529
  79.6 7.9 %collective-permute-done.9.refs_3_ = bf16[4,64,768]{2,1,0:T(8,128)(2,1)S(1)} collective-permute-done((bf16[4,64,768]{2,1,0:T(8,128)(2,1)S(1)}, bf16[4,64,768]{2,1,0:T(8,128)(2,1)S(1)}, u32[]{:S(2)}, u32[]{:S(2)}) %collective-permute-start.9) | collective-permute-done | bytes 393248 | tf_op jit(solution)/shard_map/ppermute | solution.py:529
  92.0 11.8 %qkv.1 = (bf16[1024,3072]{1,0:T(8,128)(2,1)}, bf16[1024,3072]{1,0:T(8,128)(2,1)}) custom-call(s32[3]{0:T(128)S(1)} %pad_add_fusion.where, bf16[4,128,768]{2,1,0:T(8,128)(2,1)S(1)} %pad_maximum_fusion.4.refs_0_, bf16[4,128,768]{2,1,0:T(8,128)(2,1)S(1)} %collective-permute-done.8.refs_1_, bf16[4,128,768]{2,1,0:T(8,128)(2,1)S(1)} %collective-permute-done.3.refs_2_, ...), custom_call_target="tpu_custom_call" | custom-call | flops 6442450944 | bytes 20996096 | tf_op jit(solution)/shard_map/qkv/pallas_call | solution.py:642
  103.8 12.1 %collective-permute-done.19.refs_1_ = bf16[4,128,1280]{2,1,0:T(8,128)(2,1)S(1)} collective-permute-done((bf16[4,128,1280]{2,1,0:T(8,128)(2,1)S(1)}, bf16[4,128,1280]{2,1,0:T(8,128)(2,1)S(1)}, u32[]{:S(2)}, u32[]{:S(2)}) %collective-permute-start.19) | collective-permute-done | bytes 1310752 | tf_op jit(solution)/shard_map/ppermute | solution.py:529
  121.0 3.0 collective-permute-start.5
  124.1 10.9 %collective-permute-done.20.refs_3_ = bf16[4,64,1280]{2,1,0:T(8,128)(2,1)S(1)} collective-permute-done((bf16[4,64,1280]{2,1,0:T(8,128)(2,1)S(1)}, bf16[4,64,1280]{2,1,0:T(8,128)(2,1)S(1)}, u32[]{:S(2)}, u32[]{:S(2)}) %collective-permute-start.20) | collective-permute-done | bytes 655392 | tf_op jit(solution)/shard_map/ppermute | solution.py:529
  135.5 2.8 copy-done.37
  138.3 16.7 %attn_fwd.2 = (bf16[1024,1024]{1,0:T(8,128)(2,1)S(1)}, f32[8,2,1024]{2,1,0:T(2,128)S(1)}) custom-call(bf16[1024,3072]{1,0:T(8,128)(2,1)S(1)} %copy-done.37, bf16[1024,3072]{1,0:T(8,128)(2,1)S(1)} %copy-done.37, bf16[1024,3072]{1,0:T(8,128)(2,1)S(1)} %copy-done.37, s32[1024,1]{1,0:T(8,128)S(1)} %copy.38.seg_c.refs_5_, s32[1,1024]{1,0:T(1,128)S(1)} %copy-done.22), custom_call_target="tpu_custom_call" | custom-call | flops 8589934592 | bytes 4194304 | tf_op jit(solution)/shard_map/attn_fwd/pallas_call | solution.py:385
  159.1 2.8 copy-done.38
  161.9 16.9 %attn_fwd.3 = (bf16[1024,1024]{1,0:T(8,128)(2,1)S(1)}, f32[8,2,1024]{2,1,0:T(2,128)S(1)}) custom-call(bf16[1024,3072]{1,0:T(8,128)(2,1)S(1)} %copy-done.38, bf16[1024,3072]{1,0:T(8,128)(2,1)S(1)} %copy-done.38, bf16[1024,3072]{1,0:T(8,128)(2,1)S(1)} %copy-done.38, s32[1024,1]{1,0:T(8,128)S(1)} %copy-done.13, ...), custom_call_target="tpu_custom_call", output_to_operand_aliasing={{0}: (5, {}), {1}: (6, {})} | custom-call | flops 8589934592 | bytes 4194304 | tf_op jit(solution)/shard_map/attn_fwd/pallas_call | solution.py:385
  180.1 7.9 %attn_out.1 = (f32[1024,1024]{1,0:T(8,128)}, f32[1024,128]{1,0:T(8,128)S(1)}, bf16[1024,1024]{1,0:T(8,128)(2,1)S(1)}, bf16[1024,1024]{1,0:T(8,128)(2,1)}) custom-call(s32[3]{0:T(128)S(1)} %pad_add_fusion.where, bf16[4,128,1280]{2,1,0:T(8,128)(2,1)S(1)} %pad_maximum_fusion.2.refs_0_, bf16[4,128,1280]{2,1,0:T(8,128)(2,1)S(1)} %collective-permute-done.19.refs_1_, ...), custom_call_target="tpu_custom_call" | custom-call | flops 2147483648 | bytes 15216640 | tf_op jit(solution)/shard_map/attn_out/pallas_call | solution.py:642
  191.5 20.7 %feed_in.1 = (bf16[1024,4096]{1,0:T(8,128)(2,1)}, bf16[1024,4096]{1,0:T(8,128)(2,1)}, bf16[1024,4096]{1,0:T(8,128)(2,1)}) custom-call(s32[3]{0:T(128)S(1)} %pad_add_fusion.where, bf16[4,128,1280]{2,1,0:T(8,128)(2,1)S(1)} %pad_maximum_fusion.2.refs_0_, bf16[4,128,1280]{2,1,0:T(8,128)(2,1)S(1)} %collective-permute-done.19.refs_1_, ...), custom_call_target="tpu_custom_call" | custom-call | flops 8589934592 | bytes 35667968 | tf_op jit(solution)/shard_map/feed_in/pallas_call | solution.py:642
  216.9 20.2 %feed_out.1 = (bf16[1024,1024]{1,0:T(8,128)(2,1)}, f32[1024,1024]{1,0:T(8,128)}, bf16[1024,1024]{1,0:T(8,128)(2,1)S(1)}, f32[8,1024]{1,0:T(8,128)S(1)}, bf16[4096,1024]{1,0:T(8,128)(2,1)}) custom-call(s32[3]{0:T(128)S(1)} %pad_add_fusion.where, bf16[4,512,256]{2,1,0:T(8,128)(2,1)S(1)} %pad_maximum_fusion.3.refs_0_, ...), custom_call_target="tpu_custom_call" | custom-call | flops 8589934592 | bytes 39903232 | tf_op jit(solution)/shard_map/feed_out/pallas_call | solution.py:642
  237.0 7.9 %wgrad_out_sent.1 = bf16[4,4,2,256,256]{4,3,2,1,0:T(8,128)(2,1)S(1)} custom-call(s32[3]{0:T(128)S(1)} %pad_add_fusion.where, bf16[1024,4096]{1,0:T(8,128)(2,1)} %get-tuple-element.139.refs_10_.left_ref, bf16[1024,1024]{1,0:T(8,128)(2,1)S(1)} %get-tuple-element.146.right_ref.g_ref), custom_call_target="tpu_custom_call" | custom-call | flops 4294967296 | bytes 18874368 | tf_op jit(solution)/shard_map/wgrad_out_sent/pallas_call | solution.py:1057
  245.2 12.4 %feed_out_back.1 = (bf16[1024,4096]{1,0:T(8,128)(2,1)S(1)}, f32[1,4096]{1,0:T(1,128)S(1)}) custom-call(bf16[1024,1024]{1,0:T(8,128)(2,1)S(1)} %get-tuple-element.146.right_ref.g_ref, bf16[4096,1024]{1,0:T(8,128)(2,1)} %get-tuple-element.147.w_ref, bf16[1024,4096]{1,0:T(8,128)(2,1)} %get-tuple-element.148.slope_ref), custom_call_target="tpu_custom_call" | custom-call | flops 8589934592 | bytes 27279360 | tf_op jit(solution)/shard_map/feed_out_back/pallas_call | solution.py:666
  257.6 3.3 copy-done.31
  260.9 8.9 %wgrad_out_own.1 = (bf16[4,256,256]{2,1,0:T(8,128)(2,1)S(1)}, bf16[4,256,256]{2,1,0:T(8,128)(2,1)S(1)}, bf16[2,4,256,256]{3,2,1,0:T(8,128)(2,1)}, bf16[4,256,256...) custom-call(s32[3]{0:T(128)S(1)} %pad_add_fusion.where, ...), custom_call_target="tpu_custom_call" | custom-call | flops 4294967296 | bytes 18874368 | tf_op jit(solution)/shard_map/wgrad_out_own/pallas_call | solution.py:1057
  269.9 8.8 %wgrad_in_sent.1 = bf16[4,4,2,64,1024]{4,3,2,1,0:T(8,128)(2,1)S(1)} custom-call(s32[3]{0:T(128)S(1)} %pad_add_fusion.where, bf16[1024,1024]{1,0:T(8,128)(2,1)S(1)} %copy-done.26, bf16[1024,4096]{1,0:T(8,128)(2,1)} %copy-done.31), custom_call_target="tpu_custom_call" | custom-call | flops 4294967296 | bytes 18874368 | tf_op jit(solution)/shard_map/wgrad_in_sent/pallas_call | solution.py:1057
  280.6 16.7 %feed_in_back.1 = (f32[1024,1024]{1,0:T(8,128)S(1)}, bf16[1024,1024]{1,0:T(8,128)(2,1)S(1)}, f32[8,1024]{1,0:T(8,128)S(1)}) custom-call(bf16[1024,4096]{1,0:T(8,128)(2,1)} %copy-done.31, bf16[1024,4096]{1,0:T(8,128)(2,1)} %get-tuple-element.154.w_ref, f32[1024,1024]{1,0:T(8,128)S(1)} %copy-done.36, f32[1024,1024]{1,0:T(8,128)} %get-tuple-element.142.refs_11_.n_ref, ...), custom_call_target="tpu_custom_call" | custom-call | flops 8589934592 | bytes 32018432 | tf_op jit(solution)/shard_map/feed_in_back/pallas_call | solution.py:666
  297.4 3.2 copy-done.27
  300.5 8.9 %wgrad_in_own.1 = (bf16[4,64,1024]{2,1,0:T(8,128)(2,1)S(1)}, bf16[4,64,1024]{2,1,0:T(8,128)(2,1)S(1)}, bf16[2,4,64,1024]{3,2,1,0:T(8,128)(2,1)S(1)}, bf16[4,64,1...) custom-call(s32[3]{0:T(128)S(1)} %pad_add_fusion.where, ...), custom_call_target="tpu_custom_call" | custom-call | flops 4294967296 | bytes 18874368 | tf_op jit(solution)/shard_map/wgrad_in_own/pallas_call | solution.py:1057
  310.5 2.8 wgrad_attn_sent.1
  316.6 13.0 %collective-permute-done.44 = bf16[4,256,256]{2,1,0:T(8,128)(2,1)} collective-permute-done((bf16[4,256,256]{2,1,0:T(8,128)(2,1)}, bf16[4,256,256]{2,1,0:T(8,128)(2,1)}, u32[]{:S(2)}, u32[]{:S(2)}) %collective-permute-start.44) | collective-permute-done | bytes 524320 | tf_op jit(solution)/shard_map/ppermute | solution.py:529
  334.8 3.0 attn_out_back.1.refs_4_
  337.8 1.9 wgrad_attn_own.1
  339.7 12.4 %collective-permute-done.40 = bf16[2,4,256,256]{3,2,1,0:T(8,128)(2,1)} collective-permute-done((bf16[2,4,256,256]{3,2,1,0:T(8,128)(2,1)}, bf16[2,4,256,256]{3,2,1,0:T(8,128)(2,1)}, u32[]{:S(2)}, u32[]{:S(2)}) %collective-permute-start.40) | collective-permute-done | bytes 1048608 | tf_op jit(solution)/shard_map/ppermute | solution.py:529
  353.8 2.8 copy-done.39
  356.6 13.9 %attn_bwd.4 = (bf16[3,1024,512]{2,1,0:T(8,128)(2,1)S(1)}, f32[2,512]{1,0:T(2,128)S(1)}) custom-call(bf16[1024,3072]{1,0:T(8,128)(2,1)S(1)} %copy-done.39, bf16[1024,3072]{1,0:T(8,128)(2,1)S(1)} %copy-done.39, bf16[1024,3072]{1,0:T(8,128)(2,1)S(1)} %copy-done.39, bf16[1024,1024]{1,0:T(8,128)(2,1)S(1)} %copy-done.3, ...), custom_call_target="tpu_custom_call" | custom-call | flops 10737418240 | bytes 4194304 | tf_op jit(solution)/shard_map/attn_bwd/pallas_call | solution.py:480
  370.5 3.5 collective-permute-done.39
  379.5 14.1 %attn_bwd.5 = (bf16[3,1024,512]{2,1,0:T(8,128)(2,1)S(1)}, f32[2,512]{1,0:T(2,128)S(1)}) custom-call(bf16[1024,3072]{1,0:T(8,128)(2,1)S(1)} %copy-done.39, bf16[1024,3072]{1,0:T(8,128)(2,1)S(1)} %copy-done.39, bf16[1024,3072]{1,0:T(8,128)(2,1)S(1)} %copy-done.39, bf16[1024,1024]{1,0:T(8,128)(2,1)S(1)} %copy-done.3, ...), custom_call_target="tpu_custom_call", output_to_operand_aliasing={{0}: (8, {}), {1}: (9, {})} | custom-call | flops 10737418240 | bytes 4194304 | tf_op jit(solution)/shard_map/attn_bwd/pallas_call | solution.py:480
  397.3 2.3 collective-permute-done.52
  402.9 5.5 wgrad_qkv_a_sent.1
  408.5 2.8 copy-done.40
  411.3 14.3 %attn_bwd.6 = (bf16[3,1024,512]{2,1,0:T(8,128)(2,1)S(1)}, f32[2,512]{1,0:T(2,128)S(1)}) custom-call(bf16[1024,3072]{1,0:T(8,128)(2,1)S(1)} %copy-done.40, bf16[1024,3072]{1,0:T(8,128)(2,1)S(1)} %copy-done.40, bf16[1024,3072]{1,0:T(8,128)(2,1)S(1)} %copy-done.40, bf16[1024,1024]{1,0:T(8,128)(2,1)S(1)} %copy-done.3, bf16[1024,1024]{1,0:T(8,128)(2,1)S(1)} %copy-done.33, ...), custom_call_target="tpu_custom_call" | custom-call | flops 10737418240 | bytes 4194304 | tf_op jit(solution)/shard_map/attn_bwd/pallas_call | solution.py:480
  428.5 3.1 collective-permute-start.53
  437.0 19.5 %collective-permute-done.54 = bf16[512,256]{1,0:T(8,128)(2,1)S(1)} collective-permute-done((bf16[512,256]{1,0:T(8,128)(2,1)}, bf16[512,256]{1,0:T(8,128)(2,1)S(1)}, u32[]{:S(2)}, u32[]{:S(2)}) %collective-permute-start.54) | collective-permute-done | bytes 262176 | tf_op jit(solution)/shard_map/ppermute | solution.py:529
  461.2 5.7 collective-permute-done.94
  466.9 3.7 collective-permute-done.95
  472.2 7.1 %wgrad_qkv_a_own.1 = (bf16[4,64,384]{2,1,0:T(8,128)(2,1)S(1)}, bf16[4,64,384]{2,1,0:T(8,128)(2,1)S(1)}, bf16[2,4,64,384]{3,2,1,0:T(8,128)(2,1)S(1)}, bf16[4,64,3...) custom-call(s32[3]{0:T(128)S(1)} %pad_add_fusion.where, ...), custom_call_target="tpu_custom_call" | custom-call | flops 1610612736 | bytes 8388608 | tf_op jit(solution)/shard_map/wgrad_qkv_a_own/pallas_call | solution.py:1057
  479.4 2.8 copy-done.41
  482.1 14.0 %attn_bwd.7 = (bf16[3,1024,512]{2,1,0:T(8,128)(2,1)S(1)}, f32[2,512]{1,0:T(2,128)S(1)}) custom-call(bf16[1024,3072]{1,0:T(8,128)(2,1)S(1)} %copy-done.41, bf16[1024,3072]{1,0:T(8,128)(2,1)S(1)} %copy-done.41, bf16[1024,3072]{1,0:T(8,128)(2,1)S(1)} %copy-done.41, bf16[1024,1024]{1,0:T(8,128)(2,1)S(1)} %copy-done.3, ...), custom_call_target="tpu_custom_call", output_to_operand_aliasing={{0}: (8, {}), {1}: (9, {})} | custom-call | flops 10737418240 | bytes 4194304 | tf_op jit(solution)/shard_map/attn_bwd/pallas_call | solution.py:480
  498.0 2.1 collective-permute-start.61
  501.1 3.9 collective-permute-done.61
  514.6 2.4 collective-permute-done.85
  520.8 4.0 collective-permute-done.86
  525.7 5.5 wgrad_qkv_b_sent.1
  538.2 5.4 collective-permute-done.65
  544.7 11.4 %qkv_back.1 = f32[1024,1024]{1,0:T(8,128)} custom-call(bf16[1024,3072]{1,0:T(8,128)(2,1)} %get-tuple-element.144.w_ref, bf16[3,1024,512]{2,1,0:T(8,128)(2,1)S(1)} %get-tuple-element.177.right_ref.refs_0_, bf16[3,1024,512]{2,1,0:T(8,128)(2,1)S(1)} %get-tuple-element.210.right_ref.refs_1_, f32[1024,1024]{1,0:T(8,128)S(1)} %copy-done.35), custom_call_target="tpu_custom_call" | custom-call | flops 6442450944 | bytes 20971520 | tf_op jit(solution)/shard_map/qkv_back/pallas_call | solution.py:666
  557.4 7.3 %wgrad_qkv_b_own.1 = (bf16[4,64,384]{2,1,0:T(8,128)(2,1)S(1)}, bf16[4,64,384]{2,1,0:T(8,128)(2,1)S(1)}, bf16[2,4,64,384]{3,2,1,0:T(8,128)(2,1)S(1)}, bf16[4,64,3...) custom-call(s32[3]{0:T(128)S(1)} %pad_add_fusion.where, ...), custom_call_target="tpu_custom_call" | custom-call | flops 1610612736 | bytes 8388608 | tf_op jit(solution)/shard_map/wgrad_qkv_b_own/pallas_call | solution.py:1057
  566.4 2.0 collective-permute-start.68
  569.6 2.8 collective-permute-done.69
  572.5 4.1 collective-permute-done.68
  584.7 7.1 %collective-permute-done.73 = bf16[2,4,64,384]{3,2,1,0:T(8,128)(2,1)S(1)} collective-permute-done((bf16[2,4,64,384]{3,2,1,0:T(8,128)(2,1)S(1)}, bf16[2,4,64,384]{3,2,1,0:T(8,128)(2,1)S(1)}, u32[]{:S(2)}, u32[]{:S(2)}) %collective-permute-start.73) | collective-permute-done | bytes 393248 | tf_op jit(solution)/shard_map/ppermute | solution.py:529
  594.3 3.3 collective-permute-done.74
  600.6 3.2 collective-permute-start.77
  603.8 2.2 collective-permute-done.79
  606.0 2.3 collective-permute-done.78
  611.9 3.0 collective-permute-done.80
  (450 shorter events, 143.4 us)
Async XLA Ops:
  9.2 11.5 %collective-permute-start.2 = (bf16[144,768]{1,0:T(8,128)(2,1)S(1)}, bf16[144,768]{1,0:T(8,128)(2,1)S(1)}, u32[]{:S(2)}, u32[]{:S(2)}) collective-permute-start(bf16[144,768]{1,0:T(8,128)(2,1)S(1)} %constant_dynamic-update-slice_fusion), channel_id=1, source_target_pairs={{0,6},{1,7},{2,4},{3,5},{4,2},{5,3},{6,0},{7,1},{8,14},{9,15},{10,... | collective-permute-start | bytes 663560 | tf_op jit(solution)/shard_map/ppermute | solution.py:529
  14.4 18.8 %collective-permute-start.1 = (bf16[144,768]{1,0:T(8,128)(2,1)S(1)}, bf16[144,768]{1,0:T(8,128)(2,1)S(1)}, u32[]{:S(2)}, u32[]{:S(2)}) collective-permute-start(bf16[144,768]{1,0:T(8,128)(2,1)S(1)} %constant_dynamic-update-slice_fusion), channel_id=1, source_target_pairs={{0,4},{1,5},{2,6},{3,7},{4,0},{5,1},{6,2},{7,3},{8,12},{9,13},{10,... | collective-permute-start | bytes 663560 | tf_op jit(solution)/shard_map/ppermute | solution.py:529
  14.4 18.8 %collective-permute-start = (bf16[144,768]{1,0:T(8,128)(2,1)S(1)}, bf16[144,768]{1,0:T(8,128)(2,1)S(1)}, u32[]{:S(2)}, u32[]{:S(2)}) collective-permute-start(bf16[144,768]{1,0:T(8,128)(2,1)S(1)} %constant_dynamic-update-slice_fusion), channel_id=1, source_target_pairs={{0,2},{1,3},{2,0},{3,1},{4,6},{5,7},{6,4},{7,5},{8,10},{9,11},{10,... | collective-permute-start | bytes 663560 | tf_op jit(solution)/shard_map/ppermute | solution.py:529
  34.0 42.9 %collective-permute-start.3 = (bf16[4,128,768]{2,1,0:T(8,128)(2,1)S(1)}, bf16[4,128,768]{2,1,0:T(8,128)(2,1)S(1)}, u32[]{:S(2)}, u32[]{:S(2)}) collective-permute-start(bf16[4,128,768]{2,1,0:T(8,128)(2,1)S(1)} %pad_maximum_fusion.4.refs_0_), channel_id=1, source_target_pairs={{0,16},{1,17},{2,18},{3,19},{4,20},{5,21},{6,22},{7,23},{8,24},{9,... | collective-permute-start | bytes 2359304 | tf_op jit(solution)/shard_map/ppermute | solution.py:529
  35.6 40.7 %collective-permute-start.8 = (bf16[4,128,768]{2,1,0:T(8,128)(2,1)S(1)}, bf16[4,128,768]{2,1,0:T(8,128)(2,1)S(1)}, u32[]{:S(2)}, u32[]{:S(2)}) collective-permute-start(bf16[4,128,768]{2,1,0:T(8,128)(2,1)S(1)} %pad_maximum_fusion.4.refs_0_), channel_id=1, source_target_pairs={{0,8},{1,9},{2,10},{3,11},{4,12},{5,13},{6,14},{7,15},{8,0},{9,1},... | collective-permute-start | bytes 2359304 | tf_op jit(solution)/shard_map/ppermute | solution.py:529
  37.1 42.0 %collective-permute-start.11 = (bf16[4,128,768]{2,1,0:T(8,128)(2,1)S(1)}, bf16[4,128,768]{2,1,0:T(8,128)(2,1)}, u32[]{:S(2)}, u32[]{:S(2)}) collective-permute-start(bf16[4,128,768]{2,1,0:T(8,128)(2,1)S(1)} %pad_maximum_fusion.4.refs_0_), channel_id=1, source_target_pairs={{0,1},{1,0},{2,3},{3,2},{4,5},{5,4},{6,7},{7,6},{8,9},{9,8},{10,11... | collective-permute-start | bytes 2359304 | tf_op jit(solution)/shard_map/ppermute | solution.py:529
  37.1 12.7 %collective-permute-start.4 = (bf16[128,1280]{1,0:T(8,128)(2,1)}, bf16[128,1280]{1,0:T(8,128)(2,1)}, u32[]{:S(2)}, u32[]{:S(2)}) collective-permute-start(bf16[128,1280]{1,0:T(8,128)(2,1)} %pad_maximum_fusion.6), channel_id=1, source_target_pairs={{0,6},{1,7},{2,4},{3,5},{4,2},{5,3},{6,0},{7,1},{8,14},{9,15},{10,... | collective-permute-start | bytes 983048 | tf_op jit(solution)/shard_map/ppermute | solution.py:529
  39.6 28.2 %collective-permute-start.18 = (bf16[128,1280]{1,0:T(8,128)(2,1)}, bf16[128,1280]{1,0:T(8,128)(2,1)}, u32[]{:S(2)}, u32[]{:S(2)}) collective-permute-start(bf16[128,1280]{1,0:T(8,128)(2,1)} %pad_maximum_fusion.6), channel_id=1, source_target_pairs={{0,4},{1,5},{2,6},{3,7},{4,0},{5,1},{6,2},{7,3},{8,12},{9,13},{10,... | collective-permute-start | bytes 983048 | tf_op jit(solution)/shard_map/ppermute | solution.py:529
  49.8 24.9 %collective-permute-start.17 = (bf16[128,1280]{1,0:T(8,128)(2,1)}, bf16[128,1280]{1,0:T(8,128)(2,1)}, u32[]{:S(2)}, u32[]{:S(2)}) collective-permute-start(bf16[128,1280]{1,0:T(8,128)(2,1)} %pad_maximum_fusion.6), channel_id=1, source_target_pairs={{0,2},{1,3},{2,0},{3,1},{4,6},{5,7},{6,4},{7,5},{8,10},{9,11},{10,... | collective-permute-start | bytes 983048 | tf_op jit(solution)/shard_map/ppermute | solution.py:529
  76.4 11.1 %collective-permute-start.9 = (bf16[4,64,768]{2,1,0:T(8,128)(2,1)S(1)}, bf16[4,64,768]{2,1,0:T(8,128)(2,1)S(1)}, u32[]{:S(2)}, u32[]{:S(2)}) collective-permute-start(bf16[4,64,768]{2,1,0:T(8,128)(2,1)S(1)} %slice.671), channel_id=1, source_target_pairs={{0,16},{1,17},{2,18},{3,19},{4,20},{5,21},{6,22},{7,23},{8,24},{9,... | collective-permute-start | bytes 1179656 | tf_op jit(solution)/shard_map/ppermute | solution.py:529
  77.0 12.1 %collective-permute-start.10 = (bf16[4,64,768]{2,1,0:T(8,128)(2,1)S(1)}, bf16[4,64,768]{2,1,0:T(8,128)(2,1)S(1)}, u32[]{:S(2)}, u32[]{:S(2)}) collective-permute-start(bf16[4,64,768]{2,1,0:T(8,128)(2,1)S(1)} %slice.672), channel_id=1, source_target_pairs={{0,8},{1,9},{2,10},{3,11},{4,12},{5,13},{6,14},{7,15},{8,0},{9,1},... | collective-permute-start | bytes 1179656 | tf_op jit(solution)/shard_map/ppermute | solution.py:529
  77.6 38.3 %collective-permute-start.19 = (bf16[4,128,1280]{2,1,0:T(8,128)(2,1)S(1)}, bf16[4,128,1280]{2,1,0:T(8,128)(2,1)S(1)}, u32[]{:S(2)}, u32[]{:S(2)}) collective-permute-start(bf16[4,128,1280]{2,1,0:T(8,128)(2,1)S(1)} %pad_maximum_fusion.2.refs_0_), channel_id=1, source_target_pairs={{0,8},{1,9},{2,10},{3,11},{4,12},{5,13},{6,14},{7,15},{8,0},{9,1},... | collective-permute-start | bytes 3932168 | tf_op jit(solution)/shard_map/ppermute | solution.py:529
  79.1 12.9 %collective-permute-start.13 = (bf16[4,128,768]{2,1,0:T(8,128)(2,1)S(1)}, bf16[4,128,768]{2,1,0:T(8,128)(2,1)S(1)}, u32[]{:S(2)}, u32[]{:S(2)}) collective-permute-start(bf16[4,128,768]{2,1,0:T(8,128)(2,1)S(1)} %collective-permute-done.3.refs_2_), channel_id=1, source_target_pairs={{0,1},{1,0},{2,3},{3,2},{4,5},{5,4},{6,7},{7,6},{8,9},{9,8},{10,11... | collective-permute-start | bytes 2359304 | tf_op jit(solution)/shard_map/ppermute | solution.py:529
  89.8 34.3 %collective-permute-start.21 = (bf16[4,128,1280]{2,1,0:T(8,128)(2,1)S(1)}, bf16[4,128,1280]{2,1,0:T(8,128)(2,1)S(1)}, u32[]{:S(2)}, u32[]{:S(2)}) collective-permute-start(bf16[4,128,1280]{2,1,0:T(8,128)(2,1)S(1)} %pad_maximum_fusion.2.refs_0_), channel_id=1, source_target_pairs={{0,16},{1,17},{2,18},{3,19},{4,20},{5,21},{6,22},{7,23},{8,24},{9,... | collective-permute-start | bytes 3932168 | tf_op jit(solution)/shard_map/ppermute | solution.py:529
  115.9 19.1 %collective-permute-start.20 = (bf16[4,64,1280]{2,1,0:T(8,128)(2,1)S(1)}, bf16[4,64,1280]{2,1,0:T(8,128)(2,1)S(1)}, u32[]{:S(2)}, u32[]{:S(2)}) collective-permute-start(bf16[4,64,1280]{2,1,0:T(8,128)(2,1)S(1)} %slice.536), channel_id=1, source_target_pairs={{0,16},{1,17},{2,18},{3,19},{4,20},{5,21},{6,22},{7,23},{8,24},{9,... | collective-permute-start | bytes 1966088 | tf_op jit(solution)/shard_map/ppermute | solution.py:529
  119.6 35.4 %collective-permute-start.7 = (bf16[512,256]{1,0:T(8,128)(2,1)S(1)}, bf16[512,256]{1,0:T(8,128)(2,1)S(1)}, u32[]{:S(2)}, u32[]{:S(2)}) collective-permute-start(bf16[512,256]{1,0:T(8,128)(2,1)S(1)} %copy-done.55), channel_id=1, source_target_pairs={{0,6},{1,7},{2,4},{3,5},{4,2},{5,3},{6,0},{7,1},{8,14},{9,15},{10,... | collective-permute-start | bytes 786440 | tf_op jit(solution)/shard_map/ppermute | solution.py:529
  121.0 34.1 %collective-permute-start.6 = (bf16[512,256]{1,0:T(8,128)(2,1)S(1)}, bf16[512,256]{1,0:T(8,128)(2,1)S(1)}, u32[]{:S(2)}, u32[]{:S(2)}) collective-permute-start(bf16[512,256]{1,0:T(8,128)(2,1)S(1)} %copy-done.55), channel_id=1, source_target_pairs={{0,4},{1,5},{2,6},{3,7},{4,0},{5,1},{6,2},{7,3},{8,12},{9,13},{10,... | collective-permute-start | bytes 786440 | tf_op jit(solution)/shard_map/ppermute | solution.py:529
  121.0 34.7 %collective-permute-start.5 = (bf16[512,256]{1,0:T(8,128)(2,1)S(1)}, bf16[512,256]{1,0:T(8,128)(2,1)S(1)}, u32[]{:S(2)}, u32[]{:S(2)}) collective-permute-start(bf16[512,256]{1,0:T(8,128)(2,1)S(1)} %copy-done.55), channel_id=1, source_target_pairs={{0,2},{1,3},{2,0},{3,1},{4,6},{5,7},{6,4},{7,5},{8,10},{9,11},{10,... | collective-permute-start | bytes 786440 | tf_op jit(solution)/shard_map/ppermute | solution.py:529
  124.0 33.5 %collective-permute-start.25 = (bf16[4,128,1280]{2,1,0:T(8,128)(2,1)S(1)}, bf16[4,128,1280]{2,1,0:T(8,128)(2,1)S(1)}, u32[]{:S(2)}, u32[]{:S(2)}) collective-permute-start(bf16[4,128,1280]{2,1,0:T(8,128)(2,1)S(1)} %pad_maximum_fusion.2.refs_0_), channel_id=1, source_target_pairs={{0,1},{1,0},{2,3},{3,2},{4,5},{5,4},{6,7},{7,6},{8,9},{9,8},{10,11... | collective-permute-start | bytes 3932168 | tf_op jit(solution)/shard_map/ppermute | solution.py:529
  135.0 20.9 %collective-permute-start.22 = (bf16[4,64,1280]{2,1,0:T(8,128)(2,1)S(1)}, bf16[4,64,1280]{2,1,0:T(8,128)(2,1)S(1)}, u32[]{:S(2)}, u32[]{:S(2)}) collective-permute-start(bf16[4,64,1280]{2,1,0:T(8,128)(2,1)S(1)} %slice.537), channel_id=1, source_target_pairs={{0,8},{1,9},{2,10},{3,11},{4,12},{5,13},{6,14},{7,15},{8,0},{9,1},... | collective-permute-start | bytes 1966088 | tf_op jit(solution)/shard_map/ppermute | solution.py:529
  155.1 25.0 %collective-permute-start.26 = (bf16[4,128,1280]{2,1,0:T(8,128)(2,1)S(1)}, bf16[4,128,1280]{2,1,0:T(8,128)(2,1)S(1)}, u32[]{:S(2)}, u32[]{:S(2)}) collective-permute-start(bf16[4,128,1280]{2,1,0:T(8,128)(2,1)S(1)} %collective-permute-done.19.refs_1_), channel_id=1, source_target_pairs={{0,1},{1,0},{2,3},{3,2},{4,5},{5,4},{6,7},{7,6},{8,9},{9,8},{10,11... | collective-permute-start | bytes 3932168 | tf_op jit(solution)/shard_map/ppermute | solution.py:529
  155.7 24.4 %collective-permute-start.27 = (bf16[4,128,1280]{2,1,0:T(8,128)(2,1)S(1)}, bf16[4,128,1280]{2,1,0:T(8,128)(2,1)S(1)}, u32[]{:S(2)}, u32[]{:S(2)}) collective-permute-start(bf16[4,128,1280]{2,1,0:T(8,128)(2,1)S(1)} %collective-permute-done.21.refs_2_), channel_id=1, source_target_pairs={{0,1},{1,0},{2,3},{3,2},{4,5},{5,4},{6,7},{7,6},{8,9},{9,8},{10,11... | collective-permute-start | bytes 3932168 | tf_op jit(solution)/shard_map/ppermute | solution.py:529
  155.9 32.6 %collective-permute-start.23 = (bf16[4,512,256]{2,1,0:T(8,128)(2,1)S(1)}, bf16[4,512,256]{2,1,0:T(8,128)(2,1)S(1)}, u32[]{:S(2)}, u32[]{:S(2)}) collective-permute-start(bf16[4,512,256]{2,1,0:T(8,128)(2,1)S(1)} %pad_maximum_fusion.3.refs_0_), channel_id=1, source_target_pairs={{0,8},{1,9},{2,10},{3,11},{4,12},{5,13},{6,14},{7,15},{8,0},{9,1},... | collective-permute-start | bytes 3145736 | tf_op jit(solution)/shard_map/ppermute | solution.py:529
  157.5 31.2 %collective-permute-start.24 = (bf16[4,512,256]{2,1,0:T(8,128)(2,1)S(1)}, bf16[4,512,256]{2,1,0:T(8,128)(2,1)}, u32[]{:S(2)}, u32[]{:S(2)}) collective-permute-start(bf16[4,512,256]{2,1,0:T(8,128)(2,1)S(1)} %pad_maximum_fusion.3.refs_0_), channel_id=1, source_target_pairs={{0,16},{1,17},{2,18},{3,19},{4,20},{5,21},{6,22},{7,23},{8,24},{9,... | collective-permute-start | bytes 3145736 | tf_op jit(solution)/shard_map/ppermute | solution.py:529
  159.0 21.1 %collective-permute-start.29 = (bf16[4,64,1280]{2,1,0:T(8,128)(2,1)S(1)}, bf16[4,64,1280]{2,1,0:T(8,128)(2,1)S(1)}, u32[]{:S(2)}, u32[]{:S(2)}) collective-permute-start(bf16[4,64,1280]{2,1,0:T(8,128)(2,1)S(1)} %collective-permute-done.22.refs_4_), channel_id=1, source_target_pairs={{0,1},{1,0},{2,3},{3,2},{4,5},{5,4},{6,7},{7,6},{8,9},{9,8},{10,11... | collective-permute-start | bytes 1966088 | tf_op jit(solution)/shard_map/ppermute | solution.py:529
  188.0 25.0 %collective-permute-start.32 = (bf16[4,512,256]{2,1,0:T(8,128)(2,1)S(1)}, bf16[4,512,256]{2,1,0:T(8,128)(2,1)}, u32[]{:S(2)}, u32[]{:S(2)}) collective-permute-start(bf16[4,512,256]{2,1,0:T(8,128)(2,1)S(1)} %pad_maximum_fusion.3.refs_0_), channel_id=1, source_target_pairs={{0,1},{1,0},{2,3},{3,2},{4,5},{5,4},{6,7},{7,6},{8,9},{9,8},{10,11... | collective-permute-start | bytes 3145736 | tf_op jit(solution)/shard_map/ppermute | solution.py:529
  188.6 26.7 %collective-permute-start.33 = (bf16[4,512,256]{2,1,0:T(8,128)(2,1)S(1)}, bf16[4,512,256]{2,1,0:T(8,128)(2,1)}, u32[]{:S(2)}, u32[]{:S(2)}) collective-permute-start(bf16[4,512,256]{2,1,0:T(8,128)(2,1)S(1)} %collective-permute-done.23.refs_1_), channel_id=1, source_target_pairs={{0,1},{1,0},{2,3},{3,2},{4,5},{5,4},{6,7},{7,6},{8,9},{9,8},{10,11... | collective-permute-start | bytes 3145736 | tf_op jit(solution)/shard_map/ppermute | solution.py:529
  189.8 25.5 %collective-permute-start.34 = (bf16[4,512,256]{2,1,0:T(8,128)(2,1)}, bf16[4,512,256]{2,1,0:T(8,128)(2,1)}, u32[]{:S(2)}, u32[]{:S(2)}) collective-permute-start(bf16[4,512,256]{2,1,0:T(8,128)(2,1)} %collective-permute-done.24.refs_2_), channel_id=1, source_target_pairs={{0,1},{1,0},{2,3},{3,2},{4,5},{5,4},{6,7},{7,6},{8,9},{9,8},{10,11... | collective-permute-start | bytes 3145736 | tf_op jit(solution)/shard_map/ppermute | solution.py:529
  190.3 21.9 %collective-permute-start.30 = (bf16[4,256,256]{2,1,0:T(8,128)(2,1)S(1)}, bf16[4,256,256]{2,1,0:T(8,128)(2,1)}, u32[]{:S(2)}, u32[]{:S(2)}) collective-permute-start(bf16[4,256,256]{2,1,0:T(8,128)(2,1)S(1)} %slice.562), channel_id=1, source_target_pairs={{0,16},{1,17},{2,18},{3,19},{4,20},{5,21},{6,22},{7,23},{8,24},{9,... | collective-permute-start | bytes 1572872 | tf_op jit(solution)/shard_map/ppermute | solution.py:529
  190.8 21.4 %collective-permute-start.31 = (bf16[4,256,256]{2,1,0:T(8,128)(2,1)S(1)}, bf16[4,256,256]{2,1,0:T(8,128)(2,1)}, u32[]{:S(2)}, u32[]{:S(2)}) collective-permute-start(bf16[4,256,256]{2,1,0:T(8,128)(2,1)S(1)} %slice.563), channel_id=1, source_target_pairs={{0,8},{1,9},{2,10},{3,11},{4,12},{5,13},{6,14},{7,15},{8,0},{9,1},... | collective-permute-start | bytes 1572872 | tf_op jit(solution)/shard_map/ppermute | solution.py:529
  244.9 16.0 %collective-permute-start.37 = (bf16[4,4,2,256,256]{4,3,2,1,0:T(8,128)(2,1)S(1)}, bf16[4,4,2,256,256]{4,3,2,1,0:T(8,128)(2,1)S(1)}, u32[]{:S(2)}, u32[]{:S(2)}) collective-permute-start(bf16[4,4,2,256,256]{4,3,2,1,0:T(8,128)(2,1)S(1)} %wgrad_out_sent.1), channel_id=1, source_target_pairs={{0,1},{1,0},{2,3},{3,2},{4,5},{5,4},{6,7},{7,6},{8,9},{9,8},{10,11... | collective-permute-start | bytes 12582920 | tf_op jit(solution)/shard_map/ppermute | solution.py:529
  278.7 18.6 %collective-permute-start.38 = (bf16[4,4,2,64,1024]{4,3,2,1,0:T(8,128)(2,1)S(1)}, bf16[4,4,2,64,1024]{4,3,2,1,0:T(8,128)(2,1)S(1)}, u32[]{:S(2)}, u32[]{:S(2)}) collective-permute-start(bf16[4,4,2,64,1024]{4,3,2,1,0:T(8,128)(2,1)S(1)} %wgrad_in_sent.1), channel_id=1, source_target_pairs={{0,1},{1,0},{2,3},{3,2},{4,5},{5,4},{6,7},{7,6},{8,9},{9,8},{10,11... | collective-permute-start | bytes 12582920 | tf_op jit(solution)/shard_map/ppermute | solution.py:529
  279.2 34.2 %collective-permute-start.43 = (bf16[2,4,256,256]{3,2,1,0:T(8,128)(2,1)}, bf16[2,4,256,256]{3,2,1,0:T(8,128)(2,1)S(1)}, u32[]{:S(2)}, u32[]{:S(2)}) collective-permute-start(bf16[2,4,256,256]{3,2,1,0:T(8,128)(2,1)} %get-tuple-element.181), channel_id=1, source_target_pairs={{0,16},{1,17},{2,18},{3,19},{4,20},{5,21},{6,22},{7,23},{8,24},{9,... | collective-permute-start | bytes 3145736 | tf_op jit(solution)/shard_map/ppermute | solution.py:529
  313.3 24.5 %collective-permute-start.41 = (bf16[4,4,2,64,256]{4,3,2,1,0:T(8,128)(2,1)}, bf16[4,4,2,64,256]{4,3,2,1,0:T(8,128)(2,1)S(1)}, u32[]{:S(2)}, u32[]{:S(2)}) collective-permute-start(bf16[4,4,2,64,256]{4,3,2,1,0:T(8,128)(2,1)} %wgrad_attn_sent.1), channel_id=1, source_target_pairs={{0,1},{1,0},{2,3},{3,2},{4,5},{5,4},{6,7},{7,6},{8,9},{9,8},{10,11... | collective-permute-start | bytes 3145736 | tf_op jit(solution)/shard_map/ppermute | solution.py:529
  314.5 15.0 %collective-permute-start.44 = (bf16[4,256,256]{2,1,0:T(8,128)(2,1)}, bf16[4,256,256]{2,1,0:T(8,128)(2,1)}, u32[]{:S(2)}, u32[]{:S(2)}) collective-permute-start(bf16[4,256,256]{2,1,0:T(8,128)(2,1)} %fusion.5), channel_id=1, source_target_pairs={{0,8},{1,9},{2,10},{3,11},{4,12},{5,13},{6,14},{7,15},{8,0},{9,1},... | collective-permute-start | bytes 1572872 | tf_op jit(solution)/shard_map/ppermute | solution.py:529
  316.0 36.1 %collective-permute-start.40 = (bf16[2,4,256,256]{3,2,1,0:T(8,128)(2,1)}, bf16[2,4,256,256]{3,2,1,0:T(8,128)(2,1)}, u32[]{:S(2)}, u32[]{:S(2)}) collective-permute-start(bf16[2,4,256,256]{3,2,1,0:T(8,128)(2,1)} %get-tuple-element.167), channel_id=1, source_target_pairs={{0,8},{1,9},{2,10},{3,11},{4,12},{5,13},{6,14},{7,15},{8,0},{9,1},... | collective-permute-start | bytes 3145736 | tf_op jit(solution)/shard_map/ppermute | solution.py:529
  331.1 42.9 %collective-permute-start.39 = (bf16[2,4,64,1024]{3,2,1,0:T(8,128)(2,1)}, bf16[2,4,64,1024]{3,2,1,0:T(8,128)(2,1)S(1)}, u32[]{:S(2)}, u32[]{:S(2)}) collective-permute-start(bf16[2,4,64,1024]{3,2,1,0:T(8,128)(2,1)} %copy-done.29), channel_id=1, source_target_pairs={{0,8},{1,9},{2,10},{3,11},{4,12},{5,13},{6,14},{7,15},{8,0},{9,1},... | collective-permute-start | bytes 3145736 | tf_op jit(solution)/shard_map/ppermute | solution.py:529
  332.6 44.5 %collective-permute-start.48 = (bf16[2,4,64,1024]{3,2,1,0:T(8,128)(2,1)}, bf16[2,4,64,1024]{3,2,1,0:T(8,128)(2,1)S(1)}, u32[]{:S(2)}, u32[]{:S(2)}) collective-permute-start(bf16[2,4,64,1024]{3,2,1,0:T(8,128)(2,1)} %copy-done.28), channel_id=1, source_target_pairs={{0,16},{1,17},{2,18},{3,19},{4,20},{5,21},{6,22},{7,23},{8,24},{9,... | collective-permute-start | bytes 3145736 | tf_op jit(solution)/shard_map/ppermute | solution.py:529
  353.2 46.5 %collective-permute-start.42 = (bf16[4,256,256]{2,1,0:T(8,128)(2,1)S(1)}, bf16[4,256,256]{2,1,0:T(8,128)(2,1)S(1)}, u32[]{:S(2)}, u32[]{:S(2)}) collective-permute-start(bf16[4,256,256]{2,1,0:T(8,128)(2,1)S(1)} %fusion.11), channel_id=1, source_target_pairs={{0,16},{1,17},{2,18},{3,19},{4,20},{5,21},{6,22},{7,23},{8,24},{9,... | collective-permute-start | bytes 1572872 | tf_op jit(solution)/shard_map/ppermute | solution.py:529
  375.1 50.5 %collective-permute-start.47 = (bf16[4,64,1024]{2,1,0:T(8,128)(2,1)}, bf16[4,64,1024]{2,1,0:T(8,128)(2,1)}, u32[]{:S(2)}, u32[]{:S(2)}) collective-permute-start(bf16[4,64,1024]{2,1,0:T(8,128)(2,1)} %fusion.10), channel_id=1, source_target_pairs={{0,16},{1,17},{2,18},{3,19},{4,20},{5,21},{6,22},{7,23},{8,24},{9,... | collective-permute-start | bytes 1572872 | tf_op jit(solution)/shard_map/ppermute | solution.py:529
  375.7 18.8 %collective-permute-start.45 = (bf16[2,4,64,256]{3,2,1,0:T(8,128)(2,1)S(1)}, bf16[2,4,64,256]{3,2,1,0:T(8,128)(2,1)S(1)}, u32[]{:S(2)}, u32[]{:S(2)}) collective-permute-start(bf16[2,4,64,256]{3,2,1,0:T(8,128)(2,1)S(1)} %get-tuple-element.184), channel_id=1, source_target_pairs={{0,8},{1,9},{2,10},{3,11},{4,12},{5,13},{6,14},{7,15},{8,0},{9,1},... | collective-permute-start | bytes 786440 | tf_op jit(solution)/shard_map/ppermute | solution.py:529
  377.3 51.2 %collective-permute-start.49 = (bf16[4,64,1024]{2,1,0:T(8,128)(2,1)S(1)}, bf16[4,64,1024]{2,1,0:T(8,128)(2,1)}, u32[]{:S(2)}, u32[]{:S(2)}) collective-permute-start(bf16[4,64,1024]{2,1,0:T(8,128)(2,1)S(1)} %fusion), channel_id=1, source_target_pairs={{0,8},{1,9},{2,10},{3,11},{4,12},{5,13},{6,14},{7,15},{8,0},{9,1},... | collective-permute-start | bytes 1572872 | tf_op jit(solution)/shard_map/ppermute | solution.py:529
  378.0 16.5 %collective-permute-start.51 = (bf16[2,4,64,256]{3,2,1,0:T(8,128)(2,1)S(1)}, bf16[2,4,64,256]{3,2,1,0:T(8,128)(2,1)S(1)}, u32[]{:S(2)}, u32[]{:S(2)}) collective-permute-start(bf16[2,4,64,256]{3,2,1,0:T(8,128)(2,1)S(1)} %get-tuple-element.195), channel_id=1, source_target_pairs={{0,16},{1,17},{2,18},{3,19},{4,20},{5,21},{6,22},{7,23},{8,24},{9,... | collective-permute-start | bytes 786440 | tf_op jit(solution)/shard_map/ppermute | solution.py:529
  396.7 36.2 %collective-permute-start.50 = (bf16[4,64,256]{2,1,0:T(8,128)(2,1)}, bf16[4,64,256]{2,1,0:T(8,128)(2,1)}, u32[]{:S(2)}, u32[]{:S(2)}) collective-permute-start(bf16[4,64,256]{2,1,0:T(8,128)(2,1)} %fusion.45), channel_id=1, source_target_pairs={{0,16},{1,17},{2,18},{3,19},{4,20},{5,21},{6,22},{7,23},{8,24},{9,... | collective-permute-start | bytes 393224 | tf_op jit(solution)/shard_map/ppermute | solution.py:529
  408.4 63.9 %collective-permute-start.46 = (bf16[4,4,2,64,384]{4,3,2,1,0:T(8,128)(2,1)S(1)}, bf16[4,4,2,64,384]{4,3,2,1,0:T(8,128)(2,1)S(1)}, u32[]{:S(2)}, u32[]{:S(2)}) collective-permute-start(bf16[4,4,2,64,384]{4,3,2,1,0:T(8,128)(2,1)S(1)} %wgrad_qkv_a_sent.1), channel_id=1, source_target_pairs={{0,1},{1,0},{2,3},{3,2},{4,5},{5,4},{6,7},{7,6},{8,9},{9,8},{10,11... | collective-permute-start | bytes 4718600 | tf_op jit(solution)/shard_map/ppermute | solution.py:529
  425.6 11.3 %collective-permute-start.55 = (bf16[512,256]{1,0:T(8,128)(2,1)}, bf16[512,256]{1,0:T(8,128)(2,1)S(1)}, u32[]{:S(2)}, u32[]{:S(2)}) collective-permute-start(bf16[512,256]{1,0:T(8,128)(2,1)} %get-tuple-element.240), channel_id=1, source_target_pairs={{0,6},{1,7},{2,4},{3,5},{4,2},{5,3},{6,0},{7,1},{8,14},{9,15},{10,... | collective-permute-start | bytes 786440 | tf_op jit(solution)/shard_map/ppermute | solution.py:529
  427.0 29.4 %collective-permute-start.54 = (bf16[512,256]{1,0:T(8,128)(2,1)}, bf16[512,256]{1,0:T(8,128)(2,1)S(1)}, u32[]{:S(2)}, u32[]{:S(2)}) collective-permute-start(bf16[512,256]{1,0:T(8,128)(2,1)} %get-tuple-element.239), channel_id=1, source_target_pairs={{0,4},{1,5},{2,6},{3,7},{4,0},{5,1},{6,2},{7,3},{8,12},{9,13},{10,... | collective-permute-start | bytes 786440 | tf_op jit(solution)/shard_map/ppermute | solution.py:529
  428.5 27.9 %collective-permute-start.53 = (bf16[512,256]{1,0:T(8,128)(2,1)S(1)}, bf16[512,256]{1,0:T(8,128)(2,1)S(1)}, u32[]{:S(2)}, u32[]{:S(2)}) collective-permute-start(bf16[512,256]{1,0:T(8,128)(2,1)S(1)} %copy-done.52), channel_id=1, source_target_pairs={{0,2},{1,3},{2,0},{3,1},{4,6},{5,7},{6,4},{7,5},{8,10},{9,11},{10,... | collective-permute-start | bytes 786440 | tf_op jit(solution)/shard_map/ppermute | solution.py:529
  433.9 73.2 %collective-permute-start.59 = (bf16[128,1024]{1,0:T(8,128)(2,1)}, bf16[128,1024]{1,0:T(8,128)(2,1)S(1)}, u32[]{:S(2)}, u32[]{:S(2)}) collective-permute-start(bf16[128,1024]{1,0:T(8,128)(2,1)} %get-tuple-element.236), channel_id=1, source_target_pairs={{0,6},{1,7},{2,4},{3,5},{4,2},{5,3},{6,0},{7,1},{8,14},{9,15},{10,... | collective-permute-start | bytes 786440 | tf_op jit(solution)/shard_map/ppermute | solution.py:529
  458.1 12.5 %collective-permute-start.95 = (bf16[512,256]{1,0:T(8,128)(2,1)S(1)}, bf16[512,256]{1,0:T(8,128)(2,1)S(1)}, u32[]{:S(2)}, u32[]{:S(2)}) collective-permute-start(bf16[512,256]{1,0:T(8,128)(2,1)S(1)} %add_convert_fusion.1), channel_id=1, source_target_pairs={{0,16},{1,17},{2,18},{3,19},{4,20},{5,21},{6,22},{7,23},{8,24},{9,... | collective-permute-start | bytes 786440 | tf_op jit(solution)/shard_map/ppermute | solution.py:529
  466.9 43.4 %collective-permute-start.58 = (bf16[128,1024]{1,0:T(8,128)(2,1)}, bf16[128,1024]{1,0:T(8,128)(2,1)S(1)}, u32[]{:S(2)}, u32[]{:S(2)}) collective-permute-start(bf16[128,1024]{1,0:T(8,128)(2,1)} %get-tuple-element.235), channel_id=1, source_target_pairs={{0,4},{1,5},{2,6},{3,7},{4,0},{5,1},{6,2},{7,3},{8,12},{9,13},{10,... | collective-permute-start | bytes 786440 | tf_op jit(solution)/shard_map/ppermute | solution.py:529
  470.6 41.7 %collective-permute-start.57 = (bf16[128,1024]{1,0:T(8,128)(2,1)}, bf16[128,1024]{1,0:T(8,128)(2,1)S(1)}, u32[]{:S(2)}, u32[]{:S(2)}) collective-permute-start(bf16[128,1024]{1,0:T(8,128)(2,1)} %get-tuple-element.233), channel_id=1, source_target_pairs={{0,2},{1,3},{2,0},{3,1},{4,6},{5,7},{6,4},{7,5},{8,10},{9,11},{10,... | collective-permute-start | bytes 786440 | tf_op jit(solution)/shard_map/ppermute | solution.py:529
  470.6 27.4 %collective-permute-start.62 = (bf16[128,256]{1,0:T(8,128)(2,1)S(1)}, bf16[128,256]{1,0:T(8,128)(2,1)S(1)}, u32[]{:S(2)}, u32[]{:S(2)}) collective-permute-start(bf16[128,256]{1,0:T(8,128)(2,1)S(1)} %get-tuple-element.262), channel_id=1, source_target_pairs={{0,6},{1,7},{2,4},{3,5},{4,2},{5,3},{6,0},{7,1},{8,14},{9,15},{10,... | collective-permute-start | bytes 196616 | tf_op jit(solution)/shard_map/ppermute | solution.py:529
  505.8 12.8 %collective-permute-start.88 = (bf16[128,256]{1,0:T(8,128)(2,1)S(1)}, bf16[128,256]{1,0:T(8,128)(2,1)S(1)}, u32[]{:S(2)}, u32[]{:S(2)}) collective-permute-start(bf16[128,256]{1,0:T(8,128)(2,1)S(1)} %add_convert_fusion.2), channel_id=1, source_target_pairs={{0,24},{1,25},{2,26},{3,27},{4,28},{5,29},{6,30},{7,31},{8,16},{9,... | collective-permute-start | bytes 196616 | tf_op jit(solution)/shard_map/ppermute | solution.py:529
  507.1 12.2 %collective-permute-start.89 = (bf16[128,256]{1,0:T(8,128)(2,1)S(1)}, bf16[128,256]{1,0:T(8,128)(2,1)S(1)}, u32[]{:S(2)}, u32[]{:S(2)}) collective-permute-start(bf16[128,256]{1,0:T(8,128)(2,1)S(1)} %add_convert_fusion.2), channel_id=1, source_target_pairs={{0,16},{1,17},{2,18},{3,19},{4,20},{5,21},{6,22},{7,23},{8,24},{9,... | collective-permute-start | bytes 196616 | tf_op jit(solution)/shard_map/ppermute | solution.py:529
  509.5 11.1 %collective-permute-start.90 = (bf16[128,256]{1,0:T(8,128)(2,1)S(1)}, bf16[128,256]{1,0:T(8,128)(2,1)S(1)}, u32[]{:S(2)}, u32[]{:S(2)}) collective-permute-start(bf16[128,256]{1,0:T(8,128)(2,1)S(1)} %add_convert_fusion.2), channel_id=1, source_target_pairs={{0,8},{1,9},{2,10},{3,11},{4,12},{5,13},{6,14},{7,15},{8,0},{9,1},... | collective-permute-start | bytes 196616 | tf_op jit(solution)/shard_map/ppermute | solution.py:529
  511.0 14.7 %collective-permute-start.56 = (bf16[2,4,64,384]{3,2,1,0:T(8,128)(2,1)S(1)}, bf16[2,4,64,384]{3,2,1,0:T(8,128)(2,1)S(1)}, u32[]{:S(2)}, u32[]{:S(2)}) collective-permute-start(bf16[2,4,64,384]{3,2,1,0:T(8,128)(2,1)S(1)} %get-tuple-element.204), channel_id=1, source_target_pairs={{0,8},{1,9},{2,10},{3,11},{4,12},{5,13},{6,14},{7,15},{8,0},{9,1},... | collective-permute-start | bytes 1179656 | tf_op jit(solution)/shard_map/ppermute | solution.py:529
  517.1 51.3 %collective-permute-start.91 = (bf16[128,1024]{1,0:T(8,128)(2,1)S(1)}, bf16[128,1024]{1,0:T(8,128)(2,1)S(1)}, u32[]{:S(2)}, u32[]{:S(2)}) collective-permute-start(bf16[128,1024]{1,0:T(8,128)(2,1)S(1)} %add_convert_fusion), channel_id=1, source_target_pairs={{0,24},{1,25},{2,26},{3,27},{4,28},{5,29},{6,30},{7,31},{8,16},{9,... | collective-permute-start | bytes 786440 | tf_op jit(solution)/shard_map/ppermute | solution.py:529
  518.6 50.7 %collective-permute-start.92 = (bf16[128,1024]{1,0:T(8,128)(2,1)S(1)}, bf16[128,1024]{1,0:T(8,128)(2,1)S(1)}, u32[]{:S(2)}, u32[]{:S(2)}) collective-permute-start(bf16[128,1024]{1,0:T(8,128)(2,1)S(1)} %add_convert_fusion), channel_id=1, source_target_pairs={{0,16},{1,17},{2,18},{3,19},{4,20},{5,21},{6,22},{7,23},{8,24},{9,... | collective-permute-start | bytes 786440 | tf_op jit(solution)/shard_map/ppermute | solution.py:529
  519.3 50.0 %collective-permute-start.93 = (bf16[128,1024]{1,0:T(8,128)(2,1)S(1)}, bf16[128,1024]{1,0:T(8,128)(2,1)S(1)}, u32[]{:S(2)}, u32[]{:S(2)}) collective-permute-start(bf16[128,1024]{1,0:T(8,128)(2,1)S(1)} %add_convert_fusion), channel_id=1, source_target_pairs={{0,8},{1,9},{2,10},{3,11},{4,12},{5,13},{6,14},{7,15},{8,0},{9,1},... | collective-permute-start | bytes 786440 | tf_op jit(solution)/shard_map/ppermute | solution.py:529
  531.2 26.2 %collective-permute-start.64 = (bf16[4,4,2,64,384]{4,3,2,1,0:T(8,128)(2,1)S(1)}, bf16[4,4,2,64,384]{4,3,2,1,0:T(8,128)(2,1)S(1)}, u32[]{:S(2)}, u32[]{:S(2)}) collective-permute-start(bf16[4,4,2,64,384]{4,3,2,1,0:T(8,128)(2,1)S(1)} %wgrad_qkv_b_sent.1), channel_id=1, source_target_pairs={{0,1},{1,0},{2,3},{3,2},{4,5},{5,4},{6,7},{7,6},{8,9},{9,8},{10,11... | collective-permute-start | bytes 4718600 | tf_op jit(solution)/shard_map/ppermute | solution.py:529
  532.1 11.5 %collective-permute-start.65 = (bf16[2,4,64,384]{3,2,1,0:T(8,128)(2,1)S(1)}, bf16[2,4,64,384]{3,2,1,0:T(8,128)(2,1)S(1)}, u32[]{:S(2)}, u32[]{:S(2)}) collective-permute-start(bf16[2,4,64,384]{3,2,1,0:T(8,128)(2,1)S(1)} %get-tuple-element.215), channel_id=1, source_target_pairs={{0,16},{1,17},{2,18},{3,19},{4,20},{5,21},{6,22},{7,23},{8,24},{9,... | collective-permute-start | bytes 1179656 | tf_op jit(solution)/shard_map/ppermute | solution.py:529
  543.7 12.4 %collective-permute-start.66 = (bf16[4,64,384]{2,1,0:T(8,128)(2,1)S(1)}, bf16[4,64,384]{2,1,0:T(8,128)(2,1)S(1)}, u32[]{:S(2)}, u32[]{:S(2)}) collective-permute-start(bf16[4,64,384]{2,1,0:T(8,128)(2,1)S(1)} %fusion.18), channel_id=1, source_target_pairs={{0,8},{1,9},{2,10},{3,11},{4,12},{5,13},{6,14},{7,15},{8,0},{9,1},... | collective-permute-start | bytes 589832 | tf_op jit(solution)/shard_map/ppermute | solution.py:529
  582.0 11.4 %collective-permute-start.75 = (bf16[2,4,64,384]{3,2,1,0:T(8,128)(2,1)S(1)}, bf16[2,4,64,384]{3,2,1,0:T(8,128)(2,1)S(1)}, u32[]{:S(2)}, u32[]{:S(2)}) collective-permute-start(bf16[2,4,64,384]{3,2,1,0:T(8,128)(2,1)S(1)} %get-tuple-element.220), channel_id=1, source_target_pairs={{0,16},{1,17},{2,18},{3,19},{4,20},{5,21},{6,22},{7,23},{8,24},{9,... | collective-permute-start | bytes 1179656 | tf_op jit(solution)/shard_map/ppermute | solution.py:529
  (94 other events, 938.5 us)

commit v4 on v3

--- a/solution.py
+++ b/solution.py
@@ -402,7 +402,7 @@
             jax.ShapeDtypeStruct((total, 2, length), jnp.float32),
         ],
         input_output_aliases={} if before is None else {5: 0, 6: 1},
-        compiler_params=params(40),
+        compiler_params=params(60),
         cost_estimate=pl.CostEstimate(
             flops=16 * length * length * pairs * LANES,
             bytes_accessed=8 * length * pairs * LANES,
@@ -500,7 +500,7 @@
             jax.ShapeDtypeStruct((2, size * LANES), jnp.float32),
         ],
         input_output_aliases={} if before is None else {8: 0, 9: 1},
-        compiler_params=params(40),
+        compiler_params=params(60),
         cost_estimate=pl.CostEstimate(
             flops=40 * length * length * pairs * LANES,
             bytes_accessed=16 * length * pairs * LANES,
@@ -515,18 +515,38 @@
         self.groups = groups
         self.shards = shards
         self.chips = shards // 2
-        grp = lax.axis_index("grp")
-        shard = lax.axis_index("shard")
-        self.grp = grp
-        self.shard = shard
-        self.core = shard % 2
-        self.chip = shard // 2
-        self.scalars = jnp.stack([self.core, self.chip, grp]).astype(jnp.int32)
-
-    def swap(self, array, grp=0, chip=0, core=0):
-        mask = grp * self.shards + chip * 2 + core
-        pairs = [(i, i ^ mask) for i in range(self.groups * self.shards)]
+        self.grp = lax.axis_index("grp")
+        self.shard = lax.axis_index("shard")
+        self.core = self.shard % 2
+        self.chip = self.shard // 2
+        self.scalars = jnp.stack([self.core, self.chip, self.grp]).astype(jnp.int32)
+
+    def permute(self, array, mask_of_core):
+        pairs = [(i, i ^ mask_of_core[i % 2]) for i in range(self.groups * self.shards)]
         return lax.ppermute(array, AXES, pairs)
+
+    def swap_core(self, array):
+        return self.permute(array, (1, 1))
+
+    def swap_grp(self, array, step):
+        masks = (self.shards, 2 * self.shards)
+        return self.permute(array, masks if step == 0 else masks[::-1])
+
+    def swap_chip(self, array, step):
+        masks = (2, 4)
+        return self.permute(array, masks if step == 0 else masks[::-1])
+
+    def slot_chip(self, slot):
+        return self.chip ^ turn(slot, self.core)
+
+    def slot_grp(self, slot):
+        return self.grp ^ turn(slot, self.core)
+
+
+def turn(slot, core):
+    if isinstance(slot, int):
+        return slot if slot in (0, 3) else jnp.where(core == 0, slot, 3 - slot)
+    return jnp.where((core == 0) | (slot == 0) | (slot == 3), slot, 3 - slot)
 
 
 def after(value, *others):
@@ -537,35 +557,34 @@
     def __init__(self, place, piece):
         self.place = place
         self.piece = piece
-        self.held = [None] * 5
-        self.crossed = [None] * 5
-
-    def chips(self, *wait):
-        place = self.place
+        self.held = [None] * 3
+        self.crossed = [None] * 3
+
+    def chips_near(self, *wait):
         piece = after(self.piece, *wait) if wait else self.piece
-        along = [piece] + [place.swap(piece, chip=k) for k in range(1, place.chips)]
-        self.along = along
-        self.held[0] = jnp.stack(along)
-        return along[-1]
+        self.pair = jnp.stack([piece, self.place.swap_chip(piece, 0)])
+        return self.pair
+
+    def chips_far(self, *wait):
+        pair = after(self.pair, *wait) if wait else self.pair
+        self.held[0] = jnp.concatenate([self.pair, self.place.swap_chip(pair, 1)])
+        return self.held[0]
 
     def near(self, *wait):
         piece = after(self.held[0], *wait) if wait else self.held[0]
-        self.held[1] = self.place.swap(piece, grp=1)
-        self.held[2] = self.place.swap(piece, grp=2)
+        self.held[1] = self.place.swap_grp(piece, 0)
+        return self.held[1]
+
+    def far(self, *wait):
+        both = jnp.concatenate(self.held[:2])
+        both = after(both, *wait) if wait else both
+        self.held[2] = self.place.swap_grp(both, 1)
         return self.held[2]
-
-    def far(self, *wait):
-        half = self.held[0].shape[1] // 2
-        first = after(self.held[1], *wait) if wait else self.held[1]
-        second = after(self.held[2], *wait) if wait else self.held[2]
-        self.held[3] = self.place.swap(first[:, :half], grp=2)
-        self.held[4] = self.place.swap(second[:, half:], grp=1)
-        return self.held[4]
 
     def cross(self, *which, wait=()):
         for n in which:
             piece = after(self.held[n], *wait) if wait else self.held[n]
-            self.crossed[n] = self.place.swap(piece, core=1)
+            self.crossed[n] = self.place.swap_core(piece)
 
     def pieces(self):
         return self.held + self.crossed
@@ -579,27 +598,24 @@
         self.chips, self.rows = chips, rows
 
 
-def fetch(where, window, refs, whole, sem, groups, by):
-    rows, cols = window.rows, window.cols
-    core, chip, grp = where[0], where[1], where[2]
-    for other_grp in range(groups):
-        for k in range(window.chips):
-            for n, ref in enumerate(refs):
-                other_core, kind = n // 5, n % 5
-                if min(kind, 3) != other_grp:
-                    continue
-                size = rows if kind < 3 else rows // 2
-                col = pl.multiple_of((grp ^ other_grp) * cols, LANES)
-                row = ((chip ^ k) * 2 + (core ^ other_core)) * rows + max(kind - 3, 0) * size
-                slot = {"grp": other_grp, "all": 0}[by]
+def fetch(where, window, refs, whole, sem, by):
+    rows, cols, chips = window.rows, window.cols, window.chips
+    for slot in range(4):
+        for side in range(2):
+            core = where[0] ^ side
+            ref = refs[3 * side + min(slot, 2)]
+            distance = turn(slot, core)
+            col = pl.multiple_of((where[2] ^ distance) * cols, LANES)
+            for k in range(chips):
+                row = ((where[1] ^ turn(k, core)) * 2 + core) * rows
                 pltpu.make_async_copy(
-                    ref.at[k, :, pl.ds(window.start, cols)],
-                    whole.at[pl.ds(pl.multiple_of(row, size), size), pl.ds(col, cols)],
-                    sem.at[slot],
+                    ref.at[k + (chips if slot == 3 else 0), :, pl.ds(window.start, cols)],
+                    whole.at[pl.ds(pl.multiple_of(row, rows), rows), pl.ds(col, cols)],
+                    sem.at[distance if by == "grp" else 0],
                 ).start()
 
 
-def weight_call(place, kernel, window, inputs, in_specs, outs, out_specs, steps, by, name, flops, mb=40):
+def weight_call(place, kernel, window, inputs, in_specs, outs, out_specs, steps, by, name, flops, mb=60):
     cols, groups = window.cols, place.groups
     pieces = window.arrays
     shape = (window.chips * 2 * window.rows, groups * cols)
@@ -613,7 +629,7 @@
 
         @pl.when(step == 0)
         def _():
-            fetch(where, window, taken, weight, sem, groups, by)
+            fetch(where, window, taken, weight, sem, by)
 
         def ready():
             if by == "all":
@@ -661,7 +677,7 @@
     )(place.scalars, *pieces, *inputs)
 
 
-def plain_call(kernel, inputs, in_specs, outs, out_specs, steps, name, flops, mb=40):
+def plain_call(kernel, inputs, in_specs, outs, out_specs, steps, name, flops, mb=60):
     total = sum(math.prod(x.shape) * x.dtype.itemsize for x in list(inputs) + list(outs))
     return pl.pallas_call(
         kernel,
@@ -951,43 +967,37 @@
     )[0]
 
 
-def weight_grad_kernel(where, left_ref, right_ref, *refs, own, rows, groups, split):
-    *refs, kept = refs
+def weight_grad_kernel(where, *refs, own, rows, groups, count, split):
+    lefts, rights, refs = refs[:count], refs[count : 2 * count], refs[2 * count :]
+    outs, kept = refs[:-count], refs[-count:]
     received = None
     if own:
-        received, *outs = refs
-    else:
-        outs = refs
-    core, grp = where[0], where[2]
-    keep = core if own else 1 - core
-    chips = left_ref.shape[1] // (2 * rows)
-    half = rows // 2
+        received, *outs = outs
+    keep = where[0] if own else 1 - where[0]
+    chips = lefts[0].shape[1] // (2 * rows)
 
     @pl.when(pl.program_id(1) == 0)
     def _():
-        lefts = []
-        for k in range(chips):
-            even = left_ref[:, 2 * k * rows : (2 * k + 1) * rows]
-            odd = left_ref[:, (2 * k + 1) * rows : (2 * k + 2) * rows]
-            lefts.append(jnp.where(keep == 0, even, odd))
-        left = lefts[0] if chips == 1 else jnp.concatenate(lefts, 1)
-        kept[...] = left.T
+        for left_ref, kept_ref in zip(lefts, kept):
+            chosen = []
+            for k in range(chips):
+                even = left_ref[:, 2 * k * rows : (2 * k + 1) * rows]
+                odd = left_ref[:, (2 * k + 1) * rows : (2 * k + 2) * rows]
+                chosen.append(jnp.where(keep == 0, even, odd))
+            left = chosen[0] if chips == 1 else jnp.concatenate(chosen, 1)
+            kept_ref[...] = left.T
 
     def emit(slot, part, at):
-        part = part.reshape(chips, 2, half, part.shape[-1])
+        part = part.reshape(chips, rows, part.shape[-1])
         pos = 0 if split else slot
         if own:
-            part = part + received[pos, :, :, :, at].astype(jnp.float32)
-            part = part.astype(jnp.bfloat16)
+            part = (part + received[pos, :, :, at].astype(jnp.float32)).astype(jnp.bfloat16)
 
             def store(slot):
-                for lower in range(2):
-                    near, far = ((1, 2), (2, 1))[lower]
-                    block = part[:, lower]
-                    if slot in (near, 3):
-                        outs[3 * lower + 2][0 if slot == near else 1, :, :, at] = block
-                    else:
-                        outs[3 * lower + (1 if slot == far else 0)][:, :, at] = block
+                if slot in (1, 3):
+                    outs[2][slot // 2, :, :, at] = part
+                else:
+                    outs[slot // 2][:, :, at] = part
 
             if split:
                 for n in range(groups):
@@ -995,79 +1005,93 @@
             else:
                 store(slot)
         else:
-            outs[0][pos, :, :, :, at] = part.astype(jnp.bfloat16)
-
-    if split and len(right_ref.shape) == 3:
-        size = right_ref.shape[2]
-        for n in range(right_ref.shape[0]):
-            emit(0, mxu(kept[...], right_ref[n], NN), slice(n * size, (n + 1) * size))
-    elif split:
-        size = min(512, right_ref.shape[1])
-        for n in range(right_ref.shape[1] // size):
-            at = slice(n * size, (n + 1) * size)
-            emit(0, mxu(kept[...], right_ref[:, at], NN), at)
+            outs[0][pos, :, :, at] = part.astype(jnp.bfloat16)
+
+    if split:
+        at = 0
+        for right_ref, kept_ref in zip(rights, kept):
+            if len(right_ref.shape) == 3:
+                size = right_ref.shape[2]
+                pieces = [right_ref[n] for n in range(right_ref.shape[0])]
+            else:
+                size = min(512, right_ref.shape[1])
+                pieces = [
+                    right_ref[:, n * size : (n + 1) * size]
+                    for n in range(right_ref.shape[1] // size)
+                ]
+            for piece in pieces:
+                emit(0, mxu(kept_ref[...], piece, NN), slice(at, at + size))
+                at += size
     else:
-        cols = right_ref.shape[1] // groups
+        cols = rights[0].shape[1] // groups
         for slot in range(groups):
-            at = pl.multiple_of((grp ^ slot) * cols, LANES)
-            emit(slot, mxu(kept[...], right_ref[:, pl.ds(at, cols)], NN), slice(0, cols))
-
-
-def weight_grad(place, left, right, received, split, name):
-    tokens, height = left.shape
+            start = pl.multiple_of((where[2] ^ turn(slot, keep)) * cols, LANES)
+            emit(slot, mxu(kept[0][...], rights[0][:, pl.ds(start, cols)], NN), slice(0, cols))
+
+
+def weight_grad(place, pairs, received, split, name):
+    tokens, height = pairs[0][0].shape
     groups, chips = place.groups, place.chips
     rows = height // place.shards
-    half = rows // 2
-    parts = right.shape[0] if right.ndim == 3 else 1
-    width = right.shape[-1] * parts
-    cols = width // groups
     own = received is not None
     step_chips = chips if split else max(1, 1024 // (2 * rows))
     steps = chips // step_chips
-    if split:
-        grid = (steps, groups)
-        if parts > 1:
-            right_spec = pl.BlockSpec(
-                (parts, tokens, cols // parts), lambda i, j, s: (0, 0, j ^ s[2])
+    grid = (steps, groups if split else 1)
+
+    def block(j, s):
+        return s[2] ^ turn(j, s[0] if own else 1 - s[0])
+
+    cols = 0
+    right_specs = []
+    for _, right in pairs:
+        size = right.shape[-1] // groups
+        if not split:
+            right_specs.append(pl.BlockSpec(right.shape, lambda i, j, s: (0, 0)))
+        elif right.ndim == 3:
+            right_specs.append(
+                pl.BlockSpec((right.shape[0], tokens, size), lambda i, j, s: (0, 0, block(j, s)))
             )
         else:
-            right_spec = pl.BlockSpec((tokens, cols), lambda i, j, s: (0, j ^ s[2]))
-        passed = pl.BlockSpec((1, step_chips, 2, half, cols), lambda i, j, s: (j, i, 0, 0, 0))
+            right_specs.append(pl.BlockSpec((tokens, size), lambda i, j, s: (0, block(j, s))))
+        cols += size * (right.shape[0] if right.ndim == 3 else 1)
+    left_spec = pl.BlockSpec((tokens, step_chips * 2 * rows), lambda i, j, s: (0, i))
+    if split:
+        passed = pl.BlockSpec((1, step_chips, rows, cols), lambda i, j, s: (j, i, 0, 0))
     else:
-        grid = (steps, 1)
-        right_spec = pl.BlockSpec((tokens, width), lambda i, j, s: (0, 0))
-        passed = pl.BlockSpec((groups, step_chips, 2, half, cols), lambda i, j, s: (0, i, 0, 0, 0))
-    in_specs = [pl.BlockSpec((tokens, step_chips * 2 * rows), lambda i, j, s: (0, i)), right_spec]
-    inputs = [left, right]
+        passed = pl.BlockSpec((groups, step_chips, rows, cols), lambda i, j, s: (0, i, 0, 0))
+    in_specs = [left_spec] * len(pairs) + right_specs
+    inputs = [left for left, _ in pairs] + [right for _, right in pairs]
     if own:
         in_specs.append(passed)
         inputs.append(received)
-        one = pl.BlockSpec((step_chips, half, cols), lambda i, j, s: (i, 0, 0))
-        two = pl.BlockSpec((2, step_chips, half, cols), lambda i, j, s: (0, i, 0, 0))
-        out_specs = [one, one, two] * 2
-        shape = (chips, half, cols)
+        one = pl.BlockSpec((step_chips, rows, cols), lambda i, j, s: (i, 0, 0))
+        two = pl.BlockSpec((2, step_chips, rows, cols), lambda i, j, s: (0, i, 0, 0))
+        out_specs = [one, one, two]
+        shape = (chips, rows, cols)
         out_shape = [
             shaped(shape, jnp.bfloat16),
             shaped(shape, jnp.bfloat16),
             shaped((2, *shape), jnp.bfloat16),
-        ] * 2
+        ]
     else:
         out_specs = passed
-        out_shape = shaped((groups, chips, 2, half, cols), jnp.bfloat16)
+        out_shape = shaped((groups, chips, rows, cols), jnp.bfloat16)
     return pl.pallas_call(
-        functools.partial(weight_grad_kernel, own=own, rows=rows, groups=groups, split=split),
+        functools.partial(
+            weight_grad_kernel, own=own, rows=rows, groups=groups, count=len(pairs), split=split
+        ),
         grid_spec=pltpu.PrefetchScalarGridSpec(
             num_scalar_prefetch=1,
             grid=grid,
             in_specs=in_specs,
             out_specs=out_specs,
-            scratch_shapes=[pltpu.VMEM((step_chips * rows, tokens), jnp.bfloat16)],
+            scratch_shapes=[pltpu.VMEM((step_chips * rows, tokens), jnp.bfloat16)] * len(pairs),
         ),
         out_shape=out_shape,
-        compiler_params=params(40),
+        compiler_params=params(60),
         cost_estimate=pl.CostEstimate(
-            flops=tokens * height * width,
-            bytes_accessed=2 * (tokens * (height + width) + height * width),
+            flops=tokens * height * cols * groups,
+            bytes_accessed=2 * (tokens * (height + cols * groups) + height * cols * groups),
             transcendentals=0,
         ),
         name="wgrad_" + name + ("_own" if own else "_sent"),
@@ -1082,73 +1106,77 @@
 
 
 class Reduction:
-    def __init__(self, place, left, right, split, name, *wait):
+    def __init__(self, place, pairs, split, name, *wait):
         self.place = place
-        left = after(left, *wait) if wait else left
-        self.call = (left, right, split, name)
-        self.sent = weight_grad(place, left, right, None, split, name)
-        self.received = place.swap(self.sent, core=1)
+        if wait:
+            pairs = [(after(pairs[0][0], *wait), pairs[0][1])] + pairs[1:]
+        self.call = (pairs, split, name)
+        self.sent = weight_grad(place, pairs, None, split, name)
+        self.received = place.swap_core(self.sent)
 
     def own(self, *wait):
-        left, right, split, name = self.call
+        pairs, split, name = self.call
         received = after(self.received, *wait) if wait else self.received
-        out = weight_grad(self.place, left, right, received, split, name)
-        self.kept = out
-        self.near = [self.place.swap(out[2], grp=1), self.place.swap(out[5], grp=2)]
-        return out[0]
+        self.own_0, self.own_2, both = weight_grad(self.place, pairs, received, split, name)
+        self.first = self.place.swap_grp(both, 0)
+        return self.own_0
 
     def middle(self, *wait):
-        near = after(self.near[0], *wait) if wait else self.near[0]
-        self.near[0] = near
-        upper = add(self.kept[1], near[1])
-        lower = add(self.kept[4], self.near[1][1])
-        self.far = [self.place.swap(upper, grp=2), self.place.swap(lower, grp=1)]
-        return upper
+        self.first = after(self.first, *wait) if wait else self.first
+        second = add(self.own_2, self.first[1])
+        self.second = self.place.swap_grp(second, 1)
+        return second
 
     def along(self, *wait):
         place = self.place
-        far = after(self.far[0], *wait) if wait else self.far[0]
-        mine = jnp.concatenate(
-            [
-                add(self.kept[0], self.near[0][0], far),
-                add(self.kept[3], self.near[1][0], self.far[1]),
-            ],
-            1,
-        )
-        self.terms = [lax.dynamic_index_in_dim(mine, place.chip, 0, False)]
-        for k in range(1, place.chips):
-            outgoing = lax.dynamic_index_in_dim(mine, place.chip ^ k, 0, False)
-            self.terms.append(place.swap(outgoing, chip=k))
-        return self.terms[0]
+        second = after(self.second, *wait) if wait else self.second
+        mine = add(self.own_0, self.first[0], second)
+        blocks = [
+            lax.dynamic_index_in_dim(mine, place.slot_chip(slot), 0, False) for slot in range(4)
+        ]
+        self.mine = blocks
+        self.first = place.swap_chip(jnp.stack([blocks[1], blocks[3]]), 0)
+        return mine
+
+    def along_far(self, *wait):
+        self.first = after(self.first, *wait) if wait else self.first
+        second = add(self.mine[2], self.first[1])
+        self.second = self.place.swap_chip(second, 1)
+        return second
 
     def share(self, *wait):
-        last = after(self.terms[-1], *wait) if wait else self.terms[-1]
-        share = add(*self.terms[:-1], last)
-        self.blocks = [share] + [self.place.swap(share, grp=k) for k in range(1, self.place.groups)]
-        return share
+        second = after(self.second, *wait) if wait else self.second
+        return add(self.mine[0], self.first[0], second)
+
+
+class Replication:
+    def __init__(self, place, share):
+        self.place = place
+        self.pair = jnp.stack([share, place.swap_grp(share, 0)])
+
+    def far(self, *wait):
+        pair = after(self.pair, *wait) if wait else self.pair
+        self.rest = self.place.swap_grp(pair, 1)
+        return self.rest
 
     def result(self):
-        return in_order(self.place, self.blocks)
-
-
-def in_order(place, blocks):
-    blocks = [b.astype(jnp.float32) for b in blocks]
-    ordered = []
-    for g in range(place.groups):
-        block = blocks[0]
-        for k in range(1, place.groups):
-            block = jnp.where((place.grp ^ k) == g, blocks[k], block)
-        ordered.append(block)
-    return ordered
+        place = self.place
+        slots = [self.pair[0], self.pair[1], self.rest[0], self.rest[1]]
+        ordered = []
+        for g in range(place.groups):
+            block = slots[0]
+            for slot in range(1, place.groups):
+                block = jnp.where(place.slot_grp(slot) == g, slots[slot], block)
+            ordered.append(block.astype(jnp.float32))
+        return ordered
 
 
 def sum_everywhere(place, vector):
-    for how in ({"core": 1}, {"grp": 1}, {"grp": 2}):
-        vector = vector + place.swap(vector, **how)
-    step = 1
-    while step < place.chips:
-        vector = vector + place.swap(vector, chip=step)
-        step *= 2
+    vector = vector + place.swap_core(vector)
+    for step in range(2):
+        vector = vector + place.swap_grp(vector, step)
+    for step in range(2):
+        vector = vector + place.swap_chip(vector, step)
     return vector
 
 
@@ -1198,31 +1226,33 @@
     keep = keep_flag.reshape(length, 1).astype(jnp.float32)
     pairs = width // LANES
 
-    flat = jnp.concatenate(vectors)
+    c1 = Gather(place, w_qkv)
+    wait = c1.chips_near()
+    block = jnp.concatenate([w_in, w_attn_out], 1)
+    flat = jnp.concatenate([after(vectors[0], wait), *vectors[1:]])
     extra = 16
-    flat = jnp.pad(flat, (0, extra * w_qkv.shape[1] - flat.shape[0])).reshape(extra, -1)
-    c1 = Gather(place, jnp.concatenate([w_qkv, flat], 0))
-    c2 = Gather(place, jnp.concatenate([w_in, w_attn_out], 1))
+    flat = jnp.pad(flat, (0, extra * block.shape[1] - flat.shape[0])).reshape(extra, -1)
+    c2 = Gather(place, jnp.concatenate([block, flat], 0))
     c3 = Gather(place, w_out)
-    wait = c1.chips()
-    rider = jnp.stack([p[-extra:] for p in c1.along])
-    c1.held[0] = jnp.stack([p[:-extra] for p in c1.along])
+    c1.chips_far()
     near = c1.near()
-    both = [rider, place.swap(rider, core=1)]
-    wait = c2.chips(wait)
     c1.cross(0)
-    c1.far()
-    c1.cross(1, 2)
-    c2.near(near)
-    c3.chips(near, wait)
-    c1.cross(3, 4)
+    c2.chips_near(c1.held[0])
+    far = c1.far()
+    c2.chips_far(near)
+    rider = c2.held[0][:, -extra:]
+    c2.held[0] = c2.held[0][:, :-extra]
+    both = [rider, place.swap_core(rider)]
+    c1.cross(1)
+    c1.cross(2)
+    c2.near(far)
 
     def owner(shard):
         found = both[0][0]
-        for other in range(1, shards):
-            found = jnp.where(
-                (place.shard ^ other) == shard, both[other % 2][other // 2], found
-            )
+        for side in range(2):
+            for slot in range(4):
+                here = (place.chip ^ turn(slot, place.core ^ side)) * 2 + (place.core ^ side)
+                found = jnp.where(here == shard, both[side][slot], found)
         return found.reshape(-1)
 
     parts = [owner(shard).astype(jnp.float32) for shard in range(shards)]
@@ -1249,23 +1279,30 @@
 
     mixed, full_qkv = project_qkv(place, rows, Window(c1, 0, w_qkv.shape[1]), qkv_bias, qkv_scale)
     c2.far(mixed)
-    c2.cross(0, 1, 2, wait=(mixed,))
-    forward = attention_forward(mixed, seg_col, seg_row, 0, pairs // 2)
-    done = forward[1]
-    c2.cross(3, 4, wait=(done,))
-    c3.near(done, c2.held[3], c2.held[4])
-    contexts, lse = attention_forward(
-        after(mixed, c2.held[3], c2.held[4]), seg_col, seg_row, pairs // 2, pairs // 2, forward
-    )
+    c2.cross(0, 1, wait=(mixed,))
+    c3.chips_near(mixed)
+    quarter = pairs // 4
+    forward = None
+    for n in range(4):
+        gate = ((), (c3.pair,), (c3.held[0],), (c2.held[2],))[n]
+        forward = attention_forward(
+            after(mixed, *gate) if gate else mixed, seg_col, seg_row, n * quarter, quarter, forward
+        )
+        if n == 0:
+            c3.chips_far(forward[1])
+        if n == 2:
+            c2.cross(2, wait=(forward[1],))
+            c3.near(forward[1], c2.held[2])
+    contexts, lse = forward
     normed, scale_one, normed_low, full_attn = project_out(
         place, contexts, Window(c2, w_in.shape[1], w_attn_out.shape[1]), rows, bias_attn, gain_one, shift_one
     )
     c3.far(normed_low)
-    c3.cross(0, 1, 2, wait=(normed_low,))
+    c3.cross(0, 1, wait=(normed_low,))
     hidden, slope, full_in = feed_in(
-        place, after(normed_low, c3.held[1], c3.held[2]), Window(c2, 0, w_in.shape[1]), bias_in
-    )
-    c3.cross(3, 4, wait=(hidden,))
+        place, after(normed_low, c3.held[1]), Window(c2, 0, w_in.shape[1]), bias_in
+    )
+    c3.cross(2, wait=(hidden,))
     layer_out, second_grad, out_low, second_sums, full_out = feed_out(
         place,
         hidden,
@@ -1276,24 +1313,22 @@
         (gain_one, shift_one, bias_out, gain_two, shift_two),
     )
 
-    r_out = Reduction(place, hidden, out_low, False, "out")
+    r_out = Reduction(place, [(hidden, out_low)], False, "out")
     pre_low, bias_in_grad = feed_out_back(after(out_low, r_out.sent), full_out, slope)
     own_out = r_out.own(pre_low)
-    r_in = Reduction(place, normed_low, pre_low, True, "in", own_out)
+    r_in = Reduction(place, [(normed_low, pre_low)], True, "in", own_out)
     first_grad, attn_low, first_sums = feed_in_back(
         after(pre_low, r_in.sent), full_in, second_grad, normed, scale_one, gain_one
     )
-    own_in = r_in.own(first_grad)
-    r_attn = Reduction(place, contexts, attn_low, False, "attn", own_in)
-    context_grad = project_out_back(after(attn_low, r_attn.sent), full_attn)
-    own_attn = r_attn.own(context_grad)
-    quarter = pairs // 4
+    mid_out = r_out.middle(first_grad)
+    own_in = r_in.own(first_grad, mid_out)
+    context_grad = project_out_back(after(attn_low, own_in), full_attn)
 
     def back(start, at, before=None, *wait):
         return attention_backward(
             mixed,
             contexts,
-            after(context_grad, *wait),
+            after(context_grad, *wait) if wait else context_grad,
             seg_col,
             seg_row,
             lse,
@@ -1304,30 +1339,38 @@
             before,
         )
 
-    mid_out = r_out.middle(own_attn)
-    part = back(0, 0, None, mid_out)
-    mid_in = r_in.middle(part[1])
-    low_a, late_a = back(quarter, quarter, part, mid_in)
-    along_out = r_out.along(late_a)
-    mid_attn = r_attn.middle(late_a)
-    r_qkv_a = Reduction(place, rows, low_a, True, "qkv_a", along_out, mid_attn)
-    part = back(2 * quarter, 0, None, r_qkv_a.sent)
-    along_in = r_in.along(part[1])
-    along_attn = r_attn.along(part[1])
+    part = back(0, 0)
+    along = r_out.along(part[1])
+    low_a, late_a = back(quarter, quarter, part, along)
+    mid_in = r_in.middle(late_a)
+    along = r_out.along_far(late_a)
+    r_a = Reduction(place, [(contexts, attn_low), (rows, low_a)], True, "a", mid_in, along)
+    part = back(2 * quarter, 0, None, r_a.sent)
+    along = r_in.along(part[1])
     share_out = r_out.share(part[1])
-    own_a = r_qkv_a.own(part[1], along_in, along_attn, share_out)
+    own_a = r_a.own(along, share_out)
     low_b, late_b = back(3 * quarter, quarter, part, own_a)
-    mid_a = r_qkv_a.middle(late_b)
-    share_in = r_in.share(late_b)
-    share_attn = r_attn.share(late_b)
-    r_qkv_b = Reduction(place, rows, low_b, True, "qkv_b", mid_a, share_in, share_attn)
-    input_grad = project_qkv_back((low_a, after(low_b, r_qkv_b.sent)), full_qkv, first_grad)
-    own_b = r_qkv_b.own(input_grad)
-    r_qkv_a.along(own_b)
-    r_qkv_b.middle()
-    r_qkv_a.share()
-    r_qkv_b.along()
-    r_qkv_b.share()
+    mid_a = r_a.middle(late_b)
+    along = r_in.along_far(late_b)
+    r_b = Reduction(place, [(rows, low_b)], True, "b", mid_a, along)
+    along = r_a.along(r_b.sent)
+    share_in = r_in.share(r_b.sent)
+    inner = share_in.shape[1] // groups
+    joined = jnp.concatenate(
+        [share_out] + [share_in[:, n * inner : (n + 1) * inner] for n in range(groups)]
+    )
+    all_ffn = Replication(place, joined)
+    own_b = r_b.own(along, share_in)
+    input_grad = project_qkv_back((low_a, after(low_b, own_b)), full_qkv, first_grad)
+    r_b.middle(input_grad)
+    all_ffn.far(input_grad)
+    r_a.along_far(input_grad)
+    r_b.along()
+    all_a = Replication(place, r_a.share())
+    r_b.along_far()
+    all_a.far()
+    all_b = Replication(place, r_b.share())
+    all_b.far()
 
     sums = (
         jnp.concatenate([late_a[0], late_b[0]]),
@@ -1347,8 +1390,11 @@
         vectors.append(own_part(place, summed[at : at + vector.shape[0]]))
         at += vector.shape[0]
 
-    parts_a, parts_b = r_qkv_a.result(), r_qkv_b.result()
-    heads = parts_a[0].shape[1] // 3
+    parts_a, parts_b = all_a.result(), all_b.result()
+    heads = parts_b[0].shape[1] // 3
+    skip = parts_a[0].shape[1] - 3 * heads
+    w_attn_grad = jnp.concatenate([block[:, :skip] for block in parts_a], 1)
+    parts_a = [block[:, skip:] for block in parts_a]
     w_qkv_grad = jnp.concatenate(
         [
             block[:, n * heads : (n + 1) * heads]
@@ -1358,19 +1404,31 @@
         ],
         1,
     )
+    parts = all_ffn.result()
+    height = share_out.shape[0]
+    w_out_grad = jnp.concatenate([block[:height] for block in parts], 1)
+    size = share_in.shape[0]
+    w_in_grad = jnp.concatenate(
+        [
+            block[height + n * size : height + (n + 1) * size]
+            for block in parts
+            for n in range(groups)
+        ],
+        1,
+    )
     return (
         layer_out[None],
         input_grad[None],
         w_qkv_grad,
         vectors[0],
         vectors[1],
-        jnp.concatenate(r_attn.result(), 1),
+        w_attn_grad,
         vectors[2],
         vectors[3],
         vectors[4],
-        jnp.concatenate(r_in.result(), 1),
+        w_in_grad,
         vectors[5],
-        jnp.concatenate(r_out.result(), 1),
+        w_out_grad,
         vectors[6],
         vectors[7],
         vectors[8],

time: 628 us -> 576 us (0.917)
  Pallas kernels: 258 us -> 308 us
  starting transfers between devices: 102 us -> 53 us
  waiting for transfers between devices: 171 us -> 125 us
    ppermute x97 -> x53, starting transfers between devices: 102 us -> 53 us  [permute(): return lax.ppermute(array, AXES, pairs)]
    ppermute x97 -> x53, waiting for transfers between devices: 171 us -> 125 us  [permute(): return lax.ppermute(array, AXES, pairs)]
    pallas_call x10 -> x8, Pallas kernels: 64.5 us -> 88 us  [weight_grad(): pl.pallas_call(functools.partial(weight_grad_kernel, own=own, rows=rows,...]
    unnamed x178 -> x153, local copies, waits for them, and re-layouts: 43.5 us -> 31.2 us
    pallas_call x4, Pallas kernels: 56.2 us -> 63.7 us  [attention_backward(): pl.pallas_call(body, grid=(pairs,), in_specs=[pair(0), pair(1), pair(2),...]
    pallas_call x4, Pallas kernels: 43.5 us -> 50.8 us  [plain_call(): pl.pallas_call(kernel, grid=(steps,), in_specs=in_specs, out_specs=out_sp...]
    concatenate x4 -> x9, other arithmetic: 5.76 us -> 12.7 us  [the longest x3 7.07 us: far(): both = jnp.concatenate(self.held[:2])]
    pallas_call x2 -> x4, Pallas kernels: 33.5 us -> 39.6 us  [attention_forward(): pl.pallas_call(body, grid=(pairs,), in_specs=[pair(0), pair(1), pair(2),...]
  transfers between devices with their start and end apart: 97 -> 53, of which waited for: 36 -> 26; matrix products, arithmetic and copies ran while one was open for 7% -> 12% of each run, Pallas kernels for 34% -> 39%
where the time goes in v4:
time: 576 us; the launch traced here: 566 us
  Pallas kernels  308 us (53%)
  waiting for transfers between devices  125 us (22%)
  starting transfers between devices  53 us (9%)
  local copies, waits for them, and re-layouts  47.4 us (8%)
  other arithmetic  30.4 us (5%)
    ppermute x53, waiting for transfers between devices, permute(): return lax.ppermute(array, AXES, pairs)  125 us
    pallas_call x8, Pallas kernels, weight_grad(): pl.pallas_call(functools.partial(weight_grad_kernel, own=own, rows=rows,...  88 us
    pallas_call x4, Pallas kernels, weight_call(): pl.pallas_call(body, grid_spec=pltpu.PrefetchScalarGridSpec(num_scalar_pr...  66 us
    pallas_call x4, Pallas kernels, attention_backward(): pl.pallas_call(body, grid=(pairs,), in_specs=[pair(0), pair(1), pair(2),...  63.7 us
    ppermute x53, starting transfers between devices, permute(): return lax.ppermute(array, AXES, pairs)  53 us
    pallas_call x4, Pallas kernels, plain_call(): pl.pallas_call(kernel, grid=(steps,), in_specs=in_specs, out_specs=out_sp...  50.8 us
    pallas_call x4, Pallas kernels, attention_forward(): pl.pallas_call(body, grid=(pairs,), in_specs=[pair(0), pair(1), pair(2),...  39.6 us
    unnamed x153, local copies, waits for them, and re-layouts  31.2 us
  transfers between devices with their start and end apart: 53, of which 26 were waited for; matrix products, arithmetic and copies ran while one was open for 12% of the time, Pallas kernels for 39%

profile of v4, /device:TPU:0, one launch (start us, length us, event | category | flops | bytes accessed | tf_op | source)
XLA Modules:
  0.0 566.1 jit_solution(664588391537985976)
XLA Ops:
  0.7 3.1 collective-permute-start
  3.8 5.6 collective-permute-done
  10.3 2.5 collective-permute-start.1
  21.6 1.9 pad_maximum_fusion.8.refs_0_
  23.5 2.3 collective-permute-start.2
  25.8 1.9 collective-permute-start.7
  27.8 9.5 %collective-permute-done.7 = bf16[144,1280]{1,0:T(8,128)(2,1)S(1)} collective-permute-done((bf16[144,1280]{1,0:T(8,128)(2,1)S(1)}, bf16[144,1280]{1,0:T(8,128)(2,1)S(1)}, u32[]{:S(2)}, u32[]{:S(2)}) %collective-permute-start.7) | collective-permute-done | bytes 368672 | tf_op jit(solution)/shard_map/ppermute | solution.py:526
  37.3 1.8 collective-permute-start.8
  39.9 2.4 pad_maximum_fusion.3
  42.4 2.5 collective-permute-start.3
  44.9 12.8 %collective-permute-done.8 = bf16[2,144,1280]{2,1,0:T(8,128)(2,1)S(1)} collective-permute-done((bf16[2,144,1280]{2,1,0:T(8,128)(2,1)S(1)}, bf16[2,144,1280]{2,1,0:T(8,128)(2,1)S(1)}, u32[]{:S(2)}, u32[]{:S(2)}) %collective-permute-start.8) | collective-permute-done | bytes 737312 | tf_op jit(solution)/shard_map/ppermute | solution.py:526
  73.8 11.4 %collective-permute-done.12.refs_1_ = bf16[4,128,1280]{2,1,0:T(8,128)(2,1)S(1)} collective-permute-done((bf16[4,128,1280]{2,1,0:T(8,128)(2,1)S(1)}, bf16[4,128,1280]{2,1,0:T(8,128)(2,1)S(1)}, u32[]{:S(2)}, u32[]{:S(2)}) %collective-permute-start.12) | collective-permute-done | bytes 1310752 | tf_op jit(solution)/shard_map/ppermute | solution.py:526
  85.1 1.9 pad_maximum_fusion
  88.2 12.9 %qkv.1 = (bf16[1024,3072]{1,0:T(8,128)(2,1)}, bf16[1024,3072]{1,0:T(8,128)(2,1)}) custom-call(s32[3]{0:T(128)} %pad_add_fusion.where, bf16[4,128,768]{2,1,0:T(8,128)(2,1)} %pad_maximum_fusion.8.refs_0_, bf16[4,128,768]{2,1,0:T(8,128)(2,1)} %collective-permute-done.2.refs_1_, bf16[8,128,768]{2,1,0:T(8,128)(2,1)} %collective-permute-done.3.refs_2_, ...), custom_call_target="tpu_custom_call" | custom-call | flops 6442450944 | bytes 20996096 | tf_op jit(solution)/shard_map/qkv/pallas_call | solution.py:658
  104.9 9.8 %attn_fwd.4 = (bf16[1024,1024]{1,0:T(8,128)(2,1)}, f32[8,2,1024]{2,1,0:T(2,128)}) custom-call(bf16[1024,3072]{1,0:T(8,128)(2,1)} %get-tuple-element.127.q_ref.k_ref.v_ref.refs_0_.refs_1_.refs_2_, bf16[1024,3072]{1,0:T(8,128)(2,1)} %get-tuple-element.127.q_ref.k_ref.v_ref.refs_0_.refs_1_.refs_2_, ...), custom_call_target="tpu_custom_call" | custom-call | flops 4294967296 | bytes 2097152 | tf_op jit(solution)/shard_map/attn_fwd/pallas_call | solution.py:385
  115.6 3.4 collective-permute-start.11
  118.9 10.0 %attn_fwd.5 = (bf16[1024,1024]{1,0:T(8,128)(2,1)}, f32[8,2,1024]{2,1,0:T(2,128)}) custom-call(bf16[1024,3072]{1,0:T(8,128)(2,1)} %get-tuple-element.127.q_ref.k_ref.v_ref.refs_0_.refs_1_.refs_2_, bf16[1024,3072]{1,0:T(8,128)(2,1)} %get-tuple-element.127.q_ref.k_ref.v_ref.refs_0_.refs_1_.refs_2_, ...), custom_call_target="tpu_custom_call", output_to_operand_aliasing={{0}: (5, {}), {1}: (6, {})} | custom-call | flops 4294967296 | bytes 2097152 | tf_op jit(solution)/shard_map/attn_fwd/pallas_call | solution.py:385
  128.9 2.9 collective-permute-done.11
  132.9 9.8 %attn_fwd.6 = (bf16[1024,1024]{1,0:T(8,128)(2,1)}, f32[8,2,1024]{2,1,0:T(2,128)}) custom-call(bf16[1024,3072]{1,0:T(8,128)(2,1)} %get-tuple-element.127.q_ref.k_ref.v_ref.refs_0_.refs_1_.refs_2_, bf16[1024,3072]{1,0:T(8,128)(2,1)} %get-tuple-element.127.q_ref.k_ref.v_ref.refs_0_.refs_1_.refs_2_, ...), custom_call_target="tpu_custom_call", output_to_operand_aliasing={{0}: (5, {}), {1}: (6, {})} | custom-call | flops 4294967296 | bytes 2097152 | tf_op jit(solution)/shard_map/attn_fwd/pallas_call | solution.py:385
  145.1 10.1 %attn_fwd.7 = (bf16[1024,1024]{1,0:T(8,128)(2,1)}, f32[8,2,1024]{2,1,0:T(2,128)}) custom-call(bf16[1024,3072]{1,0:T(8,128)(2,1)} %get-tuple-element.127.q_ref.k_ref.v_ref.refs_0_.refs_1_.refs_2_, bf16[1024,3072]{1,0:T(8,128)(2,1)} %get-tuple-element.127.q_ref.k_ref.v_ref.refs_0_.refs_1_.refs_2_, ...), custom_call_target="tpu_custom_call", output_to_operand_aliasing={{0}: (5, {}), {1}: (6, {})} | custom-call | flops 4294967296 | bytes 2097152 | tf_op jit(solution)/shard_map/attn_fwd/pallas_call | solution.py:385
  155.2 3.4 collective-permute-done.14.refs_1_
  158.6 2.7 pad_maximum_fusion.1
  161.3 9.8 %attn_out.1 = (f32[1024,1024]{1,0:T(8,128)}, f32[1024,128]{1,0:T(8,128)}, bf16[1024,1024]{1,0:T(8,128)(2,1)}, bf16[1024,1024]{1,0:T(8,128)(2,1)}) custom-call(s32[3]{0:T(128)} %pad_add_fusion.where, bf16[4,128,1280]{2,1,0:T(8,128)(2,1)} %copy-done, bf16[4,128,1280]{2,1,0:T(8,128)(2,1)} %copy-done.1, bf16[8,128,1280]{2,1,0:T(8,128)(2,1)} %collective-permute-done.13.refs_2_, ...), custom_call_target="tpu_custom_call" | custom-call | flops 2147483648 | bytes 15216640 | tf_op jit(solution)/shard_map/attn_out/pallas_call | solution.py:658
  174.1 22.1 %feed_in.1 = (bf16[1024,4096]{1,0:T(8,128)(2,1)}, bf16[1024,4096]{1,0:T(8,128)(2,1)}, bf16[1024,4096]{1,0:T(8,128)(2,1)}) custom-call(s32[3]{0:T(128)} %pad_add_fusion.where, bf16[4,128,1280]{2,1,0:T(8,128)(2,1)} %copy-done, bf16[4,128,1280]{2,1,0:T(8,128)(2,1)} %copy-done.1, bf16[8,128,1280]{2,1,0:T(8,128)(2,1)} %collective-permute-done.13.refs_2_, ...), custom_call_target="tpu_custom_call" | custom-call | flops 8589934592 | bytes 35667968 | tf_op jit(solution)/shard_map/feed_in/pallas_call | solution.py:658
  198.9 5.2 collective-permute-done.19.refs_3_
  205.1 21.1 %feed_out.1 = (bf16[1024,1024]{1,0:T(8,128)(2,1)}, f32[1024,1024]{1,0:T(8,128)}, bf16[1024,1024]{1,0:T(8,128)(2,1)}, f32[8,1024]{1,0:T(8,128)}, bf16[4096,1024]{1,0:T(8,128)(2,1)}) custom-call(s32[3]{0:T(128)} %pad_add_fusion.where, bf16[4,512,256]{2,1,0:T(8,128)(2,1)} %pad_maximum_fusion.6.refs_0_, bf16[4,512,256]{2,1,0:T(8,128)(2,1)} %collective-permute-done.14.refs_1_, ...), custom_call_target="tpu_custom_call" | custom-call | flops 8589934592 | bytes 39903232 | tf_op jit(solution)/shard_map/feed_out/pallas_call | solution.py:658
  226.3 10.0 %wgrad_out_sent.1 = bf16[4,4,512,256]{3,2,1,0:T(8,128)(2,1)} custom-call(s32[3]{0:T(128)} %pad_add_fusion.where, bf16[1024,4096]{1,0:T(8,128)(2,1)} %get-tuple-element.135.refs_6_.refs_0_, bf16[1024,1024]{1,0:T(8,128)(2,1)} %get-tuple-element.141.refs_1_.g_ref), custom_call_target="tpu_custom_call" | custom-call | flops 4294967296 | bytes 18874368 | tf_op jit(solution)/shard_map/wgrad_out_sent/pallas_call | solution.py:1079
  236.7 14.6 %feed_out_back.1 = (bf16[1024,4096]{1,0:T(8,128)(2,1)}, f32[1,4096]{1,0:T(1,128)}) custom-call(bf16[1024,1024]{1,0:T(8,128)(2,1)} %get-tuple-element.141.refs_1_.g_ref, bf16[4096,1024]{1,0:T(8,128)(2,1)} %get-tuple-element.142.w_ref, bf16[1024,4096]{1,0:T(8,128)(2,1)} %get-tuple-element.143.slope_ref), custom_call_target="tpu_custom_call" | custom-call | flops 8589934592 | bytes 27279360 | tf_op jit(solution)/shard_map/feed_out_back/pallas_call | solution.py:682
  251.3 10.9 %wgrad_out_own.1 = (bf16[4,512,256]{2,1,0:T(8,128)(2,1)}, bf16[4,512,256]{2,1,0:T(8,128)(2,1)}, bf16[2,4,512,256]{3,2,1,0:T(8,128)(2,1)}) custom-call(s32[3]{0:T(128)} %pad_add_fusion.where, bf16[1024,4096]{1,0:T(8,128)(2,1)} %get-tuple-element.135.refs_6_.refs_0_, bf16[1024,1024]{1,0:T(8,128)(2,1)} %get-tuple-element.141.refs_1_.g_ref, ...), custom_call_target="tpu_custom_call" | custom-call | flops 4294967296 | bytes 18874368 | tf_op jit(solution)/shard_map/wgrad_out_own/pallas_call | solution.py:1079
  262.2 10.2 %wgrad_in_sent.1 = bf16[4,4,128,1024]{3,2,1,0:T(8,128)(2,1)} custom-call(s32[3]{0:T(128)} %pad_add_fusion.where, bf16[1024,1024]{1,0:T(8,128)(2,1)} %get-tuple-element.147.refs_6_.refs_0_, bf16[1024,4096]{1,0:T(8,128)(2,1)} %get-tuple-element.148.refs_1_.p_ref), custom_call_target="tpu_custom_call" | custom-call | flops 4294967296 | bytes 18874368 | tf_op jit(solution)/shard_map/wgrad_in_sent/pallas_call | solution.py:1079
  272.8 17.7 %feed_in_back.1 = (f32[1024,1024]{1,0:T(8,128)}, bf16[1024,1024]{1,0:T(8,128)(2,1)}, f32[8,1024]{1,0:T(8,128)}) custom-call(bf16[1024,4096]{1,0:T(8,128)(2,1)} %get-tuple-element.148.refs_1_.p_ref, bf16[1024,4096]{1,0:T(8,128)(2,1)} %get-tuple-element.149.w_ref, f32[1024,1024]{1,0:T(8,128)} %get-tuple-element.150.g_ref, ...), custom_call_target="tpu_custom_call" | custom-call | flops 8589934592 | bytes 32018432 | tf_op jit(solution)/shard_map/feed_in_back/pallas_call | solution.py:682
  290.5 8.3 %collective-permute-done.24 = bf16[2,4,512,256]{3,2,1,0:T(8,128)(2,1)S(1)} collective-permute-done((bf16[2,4,512,256]{3,2,1,0:T(8,128)(2,1)}, bf16[2,4,512,256]{3,2,1,0:T(8,128)(2,1)S(1)}, u32[]{:S(2)}, u32[]{:S(2)}) %collective-permute-start.24) | collective-permute-done | bytes 2097184 | tf_op jit(solution)/shard_map/ppermute | solution.py:526
  301.1 12.4 %wgrad_in_own.1 = (bf16[4,128,1024]{2,1,0:T(8,128)(2,1)}, bf16[4,128,1024]{2,1,0:T(8,128)(2,1)}, bf16[2,4,128,1024]{3,2,1,0:T(8,128)(2,1)}) custom-call(s32[3]{0:T(128)} %pad_add_fusion.where, bf16[1024,1024]{1,0:T(8,128)(2,1)} %get-tuple-element.147.refs_6_.refs_0_, bf16[1024,4096]{1,0:T(8,128)(2,1)} %get-tuple-element.148.refs_1_.p_ref, ...), custom_call_target="tpu_custom_call" | custom-call | flops 4294967296 | bytes 18874368 | tf_op jit(solution)/shard_map/wgrad_in_own/pallas_call | solution.py:1079
  313.8 6.1 %attn_out_back.1.refs_4_ = bf16[1024,1024]{1,0:T(8,128)(2,1)} custom-call(bf16[1024,1024]{1,0:T(8,128)(2,1)} %get-tuple-element.159.g_ref.refs_2_, bf16[1024,1024]{1,0:T(8,128)(2,1)} %get-tuple-element.160.w_ref), custom_call_target="tpu_custom_call" | custom-call | flops 2147483648 | bytes 6291456 | tf_op jit(solution)/shard_map/attn_out_back/pallas_call | solution.py:682
  319.9 15.9 %attn_bwd.4 = (bf16[3,1024,512]{2,1,0:T(8,128)(2,1)}, f32[2,512]{1,0:T(2,128)}) custom-call(bf16[1024,3072]{1,0:T(8,128)(2,1)} %get-tuple-element.127.q_ref.k_ref.v_ref.refs_0_.refs_1_.refs_2_, bf16[1024,3072]{1,0:T(8,128)(2,1)} %get-tuple-element.127.q_ref.k_ref.v_ref.refs_0_.refs_1_.refs_2_, ...), custom_call_target="tpu_custom_call" | custom-call | flops 10737418240 | bytes 4194304 | tf_op jit(solution)/shard_map/attn_bwd/pallas_call | solution.py:480
  335.9 1.6 fusion.4
  337.8 15.9 %attn_bwd.5 = (bf16[3,1024,512]{2,1,0:T(8,128)(2,1)}, f32[2,512]{1,0:T(2,128)}) custom-call(bf16[1024,3072]{1,0:T(8,128)(2,1)} %get-tuple-element.127.q_ref.k_ref.v_ref.refs_0_.refs_1_.refs_2_, bf16[1024,3072]{1,0:T(8,128)(2,1)} %get-tuple-element.127.q_ref.k_ref.v_ref.refs_0_.refs_1_.refs_2_, ...), custom_call_target="tpu_custom_call", output_to_operand_aliasing={{0}: (8, {}), {1}: (9, {})} | custom-call | flops 10737418240 | bytes 4194304 | tf_op jit(solution)/shard_map/attn_bwd/pallas_call | solution.py:480
  353.9 1.6 fusion.2
  355.5 10.4 %wgrad_a_sent.1 = bf16[4,4,128,640]{3,2,1,0:T(8,128)(2,1)} custom-call(s32[3]{0:T(128)} %pad_add_fusion.where, bf16[1024,1024]{1,0:T(8,128)(2,1)} %get-tuple-element.172.refs_6_.refs_3_.refs_0_, bf16[1024,1024]{1,0:T(8,128)(2,1)} %bitcast.176, bf16[1024,1024]{1,0:T(8,128)(2,1)} %get-tuple-element.159.g_ref.refs_2_, ...), custom_call_target="tpu_custom_call" | custom-call | flops 2684354560 | bytes 12582912 | tf_op jit(solution)/shard_map/wgrad_a_sent/pallas_call | solution.py:1079
  370.9 2.7 collective-permute-start.30
  374.8 16.1 %attn_bwd.6 = (bf16[3,1024,512]{2,1,0:T(8,128)(2,1)}, f32[2,512]{1,0:T(2,128)}) custom-call(bf16[1024,3072]{1,0:T(8,128)(2,1)} %get-tuple-element.127.q_ref.k_ref.v_ref.refs_0_.refs_1_.refs_2_, bf16[1024,3072]{1,0:T(8,128)(2,1)} %get-tuple-element.127.q_ref.k_ref.v_ref.refs_0_.refs_1_.refs_2_, ...), custom_call_target="tpu_custom_call" | custom-call | flops 10737418240 | bytes 4194304 | tf_op jit(solution)/shard_map/attn_bwd/pallas_call | solution.py:480
  391.0 2.5 fusion.1
  394.1 15.9 %wgrad_a_own.1 = (bf16[4,128,640]{2,1,0:T(8,128)(2,1)}, bf16[4,128,640]{2,1,0:T(8,128)(2,1)}, bf16[2,4,128,640]{3,2,1,0:T(8,128)(2,1)}) custom-call(s32[3]{0:T(128)} %pad_add_fusion.where, bf16[1024,1024]{1,0:T(8,128)(2,1)} %get-tuple-element.172.refs_6_.refs_3_.refs_0_, bf16[1024,1024]{1,0:T(8,128)(2,1)} %bitcast.177, ...), custom_call_target="tpu_custom_call" | custom-call | flops 2684354560 | bytes 12582912 | tf_op jit(solution)/shard_map/wgrad_a_own/pallas_call | solution.py:1079
  411.4 15.8 %attn_bwd.7 = (bf16[3,1024,512]{2,1,0:T(8,128)(2,1)}, f32[2,512]{1,0:T(2,128)}) custom-call(bf16[1024,3072]{1,0:T(8,128)(2,1)} %get-tuple-element.127.q_ref.k_ref.v_ref.refs_0_.refs_1_.refs_2_, bf16[1024,3072]{1,0:T(8,128)(2,1)} %get-tuple-element.127.q_ref.k_ref.v_ref.refs_0_.refs_1_.refs_2_, ...), custom_call_target="tpu_custom_call", output_to_operand_aliasing={{0}: (8, {}), {1}: (9, {})} | custom-call | flops 10737418240 | bytes 4194304 | tf_op jit(solution)/shard_map/attn_bwd/pallas_call | solution.py:480
  434.6 1.7 fusion.16
  440.3 8.0 %wgrad_b_sent.1 = bf16[4,4,128,384]{3,2,1,0:T(8,128)(2,1)} custom-call(s32[3]{0:T(128)} %pad_add_fusion.where, bf16[1024,1024]{1,0:T(8,128)(2,1)} %bitcast.178, bf16[3,1024,512]{2,1,0:T(8,128)(2,1)} %get-tuple-element.192.refs_1_), custom_call_target="tpu_custom_call" | custom-call | flops 1610612736 | bytes 8388608 | tf_op jit(solution)/shard_map/wgrad_b_sent/pallas_call | solution.py:1079
  448.3 2.1 collective-permute-start.49
  450.4 2.1 collective-permute-done.49
  452.5 1.9 collective-permute-start.50
  454.3 3.2 collective-permute-done.50
  460.0 8.4 %collective-permute-done.34 = bf16[4,128,640]{2,1,0:T(8,128)(2,1)S(1)} collective-permute-done((bf16[4,128,640]{2,1,0:T(8,128)(2,1)}, bf16[4,128,640]{2,1,0:T(8,128)(2,1)S(1)}, u32[]{:S(2)}, u32[]{:S(2)}) %collective-permute-start.34) | collective-permute-done | bytes 655392 | tf_op jit(solution)/shard_map/ppermute | solution.py:526
  470.0 2.0 collective-permute-start.36
  473.2 10.1 %wgrad_b_own.1 = (bf16[4,128,384]{2,1,0:T(8,128)(2,1)}, bf16[4,128,384]{2,1,0:T(8,128)(2,1)}, bf16[2,4,128,384]{3,2,1,0:T(8,128)(2,1)}) custom-call(s32[3]{0:T(128)} %pad_add_fusion.where, bf16[1024,1024]{1,0:T(8,128)(2,1)} %bitcast.179, bf16[3,1024,512]{2,1,0:T(8,128)(2,1)} %get-tuple-element.192.refs_1_, bf16[4,4,128,384]{3,2,1,0:T(8,128)(2,1)} %copy-done.8), custom_call_target="tpu_custom_call" | custom-call | flops 1610612736 | bytes 8388608 | tf_op jit(solution)/shard_map/wgrad_b_own/pallas_call | solution.py:1079
  483.4 12.4 %qkv_back.1 = f32[1024,1024]{1,0:T(8,128)} custom-call(bf16[1024,3072]{1,0:T(8,128)(2,1)} %get-tuple-element.139.w_ref, bf16[3,1024,512]{2,1,0:T(8,128)(2,1)} %get-tuple-element.166.refs_3_.refs_0_, bf16[3,1024,512]{2,1,0:T(8,128)(2,1)} %get-tuple-element.192.refs_1_, f32[1024,1024]{1,0:T(8,128)} %get-tuple-element.153.refs_2_), custom_call_target="tpu_custom_call" | custom-call | flops 6442450944 | bytes 20971520 | tf_op jit(solution)/shard_map/qkv_back/pallas_call | solution.py:682
  496.8 2.3 collective-permute-start.51
  499.0 4.4 collective-permute-done.37
  514.6 6.2 %collective-permute-done.39 = bf16[2,128,640]{2,1,0:T(8,128)(2,1)S(1)} collective-permute-done((bf16[2,128,640]{2,1,0:T(8,128)(2,1)S(1)}, bf16[2,128,640]{2,1,0:T(8,128)(2,1)S(1)}, u32[]{:S(2)}, u32[]{:S(2)}) %collective-permute-start.39) | collective-permute-done | bytes 327712 | tf_op jit(solution)/shard_map/ppermute | solution.py:526
  522.0 11.2 %collective-permute-done.40 = bf16[2,4,128,384]{3,2,1,0:T(8,128)(2,1)S(1)} collective-permute-done((bf16[2,4,128,384]{3,2,1,0:T(8,128)(2,1)S(1)}, bf16[2,4,128,384]{3,2,1,0:T(8,128)(2,1)S(1)}, u32[]{:S(2)}, u32[]{:S(2)}) %collective-permute-start.40) | collective-permute-done | bytes 786464 | tf_op jit(solution)/shard_map/ppermute | solution.py:526
  534.8 6.3 %collective-permute-done.41 = bf16[4,128,384]{2,1,0:T(8,128)(2,1)S(1)} collective-permute-done((bf16[4,128,384]{2,1,0:T(8,128)(2,1)S(1)}, bf16[4,128,384]{2,1,0:T(8,128)(2,1)S(1)}, u32[]{:S(2)}, u32[]{:S(2)}) %collective-permute-start.41) | collective-permute-done | bytes 393248 | tf_op jit(solution)/shard_map/ppermute | solution.py:526
  541.4 6.7 %collective-permute-done.42 = bf16[2,128,384]{2,1,0:T(8,128)(2,1)S(1)} collective-permute-done((bf16[2,128,384]{2,1,0:T(8,128)(2,1)S(1)}, bf16[2,128,384]{2,1,0:T(8,128)(2,1)S(1)}, u32[]{:S(2)}, u32[]{:S(2)}) %collective-permute-start.42) | collective-permute-done | bytes 196640 | tf_op jit(solution)/shard_map/ppermute | solution.py:526
  548.9 5.0 collective-permute-done.43
  555.1 3.5 collective-permute-done.44
  560.5 1.6 pad_maximum_fusion.2
  562.1 2.3 collective-permute-done.45
  (336 shorter events, 91.3 us)
Async XLA Ops:
  0.6 25.1 %copy-start.23 = (bf16[128,256]{1,0:T(8,128)(2,1)S(1)}, bf16[128,256]{1,0:T(8,128)(2,1)}, u32[]{:S(2)}) copy-start(bf16[128,256]{1,0:T(8,128)(2,1)} %param.24) | copy-start | bytes 196612
  0.7 25.1 %copy-start.17 = (bf16[128,1024]{1,0:T(8,128)(2,1)S(1)}, bf16[128,1024]{1,0:T(8,128)(2,1)}, u32[]{:S(2)}) copy-start(bf16[128,1024]{1,0:T(8,128)(2,1)} %param.28) | copy-start | bytes 786436
  0.7 8.7 %collective-permute-start = (bf16[128,768]{1,0:T(8,128)(2,1)}, bf16[128,768]{1,0:T(8,128)(2,1)S(1)}, u32[]{:S(2)}, u32[]{:S(2)}) collective-permute-start(bf16[128,768]{1,0:T(8,128)(2,1)} %param.21), channel_id=1, source_target_pairs={{0,2},{1,5},{2,0},{3,7},{4,6},{5,1},{6,4},{7,3},{8,10},{9,13},{10,... | collective-permute-start | bytes 589832 | tf_op jit(solution)/shard_map/ppermute | solution.py:526
  10.3 11.3 %collective-permute-start.1 = (bf16[2,128,768]{2,1,0:T(8,128)(2,1)S(1)}, bf16[2,128,768]{2,1,0:T(8,128)(2,1)S(1)}, u32[]{:S(2)}, u32[]{:S(2)}) collective-permute-start(bf16[2,128,768]{2,1,0:T(8,128)(2,1)S(1)} %pad_maximum_fusion.14), channel_id=1, source_target_pairs={{0,4},{1,3},{2,6},{3,1},{4,0},{5,7},{6,2},{7,5},{8,12},{9,11},{10,... | collective-permute-start | bytes 1179656 | tf_op jit(solution)/shard_map/ppermute | solution.py:526
  16.1 23.8 %copy-start.7 = (bf16[128,768]{1,0:T(8,128)(2,1)S(1)}, bf16[128,768]{1,0:T(8,128)(2,1)}, u32[]{:S(2)}) copy-start(bf16[128,768]{1,0:T(8,128)(2,1)} %param.21) | copy-start | bytes 589828
  23.5 13.8 %collective-permute-start.2 = (bf16[4,128,768]{2,1,0:T(8,128)(2,1)}, bf16[4,128,768]{2,1,0:T(8,128)(2,1)}, u32[]{:S(2)}, u32[]{:S(2)}) collective-permute-start(bf16[4,128,768]{2,1,0:T(8,128)(2,1)} %pad_maximum_fusion.8.refs_0_), channel_id=1, source_target_pairs={{0,8},{1,17},{2,10},{3,19},{4,12},{5,21},{6,14},{7,23},{8,0},{9,25... | collective-permute-start | bytes 2359304 | tf_op jit(solution)/shard_map/ppermute | solution.py:526
  25.8 11.4 %collective-permute-start.7 = (bf16[144,1280]{1,0:T(8,128)(2,1)S(1)}, bf16[144,1280]{1,0:T(8,128)(2,1)S(1)}, u32[]{:S(2)}, u32[]{:S(2)}) collective-permute-start(bf16[144,1280]{1,0:T(8,128)(2,1)S(1)} %pad_maximum_fusion.15), channel_id=1, source_target_pairs={{0,2},{1,5},{2,0},{3,7},{4,6},{5,1},{6,4},{7,3},{8,10},{9,13},{10,... | collective-permute-start | bytes 1105928 | tf_op jit(solution)/shard_map/ppermute | solution.py:526
  37.3 20.4 %collective-permute-start.8 = (bf16[2,144,1280]{2,1,0:T(8,128)(2,1)S(1)}, bf16[2,144,1280]{2,1,0:T(8,128)(2,1)S(1)}, u32[]{:S(2)}, u32[]{:S(2)}) collective-permute-start(bf16[2,144,1280]{2,1,0:T(8,128)(2,1)S(1)} %pad_maximum_fusion.9), channel_id=1, source_target_pairs={{0,4},{1,3},{2,6},{3,1},{4,0},{5,7},{6,2},{7,5},{8,12},{9,11},{10,... | collective-permute-start | bytes 2211848 | tf_op jit(solution)/shard_map/ppermute | solution.py:526
  39.9 47.1 %collective-permute-start.4 = (bf16[4,128,768]{2,1,0:T(8,128)(2,1)}, bf16[4,128,768]{2,1,0:T(8,128)(2,1)}, u32[]{:S(2)}, u32[]{:S(2)}) collective-permute-start(bf16[4,128,768]{2,1,0:T(8,128)(2,1)} %pad_maximum_fusion.8.refs_0_), channel_id=1, source_target_pairs={{0,1},{1,0},{2,3},{3,2},{4,5},{5,4},{6,7},{7,6},{8,9},{9,8},{10,11... | collective-permute-start | bytes 2359304 | tf_op jit(solution)/shard_map/ppermute | solution.py:526
  42.4 25.1 %collective-permute-start.3 = (bf16[8,128,768]{2,1,0:T(8,128)(2,1)}, bf16[8,128,768]{2,1,0:T(8,128)(2,1)}, u32[]{:S(2)}, u32[]{:S(2)}) collective-permute-start(bf16[8,128,768]{2,1,0:T(8,128)(2,1)} %pad_maximum_fusion.3), channel_id=1, source_target_pairs={{0,16},{1,9},{2,18},{3,11},{4,20},{5,13},{6,22},{7,15},{8,24},{9,1... | collective-permute-start | bytes 4718600 | tf_op jit(solution)/shard_map/ppermute | solution.py:526
  44.9 42.1 %collective-permute-start.5 = (bf16[4,128,768]{2,1,0:T(8,128)(2,1)}, bf16[4,128,768]{2,1,0:T(8,128)(2,1)}, u32[]{:S(2)}, u32[]{:S(2)}) collective-permute-start(bf16[4,128,768]{2,1,0:T(8,128)(2,1)} %collective-permute-done.2.refs_1_), channel_id=1, source_target_pairs={{0,1},{1,0},{2,3},{3,2},{4,5},{5,4},{6,7},{7,6},{8,9},{9,8},{10,11... | collective-permute-start | bytes 2359304 | tf_op jit(solution)/shard_map/ppermute | solution.py:526
  57.7 1.5 collective-permute-start.9
  57.9 84.9 %copy-start = (bf16[4,128,1280]{2,1,0:T(8,128)(2,1)}, bf16[4,128,1280]{2,1,0:T(8,128)(2,1)S(1)}, u32[]{:S(2)}) copy-start(bf16[4,128,1280]{2,1,0:T(8,128)(2,1)S(1)} %pad_maximum_fusion.4.refs_0_) | copy-start | bytes 3932164
  67.5 17.7 %collective-permute-start.12 = (bf16[4,128,1280]{2,1,0:T(8,128)(2,1)S(1)}, bf16[4,128,1280]{2,1,0:T(8,128)(2,1)S(1)}, u32[]{:S(2)}, u32[]{:S(2)}) collective-permute-start(bf16[4,128,1280]{2,1,0:T(8,128)(2,1)S(1)} %pad_maximum_fusion.4.refs_0_), channel_id=1, source_target_pairs={{0,8},{1,17},{2,10},{3,19},{4,12},{5,21},{6,14},{7,23},{8,0},{9,25... | collective-permute-start | bytes 3932168 | tf_op jit(solution)/shard_map/ppermute | solution.py:526
  68.2 18.8 %collective-permute-start.6 = (bf16[8,128,768]{2,1,0:T(8,128)(2,1)}, bf16[8,128,768]{2,1,0:T(8,128)(2,1)S(1)}, u32[]{:S(2)}, u32[]{:S(2)}) collective-permute-start(bf16[8,128,768]{2,1,0:T(8,128)(2,1)} %collective-permute-done.3.refs_2_), channel_id=1, source_target_pairs={{0,1},{1,0},{2,3},{3,2},{4,5},{5,4},{6,7},{7,6},{8,9},{9,8},{10,11... | collective-permute-start | bytes 4718600 | tf_op jit(solution)/shard_map/ppermute | solution.py:526
  85.1 58.2 %copy-start.1 = (bf16[4,128,1280]{2,1,0:T(8,128)(2,1)}, bf16[4,128,1280]{2,1,0:T(8,128)(2,1)S(1)}, u32[]{:S(2)}) copy-start(bf16[4,128,1280]{2,1,0:T(8,128)(2,1)S(1)} %collective-permute-done.12.refs_1_) | copy-start | bytes 3932164
  101.1 41.6 %collective-permute-start.13 = (bf16[8,128,1280]{2,1,0:T(8,128)(2,1)}, bf16[8,128,1280]{2,1,0:T(8,128)(2,1)}, u32[]{:S(2)}, u32[]{:S(2)}) collective-permute-start(bf16[8,128,1280]{2,1,0:T(8,128)(2,1)} %pad_maximum_fusion), channel_id=1, source_target_pairs={{0,16},{1,9},{2,18},{3,11},{4,20},{5,13},{6,22},{7,15},{8,24},{9,1... | collective-permute-start | bytes 7864328 | tf_op jit(solution)/shard_map/ppermute | solution.py:526
  103.6 11.1 %collective-permute-start.10 = (bf16[512,256]{1,0:T(8,128)(2,1)S(1)}, bf16[512,256]{1,0:T(8,128)(2,1)S(1)}, u32[]{:S(2)}, u32[]{:S(2)}) collective-permute-start(bf16[512,256]{1,0:T(8,128)(2,1)S(1)} %copy-done.2), channel_id=1, source_target_pairs={{0,2},{1,5},{2,0},{3,7},{4,6},{5,1},{6,4},{7,3},{8,10},{9,13},{10,... | collective-permute-start | bytes 786440 | tf_op jit(solution)/shard_map/ppermute | solution.py:526
  115.6 16.2 %collective-permute-start.11 = (bf16[2,512,256]{2,1,0:T(8,128)(2,1)}, bf16[2,512,256]{2,1,0:T(8,128)(2,1)S(1)}, u32[]{:S(2)}, u32[]{:S(2)}) collective-permute-start(bf16[2,512,256]{2,1,0:T(8,128)(2,1)} %pad_maximum_fusion.10), channel_id=1, source_target_pairs={{0,4},{1,3},{2,6},{3,1},{4,0},{5,7},{6,2},{7,5},{8,12},{9,11},{10,... | collective-permute-start | bytes 1572872 | tf_op jit(solution)/shard_map/ppermute | solution.py:526
  142.8 18.5 %collective-permute-start.17 = (bf16[8,128,1280]{2,1,0:T(8,128)(2,1)}, bf16[8,128,1280]{2,1,0:T(8,128)(2,1)}, u32[]{:S(2)}, u32[]{:S(2)}) collective-permute-start(bf16[8,128,1280]{2,1,0:T(8,128)(2,1)} %collective-permute-done.13.refs_2_), channel_id=1, source_target_pairs={{0,1},{1,0},{2,3},{3,2},{4,5},{5,4},{6,7},{7,6},{8,9},{9,8},{10,11... | collective-permute-start | bytes 7864328 | tf_op jit(solution)/shard_map/ppermute | solution.py:526
  142.9 18.4 %collective-permute-start.15 = (bf16[4,128,1280]{2,1,0:T(8,128)(2,1)S(1)}, bf16[4,128,1280]{2,1,0:T(8,128)(2,1)}, u32[]{:S(2)}, u32[]{:S(2)}) collective-permute-start(bf16[4,128,1280]{2,1,0:T(8,128)(2,1)S(1)} %pad_maximum_fusion.4.refs_0_), channel_id=1, source_target_pairs={{0,1},{1,0},{2,3},{3,2},{4,5},{5,4},{6,7},{7,6},{8,9},{9,8},{10,11... | collective-permute-start | bytes 3932168 | tf_op jit(solution)/shard_map/ppermute | solution.py:526
  143.3 18.0 %collective-permute-start.16 = (bf16[4,128,1280]{2,1,0:T(8,128)(2,1)S(1)}, bf16[4,128,1280]{2,1,0:T(8,128)(2,1)}, u32[]{:S(2)}, u32[]{:S(2)}) collective-permute-start(bf16[4,128,1280]{2,1,0:T(8,128)(2,1)S(1)} %collective-permute-done.12.refs_1_), channel_id=1, source_target_pairs={{0,1},{1,0},{2,3},{3,2},{4,5},{5,4},{6,7},{7,6},{8,9},{9,8},{10,11... | collective-permute-start | bytes 3932168 | tf_op jit(solution)/shard_map/ppermute | solution.py:526
  143.4 15.1 %collective-permute-start.14 = (bf16[4,512,256]{2,1,0:T(8,128)(2,1)}, bf16[4,512,256]{2,1,0:T(8,128)(2,1)}, u32[]{:S(2)}, u32[]{:S(2)}) collective-permute-start(bf16[4,512,256]{2,1,0:T(8,128)(2,1)} %pad_maximum_fusion.6.refs_0_), channel_id=1, source_target_pairs={{0,8},{1,17},{2,10},{3,19},{4,12},{5,21},{6,14},{7,23},{8,0},{9,25... | collective-permute-start | bytes 3145736 | tf_op jit(solution)/shard_map/ppermute | solution.py:526
  171.2 26.2 %collective-permute-start.18 = (bf16[8,512,256]{2,1,0:T(8,128)(2,1)S(1)}, bf16[8,512,256]{2,1,0:T(8,128)(2,1)}, u32[]{:S(2)}, u32[]{:S(2)}) collective-permute-start(bf16[8,512,256]{2,1,0:T(8,128)(2,1)S(1)} %copy-done.4), channel_id=1, source_target_pairs={{0,16},{1,9},{2,18},{3,11},{4,20},{5,13},{6,22},{7,15},{8,24},{9,1... | collective-permute-start | bytes 6291464 | tf_op jit(solution)/shard_map/ppermute | solution.py:526
  174.1 23.3 %copy-start.12 = (bf16[4,512,256]{2,1,0:T(8,128)(2,1)S(1)}, bf16[4,512,256]{2,1,0:T(8,128)(2,1)}, u32[]{:S(2)}) copy-start(bf16[4,512,256]{2,1,0:T(8,128)(2,1)} %pad_maximum_fusion.6.refs_0_) | copy-start | bytes 3145732
  174.1 23.8 %copy-start.31 = (s32[1,1024]{1,0:T(1,128)S(1)}, s32[1,1024]{1,0:T(1,128)}, u32[]{:S(2)}) copy-start(s32[1,1024]{1,0:T(1,128)} %param.19) | copy-start | bytes 12292
  197.4 7.5 %collective-permute-start.21 = (bf16[8,512,256]{2,1,0:T(8,128)(2,1)}, bf16[8,512,256]{2,1,0:T(8,128)(2,1)}, u32[]{:S(2)}, u32[]{:S(2)}) collective-permute-start(bf16[8,512,256]{2,1,0:T(8,128)(2,1)} %collective-permute-done.18.refs_2_), channel_id=1, source_target_pairs={{0,1},{1,0},{2,3},{3,2},{4,5},{5,4},{6,7},{7,6},{8,9},{9,8},{10,11... | collective-permute-start | bytes 6291464 | tf_op jit(solution)/shard_map/ppermute | solution.py:526
  197.4 6.8 %collective-permute-start.19 = (bf16[4,512,256]{2,1,0:T(8,128)(2,1)S(1)}, bf16[4,512,256]{2,1,0:T(8,128)(2,1)S(1)}, u32[]{:S(2)}, u32[]{:S(2)}) collective-permute-start(bf16[4,512,256]{2,1,0:T(8,128)(2,1)S(1)} %copy-done.12), channel_id=1, source_target_pairs={{0,1},{1,0},{2,3},{3,2},{4,5},{5,4},{6,7},{7,6},{8,9},{9,8},{10,11... | collective-permute-start | bytes 3145736 | tf_op jit(solution)/shard_map/ppermute | solution.py:526
  197.9 7.0 %collective-permute-start.20 = (bf16[4,512,256]{2,1,0:T(8,128)(2,1)}, bf16[4,512,256]{2,1,0:T(8,128)(2,1)}, u32[]{:S(2)}, u32[]{:S(2)}) collective-permute-start(bf16[4,512,256]{2,1,0:T(8,128)(2,1)} %collective-permute-done.14.refs_1_), channel_id=1, source_target_pairs={{0,1},{1,0},{2,3},{3,2},{4,5},{5,4},{6,7},{7,6},{8,9},{9,8},{10,11... | collective-permute-start | bytes 3145736 | tf_op jit(solution)/shard_map/ppermute | solution.py:526
  236.3 15.0 %collective-permute-start.22 = (bf16[4,4,512,256]{3,2,1,0:T(8,128)(2,1)}, bf16[4,4,512,256]{3,2,1,0:T(8,128)(2,1)}, u32[]{:S(2)}, u32[]{:S(2)}) collective-permute-start(bf16[4,4,512,256]{3,2,1,0:T(8,128)(2,1)} %wgrad_out_sent.1), channel_id=1, source_target_pairs={{0,1},{1,0},{2,3},{3,2},{4,5},{5,4},{6,7},{7,6},{8,9},{9,8},{10,11... | collective-permute-start | bytes 12582920 | tf_op jit(solution)/shard_map/ppermute | solution.py:526
  272.4 28.6 %collective-permute-start.23 = (bf16[4,4,128,1024]{3,2,1,0:T(8,128)(2,1)}, bf16[4,4,128,1024]{3,2,1,0:T(8,128)(2,1)}, u32[]{:S(2)}, u32[]{:S(2)}) collective-permute-start(bf16[4,4,128,1024]{3,2,1,0:T(8,128)(2,1)} %wgrad_in_sent.1), channel_id=1, source_target_pairs={{0,1},{1,0},{2,3},{3,2},{4,5},{5,4},{6,7},{7,6},{8,9},{9,8},{10,11... | collective-permute-start | bytes 12582920 | tf_op jit(solution)/shard_map/ppermute | solution.py:526
  272.5 26.2 %collective-permute-start.24 = (bf16[2,4,512,256]{3,2,1,0:T(8,128)(2,1)}, bf16[2,4,512,256]{3,2,1,0:T(8,128)(2,1)S(1)}, u32[]{:S(2)}, u32[]{:S(2)}) collective-permute-start(bf16[2,4,512,256]{3,2,1,0:T(8,128)(2,1)} %get-tuple-element.155), channel_id=1, source_target_pairs={{0,8},{1,17},{2,10},{3,19},{4,12},{5,21},{6,14},{7,23},{8,0},{9,25... | collective-permute-start | bytes 6291464 | tf_op jit(solution)/shard_map/ppermute | solution.py:526
  272.8 25.9 %copy-start.10 = (bf16[4,512,256]{2,1,0:T(8,128)(2,1)S(1)}, bf16[4,512,256]{2,1,0:T(8,128)(2,1)}, u32[]{:S(2)}) copy-start(bf16[4,512,256]{2,1,0:T(8,128)(2,1)} %get-tuple-element.154) | copy-start | bytes 3145732
  300.2 35.6 %collective-permute-start.25 = (bf16[4,512,256]{2,1,0:T(8,128)(2,1)}, bf16[4,512,256]{2,1,0:T(8,128)(2,1)S(1)}, u32[]{:S(2)}, u32[]{:S(2)}) collective-permute-start(bf16[4,512,256]{2,1,0:T(8,128)(2,1)} %fusion.5), channel_id=1, source_target_pairs={{0,16},{1,9},{2,18},{3,11},{4,20},{5,13},{6,22},{7,15},{8,24},{9,1... | collective-permute-start | bytes 3145736 | tf_op jit(solution)/shard_map/ppermute | solution.py:526
  313.5 40.4 %collective-permute-start.26 = (bf16[2,4,128,1024]{3,2,1,0:T(8,128)(2,1)}, bf16[2,4,128,1024]{3,2,1,0:T(8,128)(2,1)}, u32[]{:S(2)}, u32[]{:S(2)}) collective-permute-start(bf16[2,4,128,1024]{3,2,1,0:T(8,128)(2,1)} %get-tuple-element.168), channel_id=1, source_target_pairs={{0,8},{1,17},{2,10},{3,19},{4,12},{5,21},{6,14},{7,23},{8,0},{9,25... | collective-permute-start | bytes 6291464 | tf_op jit(solution)/shard_map/ppermute | solution.py:526
  337.6 16.1 %collective-permute-start.27 = (bf16[2,512,256]{2,1,0:T(8,128)(2,1)S(1)}, bf16[2,512,256]{2,1,0:T(8,128)(2,1)S(1)}, u32[]{:S(2)}, u32[]{:S(2)}) collective-permute-start(bf16[2,512,256]{2,1,0:T(8,128)(2,1)S(1)} %pad_maximum_fusion.11), channel_id=1, source_target_pairs={{0,2},{1,5},{2,0},{3,7},{4,6},{5,1},{6,4},{7,3},{8,10},{9,13},{10,... | collective-permute-start | bytes 1572872 | tf_op jit(solution)/shard_map/ppermute | solution.py:526
  365.9 28.1 %collective-permute-start.28 = (bf16[4,4,128,640]{3,2,1,0:T(8,128)(2,1)}, bf16[4,4,128,640]{3,2,1,0:T(8,128)(2,1)}, u32[]{:S(2)}, u32[]{:S(2)}) collective-permute-start(bf16[4,4,128,640]{3,2,1,0:T(8,128)(2,1)} %wgrad_a_sent.1), channel_id=1, source_target_pairs={{0,1},{1,0},{2,3},{3,2},{4,5},{5,4},{6,7},{7,6},{8,9},{9,8},{10,11... | collective-permute-start | bytes 7864328 | tf_op jit(solution)/shard_map/ppermute | solution.py:526
  370.9 19.9 %collective-permute-start.30 = (bf16[512,256]{1,0:T(8,128)(2,1)S(1)}, bf16[512,256]{1,0:T(8,128)(2,1)S(1)}, u32[]{:S(2)}, u32[]{:S(2)}) collective-permute-start(bf16[512,256]{1,0:T(8,128)(2,1)S(1)} %fusion.15), channel_id=1, source_target_pairs={{0,4},{1,3},{2,6},{3,1},{4,0},{5,7},{6,2},{7,5},{8,12},{9,11},{10,... | collective-permute-start | bytes 786440 | tf_op jit(solution)/shard_map/ppermute | solution.py:526
  373.6 17.3 %collective-permute-start.29 = (bf16[4,128,1024]{2,1,0:T(8,128)(2,1)S(1)}, bf16[4,128,1024]{2,1,0:T(8,128)(2,1)}, u32[]{:S(2)}, u32[]{:S(2)}) collective-permute-start(bf16[4,128,1024]{2,1,0:T(8,128)(2,1)S(1)} %fusion.2), channel_id=1, source_target_pairs={{0,16},{1,9},{2,18},{3,11},{4,20},{5,13},{6,22},{7,15},{8,24},{9,1... | collective-permute-start | bytes 3145736 | tf_op jit(solution)/shard_map/ppermute | solution.py:526
  393.6 39.1 %collective-permute-start.32 = (bf16[2,128,1024]{2,1,0:T(8,128)(2,1)S(1)}, bf16[2,128,1024]{2,1,0:T(8,128)(2,1)}, u32[]{:S(2)}, u32[]{:S(2)}) collective-permute-start(bf16[2,128,1024]{2,1,0:T(8,128)(2,1)S(1)} %pad_maximum_fusion.12), channel_id=1, source_target_pairs={{0,2},{1,5},{2,0},{3,7},{4,6},{5,1},{6,4},{7,3},{8,10},{9,13},{10,... | collective-permute-start | bytes 1572872 | tf_op jit(solution)/shard_map/ppermute | solution.py:526
  409.9 29.1 %collective-permute-start.31 = (bf16[2,4,128,640]{3,2,1,0:T(8,128)(2,1)}, bf16[2,4,128,640]{3,2,1,0:T(8,128)(2,1)S(1)}, u32[]{:S(2)}, u32[]{:S(2)}) collective-permute-start(bf16[2,4,128,640]{3,2,1,0:T(8,128)(2,1)} %get-tuple-element.183), channel_id=1, source_target_pairs={{0,8},{1,17},{2,10},{3,19},{4,12},{5,21},{6,14},{7,23},{8,0},{9,25... | collective-permute-start | bytes 3932168 | tf_op jit(solution)/shard_map/ppermute | solution.py:526
  411.4 19.3 %copy-start.24 = (f32[1,4096]{1,0:T(1,128)S(1)}, f32[1,4096]{1,0:T(1,128)}, u32[]{:S(2)}) copy-start(f32[1,4096]{1,0:T(1,128)} %get-tuple-element.198) | copy-start | bytes 49156
  411.4 27.6 %copy-start.14 = (bf16[4,128,640]{2,1,0:T(8,128)(2,1)S(1)}, bf16[4,128,640]{2,1,0:T(8,128)(2,1)}, u32[]{:S(2)}) copy-start(bf16[4,128,640]{2,1,0:T(8,128)(2,1)} %get-tuple-element.182) | copy-start | bytes 1966084
  432.7 1.2 collective-permute-start.46
  434.0 4.1 collective-permute-start.47
  436.3 22.5 %collective-permute-start.35 = (bf16[128,1024]{1,0:T(8,128)(2,1)}, bf16[128,1024]{1,0:T(8,128)(2,1)}, u32[]{:S(2)}, u32[]{:S(2)}) collective-permute-start(bf16[128,1024]{1,0:T(8,128)(2,1)} %fusion.16), channel_id=1, source_target_pairs={{0,4},{1,3},{2,6},{3,1},{4,0},{5,7},{6,2},{7,5},{8,12},{9,11},{10,... | collective-permute-start | bytes 786440 | tf_op jit(solution)/shard_map/ppermute | solution.py:526
  438.1 10.2 %collective-permute-start.48 = (f32[96,128]{1,0:T(8,128)S(1)}, f32[96,128]{1,0:T(8,128)S(1)}, u32[]{:S(2)}, u32[]{:S(2)}) collective-permute-start(f32[96,128]{1,0:T(8,128)S(1)} %fusion.25), channel_id=1, source_target_pairs={{0,16},{1,9},{2,18},{3,11},{4,20},{5,13},{6,22},{7,15},{8,24},{9,1... | collective-permute-start | bytes 147464 | tf_op jit(solution)/shard_map/ppermute | solution.py:526
  448.3 23.8 %collective-permute-start.33 = (bf16[4,4,128,384]{3,2,1,0:T(8,128)(2,1)}, bf16[4,4,128,384]{3,2,1,0:T(8,128)(2,1)S(1)}, u32[]{:S(2)}, u32[]{:S(2)}) collective-permute-start(bf16[4,4,128,384]{3,2,1,0:T(8,128)(2,1)} %wgrad_b_sent.1), channel_id=1, source_target_pairs={{0,1},{1,0},{2,3},{3,2},{4,5},{5,4},{6,7},{7,6},{8,9},{9,8},{10,11... | collective-permute-start | bytes 4718600 | tf_op jit(solution)/shard_map/ppermute | solution.py:526
  448.3 4.2 collective-permute-start.49
  452.5 5.0 collective-permute-start.50
  457.5 10.9 %collective-permute-start.34 = (bf16[4,128,640]{2,1,0:T(8,128)(2,1)}, bf16[4,128,640]{2,1,0:T(8,128)(2,1)S(1)}, u32[]{:S(2)}, u32[]{:S(2)}) collective-permute-start(bf16[4,128,640]{2,1,0:T(8,128)(2,1)} %fusion.8), channel_id=1, source_target_pairs={{0,16},{1,9},{2,18},{3,11},{4,20},{5,13},{6,22},{7,15},{8,24},{9,1... | collective-permute-start | bytes 1966088 | tf_op jit(solution)/shard_map/ppermute | solution.py:526
  470.0 25.8 %collective-permute-start.36 = (bf16[2,128,640]{2,1,0:T(8,128)(2,1)S(1)}, bf16[2,128,640]{2,1,0:T(8,128)(2,1)S(1)}, u32[]{:S(2)}, u32[]{:S(2)}) collective-permute-start(bf16[2,128,640]{2,1,0:T(8,128)(2,1)S(1)} %pad_maximum_fusion.16), channel_id=1, source_target_pairs={{0,2},{1,5},{2,0},{3,7},{4,6},{5,1},{6,4},{7,3},{8,10},{9,13},{10,... | collective-permute-start | bytes 983048 | tf_op jit(solution)/shard_map/ppermute | solution.py:526
  495.8 16.8 %copy-start.38 = (bf16[2,4,128,384]{3,2,1,0:T(8,128)(2,1)S(1)}, bf16[2,4,128,384]{3,2,1,0:T(8,128)(2,1)}, u32[]{:S(2)}) copy-start(bf16[2,4,128,384]{3,2,1,0:T(8,128)(2,1)} %get-tuple-element.194) | copy-start | bytes 2359300
  495.9 7.5 %collective-permute-start.37 = (bf16[128,640]{1,0:T(8,128)(2,1)S(1)}, bf16[128,640]{1,0:T(8,128)(2,1)S(1)}, u32[]{:S(2)}, u32[]{:S(2)}) collective-permute-start(bf16[128,640]{1,0:T(8,128)(2,1)S(1)} %fusion.18), channel_id=1, source_target_pairs={{0,4},{1,3},{2,6},{3,1},{4,0},{5,7},{6,2},{7,5},{8,12},{9,11},{10,... | collective-permute-start | bytes 491528 | tf_op jit(solution)/shard_map/ppermute | solution.py:526
  496.8 15.7 %collective-permute-start.51 = (bf16[1024,256]{1,0:T(8,128)(2,1)S(1)}, bf16[1024,256]{1,0:T(8,128)(2,1)S(1)}, u32[]{:S(2)}, u32[]{:S(2)}) collective-permute-start(bf16[1024,256]{1,0:T(8,128)(2,1)S(1)} %constant_dynamic-update-slice_fusion.34), channel_id=1, source_target_pairs={{0,8},{1,17},{2,10},{3,19},{4,12},{5,21},{6,14},{7,23},{8,0},{9,25... | collective-permute-start | bytes 1572872 | tf_op jit(solution)/shard_map/ppermute | solution.py:526
  503.4 7.1 %collective-permute-start.38 = (bf16[128,640]{1,0:T(8,128)(2,1)S(1)}, bf16[128,640]{1,0:T(8,128)(2,1)S(1)}, u32[]{:S(2)}, u32[]{:S(2)}) collective-permute-start(bf16[128,640]{1,0:T(8,128)(2,1)S(1)} %fusion.14), channel_id=1, source_target_pairs={{0,8},{1,17},{2,10},{3,19},{4,12},{5,21},{6,14},{7,23},{8,0},{9,25... | collective-permute-start | bytes 491528 | tf_op jit(solution)/shard_map/ppermute | solution.py:526
  510.5 10.3 %collective-permute-start.39 = (bf16[2,128,640]{2,1,0:T(8,128)(2,1)S(1)}, bf16[2,128,640]{2,1,0:T(8,128)(2,1)S(1)}, u32[]{:S(2)}, u32[]{:S(2)}) collective-permute-start(bf16[2,128,640]{2,1,0:T(8,128)(2,1)S(1)} %pad_maximum_fusion.17), channel_id=1, source_target_pairs={{0,16},{1,9},{2,18},{3,11},{4,20},{5,13},{6,22},{7,15},{8,24},{9,1... | collective-permute-start | bytes 983048 | tf_op jit(solution)/shard_map/ppermute | solution.py:526
  512.6 20.5 %collective-permute-start.40 = (bf16[2,4,128,384]{3,2,1,0:T(8,128)(2,1)S(1)}, bf16[2,4,128,384]{3,2,1,0:T(8,128)(2,1)S(1)}, u32[]{:S(2)}, u32[]{:S(2)}) collective-permute-start(bf16[2,4,128,384]{3,2,1,0:T(8,128)(2,1)S(1)} %copy-done.38), channel_id=1, source_target_pairs={{0,8},{1,17},{2,10},{3,19},{4,12},{5,21},{6,14},{7,23},{8,0},{9,25... | collective-permute-start | bytes 2359304 | tf_op jit(solution)/shard_map/ppermute | solution.py:526
  513.8 20.4 %collective-permute-start.52 = (bf16[2,1024,256]{2,1,0:T(8,128)(2,1)S(1)}, bf16[2,1024,256]{2,1,0:T(8,128)(2,1)S(1)}, u32[]{:S(2)}, u32[]{:S(2)}) collective-permute-start(bf16[2,1024,256]{2,1,0:T(8,128)(2,1)S(1)} %pad_maximum_fusion.7), channel_id=1, source_target_pairs={{0,16},{1,9},{2,18},{3,11},{4,20},{5,13},{6,22},{7,15},{8,24},{9,1... | collective-permute-start | bytes 3145736 | tf_op jit(solution)/shard_map/ppermute | solution.py:526
  533.2 7.8 %collective-permute-start.41 = (bf16[4,128,384]{2,1,0:T(8,128)(2,1)S(1)}, bf16[4,128,384]{2,1,0:T(8,128)(2,1)S(1)}, u32[]{:S(2)}, u32[]{:S(2)}) collective-permute-start(bf16[4,128,384]{2,1,0:T(8,128)(2,1)S(1)} %fusion.9), channel_id=1, source_target_pairs={{0,16},{1,9},{2,18},{3,11},{4,20},{5,13},{6,22},{7,15},{8,24},{9,1... | collective-permute-start | bytes 1179656 | tf_op jit(solution)/shard_map/ppermute | solution.py:526
  541.3 6.8 %collective-permute-start.42 = (bf16[2,128,384]{2,1,0:T(8,128)(2,1)S(1)}, bf16[2,128,384]{2,1,0:T(8,128)(2,1)S(1)}, u32[]{:S(2)}, u32[]{:S(2)}) collective-permute-start(bf16[2,128,384]{2,1,0:T(8,128)(2,1)S(1)} %pad_maximum_fusion.18), channel_id=1, source_target_pairs={{0,2},{1,5},{2,0},{3,7},{4,6},{5,1},{6,4},{7,3},{8,10},{9,13},{10,... | collective-permute-start | bytes 589832 | tf_op jit(solution)/shard_map/ppermute | solution.py:526
  548.1 5.8 %collective-permute-start.43 = (bf16[128,384]{1,0:T(8,128)(2,1)S(1)}, bf16[128,384]{1,0:T(8,128)(2,1)S(1)}, u32[]{:S(2)}, u32[]{:S(2)}) collective-permute-start(bf16[128,384]{1,0:T(8,128)(2,1)S(1)} %fusion.19), channel_id=1, source_target_pairs={{0,4},{1,3},{2,6},{3,1},{4,0},{5,7},{6,2},{7,5},{8,12},{9,11},{10,... | collective-permute-start | bytes 294920 | tf_op jit(solution)/shard_map/ppermute | solution.py:526
  553.9 4.7 collective-permute-start.44
  558.6 5.7 %collective-permute-start.45 = (bf16[2,128,384]{2,1,0:T(8,128)(2,1)S(1)}, bf16[2,128,384]{2,1,0:T(8,128)(2,1)S(1)}, u32[]{:S(2)}, u32[]{:S(2)}) collective-permute-start(bf16[2,128,384]{2,1,0:T(8,128)(2,1)S(1)} %pad_maximum_fusion.19), channel_id=1, source_target_pairs={{0,16},{1,9},{2,18},{3,11},{4,20},{5,13},{6,22},{7,15},{8,24},{9,1... | collective-permute-start | bytes 589832 | tf_op jit(solution)/shard_map/ppermute | solution.py:526
  (29 other events, 239.5 us)

commit v5 on v4

--- a/solution.py
+++ b/solution.py
@@ -557,29 +557,33 @@
     def __init__(self, place, piece):
         self.place = place
         self.piece = piece
-        self.held = [None] * 3
-        self.crossed = [None] * 3
+        self.held = [None] * 4
+        self.crossed = [None] * 4
 
     def chips_near(self, *wait):
         piece = after(self.piece, *wait) if wait else self.piece
-        self.pair = jnp.stack([piece, self.place.swap_chip(piece, 0)])
-        return self.pair
+        self.pair = [piece, self.place.swap_chip(piece, 0)]
+        return self.pair[1]
 
     def chips_far(self, *wait):
-        pair = after(self.pair, *wait) if wait else self.pair
-        self.held[0] = jnp.concatenate([self.pair, self.place.swap_chip(pair, 1)])
+        pair = jnp.stack([self.pair[0], after(self.pair[1], *wait)])
+        self.rest = [pair, self.place.swap_chip(pair, 1)]
+        return self.rest[1]
+
+    def join(self, *wait):
+        rest = after(self.rest[1], *wait) if wait else self.rest[1]
+        self.held[0] = jnp.concatenate([self.rest[0], rest])
         return self.held[0]
 
-    def near(self, *wait):
-        piece = after(self.held[0], *wait) if wait else self.held[0]
-        self.held[1] = self.place.swap_grp(piece, 0)
-        return self.held[1]
+    def near(self):
+        self.held[1] = self.place.swap_grp(self.held[0], 0)
+        self.held[2] = self.place.swap_grp(self.held[0], 1)
+        return self.held[2]
 
     def far(self, *wait):
-        both = jnp.concatenate(self.held[:2])
-        both = after(both, *wait) if wait else both
-        self.held[2] = self.place.swap_grp(both, 1)
-        return self.held[2]
+        first = after(self.held[1], *wait) if wait else self.held[1]
+        self.held[3] = self.place.swap_grp(first, 1)
+        return self.held[3]
 
     def cross(self, *which, wait=()):
         for n in which:
@@ -603,13 +607,13 @@
     for slot in range(4):
         for side in range(2):
             core = where[0] ^ side
-            ref = refs[3 * side + min(slot, 2)]
+            ref = refs[4 * side + slot]
             distance = turn(slot, core)
             col = pl.multiple_of((where[2] ^ distance) * cols, LANES)
             for k in range(chips):
                 row = ((where[1] ^ turn(k, core)) * 2 + core) * rows
                 pltpu.make_async_copy(
-                    ref.at[k + (chips if slot == 3 else 0), :, pl.ds(window.start, cols)],
+                    ref.at[k, :, pl.ds(window.start, cols)],
                     whole.at[pl.ds(pl.multiple_of(row, rows), rows), pl.ds(col, cols)],
                     sem.at[distance if by == "grp" else 0],
                 ).start()
@@ -710,6 +714,87 @@
     return jax.ShapeDtypeStruct(shape, dtype)
 
 
+B_QUERY, B_VALUE, B_ATTN, GAIN_ONE, SHIFT_ONE, B_OUT, GAIN_TWO, SHIFT_TWO, B_IN = range(9)
+
+
+def row(ref, n):
+    return ref[n : n + 1, :]
+
+
+class Vectors:
+    def __init__(self, place, vectors, *wait):
+        flat = jnp.concatenate([after(vectors[0], *wait), *vectors[1:]])
+        own = jnp.pad(flat.reshape(-1, LANES), ((0, -(flat.shape[0] // LANES) % 16), (0, 0)))
+        own = jnp.stack([own, place.swap_core(own)])
+        pair = jnp.stack([own, place.swap_chip(own, 0)])
+        self.slots = jnp.concatenate([pair, place.swap_chip(pair, 1)])
+        self.place = place
+
+    def unpack(self):
+        place = self.place
+        slots, sides, rows, lanes = self.slots.shape
+        shards = place.shards
+
+        def kernel(where, in_ref, rows_ref, inner_ref, qkv_ref):
+            width = shards * lanes
+            qkv_ref[...] = jnp.zeros_like(qkv_ref)
+            for slot in range(slots):
+                for side in range(sides):
+                    core = where[0] ^ side
+                    shard = (where[1] ^ turn(slot, where[0])) * 2 + core
+                    part = in_ref[slot, side].astype(jnp.float32)
+                    at = pl.multiple_of(shard * lanes, lanes)
+                    rows_ref[:, pl.ds(at, lanes)] = part
+                    qkv_ref[:, pl.ds(at, lanes)] = part[B_QUERY : B_QUERY + 1]
+                    qkv_ref[:, pl.ds(2 * width + at, lanes)] = part[B_VALUE : B_VALUE + 1]
+                    for n in range(4):
+                        start = pl.multiple_of((shard * 4 + n) * lanes, lanes)
+                        inner_ref[:, pl.ds(start, lanes)] = part[B_IN + n : B_IN + n + 1]
+
+        in_vmem = pl.BlockSpec(memory_space=pltpu.VMEM)
+        return pl.pallas_call(
+            kernel,
+            in_specs=[pl.BlockSpec(memory_space=pltpu.SMEM), in_vmem],
+            out_specs=[in_vmem] * 3,
+            out_shape=[
+                shaped((rows, shards * lanes), jnp.float32),
+                shaped((1, 4 * shards * lanes), jnp.float32),
+                shaped((1, 3 * shards * lanes), jnp.float32),
+            ],
+            name="vectors",
+        )(place.scalars, self.slots)
+
+
+def pack_sums(late_a, late_b, first_sums, second_sums, inner_sums):
+    width = first_sums.shape[1]
+    half = late_a.shape[1]
+
+    def kernel(a_ref, b_ref, one_ref, two_ref, inner_ref, out_ref):
+        out_ref[...] = jnp.zeros_like(out_ref)
+        out_ref[0:2, 0:half] = a_ref[...]
+        out_ref[0:2, half:width] = b_ref[...]
+        for n, source in (
+            (GAIN_ONE, one_ref[0:1, :]),
+            (SHIFT_ONE, one_ref[1:2, :]),
+            (B_ATTN, one_ref[2:3, :]),
+            (GAIN_TWO, two_ref[0:1, :]),
+            (SHIFT_TWO, two_ref[1:2, :]),
+            (B_OUT, two_ref[2:3, :]),
+        ):
+            out_ref[n : n + 1, :] = source
+        for n in range(4):
+            out_ref[B_IN + n : B_IN + n + 1, :] = inner_ref[:, n * width : (n + 1) * width]
+
+    in_vmem = pl.BlockSpec(memory_space=pltpu.VMEM)
+    return pl.pallas_call(
+        kernel,
+        in_specs=[in_vmem] * 5,
+        out_specs=in_vmem,
+        out_shape=shaped((16, width), jnp.float32),
+        name="pack_sums",
+    )(late_a, late_b, first_sums, second_sums, inner_sums)
+
+
 def project_qkv(place, rows, window, bias, scale):
     length, width = rows.shape
     cols = window.cols
@@ -762,23 +847,24 @@
         sum_ref[n : n + 1, :] += jnp.sum(term, 0, keepdims=True)
 
 
-def project_out(place, contexts, window, rows, bias, gain, shift):
+def project_out(place, contexts, window, rows, vectors):
     length, width = rows.shape
 
-    def kernel(where, ready, weight, c_ref, x_ref, b_ref, g_ref, s_ref, n_ref, r_ref, low_ref):
+    def kernel(where, ready, weight, c_ref, x_ref, v_ref, n_ref, r_ref, low_ref):
         ready()
-        first_sum = mxu(c_ref[...], weight[...], NN) + b_ref[...] + x_ref[...].astype(jnp.float32)
+        first_sum = mxu(c_ref[...], weight[...], NN) + row(v_ref, B_ATTN)
+        first_sum = first_sum + x_ref[...].astype(jnp.float32)
         normed, scale = norm_parts(first_sum)
         n_ref[...] = normed
         r_ref[...] = jnp.broadcast_to(scale, r_ref.shape)
-        low_ref[...] = (normed * g_ref[...] + s_ref[...]).astype(jnp.bfloat16)
+        low_ref[...] = (normed * row(v_ref, GAIN_ONE) + row(v_ref, SHIFT_ONE)).astype(jnp.bfloat16)
 
     return weight_call(
         place,
         kernel,
         window,
-        (contexts, rows, bias, gain, shift),
-        [row_tiles(width), row_tiles(width)] + [fixed(1, width)] * 3,
+        (contexts, rows, vectors),
+        [row_tiles(width), row_tiles(width), fixed(*vectors.shape)],
         [
             shaped((length, width), jnp.float32),
             shaped((length, LANES), jnp.float32),
@@ -828,15 +914,16 @@
     length, inner = hidden.shape
     width = normed.shape[1]
 
-    def kernel(where, ready, weight, h_ref, n_ref, cot_ref, keep_ref, g1, s1, b2, g2, s2, *outs):
+    def kernel(where, ready, weight, h_ref, n_ref, cot_ref, keep_ref, v_ref, *outs):
         out_ref, grad_ref, low_ref, sum_ref = outs
         ready()
         fed = mxu(h_ref[...], weight[...], NN)
-        second_sum = n_ref[...] * g1[...] + s1[...] + (fed + b2[...])
+        normed_one = n_ref[...] * row(v_ref, GAIN_ONE) + row(v_ref, SHIFT_ONE)
+        second_sum = normed_one + (fed + row(v_ref, B_OUT))
         second, scale = norm_parts(second_sum)
-        out_ref[...] = (second * g2[...] + s2[...]).astype(jnp.bfloat16)
+        out_ref[...] = (second * row(v_ref, GAIN_TWO) + row(v_ref, SHIFT_TWO)).astype(jnp.bfloat16)
         masked = cot_ref[...].astype(jnp.float32) * keep_ref[...]
-        grad = norm_back(masked * g2[...], second, scale)
+        grad = norm_back(masked * row(v_ref, GAIN_TWO), second, scale)
         grad_ref[...] = grad
         low_ref[...] = grad.astype(jnp.bfloat16)
         add_rows(sum_ref, masked * second, masked, grad)
@@ -845,8 +932,8 @@
         place,
         kernel,
         window,
-        (hidden, normed, cot, keep, *vectors),
-        [row_tiles(inner), row_tiles(width), row_tiles(width), row_tiles(1)] + [fixed(1, width)] * 5,
+        (hidden, normed, cot, keep, vectors),
+        [row_tiles(inner), row_tiles(width), row_tiles(width), row_tiles(1), fixed(*vectors.shape)],
         [
             shaped((length, width), jnp.bfloat16),
             shaped((length, width), jnp.float32),
@@ -888,27 +975,27 @@
     )
 
 
-def feed_in_back(pre_low, weight, second_grad, normed, scale, gain):
+def feed_in_back(pre_low, weight, second_grad, normed, scale, vectors):
     length, inner = pre_low.shape
     width = normed.shape[1]
 
-    def kernel(p_ref, w_ref, g_ref, n_ref, r_ref, gain_ref, first_ref, low_ref, sum_ref):
+    def kernel(p_ref, w_ref, g_ref, n_ref, r_ref, v_ref, first_ref, low_ref, sum_ref):
         grad = g_ref[...] + mxu(p_ref[...], w_ref[...], NT)
-        first = norm_back(grad * gain_ref[...], n_ref[...], r_ref[:, :1])
+        first = norm_back(grad * row(v_ref, GAIN_ONE), n_ref[...], r_ref[:, :1])
         first_ref[...] = first
         low_ref[...] = first.astype(jnp.bfloat16)
         add_rows(sum_ref, grad * n_ref[...], grad, first)
 
     return plain_call(
         kernel,
-        (pre_low, weight, second_grad, normed, scale, gain),
+        (pre_low, weight, second_grad, normed, scale, vectors),
         [
             row_tiles(inner),
             whole_once(weight.shape),
             row_tiles(width),
             row_tiles(width),
             row_tiles(LANES),
-            fixed(1, width),
+            fixed(*vectors.shape),
         ],
         [
             shaped((length, width), jnp.float32),
@@ -1171,15 +1258,6 @@
         return ordered
 
 
-def sum_everywhere(place, vector):
-    vector = vector + place.swap_core(vector)
-    for step in range(2):
-        vector = vector + place.swap_grp(vector, step)
-    for step in range(2):
-        vector = vector + place.swap_chip(vector, step)
-    return vector
-
-
 def own_part(place, vector):
     size = vector.shape[0] // place.shards
     return lax.dynamic_slice_in_dim(vector, place.shard * size, size)
@@ -1209,17 +1287,6 @@
 ):
     place = Place(groups, shards)
     _, length, width = tokens.shape
-    vectors = (
-        b_query,
-        b_value,
-        b_attn_out,
-        norm1_gain,
-        norm1_bias,
-        b_in,
-        b_out,
-        norm2_gain,
-        norm2_bias,
-    )
     rows = tokens[0]
     seg_row = segment_ids.reshape(1, length)
     seg_col = segment_ids.reshape(length, 1)
@@ -1227,90 +1294,64 @@
     pairs = width // LANES
 
     c1 = Gather(place, w_qkv)
-    wait = c1.chips_near()
-    block = jnp.concatenate([w_in, w_attn_out], 1)
-    flat = jnp.concatenate([after(vectors[0], wait), *vectors[1:]])
-    extra = 16
-    flat = jnp.pad(flat, (0, extra * block.shape[1] - flat.shape[0])).reshape(extra, -1)
-    c2 = Gather(place, jnp.concatenate([block, flat], 0))
+    c2 = Gather(place, jnp.concatenate([w_in, w_attn_out], 1))
     c3 = Gather(place, w_out)
+    c1.chips_near()
     c1.chips_far()
-    near = c1.near()
+    joined = c1.join()
+    c1.near()
+    c2.chips_near(joined)
+    small = Vectors(
+        place,
+        (b_query, b_value, b_attn_out, norm1_gain, norm1_bias, b_out, norm2_gain, norm2_bias, b_in),
+        c1.pair[1],
+    )
     c1.cross(0)
-    c2.chips_near(c1.held[0])
     far = c1.far()
-    c2.chips_far(near)
-    rider = c2.held[0][:, -extra:]
-    c2.held[0] = c2.held[0][:, :-extra]
-    both = [rider, place.swap_core(rider)]
-    c1.cross(1)
-    c1.cross(2)
-    c2.near(far)
-
-    def owner(shard):
-        found = both[0][0]
-        for side in range(2):
-            for slot in range(4):
-                here = (place.chip ^ turn(slot, place.core ^ side)) * 2 + (place.core ^ side)
-                found = jnp.where(here == shard, both[side][slot], found)
-        return found.reshape(-1)
-
-    parts = [owner(shard).astype(jnp.float32) for shard in range(shards)]
-    unpacked = []
-    at = 0
-    for vector in vectors:
-        size = vector.shape[0]
-        unpacked.append(jnp.concatenate([p[at : at + size] for p in parts]).reshape(1, -1))
-        at += size
-    (
-        bias_query,
-        bias_value,
-        bias_attn,
-        gain_one,
-        shift_one,
-        bias_in,
-        bias_out,
-        gain_two,
-        shift_two,
-    ) = unpacked
-    blank = jnp.zeros_like(bias_query)
-    qkv_bias = jnp.concatenate([bias_query, blank, bias_value], 1)
-    qkv_scale = jnp.concatenate([blank + 1.0 / math.sqrt(HD), blank + 1.0, blank + 1.0], 1)
+    c2.chips_far()
+    c1.cross(1, 2)
+    c1.cross(3)
+    c2.join(far)
+    c2.near()
+    vectors, bias_in, qkv_bias = small.unpack()
+    blank = jnp.ones((1, width), jnp.float32)
+    qkv_scale = jnp.concatenate([blank / math.sqrt(HD), blank, blank], 1)
 
     mixed, full_qkv = project_qkv(place, rows, Window(c1, 0, w_qkv.shape[1]), qkv_bias, qkv_scale)
-    c2.far(mixed)
-    c2.cross(0, 1, wait=(mixed,))
     c3.chips_near(mixed)
+    c2.cross(0, wait=(mixed,))
     quarter = pairs // 4
     forward = None
     for n in range(4):
-        gate = ((), (c3.pair,), (c3.held[0],), (c2.held[2],))[n]
+        gate = ()
+        if n == 2:
+            gate = (c3.rest[1],)
+        if n == 3:
+            gate = (c2.held[3],)
         forward = attention_forward(
             after(mixed, *gate) if gate else mixed, seg_col, seg_row, n * quarter, quarter, forward
         )
+        done = forward[1]
         if n == 0:
-            c3.chips_far(forward[1])
+            c3.chips_far(done)
+            c2.far(done)
+            c2.cross(1, 2, wait=(done,))
         if n == 2:
-            c2.cross(2, wait=(forward[1],))
-            c3.near(forward[1], c2.held[2])
+            c2.cross(3, wait=(done,))
+            c3.join(done)
+            c3.near()
     contexts, lse = forward
     normed, scale_one, normed_low, full_attn = project_out(
-        place, contexts, Window(c2, w_in.shape[1], w_attn_out.shape[1]), rows, bias_attn, gain_one, shift_one
+        place, contexts, Window(c2, w_in.shape[1], w_attn_out.shape[1]), rows, vectors
     )
     c3.far(normed_low)
-    c3.cross(0, 1, wait=(normed_low,))
+    c3.cross(0, 1, 2, wait=(normed_low,))
     hidden, slope, full_in = feed_in(
         place, after(normed_low, c3.held[1]), Window(c2, 0, w_in.shape[1]), bias_in
     )
-    c3.cross(2, wait=(hidden,))
+    c3.cross(3, wait=(hidden,))
     layer_out, second_grad, out_low, second_sums, full_out = feed_out(
-        place,
-        hidden,
-        Window(c3, 0, w_out.shape[1]),
-        normed,
-        cotangent[0],
-        keep,
-        (gain_one, shift_one, bias_out, gain_two, shift_two),
+        place, hidden, Window(c3, 0, w_out.shape[1]), normed, cotangent[0], keep, vectors
     )
 
     r_out = Reduction(place, [(hidden, out_low)], False, "out")
@@ -1318,7 +1359,7 @@
     own_out = r_out.own(pre_low)
     r_in = Reduction(place, [(normed_low, pre_low)], True, "in", own_out)
     first_grad, attn_low, first_sums = feed_in_back(
-        after(pre_low, r_in.sent), full_in, second_grad, normed, scale_one, gain_one
+        after(pre_low, r_in.sent), full_in, second_grad, normed, scale_one, vectors
     )
     mid_out = r_out.middle(first_grad)
     own_in = r_in.own(first_grad, mid_out)
@@ -1352,7 +1393,9 @@
     low_b, late_b = back(3 * quarter, quarter, part, own_a)
     mid_a = r_a.middle(late_b)
     along = r_in.along_far(late_b)
-    r_b = Reduction(place, [(rows, low_b)], True, "b", mid_a, along)
+    sums = pack_sums(late_a, late_b, first_sums, second_sums, bias_in_grad)
+    r_b = Reduction(place, [(rows, low_b)], True, "b", mid_a, along, sums)
+    sums = sums + place.swap_core(sums)
     along = r_a.along(r_b.sent)
     share_in = r_in.share(r_b.sent)
     inner = share_in.shape[1] // groups
@@ -1360,35 +1403,26 @@
         [share_out] + [share_in[:, n * inner : (n + 1) * inner] for n in range(groups)]
     )
     all_ffn = Replication(place, joined)
-    own_b = r_b.own(along, share_in)
-    input_grad = project_qkv_back((low_a, after(low_b, own_b)), full_qkv, first_grad)
-    r_b.middle(input_grad)
-    all_ffn.far(input_grad)
-    r_a.along_far(input_grad)
-    r_b.along()
-    all_a = Replication(place, r_a.share())
-    r_b.along_far()
-    all_a.far()
+    own_b = r_b.own(along, joined, sums)
+    sums = after(sums, own_b)
+    sums = sums + place.swap_grp(after(sums, own_b), 0)
+    along = r_a.along_far(own_b)
+    input_grad = project_qkv_back(
+        (low_a, after(low_b, own_b, along, all_ffn.pair)), full_qkv, first_grad
+    )
+    mid_b = r_b.middle(input_grad)
+    sums = sums + place.swap_grp(after(sums, mid_b), 1)
+    all_ffn.far(mid_b)
+    all_a = Replication(place, r_a.share(mid_b))
+    along = r_b.along()
+    sums = sums + place.swap_chip(after(sums, along), 0)
+    all_a.far(along)
+    along = r_b.along_far()
+    sums = sums + place.swap_chip(after(sums, along), 1)
     all_b = Replication(place, r_b.share())
     all_b.far()
-
-    sums = (
-        jnp.concatenate([late_a[0], late_b[0]]),
-        jnp.concatenate([late_a[1], late_b[1]]),
-        first_sums[2],
-        first_sums[0],
-        first_sums[1],
-        bias_in_grad[0],
-        second_sums[2],
-        second_sums[0],
-        second_sums[1],
-    )
-    summed = sum_everywhere(place, jnp.concatenate(sums).reshape(-1, LANES)).reshape(-1)
-    vectors = []
-    at = 0
-    for vector in sums:
-        vectors.append(own_part(place, summed[at : at + vector.shape[0]]))
-        at += vector.shape[0]
+    mine = lax.dynamic_slice_in_dim(sums, place.shard * LANES, LANES, 1)
+    inner_mine = own_part(place, sums[B_IN : B_IN + 4].reshape(-1))
 
     parts_a, parts_b = all_a.result(), all_b.result()
     heads = parts_b[0].shape[1] // 3
@@ -1420,18 +1454,18 @@
         layer_out[None],
         input_grad[None],
         w_qkv_grad,
-        vectors[0],
-        vectors[1],
+        mine[B_QUERY],
+        mine[B_VALUE],
         w_attn_grad,
-        vectors[2],
-        vectors[3],
-        vectors[4],
+        mine[B_ATTN],
+        mine[GAIN_ONE],
+        mine[SHIFT_ONE],
         w_in_grad,
-        vectors[5],
+        inner_mine,
         w_out_grad,
-        vectors[6],
-        vectors[7],
-        vectors[8],
+        mine[B_OUT],
+        mine[GAIN_TWO],
+        mine[SHIFT_TWO],
     )
 
 

time: 576 us -> 512 us (0.89)
  local copies, waits for them, and re-layouts: 47.4 us -> 9.78 us
  waiting for transfers between devices: 125 us -> 88.5 us
  starting transfers between devices: 53 us -> 61.4 us
    ppermute x53 -> x61, waiting for transfers between devices: 125 us -> 88.5 us  [permute(): return lax.ppermute(array, AXES, pairs)]
    unnamed x153 -> x121, local copies, waits for them, and re-layouts: 31.2 us -> 5.31 us
    ppermute x53 -> x61, starting transfers between devices: 53 us -> 61.4 us  [permute(): return lax.ppermute(array, AXES, pairs)]
    concatenate x8 -> x5, other arithmetic: 10.9 us -> 3.9 us  [the longest x3 3.25 us: join(): self.held[0] = jnp.concatenate([self.rest[0], rest])]
  transfers between devices with their start and end apart: 53 -> 61, of which waited for: 26 -> 21; matrix products, arithmetic and copies ran while one was open for 12% -> 6% of each run, Pallas kernels for 39% -> 46%
where the time goes in v5:
time: 512 us; the launch traced here: 503 us
  Pallas kernels  311 us (61%)
  waiting for transfers between devices  88.5 us (17%)
  starting transfers between devices  61.4 us (12%)
  other arithmetic  30.4 us (6%)
  local copies, waits for them, and re-layouts  9.78 us (2%)
    ppermute x61, waiting for transfers between devices, permute(): return lax.ppermute(array, AXES, pairs)  88.5 us
    pallas_call x8, Pallas kernels, weight_grad(): pl.pallas_call(functools.partial(weight_grad_kernel, own=own, rows=rows,...  87.7 us
    pallas_call x4, Pallas kernels, weight_call(): pl.pallas_call(body, grid_spec=pltpu.PrefetchScalarGridSpec(num_scalar_pr...  66.5 us
    pallas_call x4, Pallas kernels, attention_backward(): pl.pallas_call(body, grid=(pairs,), in_specs=[pair(0), pair(1), pair(2),...  63.7 us
    ppermute x61, starting transfers between devices, permute(): return lax.ppermute(array, AXES, pairs)  61.4 us
    pallas_call x4, Pallas kernels, plain_call(): pl.pallas_call(kernel, grid=(steps,), in_specs=in_specs, out_specs=out_sp...  50.8 us
    pallas_call x4, Pallas kernels, attention_forward(): pl.pallas_call(body, grid=(pairs,), in_specs=[pair(0), pair(1), pair(2),...  39.7 us
    convert_element_type x15, other arithmetic, add(): return total.astype(jnp.bfloat16)  16.8 us
  transfers between devices with their start and end apart: 61, of which 21 were waited for; matrix products, arithmetic and copies ran while one was open for 6% of the time, Pallas kernels for 46%

profile of v5, /device:TPU:0, one launch (start us, length us, event | category | flops | bytes accessed | tf_op | source)
XLA Modules:
  0.0 503.4 jit_solution(16290621717209261529)
XLA Ops:
  0.7 3.1 collective-permute-start
  3.8 5.6 %collective-permute-done = bf16[128,768]{1,0:T(8,128)(2,1)S(1)} collective-permute-done((bf16[128,768]{1,0:T(8,128)(2,1)}, bf16[128,768]{1,0:T(8,128)(2,1)S(1)}, u32[]{:S(2)}, u32[]{:S(2)}) %collective-permute-start) | collective-permute-done | bytes 196640 | tf_op jit(solution)/shard_map/ppermute | solution.py:526
  10.5 2.5 collective-permute-start.1
  12.9 8.8 %collective-permute-done.1 = bf16[2,128,768]{2,1,0:T(8,128)(2,1)S(1)} collective-permute-done((bf16[2,128,768]{2,1,0:T(8,128)(2,1)S(1)}, bf16[2,128,768]{2,1,0:T(8,128)(2,1)S(1)}, u32[]{:S(2)}, u32[]{:S(2)}) %collective-permute-start.1) | collective-permute-done | bytes 393248 | tf_op jit(solution)/shard_map/ppermute | solution.py:526
  22.8 2.3 collective-permute-start.2
  25.2 1.9 collective-permute-start.16
  28.6 13.7 %collective-permute-done.2.refs_1_ = bf16[4,128,768]{2,1,0:T(8,128)(2,1)} collective-permute-done((bf16[4,128,768]{2,1,0:T(8,128)(2,1)S(1)}, bf16[4,128,768]{2,1,0:T(8,128)(2,1)}, u32[]{:S(2)}, u32[]{:S(2)}) %collective-permute-start.2) | collective-permute-done | bytes 786464 | tf_op jit(solution)/shard_map/ppermute | solution.py:526
  42.4 3.3 collective-permute-start.4
  50.2 3.3 collective-permute-start.10
  53.5 2.1 collective-permute-done.10
  55.6 3.6 collective-permute-start.6
  59.7 4.9 collective-permute-done.17
  64.8 4.5 collective-permute-done.11
  74.5 12.9 %qkv.1 = (bf16[1024,3072]{1,0:T(8,128)(2,1)}, bf16[1024,3072]{1,0:T(8,128)(2,1)}) custom-call(s32[3]{0:T(128)} %pad_add_fusion.where, bf16[4,128,768]{2,1,0:T(8,128)(2,1)} %copy-done.11, bf16[4,128,768]{2,1,0:T(8,128)(2,1)} %collective-permute-done.2.refs_1_, bf16[4,128,768]{2,1,0:T(8,128)(2,1)} %collective-permute-done.3.refs_2_, ...), custom_call_target="tpu_custom_call" | custom-call | flops 6442450944 | bytes 20996096 | tf_op jit(solution)/shard_map/qkv/pallas_call | solution.py:662
  87.5 9.8 %attn_fwd.4 = (bf16[1024,1024]{1,0:T(8,128)(2,1)}, f32[8,2,1024]{2,1,0:T(2,128)}) custom-call(bf16[1024,3072]{1,0:T(8,128)(2,1)} %get-tuple-element.134.q_ref.k_ref.v_ref.refs_0_.refs_1_.refs_2_, bf16[1024,3072]{1,0:T(8,128)(2,1)} %get-tuple-element.134.q_ref.k_ref.v_ref.refs_0_.refs_1_.refs_2_, ...), custom_call_target="tpu_custom_call" | custom-call | flops 4294967296 | bytes 2097152 | tf_op jit(solution)/shard_map/attn_fwd/pallas_call | solution.py:385
  97.3 3.7 collective-permute-done.18.refs_1_
  102.8 10.3 %attn_fwd.5 = (bf16[1024,1024]{1,0:T(8,128)(2,1)}, f32[8,2,1024]{2,1,0:T(2,128)}) custom-call(bf16[1024,3072]{1,0:T(8,128)(2,1)} %get-tuple-element.134.q_ref.k_ref.v_ref.refs_0_.refs_1_.refs_2_, bf16[1024,3072]{1,0:T(8,128)(2,1)} %get-tuple-element.134.q_ref.k_ref.v_ref.refs_0_.refs_1_.refs_2_, ...), custom_call_target="tpu_custom_call", output_to_operand_aliasing={{0}: (5, {}), {1}: (6, {})} | custom-call | flops 4294967296 | bytes 2097152 | tf_op jit(solution)/shard_map/attn_fwd/pallas_call | solution.py:385
  113.2 3.5 collective-permute-done.13
  116.7 9.8 %attn_fwd.6 = (bf16[1024,1024]{1,0:T(8,128)(2,1)}, f32[8,2,1024]{2,1,0:T(2,128)}) custom-call(bf16[1024,3072]{1,0:T(8,128)(2,1)} %get-tuple-element.134.q_ref.k_ref.v_ref.refs_0_.refs_1_.refs_2_, bf16[1024,3072]{1,0:T(8,128)(2,1)} %get-tuple-element.134.q_ref.k_ref.v_ref.refs_0_.refs_1_.refs_2_, ...), custom_call_target="tpu_custom_call", output_to_operand_aliasing={{0}: (5, {}), {1}: (6, {})} | custom-call | flops 4294967296 | bytes 2097152 | tf_op jit(solution)/shard_map/attn_fwd/pallas_call | solution.py:385
  126.6 2.1 pad_maximum_fusion.2.refs_0_
  129.9 1.9 collective-permute-start.15
  131.8 9.8 %attn_fwd.7 = (bf16[1024,1024]{1,0:T(8,128)(2,1)}, f32[8,2,1024]{2,1,0:T(2,128)}) custom-call(bf16[1024,3072]{1,0:T(8,128)(2,1)} %get-tuple-element.134.q_ref.k_ref.v_ref.refs_0_.refs_1_.refs_2_, bf16[1024,3072]{1,0:T(8,128)(2,1)} %get-tuple-element.134.q_ref.k_ref.v_ref.refs_0_.refs_1_.refs_2_, ...), custom_call_target="tpu_custom_call", output_to_operand_aliasing={{0}: (5, {}), {1}: (6, {})} | custom-call | flops 4294967296 | bytes 2097152 | tf_op jit(solution)/shard_map/attn_fwd/pallas_call | solution.py:385
  141.6 9.8 %attn_out.1 = (f32[1024,1024]{1,0:T(8,128)}, f32[1024,128]{1,0:T(8,128)}, bf16[1024,1024]{1,0:T(8,128)(2,1)}, bf16[1024,1024]{1,0:T(8,128)(2,1)}) custom-call(s32[3]{0:T(128)} %pad_add_fusion.where, bf16[4,128,1280]{2,1,0:T(8,128)(2,1)} %copy-done, bf16[4,128,1280]{2,1,0:T(8,128)(2,1)} %copy-done.4, bf16[4,128,1280]{2,1,0:T(8,128)(2,1)} %collective-permute-done.19.refs_2_, ...), custom_call_target="tpu_custom_call" | custom-call | flops 2147483648 | bytes 15269888 | tf_op jit(solution)/shard_map/attn_out/pallas_call | solution.py:662
  151.4 2.8 collective-permute-done.14.refs_1_
  154.2 2.1 collective-permute-start.25
  156.9 22.1 %feed_in.1 = (bf16[1024,4096]{1,0:T(8,128)(2,1)}, bf16[1024,4096]{1,0:T(8,128)(2,1)}, bf16[1024,4096]{1,0:T(8,128)(2,1)}) custom-call(s32[3]{0:T(128)} %pad_add_fusion.where, bf16[4,128,1280]{2,1,0:T(8,128)(2,1)} %copy-done, bf16[4,128,1280]{2,1,0:T(8,128)(2,1)} %copy-done.4, bf16[4,128,1280]{2,1,0:T(8,128)(2,1)} %collective-permute-done.19.refs_2_, ...), custom_call_target="tpu_custom_call" | custom-call | flops 8589934592 | bytes 35667968 | tf_op jit(solution)/shard_map/feed_in/pallas_call | solution.py:662
  182.1 21.6 %feed_out.1 = (bf16[1024,1024]{1,0:T(8,128)(2,1)}, f32[1024,1024]{1,0:T(8,128)}, bf16[1024,1024]{1,0:T(8,128)(2,1)}, f32[8,1024]{1,0:T(8,128)}, bf16[4096,1024]{1,0:T(8,128)(2,1)}) custom-call(s32[3]{0:T(128)} %pad_add_fusion.where, bf16[4,512,256]{2,1,0:T(8,128)(2,1)} %pad_maximum_fusion.2.refs_0_, bf16[4,512,256]{2,1,0:T(8,128)(2,1)} %collective-permute-done.14.refs_1_, ...), custom_call_target="tpu_custom_call" | custom-call | flops 8589934592 | bytes 39948288 | tf_op jit(solution)/shard_map/feed_out/pallas_call | solution.py:662
  203.7 10.0 %wgrad_out_sent.1 = bf16[4,4,512,256]{3,2,1,0:T(8,128)(2,1)} custom-call(s32[3]{0:T(128)} %pad_add_fusion.where, bf16[1024,4096]{1,0:T(8,128)(2,1)} %get-tuple-element.144.refs_8_.refs_0_, bf16[1024,1024]{1,0:T(8,128)(2,1)} %get-tuple-element.150.refs_1_.g_ref), custom_call_target="tpu_custom_call" | custom-call | flops 4294967296 | bytes 18874368 | tf_op jit(solution)/shard_map/wgrad_out_sent/pallas_call | solution.py:1166
  214.1 14.6 %feed_out_back.1 = (bf16[1024,4096]{1,0:T(8,128)(2,1)}, f32[1,4096]{1,0:T(1,128)}) custom-call(bf16[1024,1024]{1,0:T(8,128)(2,1)} %get-tuple-element.150.refs_1_.g_ref, bf16[4096,1024]{1,0:T(8,128)(2,1)} %get-tuple-element.151.w_ref, bf16[1024,4096]{1,0:T(8,128)(2,1)} %get-tuple-element.152.slope_ref), custom_call_target="tpu_custom_call" | custom-call | flops 8589934592 | bytes 27279360 | tf_op jit(solution)/shard_map/feed_out_back/pallas_call | solution.py:686
  228.7 10.5 %wgrad_out_own.1 = (bf16[4,512,256]{2,1,0:T(8,128)(2,1)}, bf16[4,512,256]{2,1,0:T(8,128)(2,1)}, bf16[2,4,512,256]{3,2,1,0:T(8,128)(2,1)}) custom-call(s32[3]{0:T(128)} %pad_add_fusion.where, bf16[1024,4096]{1,0:T(8,128)(2,1)} %get-tuple-element.144.refs_8_.refs_0_, bf16[1024,1024]{1,0:T(8,128)(2,1)} %get-tuple-element.150.refs_1_.g_ref, ...), custom_call_target="tpu_custom_call" | custom-call | flops 4294967296 | bytes 18874368 | tf_op jit(solution)/shard_map/wgrad_out_own/pallas_call | solution.py:1166
  239.2 10.4 %wgrad_in_sent.1 = bf16[4,4,128,1024]{3,2,1,0:T(8,128)(2,1)} custom-call(s32[3]{0:T(128)} %pad_add_fusion.where, bf16[1024,1024]{1,0:T(8,128)(2,1)} %get-tuple-element.156.refs_8_.refs_0_, bf16[1024,4096]{1,0:T(8,128)(2,1)} %get-tuple-element.157.refs_1_.p_ref), custom_call_target="tpu_custom_call" | custom-call | flops 4294967296 | bytes 18874368 | tf_op jit(solution)/shard_map/wgrad_in_sent/pallas_call | solution.py:1166
  251.1 17.7 %feed_in_back.1 = (f32[1024,1024]{1,0:T(8,128)}, bf16[1024,1024]{1,0:T(8,128)(2,1)}, f32[8,1024]{1,0:T(8,128)}) custom-call(bf16[1024,4096]{1,0:T(8,128)(2,1)} %get-tuple-element.157.refs_1_.p_ref, bf16[1024,4096]{1,0:T(8,128)(2,1)} %get-tuple-element.158.w_ref, f32[1024,1024]{1,0:T(8,128)} %get-tuple-element.159.g_ref, ...), custom_call_target="tpu_custom_call" | custom-call | flops 8589934592 | bytes 32079872 | tf_op jit(solution)/shard_map/feed_in_back/pallas_call | solution.py:686
  268.7 7.2 %collective-permute-done.32 = bf16[2,4,512,256]{3,2,1,0:T(8,128)(2,1)S(1)} collective-permute-done((bf16[2,4,512,256]{3,2,1,0:T(8,128)(2,1)}, bf16[2,4,512,256]{3,2,1,0:T(8,128)(2,1)S(1)}, u32[]{:S(2)}, u32[]{:S(2)}) %collective-permute-start.32) | collective-permute-done | bytes 2097184 | tf_op jit(solution)/shard_map/ppermute | solution.py:526
  277.4 12.4 %wgrad_in_own.1 = (bf16[4,128,1024]{2,1,0:T(8,128)(2,1)}, bf16[4,128,1024]{2,1,0:T(8,128)(2,1)}, bf16[2,4,128,1024]{3,2,1,0:T(8,128)(2,1)}) custom-call(s32[3]{0:T(128)} %pad_add_fusion.where, bf16[1024,1024]{1,0:T(8,128)(2,1)} %get-tuple-element.156.refs_8_.refs_0_, bf16[1024,4096]{1,0:T(8,128)(2,1)} %get-tuple-element.157.refs_1_.p_ref, ...), custom_call_target="tpu_custom_call" | custom-call | flops 4294967296 | bytes 18874368 | tf_op jit(solution)/shard_map/wgrad_in_own/pallas_call | solution.py:1166
  291.2 6.1 %attn_out_back.1.refs_4_ = bf16[1024,1024]{1,0:T(8,128)(2,1)} custom-call(bf16[1024,1024]{1,0:T(8,128)(2,1)} %get-tuple-element.168.g_ref.refs_2_, bf16[1024,1024]{1,0:T(8,128)(2,1)} %get-tuple-element.169.w_ref), custom_call_target="tpu_custom_call" | custom-call | flops 2147483648 | bytes 6291456 | tf_op jit(solution)/shard_map/attn_out_back/pallas_call | solution.py:686
  297.3 16.0 %attn_bwd.4 = (bf16[3,1024,512]{2,1,0:T(8,128)(2,1)}, f32[2,512]{1,0:T(2,128)}) custom-call(bf16[1024,3072]{1,0:T(8,128)(2,1)} %get-tuple-element.134.q_ref.k_ref.v_ref.refs_0_.refs_1_.refs_2_, bf16[1024,3072]{1,0:T(8,128)(2,1)} %get-tuple-element.134.q_ref.k_ref.v_ref.refs_0_.refs_1_.refs_2_, ...), custom_call_target="tpu_custom_call" | custom-call | flops 10737418240 | bytes 4194304 | tf_op jit(solution)/shard_map/attn_bwd/pallas_call | solution.py:480
  313.2 1.6 fusion.4
  315.1 16.1 %attn_bwd.5 = (bf16[3,1024,512]{2,1,0:T(8,128)(2,1)}, f32[2,512]{1,0:T(2,128)}) custom-call(bf16[1024,3072]{1,0:T(8,128)(2,1)} %get-tuple-element.134.q_ref.k_ref.v_ref.refs_0_.refs_1_.refs_2_, bf16[1024,3072]{1,0:T(8,128)(2,1)} %get-tuple-element.134.q_ref.k_ref.v_ref.refs_0_.refs_1_.refs_2_, ...), custom_call_target="tpu_custom_call", output_to_operand_aliasing={{0}: (8, {}), {1}: (9, {})} | custom-call | flops 10737418240 | bytes 4194304 | tf_op jit(solution)/shard_map/attn_bwd/pallas_call | solution.py:480
  331.3 1.6 fusion.2
  333.0 10.3 %wgrad_a_sent.1 = bf16[4,4,128,640]{3,2,1,0:T(8,128)(2,1)} custom-call(s32[3]{0:T(128)} %pad_add_fusion.where, bf16[1024,1024]{1,0:T(8,128)(2,1)} %get-tuple-element.181.refs_8_.refs_3_.refs_0_, bf16[1024,1024]{1,0:T(8,128)(2,1)} %bitcast.161, bf16[1024,1024]{1,0:T(8,128)(2,1)} %get-tuple-element.168.g_ref.refs_2_, ...), custom_call_target="tpu_custom_call" | custom-call | flops 2684354560 | bytes 12582912 | tf_op jit(solution)/shard_map/wgrad_a_sent/pallas_call | solution.py:1166
  343.2 2.2 collective-permute-start.38
  345.4 2.0 collective-permute-start.37
  347.4 15.8 %attn_bwd.6 = (bf16[3,1024,512]{2,1,0:T(8,128)(2,1)}, f32[2,512]{1,0:T(2,128)}) custom-call(bf16[1024,3072]{1,0:T(8,128)(2,1)} %get-tuple-element.134.q_ref.k_ref.v_ref.refs_0_.refs_1_.refs_2_, bf16[1024,3072]{1,0:T(8,128)(2,1)} %get-tuple-element.134.q_ref.k_ref.v_ref.refs_0_.refs_1_.refs_2_, ...), custom_call_target="tpu_custom_call" | custom-call | flops 10737418240 | bytes 4194304 | tf_op jit(solution)/shard_map/attn_bwd/pallas_call | solution.py:480
  363.4 2.5 fusion.1
  365.9 15.9 %wgrad_a_own.1 = (bf16[4,128,640]{2,1,0:T(8,128)(2,1)}, bf16[4,128,640]{2,1,0:T(8,128)(2,1)}, bf16[2,4,128,640]{3,2,1,0:T(8,128)(2,1)}) custom-call(s32[3]{0:T(128)} %pad_add_fusion.where, bf16[1024,1024]{1,0:T(8,128)(2,1)} %get-tuple-element.181.refs_8_.refs_3_.refs_0_, bf16[1024,1024]{1,0:T(8,128)(2,1)} %bitcast.162, ...), custom_call_target="tpu_custom_call" | custom-call | flops 2684354560 | bytes 12582912 | tf_op jit(solution)/shard_map/wgrad_a_own/pallas_call | solution.py:1166
  383.3 15.8 %attn_bwd.7 = (bf16[3,1024,512]{2,1,0:T(8,128)(2,1)}, f32[2,512]{1,0:T(2,128)}) custom-call(bf16[1024,3072]{1,0:T(8,128)(2,1)} %get-tuple-element.134.q_ref.k_ref.v_ref.refs_0_.refs_1_.refs_2_, bf16[1024,3072]{1,0:T(8,128)(2,1)} %get-tuple-element.134.q_ref.k_ref.v_ref.refs_0_.refs_1_.refs_2_, ...), custom_call_target="tpu_custom_call", output_to_operand_aliasing={{0}: (8, {}), {1}: (9, {})} | custom-call | flops 10737418240 | bytes 4194304 | tf_op jit(solution)/shard_map/attn_bwd/pallas_call | solution.py:480
  400.6 2.8 collective-permute-start.43
  406.2 8.1 %wgrad_b_sent.1 = bf16[4,4,128,384]{3,2,1,0:T(8,128)(2,1)} custom-call(s32[3]{0:T(128)} %pad_add_fusion.where, bf16[1024,1024]{1,0:T(8,128)(2,1)} %bitcast.163, bf16[3,1024,512]{2,1,0:T(8,128)(2,1)} %get-tuple-element.205.refs_1_), custom_call_target="tpu_custom_call" | custom-call | flops 1610612736 | bytes 8388608 | tf_op jit(solution)/shard_map/wgrad_b_sent/pallas_call | solution.py:1166
  417.7 1.7 fusion.7
  420.4 5.7 %collective-permute-done.46 = bf16[1024,256]{1,0:T(8,128)(2,1)S(1)} collective-permute-done((bf16[1024,256]{1,0:T(8,128)(2,1)S(1)}, bf16[1024,256]{1,0:T(8,128)(2,1)S(1)}, u32[]{:S(2)}, u32[]{:S(2)}) %collective-permute-start.46) | collective-permute-done | bytes 524320 | tf_op jit(solution)/shard_map/ppermute | solution.py:526
  428.4 10.1 %wgrad_b_own.1 = (bf16[4,128,384]{2,1,0:T(8,128)(2,1)}, bf16[4,128,384]{2,1,0:T(8,128)(2,1)}, bf16[2,4,128,384]{3,2,1,0:T(8,128)(2,1)}) custom-call(s32[3]{0:T(128)} %pad_add_fusion.where, bf16[1024,1024]{1,0:T(8,128)(2,1)} %bitcast.164, bf16[3,1024,512]{2,1,0:T(8,128)(2,1)} %get-tuple-element.205.refs_1_, bf16[4,4,128,384]{3,2,1,0:T(8,128)(2,1)} %copy-done.3), custom_call_target="tpu_custom_call" | custom-call | flops 1610612736 | bytes 8388608 | tf_op jit(solution)/shard_map/wgrad_b_own/pallas_call | solution.py:1166
  439.2 1.6 fusion.18
  440.8 12.5 %qkv_back.1 = f32[1024,1024]{1,0:T(8,128)} custom-call(bf16[1024,3072]{1,0:T(8,128)(2,1)} %get-tuple-element.148.w_ref, bf16[3,1024,512]{2,1,0:T(8,128)(2,1)} %get-tuple-element.175.refs_3_.refs_0_, bf16[3,1024,512]{2,1,0:T(8,128)(2,1)} %get-tuple-element.205.refs_1_, f32[1024,1024]{1,0:T(8,128)} %get-tuple-element.162.refs_2_), custom_call_target="tpu_custom_call" | custom-call | flops 6442450944 | bytes 20971520 | tf_op jit(solution)/shard_map/qkv_back/pallas_call | solution.py:686
  456.1 4.6 collective-permute-done.56
  463.1 2.8 collective-permute-done.57
  471.8 1.7 collective-permute-start.60
  473.4 1.9 collective-permute-done.58
  476.5 1.9 collective-permute-done.49
  479.2 2.1 collective-permute-start.53
  482.6 3.2 collective-permute-done.53
  487.4 3.8 collective-permute-done.51
  492.3 1.7 collective-permute-start.55
  494.0 4.0 collective-permute-done.55
  501.1 1.8 pad_maximum_fusion
  (276 shorter events, 58.5 us)
Async XLA Ops:
  0.7 8.7 %collective-permute-start = (bf16[128,768]{1,0:T(8,128)(2,1)}, bf16[128,768]{1,0:T(8,128)(2,1)S(1)}, u32[]{:S(2)}, u32[]{:S(2)}) collective-permute-start(bf16[128,768]{1,0:T(8,128)(2,1)} %param.21), channel_id=1, source_target_pairs={{0,2},{1,5},{2,0},{3,7},{4,6},{5,1},{6,4},{7,3},{8,10},{9,13},{10,... | collective-permute-start | bytes 589832 | tf_op jit(solution)/shard_map/ppermute | solution.py:526
  9.4 39.6 %copy-start.23 = (bf16[512]{0:T(512)(128)(2,1)S(1)}, bf16[512]{0:T(512)(128)(2,1)}, u32[]{:S(2)}) copy-start(bf16[512]{0:T(512)(128)(2,1)} %param.29) | copy-start | bytes 3076
  10.5 11.3 %collective-permute-start.1 = (bf16[2,128,768]{2,1,0:T(8,128)(2,1)S(1)}, bf16[2,128,768]{2,1,0:T(8,128)(2,1)S(1)}, u32[]{:S(2)}, u32[]{:S(2)}) collective-permute-start(bf16[2,128,768]{2,1,0:T(8,128)(2,1)S(1)} %pad_maximum_fusion.10), channel_id=1, source_target_pairs={{0,4},{1,3},{2,6},{3,1},{4,0},{5,7},{6,2},{7,5},{8,12},{9,11},{10,... | collective-permute-start | bytes 1179656 | tf_op jit(solution)/shard_map/ppermute | solution.py:526
  22.8 42.0 %copy-start.11 = (bf16[4,128,768]{2,1,0:T(8,128)(2,1)}, bf16[4,128,768]{2,1,0:T(8,128)(2,1)S(1)}, u32[]{:S(2)}) copy-start(bf16[4,128,768]{2,1,0:T(8,128)(2,1)S(1)} %pad_maximum_fusion.4.refs_0_) | copy-start | bytes 2359300
  22.8 19.6 %collective-permute-start.2 = (bf16[4,128,768]{2,1,0:T(8,128)(2,1)S(1)}, bf16[4,128,768]{2,1,0:T(8,128)(2,1)}, u32[]{:S(2)}, u32[]{:S(2)}) collective-permute-start(bf16[4,128,768]{2,1,0:T(8,128)(2,1)S(1)} %pad_maximum_fusion.4.refs_0_), channel_id=1, source_target_pairs={{0,8},{1,17},{2,10},{3,19},{4,12},{5,21},{6,14},{7,23},{8,0},{9,25... | collective-permute-start | bytes 2359304 | tf_op jit(solution)/shard_map/ppermute | solution.py:526
  25.2 45.6 %copy-start.18 = (s32[1,1024]{1,0:T(1,128)S(1)}, s32[1,1024]{1,0:T(1,128)}, u32[]{:S(2)}) copy-start(s32[1,1024]{1,0:T(1,128)} %refs_6_.7) | copy-start | bytes 12292
  25.2 20.5 %collective-permute-start.16 = (bf16[128,1280]{1,0:T(8,128)(2,1)S(1)}, bf16[128,1280]{1,0:T(8,128)(2,1)S(1)}, u32[]{:S(2)}, u32[]{:S(2)}) collective-permute-start(bf16[128,1280]{1,0:T(8,128)(2,1)S(1)} %pad_maximum_fusion.11), channel_id=1, source_target_pairs={{0,2},{1,5},{2,0},{3,7},{4,6},{5,1},{6,4},{7,3},{8,10},{9,13},{10,... | collective-permute-start | bytes 983048 | tf_op jit(solution)/shard_map/ppermute | solution.py:526
  27.1 32.1 %collective-permute-start.3 = (bf16[4,128,768]{2,1,0:T(8,128)(2,1)S(1)}, bf16[4,128,768]{2,1,0:T(8,128)(2,1)}, u32[]{:S(2)}, u32[]{:S(2)}) collective-permute-start(bf16[4,128,768]{2,1,0:T(8,128)(2,1)S(1)} %pad_maximum_fusion.4.refs_0_), channel_id=1, source_target_pairs={{0,16},{1,9},{2,18},{3,11},{4,20},{5,13},{6,22},{7,15},{8,24},{9,1... | collective-permute-start | bytes 2359304 | tf_op jit(solution)/shard_map/ppermute | solution.py:526
  42.4 16.9 %collective-permute-start.4 = (bf16[4,128,768]{2,1,0:T(8,128)(2,1)}, bf16[4,128,768]{2,1,0:T(8,128)(2,1)}, u32[]{:S(2)}, u32[]{:S(2)}) collective-permute-start(bf16[4,128,768]{2,1,0:T(8,128)(2,1)} %collective-permute-done.2.refs_1_), channel_id=1, source_target_pairs={{0,16},{1,9},{2,18},{3,11},{4,20},{5,13},{6,22},{7,15},{8,24},{9,1... | collective-permute-start | bytes 2359304 | tf_op jit(solution)/shard_map/ppermute | solution.py:526
  45.8 18.9 %collective-permute-start.17 = (bf16[2,128,1280]{2,1,0:T(8,128)(2,1)S(1)}, bf16[2,128,1280]{2,1,0:T(8,128)(2,1)S(1)}, u32[]{:S(2)}, u32[]{:S(2)}) collective-permute-start(bf16[2,128,1280]{2,1,0:T(8,128)(2,1)S(1)} %pad_maximum_fusion.5), channel_id=1, source_target_pairs={{0,4},{1,3},{2,6},{3,1},{4,0},{5,7},{6,2},{7,5},{8,12},{9,11},{10,... | collective-permute-start | bytes 1966088 | tf_op jit(solution)/shard_map/ppermute | solution.py:526
  49.0 1.2 collective-permute-start.9
  50.2 5.3 %collective-permute-start.10 = (bf16[2,16,128]{2,1,0:T(8,128)(2,1)S(1)}, bf16[2,16,128]{2,1,0:T(8,128)(2,1)S(1)}, u32[]{:S(2)}, u32[]{:S(2)}) collective-permute-start(bf16[2,16,128]{2,1,0:T(8,128)(2,1)S(1)} %get-tuple-element.245), channel_id=1, source_target_pairs={{0,2},{1,5},{2,0},{3,7},{4,6},{5,1},{6,4},{7,3},{8,10},{9,13},{10,... | collective-permute-start | bytes 24584 | tf_op jit(solution)/shard_map/ppermute | solution.py:526
  53.5 20.9 %collective-permute-start.5 = (bf16[4,128,768]{2,1,0:T(8,128)(2,1)S(1)}, bf16[4,128,768]{2,1,0:T(8,128)(2,1)}, u32[]{:S(2)}, u32[]{:S(2)}) collective-permute-start(bf16[4,128,768]{2,1,0:T(8,128)(2,1)S(1)} %pad_maximum_fusion.4.refs_0_), channel_id=1, source_target_pairs={{0,1},{1,0},{2,3},{3,2},{4,5},{5,4},{6,7},{7,6},{8,9},{9,8},{10,11... | collective-permute-start | bytes 2359304 | tf_op jit(solution)/shard_map/ppermute | solution.py:526
  55.6 18.9 %collective-permute-start.6 = (bf16[4,128,768]{2,1,0:T(8,128)(2,1)}, bf16[4,128,768]{2,1,0:T(8,128)(2,1)}, u32[]{:S(2)}, u32[]{:S(2)}) collective-permute-start(bf16[4,128,768]{2,1,0:T(8,128)(2,1)} %collective-permute-done.2.refs_1_), channel_id=1, source_target_pairs={{0,1},{1,0},{2,3},{3,2},{4,5},{5,4},{6,7},{7,6},{8,9},{9,8},{10,11... | collective-permute-start | bytes 2359304 | tf_op jit(solution)/shard_map/ppermute | solution.py:526
  59.2 15.2 %collective-permute-start.7 = (bf16[4,128,768]{2,1,0:T(8,128)(2,1)}, bf16[4,128,768]{2,1,0:T(8,128)(2,1)}, u32[]{:S(2)}, u32[]{:S(2)}) collective-permute-start(bf16[4,128,768]{2,1,0:T(8,128)(2,1)} %collective-permute-done.3.refs_2_), channel_id=1, source_target_pairs={{0,1},{1,0},{2,3},{3,2},{4,5},{5,4},{6,7},{7,6},{8,9},{9,8},{10,11... | collective-permute-start | bytes 2359304 | tf_op jit(solution)/shard_map/ppermute | solution.py:526
  59.2 15.2 %collective-permute-start.8 = (bf16[4,128,768]{2,1,0:T(8,128)(2,1)}, bf16[4,128,768]{2,1,0:T(8,128)(2,1)}, u32[]{:S(2)}, u32[]{:S(2)}) collective-permute-start(bf16[4,128,768]{2,1,0:T(8,128)(2,1)} %collective-permute-done.4.refs_3_), channel_id=1, source_target_pairs={{0,1},{1,0},{2,3},{3,2},{4,5},{5,4},{6,7},{7,6},{8,9},{9,8},{10,11... | collective-permute-start | bytes 2359304 | tf_op jit(solution)/shard_map/ppermute | solution.py:526
  64.6 4.6 collective-permute-start.11
  69.2 31.7 %collective-permute-start.18 = (bf16[4,128,1280]{2,1,0:T(8,128)(2,1)S(1)}, bf16[4,128,1280]{2,1,0:T(8,128)(2,1)S(1)}, u32[]{:S(2)}, u32[]{:S(2)}) collective-permute-start(bf16[4,128,1280]{2,1,0:T(8,128)(2,1)S(1)} %pad_maximum_fusion.1.refs_0_), channel_id=1, source_target_pairs={{0,8},{1,17},{2,10},{3,19},{4,12},{5,21},{6,14},{7,23},{8,0},{9,25... | collective-permute-start | bytes 3932168 | tf_op jit(solution)/shard_map/ppermute | solution.py:526
  74.4 28.4 %collective-permute-start.19 = (bf16[4,128,1280]{2,1,0:T(8,128)(2,1)S(1)}, bf16[4,128,1280]{2,1,0:T(8,128)(2,1)}, u32[]{:S(2)}, u32[]{:S(2)}) collective-permute-start(bf16[4,128,1280]{2,1,0:T(8,128)(2,1)S(1)} %pad_maximum_fusion.1.refs_0_), channel_id=1, source_target_pairs={{0,16},{1,9},{2,18},{3,11},{4,20},{5,13},{6,22},{7,15},{8,24},{9,1... | collective-permute-start | bytes 3932168 | tf_op jit(solution)/shard_map/ppermute | solution.py:526
  87.3 13.6 %collective-permute-start.12 = (bf16[512,256]{1,0:T(8,128)(2,1)S(1)}, bf16[512,256]{1,0:T(8,128)(2,1)S(1)}, u32[]{:S(2)}, u32[]{:S(2)}) collective-permute-start(bf16[512,256]{1,0:T(8,128)(2,1)S(1)} %copy-done.10), channel_id=1, source_target_pairs={{0,2},{1,5},{2,0},{3,7},{4,6},{5,1},{6,4},{7,3},{8,10},{9,13},{10,... | collective-permute-start | bytes 786440 | tf_op jit(solution)/shard_map/ppermute | solution.py:526
  101.0 25.6 %collective-permute-start.20 = (bf16[4,128,1280]{2,1,0:T(8,128)(2,1)S(1)}, bf16[4,128,1280]{2,1,0:T(8,128)(2,1)}, u32[]{:S(2)}, u32[]{:S(2)}) collective-permute-start(bf16[4,128,1280]{2,1,0:T(8,128)(2,1)S(1)} %collective-permute-done.18.refs_1_), channel_id=1, source_target_pairs={{0,16},{1,9},{2,18},{3,11},{4,20},{5,13},{6,22},{7,15},{8,24},{9,1... | collective-permute-start | bytes 3932168 | tf_op jit(solution)/shard_map/ppermute | solution.py:526
  101.0 15.7 %collective-permute-start.13 = (bf16[2,512,256]{2,1,0:T(8,128)(2,1)S(1)}, bf16[2,512,256]{2,1,0:T(8,128)(2,1)}, u32[]{:S(2)}, u32[]{:S(2)}) collective-permute-start(bf16[2,512,256]{2,1,0:T(8,128)(2,1)S(1)} %pad_maximum_fusion.6), channel_id=1, source_target_pairs={{0,4},{1,3},{2,6},{3,1},{4,0},{5,7},{6,2},{7,5},{8,12},{9,11},{10,... | collective-permute-start | bytes 1572872 | tf_op jit(solution)/shard_map/ppermute | solution.py:526
  102.3 27.6 %collective-permute-start.21 = (bf16[4,128,1280]{2,1,0:T(8,128)(2,1)S(1)}, bf16[4,128,1280]{2,1,0:T(8,128)(2,1)}, u32[]{:S(2)}, u32[]{:S(2)}) collective-permute-start(bf16[4,128,1280]{2,1,0:T(8,128)(2,1)S(1)} %pad_maximum_fusion.1.refs_0_), channel_id=1, source_target_pairs={{0,1},{1,0},{2,3},{3,2},{4,5},{5,4},{6,7},{7,6},{8,9},{9,8},{10,11... | collective-permute-start | bytes 3932168 | tf_op jit(solution)/shard_map/ppermute | solution.py:526
  102.3 39.3 %collective-permute-start.22 = (bf16[4,128,1280]{2,1,0:T(8,128)(2,1)S(1)}, bf16[4,128,1280]{2,1,0:T(8,128)(2,1)}, u32[]{:S(2)}, u32[]{:S(2)}) collective-permute-start(bf16[4,128,1280]{2,1,0:T(8,128)(2,1)S(1)} %collective-permute-done.18.refs_1_), channel_id=1, source_target_pairs={{0,1},{1,0},{2,3},{3,2},{4,5},{5,4},{6,7},{7,6},{8,9},{9,8},{10,11... | collective-permute-start | bytes 3932168 | tf_op jit(solution)/shard_map/ppermute | solution.py:526
  113.1 28.5 %collective-permute-start.23 = (bf16[4,128,1280]{2,1,0:T(8,128)(2,1)}, bf16[4,128,1280]{2,1,0:T(8,128)(2,1)}, u32[]{:S(2)}, u32[]{:S(2)}) collective-permute-start(bf16[4,128,1280]{2,1,0:T(8,128)(2,1)} %collective-permute-done.19.refs_2_), channel_id=1, source_target_pairs={{0,1},{1,0},{2,3},{3,2},{4,5},{5,4},{6,7},{7,6},{8,9},{9,8},{10,11... | collective-permute-start | bytes 3932168 | tf_op jit(solution)/shard_map/ppermute | solution.py:526
  126.5 15.1 %collective-permute-start.24 = (bf16[4,128,1280]{2,1,0:T(8,128)(2,1)}, bf16[4,128,1280]{2,1,0:T(8,128)(2,1)}, u32[]{:S(2)}, u32[]{:S(2)}) collective-permute-start(bf16[4,128,1280]{2,1,0:T(8,128)(2,1)} %collective-permute-done.20.refs_3_), channel_id=1, source_target_pairs={{0,1},{1,0},{2,3},{3,2},{4,5},{5,4},{6,7},{7,6},{8,9},{9,8},{10,11... | collective-permute-start | bytes 3932168 | tf_op jit(solution)/shard_map/ppermute | solution.py:526
  128.7 25.5 %collective-permute-start.14 = (bf16[4,512,256]{2,1,0:T(8,128)(2,1)}, bf16[4,512,256]{2,1,0:T(8,128)(2,1)}, u32[]{:S(2)}, u32[]{:S(2)}) collective-permute-start(bf16[4,512,256]{2,1,0:T(8,128)(2,1)} %pad_maximum_fusion.2.refs_0_), channel_id=1, source_target_pairs={{0,8},{1,17},{2,10},{3,19},{4,12},{5,21},{6,14},{7,23},{8,0},{9,25... | collective-permute-start | bytes 3145736 | tf_op jit(solution)/shard_map/ppermute | solution.py:526
  129.9 27.0 %collective-permute-start.15 = (bf16[4,512,256]{2,1,0:T(8,128)(2,1)}, bf16[4,512,256]{2,1,0:T(8,128)(2,1)S(1)}, u32[]{:S(2)}, u32[]{:S(2)}) collective-permute-start(bf16[4,512,256]{2,1,0:T(8,128)(2,1)} %pad_maximum_fusion.2.refs_0_), channel_id=1, source_target_pairs={{0,16},{1,9},{2,18},{3,11},{4,20},{5,13},{6,22},{7,15},{8,24},{9,1... | collective-permute-start | bytes 3145736 | tf_op jit(solution)/shard_map/ppermute | solution.py:526
  154.2 24.9 %collective-permute-start.25 = (bf16[4,512,256]{2,1,0:T(8,128)(2,1)}, bf16[4,512,256]{2,1,0:T(8,128)(2,1)S(1)}, u32[]{:S(2)}, u32[]{:S(2)}) collective-permute-start(bf16[4,512,256]{2,1,0:T(8,128)(2,1)} %collective-permute-done.14.refs_1_), channel_id=1, source_target_pairs={{0,16},{1,9},{2,18},{3,11},{4,20},{5,13},{6,22},{7,15},{8,24},{9,1... | collective-permute-start | bytes 3145736 | tf_op jit(solution)/shard_map/ppermute | solution.py:526
  156.3 24.3 %collective-permute-start.27 = (bf16[4,512,256]{2,1,0:T(8,128)(2,1)}, bf16[4,512,256]{2,1,0:T(8,128)(2,1)S(1)}, u32[]{:S(2)}, u32[]{:S(2)}) collective-permute-start(bf16[4,512,256]{2,1,0:T(8,128)(2,1)} %collective-permute-done.14.refs_1_), channel_id=1, source_target_pairs={{0,1},{1,0},{2,3},{3,2},{4,5},{5,4},{6,7},{7,6},{8,9},{9,8},{10,11... | collective-permute-start | bytes 3145736 | tf_op jit(solution)/shard_map/ppermute | solution.py:526
  156.3 24.3 %collective-permute-start.26 = (bf16[4,512,256]{2,1,0:T(8,128)(2,1)}, bf16[4,512,256]{2,1,0:T(8,128)(2,1)}, u32[]{:S(2)}, u32[]{:S(2)}) collective-permute-start(bf16[4,512,256]{2,1,0:T(8,128)(2,1)} %pad_maximum_fusion.2.refs_0_), channel_id=1, source_target_pairs={{0,1},{1,0},{2,3},{3,2},{4,5},{5,4},{6,7},{7,6},{8,9},{9,8},{10,11... | collective-permute-start | bytes 3145736 | tf_op jit(solution)/shard_map/ppermute | solution.py:526
  156.9 23.8 %collective-permute-start.28 = (bf16[4,512,256]{2,1,0:T(8,128)(2,1)S(1)}, bf16[4,512,256]{2,1,0:T(8,128)(2,1)}, u32[]{:S(2)}, u32[]{:S(2)}) collective-permute-start(bf16[4,512,256]{2,1,0:T(8,128)(2,1)S(1)} %collective-permute-done.15.refs_2_), channel_id=1, source_target_pairs={{0,1},{1,0},{2,3},{3,2},{4,5},{5,4},{6,7},{7,6},{8,9},{9,8},{10,11... | collective-permute-start | bytes 3145736 | tf_op jit(solution)/shard_map/ppermute | solution.py:526
  179.1 2.9 collective-permute-start.29
  213.7 15.0 %collective-permute-start.30 = (bf16[4,4,512,256]{3,2,1,0:T(8,128)(2,1)}, bf16[4,4,512,256]{3,2,1,0:T(8,128)(2,1)}, u32[]{:S(2)}, u32[]{:S(2)}) collective-permute-start(bf16[4,4,512,256]{3,2,1,0:T(8,128)(2,1)} %wgrad_out_sent.1), channel_id=1, source_target_pairs={{0,1},{1,0},{2,3},{3,2},{4,5},{5,4},{6,7},{7,6},{8,9},{9,8},{10,11... | collective-permute-start | bytes 12582920 | tf_op jit(solution)/shard_map/ppermute | solution.py:526
  249.6 27.8 %collective-permute-start.31 = (bf16[4,4,128,1024]{3,2,1,0:T(8,128)(2,1)}, bf16[4,4,128,1024]{3,2,1,0:T(8,128)(2,1)}, u32[]{:S(2)}, u32[]{:S(2)}) collective-permute-start(bf16[4,4,128,1024]{3,2,1,0:T(8,128)(2,1)} %wgrad_in_sent.1), channel_id=1, source_target_pairs={{0,1},{1,0},{2,3},{3,2},{4,5},{5,4},{6,7},{7,6},{8,9},{9,8},{10,11... | collective-permute-start | bytes 12582920 | tf_op jit(solution)/shard_map/ppermute | solution.py:526
  249.7 26.2 %collective-permute-start.32 = (bf16[2,4,512,256]{3,2,1,0:T(8,128)(2,1)}, bf16[2,4,512,256]{3,2,1,0:T(8,128)(2,1)S(1)}, u32[]{:S(2)}, u32[]{:S(2)}) collective-permute-start(bf16[2,4,512,256]{3,2,1,0:T(8,128)(2,1)} %get-tuple-element.164), channel_id=1, source_target_pairs={{0,8},{1,17},{2,10},{3,19},{4,12},{5,21},{6,14},{7,23},{8,0},{9,25... | collective-permute-start | bytes 6291464 | tf_op jit(solution)/shard_map/ppermute | solution.py:526
  277.4 35.8 %collective-permute-start.33 = (bf16[4,512,256]{2,1,0:T(8,128)(2,1)}, bf16[4,512,256]{2,1,0:T(8,128)(2,1)S(1)}, u32[]{:S(2)}, u32[]{:S(2)}) collective-permute-start(bf16[4,512,256]{2,1,0:T(8,128)(2,1)} %fusion.5), channel_id=1, source_target_pairs={{0,16},{1,9},{2,18},{3,11},{4,20},{5,13},{6,22},{7,15},{8,24},{9,1... | collective-permute-start | bytes 3145736 | tf_op jit(solution)/shard_map/ppermute | solution.py:526
  289.8 41.5 %collective-permute-start.34 = (bf16[2,4,128,1024]{3,2,1,0:T(8,128)(2,1)}, bf16[2,4,128,1024]{3,2,1,0:T(8,128)(2,1)}, u32[]{:S(2)}, u32[]{:S(2)}) collective-permute-start(bf16[2,4,128,1024]{3,2,1,0:T(8,128)(2,1)} %get-tuple-element.177), channel_id=1, source_target_pairs={{0,8},{1,17},{2,10},{3,19},{4,12},{5,21},{6,14},{7,23},{8,0},{9,25... | collective-permute-start | bytes 6291464 | tf_op jit(solution)/shard_map/ppermute | solution.py:526
  315.0 16.2 %collective-permute-start.35 = (bf16[2,512,256]{2,1,0:T(8,128)(2,1)S(1)}, bf16[2,512,256]{2,1,0:T(8,128)(2,1)S(1)}, u32[]{:S(2)}, u32[]{:S(2)}) collective-permute-start(bf16[2,512,256]{2,1,0:T(8,128)(2,1)S(1)} %pad_maximum_fusion.7), channel_id=1, source_target_pairs={{0,2},{1,5},{2,0},{3,7},{4,6},{5,1},{6,4},{7,3},{8,10},{9,13},{10,... | collective-permute-start | bytes 1572872 | tf_op jit(solution)/shard_map/ppermute | solution.py:526
  343.2 22.7 %collective-permute-start.36 = (bf16[4,4,128,640]{3,2,1,0:T(8,128)(2,1)}, bf16[4,4,128,640]{3,2,1,0:T(8,128)(2,1)}, u32[]{:S(2)}, u32[]{:S(2)}) collective-permute-start(bf16[4,4,128,640]{3,2,1,0:T(8,128)(2,1)} %wgrad_a_sent.1), channel_id=1, source_target_pairs={{0,1},{1,0},{2,3},{3,2},{4,5},{5,4},{6,7},{7,6},{8,9},{9,8},{10,11... | collective-permute-start | bytes 7864328 | tf_op jit(solution)/shard_map/ppermute | solution.py:526
  343.2 20.0 %collective-permute-start.38 = (bf16[512,256]{1,0:T(8,128)(2,1)S(1)}, bf16[512,256]{1,0:T(8,128)(2,1)S(1)}, u32[]{:S(2)}, u32[]{:S(2)}) collective-permute-start(bf16[512,256]{1,0:T(8,128)(2,1)S(1)} %fusion.15), channel_id=1, source_target_pairs={{0,4},{1,3},{2,6},{3,1},{4,0},{5,7},{6,2},{7,5},{8,12},{9,11},{10,... | collective-permute-start | bytes 786440 | tf_op jit(solution)/shard_map/ppermute | solution.py:526
  345.4 17.9 %collective-permute-start.37 = (bf16[4,128,1024]{2,1,0:T(8,128)(2,1)S(1)}, bf16[4,128,1024]{2,1,0:T(8,128)(2,1)}, u32[]{:S(2)}, u32[]{:S(2)}) collective-permute-start(bf16[4,128,1024]{2,1,0:T(8,128)(2,1)S(1)} %fusion.2), channel_id=1, source_target_pairs={{0,16},{1,9},{2,18},{3,11},{4,20},{5,13},{6,22},{7,15},{8,24},{9,1... | collective-permute-start | bytes 3145736 | tf_op jit(solution)/shard_map/ppermute | solution.py:526
  381.8 23.1 %collective-permute-start.39 = (bf16[2,4,128,640]{3,2,1,0:T(8,128)(2,1)}, bf16[2,4,128,640]{3,2,1,0:T(8,128)(2,1)S(1)}, u32[]{:S(2)}, u32[]{:S(2)}) collective-permute-start(bf16[2,4,128,640]{3,2,1,0:T(8,128)(2,1)} %get-tuple-element.192), channel_id=1, source_target_pairs={{0,8},{1,17},{2,10},{3,19},{4,12},{5,21},{6,14},{7,23},{8,0},{9,25... | collective-permute-start | bytes 3932168 | tf_op jit(solution)/shard_map/ppermute | solution.py:526
  383.2 15.9 %collective-permute-start.40 = (bf16[2,128,1024]{2,1,0:T(8,128)(2,1)}, bf16[2,128,1024]{2,1,0:T(8,128)(2,1)S(1)}, u32[]{:S(2)}, u32[]{:S(2)}) collective-permute-start(bf16[2,128,1024]{2,1,0:T(8,128)(2,1)} %pad_maximum_fusion.8), channel_id=1, source_target_pairs={{0,2},{1,5},{2,0},{3,7},{4,6},{5,1},{6,4},{7,3},{8,10},{9,13},{10,... | collective-permute-start | bytes 1572872 | tf_op jit(solution)/shard_map/ppermute | solution.py:526
  400.6 15.1 %collective-permute-start.43 = (bf16[128,1024]{1,0:T(8,128)(2,1)}, bf16[128,1024]{1,0:T(8,128)(2,1)}, u32[]{:S(2)}, u32[]{:S(2)}) collective-permute-start(bf16[128,1024]{1,0:T(8,128)(2,1)} %fusion.16), channel_id=1, source_target_pairs={{0,4},{1,3},{2,6},{3,1},{4,0},{5,7},{6,2},{7,5},{8,12},{9,11},{10,... | collective-permute-start | bytes 786440 | tf_op jit(solution)/shard_map/ppermute | solution.py:526
  404.9 14.7 %collective-permute-start.44 = (f32[16,1024]{1,0:T(8,128)}, f32[16,1024]{1,0:T(8,128)}, u32[]{:S(2)}, u32[]{:S(2)}) collective-permute-start(f32[16,1024]{1,0:T(8,128)} %pack_sums.1), channel_id=1, source_target_pairs={{0,1},{1,0},{2,3},{3,2},{4,5},{5,4},{6,7},{7,6},{8,9},{9,8},{10,11... | collective-permute-start | bytes 196616 | tf_op jit(solution)/shard_map/ppermute | solution.py:526
  406.1 11.6 %collective-permute-start.42 = (bf16[4,128,640]{2,1,0:T(8,128)(2,1)}, bf16[4,128,640]{2,1,0:T(8,128)(2,1)}, u32[]{:S(2)}, u32[]{:S(2)}) collective-permute-start(bf16[4,128,640]{2,1,0:T(8,128)(2,1)} %fusion.8), channel_id=1, source_target_pairs={{0,16},{1,9},{2,18},{3,11},{4,20},{5,13},{6,22},{7,15},{8,24},{9,1... | collective-permute-start | bytes 1966088 | tf_op jit(solution)/shard_map/ppermute | solution.py:526
  414.3 12.9 %collective-permute-start.41 = (bf16[4,4,128,384]{3,2,1,0:T(8,128)(2,1)}, bf16[4,4,128,384]{3,2,1,0:T(8,128)(2,1)S(1)}, u32[]{:S(2)}, u32[]{:S(2)}) collective-permute-start(bf16[4,4,128,384]{3,2,1,0:T(8,128)(2,1)} %wgrad_b_sent.1), channel_id=1, source_target_pairs={{0,1},{1,0},{2,3},{3,2},{4,5},{5,4},{6,7},{7,6},{8,9},{9,8},{10,11... | collective-permute-start | bytes 4718600 | tf_op jit(solution)/shard_map/ppermute | solution.py:526
  416.9 9.2 %collective-permute-start.46 = (bf16[1024,256]{1,0:T(8,128)(2,1)S(1)}, bf16[1024,256]{1,0:T(8,128)(2,1)S(1)}, u32[]{:S(2)}, u32[]{:S(2)}) collective-permute-start(bf16[1024,256]{1,0:T(8,128)(2,1)S(1)} %constant_dynamic-update-slice_fusion), channel_id=1, source_target_pairs={{0,8},{1,17},{2,10},{3,19},{4,12},{5,21},{6,14},{7,23},{8,0},{9,25... | collective-permute-start | bytes 1572872 | tf_op jit(solution)/shard_map/ppermute | solution.py:526
  419.5 19.0 %collective-permute-start.45 = (bf16[2,128,640]{2,1,0:T(8,128)(2,1)S(1)}, bf16[2,128,640]{2,1,0:T(8,128)(2,1)}, u32[]{:S(2)}, u32[]{:S(2)}) collective-permute-start(bf16[2,128,640]{2,1,0:T(8,128)(2,1)S(1)} %pad_maximum_fusion.12), channel_id=1, source_target_pairs={{0,2},{1,5},{2,0},{3,7},{4,6},{5,1},{6,4},{7,3},{8,10},{9,13},{10,... | collective-permute-start | bytes 983048 | tf_op jit(solution)/shard_map/ppermute | solution.py:526
  438.5 14.8 %collective-permute-start.48 = (bf16[2,4,128,384]{3,2,1,0:T(8,128)(2,1)}, bf16[2,4,128,384]{3,2,1,0:T(8,128)(2,1)S(1)}, u32[]{:S(2)}, u32[]{:S(2)}) collective-permute-start(bf16[2,4,128,384]{3,2,1,0:T(8,128)(2,1)} %get-tuple-element.207), channel_id=1, source_target_pairs={{0,8},{1,17},{2,10},{3,19},{4,12},{5,21},{6,14},{7,23},{8,0},{9,25... | collective-permute-start | bytes 2359304 | tf_op jit(solution)/shard_map/ppermute | solution.py:526
  454.2 12.6 %collective-permute-start.50 = (bf16[4,128,384]{2,1,0:T(8,128)(2,1)}, bf16[4,128,384]{2,1,0:T(8,128)(2,1)}, u32[]{:S(2)}, u32[]{:S(2)}) collective-permute-start(bf16[4,128,384]{2,1,0:T(8,128)(2,1)} %fusion.11), channel_id=1, source_target_pairs={{0,16},{1,9},{2,18},{3,11},{4,20},{5,13},{6,22},{7,15},{8,24},{9,1... | collective-permute-start | bytes 1179656 | tf_op jit(solution)/shard_map/ppermute | solution.py:526
  455.3 7.8 %collective-permute-start.47 = (bf16[128,640]{1,0:T(8,128)(2,1)}, bf16[128,640]{1,0:T(8,128)(2,1)}, u32[]{:S(2)}, u32[]{:S(2)}) collective-permute-start(bf16[128,640]{1,0:T(8,128)(2,1)} %fusion.18), channel_id=1, source_target_pairs={{0,4},{1,3},{2,6},{3,1},{4,0},{5,7},{6,2},{7,5},{8,12},{9,11},{10,... | collective-permute-start | bytes 491528 | tf_op jit(solution)/shard_map/ppermute | solution.py:526
  455.6 5.0 collective-permute-start.56
  461.3 4.6 collective-permute-start.57
  468.1 7.3 %collective-permute-start.52 = (bf16[2,128,384]{2,1,0:T(8,128)(2,1)S(1)}, bf16[2,128,384]{2,1,0:T(8,128)(2,1)S(1)}, u32[]{:S(2)}, u32[]{:S(2)}) collective-permute-start(bf16[2,128,384]{2,1,0:T(8,128)(2,1)S(1)} %pad_maximum_fusion.14), channel_id=1, source_target_pairs={{0,2},{1,5},{2,0},{3,7},{4,6},{5,1},{6,4},{7,3},{8,10},{9,13},{10,... | collective-permute-start | bytes 589832 | tf_op jit(solution)/shard_map/ppermute | solution.py:526
  469.4 6.0 %collective-permute-start.58 = (f32[16,1024]{1,0:T(8,128)S(1)}, f32[16,1024]{1,0:T(8,128)S(1)}, u32[]{:S(2)}, u32[]{:S(2)}) collective-permute-start(f32[16,1024]{1,0:T(8,128)S(1)} %add.179), channel_id=1, source_target_pairs={{0,2},{1,5},{2,0},{3,7},{4,6},{5,1},{6,4},{7,3},{8,10},{9,13},{10,... | collective-permute-start | bytes 196616 | tf_op jit(solution)/shard_map/ppermute | solution.py:526
  471.3 7.2 %collective-permute-start.49 = (bf16[128,640]{1,0:T(8,128)(2,1)S(1)}, bf16[128,640]{1,0:T(8,128)(2,1)S(1)}, u32[]{:S(2)}, u32[]{:S(2)}) collective-permute-start(bf16[128,640]{1,0:T(8,128)(2,1)S(1)} %fusion.14), channel_id=1, source_target_pairs={{0,8},{1,17},{2,10},{3,19},{4,12},{5,21},{6,14},{7,23},{8,0},{9,25... | collective-permute-start | bytes 491528 | tf_op jit(solution)/shard_map/ppermute | solution.py:526
  471.8 26.7 %collective-permute-start.60 = (bf16[2,1024,256]{2,1,0:T(8,128)(2,1)S(1)}, bf16[2,1024,256]{2,1,0:T(8,128)(2,1)S(1)}, u32[]{:S(2)}, u32[]{:S(2)}) collective-permute-start(bf16[2,1024,256]{2,1,0:T(8,128)(2,1)S(1)} %copy-done.8), channel_id=1, source_target_pairs={{0,16},{1,9},{2,18},{3,11},{4,20},{5,13},{6,22},{7,15},{8,24},{9,1... | collective-permute-start | bytes 3145736 | tf_op jit(solution)/shard_map/ppermute | solution.py:526
  475.5 5.8 %collective-permute-start.59 = (f32[16,1024]{1,0:T(8,128)S(1)}, f32[16,1024]{1,0:T(8,128)S(1)}, u32[]{:S(2)}, u32[]{:S(2)}) collective-permute-start(f32[16,1024]{1,0:T(8,128)S(1)} %add.180), channel_id=1, source_target_pairs={{0,4},{1,3},{2,6},{3,1},{4,0},{5,7},{6,2},{7,5},{8,12},{9,11},{10,... | collective-permute-start | bytes 196616 | tf_op jit(solution)/shard_map/ppermute | solution.py:526
  478.5 12.6 %collective-permute-start.51 = (bf16[2,128,640]{2,1,0:T(8,128)(2,1)S(1)}, bf16[2,128,640]{2,1,0:T(8,128)(2,1)S(1)}, u32[]{:S(2)}, u32[]{:S(2)}) collective-permute-start(bf16[2,128,640]{2,1,0:T(8,128)(2,1)S(1)} %pad_maximum_fusion.13), channel_id=1, source_target_pairs={{0,16},{1,9},{2,18},{3,11},{4,20},{5,13},{6,22},{7,15},{8,24},{9,1... | collective-permute-start | bytes 983048 | tf_op jit(solution)/shard_map/ppermute | solution.py:526
  479.2 6.6 %collective-permute-start.53 = (bf16[128,384]{1,0:T(8,128)(2,1)S(1)}, bf16[128,384]{1,0:T(8,128)(2,1)S(1)}, u32[]{:S(2)}, u32[]{:S(2)}) collective-permute-start(bf16[128,384]{1,0:T(8,128)(2,1)S(1)} %fusion.19), channel_id=1, source_target_pairs={{0,4},{1,3},{2,6},{3,1},{4,0},{5,7},{6,2},{7,5},{8,12},{9,11},{10,... | collective-permute-start | bytes 294920 | tf_op jit(solution)/shard_map/ppermute | solution.py:526
  485.8 6.4 %collective-permute-start.54 = (bf16[128,384]{1,0:T(8,128)(2,1)S(1)}, bf16[128,384]{1,0:T(8,128)(2,1)S(1)}, u32[]{:S(2)}, u32[]{:S(2)}) collective-permute-start(bf16[128,384]{1,0:T(8,128)(2,1)S(1)} %fusion.17), channel_id=1, source_target_pairs={{0,8},{1,17},{2,10},{3,19},{4,12},{5,21},{6,14},{7,23},{8,0},{9,25... | collective-permute-start | bytes 294920 | tf_op jit(solution)/shard_map/ppermute | solution.py:526
  492.3 5.7 %collective-permute-start.55 = (bf16[2,128,384]{2,1,0:T(8,128)(2,1)S(1)}, bf16[2,128,384]{2,1,0:T(8,128)(2,1)S(1)}, u32[]{:S(2)}, u32[]{:S(2)}) collective-permute-start(bf16[2,128,384]{2,1,0:T(8,128)(2,1)S(1)} %pad_maximum_fusion.15), channel_id=1, source_target_pairs={{0,16},{1,9},{2,18},{3,11},{4,20},{5,13},{6,22},{7,15},{8,24},{9,1... | collective-permute-start | bytes 589832 | tf_op jit(solution)/shard_map/ppermute | solution.py:526
  (33 other events, 614.3 us)

commit v6 on v5

--- a/solution.py
+++ b/solution.py
@@ -770,27 +770,38 @@
     half = late_a.shape[1]
 
     def kernel(a_ref, b_ref, one_ref, two_ref, inner_ref, out_ref):
+        def place_of(n):
+            return n // 3 * 8 + n % 3
+
         out_ref[...] = jnp.zeros_like(out_ref)
-        out_ref[0:2, 0:half] = a_ref[...]
-        out_ref[0:2, half:width] = b_ref[...]
-        for n, source in (
-            (GAIN_ONE, one_ref[0:1, :]),
-            (SHIFT_ONE, one_ref[1:2, :]),
-            (B_ATTN, one_ref[2:3, :]),
-            (GAIN_TWO, two_ref[0:1, :]),
-            (SHIFT_TWO, two_ref[1:2, :]),
-            (B_OUT, two_ref[2:3, :]),
+        for n in (B_QUERY, B_VALUE):
+            at = place_of(n)
+            out_ref[at : at + 1, 0:half] = a_ref[n : n + 1, :]
+            out_ref[at : at + 1, half:width] = b_ref[n : n + 1, :]
+        for n, source, line in (
+            (GAIN_ONE, one_ref, 0),
+            (SHIFT_ONE, one_ref, 1),
+            (B_ATTN, one_ref, 2),
+            (GAIN_TWO, two_ref, 0),
+            (SHIFT_TWO, two_ref, 1),
+            (B_OUT, two_ref, 2),
         ):
-            out_ref[n : n + 1, :] = source
+            at = place_of(n)
+            out_ref[at : at + 1, :] = source[line : line + 1, :]
         for n in range(4):
-            out_ref[B_IN + n : B_IN + n + 1, :] = inner_ref[:, n * width : (n + 1) * width]
+            at = place_of(B_IN + n)
+            for shard in range(width // LANES):
+                start = (4 * shard + n) * LANES
+                out_ref[at : at + 1, shard * LANES : (shard + 1) * LANES] = inner_ref[
+                    :, start : start + LANES
+                ]
 
     in_vmem = pl.BlockSpec(memory_space=pltpu.VMEM)
     return pl.pallas_call(
         kernel,
         in_specs=[in_vmem] * 5,
         out_specs=in_vmem,
-        out_shape=shaped((16, width), jnp.float32),
+        out_shape=shaped((32, width), jnp.float32),
         name="pack_sums",
     )(late_a, late_b, first_sums, second_sums, inner_sums)
 
@@ -878,6 +889,16 @@
     )
 
 
+def normal_share(values):
+    power = jnp.exp(-0.5 * values * values)
+    t = 1.0 / (1.0 + (0.3275911 / math.sqrt(2.0)) * jnp.abs(values))
+    tail = 0.5 * 1.061405429
+    for factor in (-1.453152027, 1.421413741, -0.284496736, 0.254829592):
+        tail = tail * t + 0.5 * factor
+    tail = tail * t * power
+    return jnp.where(values >= 0, 1.0 - tail, tail), power * (1.0 / math.sqrt(2.0 * math.pi))
+
+
 def feed_in(place, normed_low, window, bias):
     length, width = normed_low.shape
     cols = window.cols
@@ -888,8 +909,7 @@
         for tile in range(length // TILE):
             here = pl.ds(tile * TILE, TILE)
             pre = mxu(x_ref[here, :], weight[:, at], NN) + bias_ref[:, at]
-            share = 0.5 + 0.5 * lax.erf(pre * (1.0 / math.sqrt(2.0)))
-            bell = jnp.exp(-0.5 * pre * pre) * (1.0 / math.sqrt(2.0 * math.pi))
+            share, bell = normal_share(pre)
             hid_ref[here, :] = (pre * share).astype(jnp.bfloat16)
             slope_ref[here, :] = (share + pre * bell).astype(jnp.bfloat16)
 
@@ -975,20 +995,22 @@
     )
 
 
-def feed_in_back(pre_low, weight, second_grad, normed, scale, vectors):
+def feed_in_back(pre_low, weight, second_grad, normed, scale, vectors, attn_weight):
     length, inner = pre_low.shape
     width = normed.shape[1]
 
-    def kernel(p_ref, w_ref, g_ref, n_ref, r_ref, v_ref, first_ref, low_ref, sum_ref):
+    def kernel(p_ref, w_ref, g_ref, n_ref, r_ref, v_ref, a_ref, first_ref, low_ref, ctx_ref, sum_ref):
         grad = g_ref[...] + mxu(p_ref[...], w_ref[...], NT)
         first = norm_back(grad * row(v_ref, GAIN_ONE), n_ref[...], r_ref[:, :1])
+        low = first.astype(jnp.bfloat16)
         first_ref[...] = first
-        low_ref[...] = first.astype(jnp.bfloat16)
+        low_ref[...] = low
+        ctx_ref[...] = mxu(low, a_ref[...], NT).astype(jnp.bfloat16)
         add_rows(sum_ref, grad * n_ref[...], grad, first)
 
     return plain_call(
         kernel,
-        (pre_low, weight, second_grad, normed, scale, vectors),
+        (pre_low, weight, second_grad, normed, scale, vectors, attn_weight),
         [
             row_tiles(inner),
             whole_once(weight.shape),
@@ -996,35 +1018,19 @@
             row_tiles(width),
             row_tiles(LANES),
             fixed(*vectors.shape),
+            whole_once(attn_weight.shape),
         ],
         [
             shaped((length, width), jnp.float32),
             shaped((length, width), jnp.bfloat16),
+            shaped((length, width), jnp.bfloat16),
             shaped((8, width), jnp.float32),
         ],
-        [row_tiles(width), row_tiles(width), fixed(8, width)],
+        [row_tiles(width), row_tiles(width), row_tiles(width), fixed(8, width)],
         length // TILE,
         "feed_in_back",
-        2 * length * width * inner,
-    )
-
-
-def project_out_back(attn_low, weight):
-    length, width = attn_low.shape
-
-    def kernel(g_ref, w_ref, out_ref):
-        out_ref[...] = mxu(g_ref[...], w_ref[...], NT).astype(jnp.bfloat16)
-
-    return plain_call(
-        kernel,
-        (attn_low, weight),
-        [row_tiles(width), whole_once(weight.shape)],
-        [shaped((length, width), jnp.bfloat16)],
-        [row_tiles(width)],
-        length // TILE,
-        "attn_out_back",
-        2 * length * width * width,
-    )[0]
+        2 * length * width * (inner + width),
+    )
 
 
 def project_qkv_back(grads, weight, first_grad):
@@ -1054,51 +1060,38 @@
     )[0]
 
 
-def weight_grad_kernel(where, *refs, own, rows, groups, count, split):
+ORDER = (1, 3, 0, 2)
+
+
+def ordered_slot(j):
+    return jnp.where(j < 2, 2 * j + 1, 2 * j - 4)
+
+
+def weight_grad_kernel(where, *refs, rows, groups, count, split, extra):
     lefts, rights, refs = refs[:count], refs[count : 2 * count], refs[2 * count :]
-    outs, kept = refs[:-count], refs[-count:]
-    received = None
-    if own:
-        received, *outs = outs
-    keep = where[0] if own else 1 - where[0]
+    sums_ref = None
+    if extra:
+        sums_ref, *refs = refs
+    (leave, keep, sent), kept = refs[:3], refs[3:]
+    core = where[0]
     chips = lefts[0].shape[1] // (2 * rows)
 
     @pl.when(pl.program_id(1) == 0)
     def _():
         for left_ref, kept_ref in zip(lefts, kept):
-            chosen = []
-            for k in range(chips):
-                even = left_ref[:, 2 * k * rows : (2 * k + 1) * rows]
-                odd = left_ref[:, (2 * k + 1) * rows : (2 * k + 2) * rows]
-                chosen.append(jnp.where(keep == 0, even, odd))
-            left = chosen[0] if chips == 1 else jnp.concatenate(chosen, 1)
-            kept_ref[...] = left.T
-
-    def emit(slot, part, at):
-        part = part.reshape(chips, rows, part.shape[-1])
-        pos = 0 if split else slot
-        if own:
-            part = (part + received[pos, :, :, at].astype(jnp.float32)).astype(jnp.bfloat16)
-
-            def store(slot):
-                if slot in (1, 3):
-                    outs[2][slot // 2, :, :, at] = part
-                else:
-                    outs[slot // 2][:, :, at] = part
-
-            if split:
-                for n in range(groups):
-                    pl.when(pl.program_id(1) == n)(functools.partial(store, n))
-            else:
-                store(slot)
-        else:
-            outs[0][pos, :, :, at] = part.astype(jnp.bfloat16)
-
-    if split:
+            for side in range(2):
+                chosen = []
+                for k in range(chips):
+                    even = left_ref[:, 2 * k * rows : (2 * k + 1) * rows]
+                    odd = left_ref[:, (2 * k + 1) * rows : (2 * k + 2) * rows]
+                    chosen.append(jnp.where(core == side, even, odd))
+                left = chosen[0] if chips == 1 else jnp.concatenate(chosen, 1)
+                kept_ref[side] = left.T
+
+    def write(ref, pos, side):
         at = 0
         for right_ref, kept_ref in zip(rights, kept):
             if len(right_ref.shape) == 3:
-                size = right_ref.shape[2]
                 pieces = [right_ref[n] for n in range(right_ref.shape[0])]
             else:
                 size = min(512, right_ref.shape[1])
@@ -1107,26 +1100,60 @@
                     for n in range(right_ref.shape[1] // size)
                 ]
             for piece in pieces:
-                emit(0, mxu(kept_ref[...], piece, NN), slice(at, at + size))
+                part = mxu(kept_ref[side], piece, NN).astype(jnp.bfloat16)
+                size = piece.shape[1]
+                ref[pos, :, 0:rows, at : at + size] = part.reshape(chips, rows, size)
                 at += size
+        if extra:
+            block = where[2] ^ turn(ordered_slot(pl.program_id(1)), core)
+            blank = jnp.zeros((extra, at), jnp.bfloat16)
+            for k in range(chips):
+                start = pl.multiple_of((2 * k + (core ^ side)) * LANES, LANES)
+                ref[pos, k, rows : rows + extra, :] = blank
+                lines = sums_ref[pl.ds(pl.multiple_of(block * 8, 8), 8), pl.ds(start, LANES)]
+                for n in range(3):
+                    ref[pos, k, rows : rows + 1, n * LANES : (n + 1) * LANES] = lines[
+                        n : n + 1
+                    ].astype(jnp.bfloat16)
+
+    if split:
+        write(sent, 0, 1)
+
+        @pl.when(pl.program_id(1) < 2)
+        def _():
+            write(leave, 0, 0)
+
+        @pl.when(pl.program_id(1) >= 2)
+        def _():
+            write(keep, 0, 0)
+
     else:
         cols = rights[0].shape[1] // groups
-        for slot in range(groups):
-            start = pl.multiple_of((where[2] ^ turn(slot, keep)) * cols, LANES)
-            emit(slot, mxu(kept[0][...], rights[0][:, pl.ds(start, cols)], NN), slice(0, cols))
-
-
-def weight_grad(place, pairs, received, split, name):
+        for side in range(2):
+            for pos, slot in enumerate(ORDER):
+                start = pl.multiple_of((where[2] ^ turn(slot, core ^ side)) * cols, LANES)
+                part = mxu(kept[0][side], rights[0][:, pl.ds(start, cols)], NN)
+                part = part.astype(jnp.bfloat16).reshape(chips, rows, cols)
+                if side == 1:
+                    sent[pos] = part
+                else:
+                    (leave if pos < 2 else keep)[pos % 2] = part
+
+
+def weight_grad(place, pairs, split, name, sums=None):
     tokens, height = pairs[0][0].shape
     groups, chips = place.groups, place.chips
     rows = height // place.shards
-    own = received is not None
     step_chips = chips if split else max(1, 1024 // (2 * rows))
     steps = chips // step_chips
     grid = (steps, groups if split else 1)
+    extra = 0 if sums is None else 16
 
     def block(j, s):
-        return s[2] ^ turn(j, s[0] if own else 1 - s[0])
+        return s[2] ^ turn(ordered_slot(j), s[0])
+
+    def position(j):
+        return jnp.where(j == 0, 3, jnp.where(j == 3, 0, j))
 
     cols = 0
     right_specs = []
@@ -1142,46 +1169,48 @@
             right_specs.append(pl.BlockSpec((tokens, size), lambda i, j, s: (0, block(j, s))))
         cols += size * (right.shape[0] if right.ndim == 3 else 1)
     left_spec = pl.BlockSpec((tokens, step_chips * 2 * rows), lambda i, j, s: (0, i))
-    if split:
-        passed = pl.BlockSpec((1, step_chips, rows, cols), lambda i, j, s: (j, i, 0, 0))
-    else:
-        passed = pl.BlockSpec((groups, step_chips, rows, cols), lambda i, j, s: (0, i, 0, 0))
     in_specs = [left_spec] * len(pairs) + right_specs
     inputs = [left for left, _ in pairs] + [right for _, right in pairs]
-    if own:
-        in_specs.append(passed)
-        inputs.append(received)
-        one = pl.BlockSpec((step_chips, rows, cols), lambda i, j, s: (i, 0, 0))
-        two = pl.BlockSpec((2, step_chips, rows, cols), lambda i, j, s: (0, i, 0, 0))
-        out_specs = [one, one, two]
-        shape = (chips, rows, cols)
-        out_shape = [
-            shaped(shape, jnp.bfloat16),
-            shaped(shape, jnp.bfloat16),
-            shaped((2, *shape), jnp.bfloat16),
+    if extra:
+        in_specs.append(pl.BlockSpec(sums.shape, lambda i, j, s: (0, 0)))
+        inputs.append(sums)
+    tall = rows + extra
+    if split:
+        one = (1, step_chips, tall, cols)
+        out_specs = [
+            pl.BlockSpec(one, lambda i, j, s: (jnp.minimum(j, 1), i, 0, 0)),
+            pl.BlockSpec(one, lambda i, j, s: (jnp.maximum(j - 2, 0), i, 0, 0)),
+            pl.BlockSpec(one, lambda i, j, s: (position(j), i, 0, 0)),
         ]
     else:
-        out_specs = passed
-        out_shape = shaped((groups, chips, rows, cols), jnp.bfloat16)
+        out_specs = [
+            pl.BlockSpec((n, step_chips, tall, cols), lambda i, j, s: (0, i, 0, 0))
+            for n in (2, 2, groups)
+        ]
     return pl.pallas_call(
         functools.partial(
-            weight_grad_kernel, own=own, rows=rows, groups=groups, count=len(pairs), split=split
+            weight_grad_kernel,
+            rows=rows,
+            groups=groups,
+            count=len(pairs),
+            split=split,
+            extra=extra,
         ),
         grid_spec=pltpu.PrefetchScalarGridSpec(
             num_scalar_prefetch=1,
             grid=grid,
             in_specs=in_specs,
             out_specs=out_specs,
-            scratch_shapes=[pltpu.VMEM((step_chips * rows, tokens), jnp.bfloat16)] * len(pairs),
+            scratch_shapes=[pltpu.VMEM((2, step_chips * rows, tokens), jnp.bfloat16)] * len(pairs),
         ),
-        out_shape=out_shape,
+        out_shape=[shaped((n, chips, tall, cols), jnp.bfloat16) for n in (2, 2, groups)],
         compiler_params=params(60),
         cost_estimate=pl.CostEstimate(
-            flops=tokens * height * cols * groups,
+            flops=2 * tokens * height * cols * groups,
             bytes_accessed=2 * (tokens * (height + cols * groups) + height * cols * groups),
             transcendentals=0,
         ),
-        name="wgrad_" + name + ("_own" if own else "_sent"),
+        name="wgrad_" + name,
     )(place.scalars, *inputs)
 
 
@@ -1193,36 +1222,36 @@
 
 
 class Reduction:
-    def __init__(self, place, pairs, split, name, *wait):
+    def __init__(self, place, pairs, split, name, *wait, sums=None):
         self.place = place
         if wait:
             pairs = [(after(pairs[0][0], *wait), pairs[0][1])] + pairs[1:]
-        self.call = (pairs, split, name)
-        self.sent = weight_grad(place, pairs, None, split, name)
-        self.received = place.swap_core(self.sent)
-
-    def own(self, *wait):
-        pairs, split, name = self.call
-        received = after(self.received, *wait) if wait else self.received
-        self.own_0, self.own_2, both = weight_grad(self.place, pairs, received, split, name)
-        self.first = self.place.swap_grp(both, 0)
-        return self.own_0
+        self.leave, self.keep, sent = weight_grad(place, pairs, split, name, sums)
+        self.made = self.leave
+        self.core = place.swap_core(sent)
+
+    def near(self, *wait):
+        self.core = after(self.core, *wait) if wait else self.core
+        leave = add(self.leave, self.core[:2])
+        self.first = self.place.swap_grp(leave, 0)
+        return leave
 
     def middle(self, *wait):
         self.first = after(self.first, *wait) if wait else self.first
-        second = add(self.own_2, self.first[1])
+        second = add(self.keep[1], self.core[3], self.first[1])
         self.second = self.place.swap_grp(second, 1)
         return second
 
+    def column(self, *wait):
+        second = after(self.second, *wait) if wait else self.second
+        mine = add(self.keep[0], self.core[2], self.first[0], second)
+        return mine, lambda chip: lax.dynamic_index_in_dim(mine, chip, 0, False)
+
     def along(self, *wait):
         place = self.place
-        second = after(self.second, *wait) if wait else self.second
-        mine = add(self.own_0, self.first[0], second)
-        blocks = [
-            lax.dynamic_index_in_dim(mine, place.slot_chip(slot), 0, False) for slot in range(4)
-        ]
-        self.mine = blocks
-        self.first = place.swap_chip(jnp.stack([blocks[1], blocks[3]]), 0)
+        mine, at = self.column(*wait)
+        self.mine = [at(place.slot_chip(slot)) for slot in range(4)]
+        self.first = place.swap_chip(jnp.stack([self.mine[1], self.mine[3]]), 0)
         return mine
 
     def along_far(self, *wait):
@@ -1235,32 +1264,42 @@
         second = after(self.second, *wait) if wait else self.second
         return add(self.mine[0], self.first[0], second)
 
+    def share_direct(self, *wait):
+        place = self.place
+        mine, at = self.column(*wait)
+        terms = [
+            place.permute(at(place.chip ^ k), (2 * k, 2 * k)) for k in range(place.chips - 1, 0, -1)
+        ]
+        return add(at(place.chip), *terms)
+
 
 class Replication:
-    def __init__(self, place, share):
+    def __init__(self, place, share, direct=False):
         self.place = place
-        self.pair = jnp.stack([share, place.swap_grp(share, 0)])
+        if direct:
+            size = place.shards
+            self.blocks = [share] + [None] * 3
+            for mask in (3, 1, 2):
+                self.blocks[mask] = place.permute(share, (mask * size, mask * size))
+            self.owner = lambda n: place.grp ^ n
+        else:
+            self.blocks = [share, place.swap_grp(share, 0), None, None]
+            self.owner = place.slot_grp
 
     def far(self, *wait):
-        pair = after(self.pair, *wait) if wait else self.pair
-        self.rest = self.place.swap_grp(pair, 1)
-        return self.rest
+        pair = jnp.stack([self.blocks[0], after(self.blocks[1], *wait)])
+        rest = self.place.swap_grp(pair, 1)
+        self.blocks[2:] = [rest[0], rest[1]]
+        return rest
 
     def result(self):
-        place = self.place
-        slots = [self.pair[0], self.pair[1], self.rest[0], self.rest[1]]
         ordered = []
-        for g in range(place.groups):
-            block = slots[0]
-            for slot in range(1, place.groups):
-                block = jnp.where(place.slot_grp(slot) == g, slots[slot], block)
+        for g in range(self.place.groups):
+            block = self.blocks[0]
+            for n in range(1, self.place.groups):
+                block = jnp.where(self.owner(n) == g, self.blocks[n], block)
             ordered.append(block.astype(jnp.float32))
         return ordered
-
-
-def own_part(place, vector):
-    size = vector.shape[0] // place.shards
-    return lax.dynamic_slice_in_dim(vector, place.shard * size, size)
 
 
 def on_device_permutes(
@@ -1300,46 +1339,44 @@
     c1.chips_far()
     joined = c1.join()
     c1.near()
-    c2.chips_near(joined)
     small = Vectors(
         place,
         (b_query, b_value, b_attn_out, norm1_gain, norm1_bias, b_out, norm2_gain, norm2_bias, b_in),
         c1.pair[1],
     )
+    vectors, bias_in, qkv_bias = small.unpack()
+    c2.chips_near(joined)
     c1.cross(0)
-    far = c1.far()
     c2.chips_far()
+    far = c1.far(c2.rest[0], vectors)
     c1.cross(1, 2)
     c1.cross(3)
     c2.join(far)
     c2.near()
-    vectors, bias_in, qkv_bias = small.unpack()
     blank = jnp.ones((1, width), jnp.float32)
     qkv_scale = jnp.concatenate([blank / math.sqrt(HD), blank, blank], 1)
 
     mixed, full_qkv = project_qkv(place, rows, Window(c1, 0, w_qkv.shape[1]), qkv_bias, qkv_scale)
     c3.chips_near(mixed)
     c2.cross(0, wait=(mixed,))
-    quarter = pairs // 4
+    share_of = (pairs // 2 - pairs // 8, pairs // 4, pairs // 2 - pairs // 8)
     forward = None
-    for n in range(4):
-        gate = ()
-        if n == 2:
-            gate = (c3.rest[1],)
-        if n == 3:
-            gate = (c2.held[3],)
+    start = 0
+    for n, count in enumerate(share_of):
+        wait = (c2.held[3],) if n == 2 else ()
         forward = attention_forward(
-            after(mixed, *gate) if gate else mixed, seg_col, seg_row, n * quarter, quarter, forward
+            after(mixed, *wait) if wait else mixed, seg_col, seg_row, start, count, forward
         )
+        start += count
         done = forward[1]
         if n == 0:
+            c2.far(done)
             c3.chips_far(done)
-            c2.far(done)
             c2.cross(1, 2, wait=(done,))
-        if n == 2:
-            c2.cross(3, wait=(done,))
+        if n == 1:
             c3.join(done)
             c3.near()
+            c2.cross(3, wait=(done,))
     contexts, lse = forward
     normed, scale_one, normed_low, full_attn = project_out(
         place, contexts, Window(c2, w_in.shape[1], w_attn_out.shape[1]), rows, vectors
@@ -1355,15 +1392,13 @@
     )
 
     r_out = Reduction(place, [(hidden, out_low)], False, "out")
-    pre_low, bias_in_grad = feed_out_back(after(out_low, r_out.sent), full_out, slope)
-    own_out = r_out.own(pre_low)
-    r_in = Reduction(place, [(normed_low, pre_low)], True, "in", own_out)
-    first_grad, attn_low, first_sums = feed_in_back(
-        after(pre_low, r_in.sent), full_in, second_grad, normed, scale_one, vectors
-    )
-    mid_out = r_out.middle(first_grad)
-    own_in = r_in.own(first_grad, mid_out)
-    context_grad = project_out_back(after(attn_low, own_in), full_attn)
+    pre_low, bias_in_grad = feed_out_back(after(out_low, r_out.made), full_out, slope)
+    near = r_out.near(pre_low)
+    r_in = Reduction(place, [(normed_low, pre_low)], True, "in", near)
+    first_grad, attn_low, context_grad, first_sums = feed_in_back(
+        after(pre_low, r_in.made), full_in, second_grad, normed, scale_one, vectors, full_attn
+    )
+    quarter = pairs // 4
 
     def back(start, at, before=None, *wait):
         return attention_backward(
@@ -1380,51 +1415,46 @@
             before,
         )
 
-    part = back(0, 0)
+    middle = r_out.middle(first_grad)
+    near = r_in.near(first_grad)
+    part = back(0, 0, None, middle, near)
     along = r_out.along(part[1])
     low_a, late_a = back(quarter, quarter, part, along)
-    mid_in = r_in.middle(late_a)
+    middle = r_in.middle(late_a)
     along = r_out.along_far(late_a)
-    r_a = Reduction(place, [(contexts, attn_low), (rows, low_a)], True, "a", mid_in, along)
-    part = back(2 * quarter, 0, None, r_a.sent)
+    r_a = Reduction(place, [(contexts, attn_low), (rows, low_a)], True, "a", middle, along)
+    part = back(2 * quarter, 0, None, r_a.made)
+    share_out = r_out.share(part[1])
     along = r_in.along(part[1])
-    share_out = r_out.share(part[1])
-    own_a = r_a.own(along, share_out)
-    low_b, late_b = back(3 * quarter, quarter, part, own_a)
-    mid_a = r_a.middle(late_b)
+    near = r_a.near(part[1])
+    low_b, late_b = back(3 * quarter, quarter, part, share_out, along, near)
+    middle = r_a.middle(late_b)
     along = r_in.along_far(late_b)
     sums = pack_sums(late_a, late_b, first_sums, second_sums, bias_in_grad)
-    r_b = Reduction(place, [(rows, low_b)], True, "b", mid_a, along, sums)
-    sums = sums + place.swap_core(sums)
-    along = r_a.along(r_b.sent)
-    share_in = r_in.share(r_b.sent)
+    r_b = Reduction(place, [(rows, low_b)], True, "b", middle, along, sums=sums)
+    along = r_a.along(r_b.made)
+    share_in = r_in.share(r_b.made)
     inner = share_in.shape[1] // groups
     joined = jnp.concatenate(
         [share_out] + [share_in[:, n * inner : (n + 1) * inner] for n in range(groups)]
     )
     all_ffn = Replication(place, joined)
-    own_b = r_b.own(along, joined, sums)
-    sums = after(sums, own_b)
-    sums = sums + place.swap_grp(after(sums, own_b), 0)
-    along = r_a.along_far(own_b)
-    input_grad = project_qkv_back(
-        (low_a, after(low_b, own_b, along, all_ffn.pair)), full_qkv, first_grad
-    )
-    mid_b = r_b.middle(input_grad)
-    sums = sums + place.swap_grp(after(sums, mid_b), 1)
-    all_ffn.far(mid_b)
-    all_a = Replication(place, r_a.share(mid_b))
-    along = r_b.along()
-    sums = sums + place.swap_chip(after(sums, along), 0)
-    all_a.far(along)
-    along = r_b.along_far()
-    sums = sums + place.swap_chip(after(sums, along), 1)
-    all_b = Replication(place, r_b.share())
-    all_b.far()
-    mine = lax.dynamic_slice_in_dim(sums, place.shard * LANES, LANES, 1)
-    inner_mine = own_part(place, sums[B_IN : B_IN + 4].reshape(-1))
+    near = r_b.near(along, joined)
+    input_grad = project_qkv_back((low_a, after(low_b, near)), full_qkv, first_grad)
+    middle = r_b.middle(input_grad)
+    along = r_a.along_far(middle)
+    all_ffn.far(middle)
+    share_b = r_b.share_direct()
+    all_a = Replication(place, r_a.share(along))
+    all_b = Replication(place, share_b, direct=True)
+    all_a.far()
 
     parts_a, parts_b = all_a.result(), all_b.result()
+    small = [
+        block[-16, n * LANES : (n + 1) * LANES] for block in parts_b for n in range(3)
+    ]
+    inner_mine = jnp.concatenate(small[B_IN:])
+    parts_b = [block[:-16] for block in parts_b]
     heads = parts_b[0].shape[1] // 3
     skip = parts_a[0].shape[1] - 3 * heads
     w_attn_grad = jnp.concatenate([block[:, :skip] for block in parts_a], 1)
@@ -1454,18 +1484,18 @@
         layer_out[None],
         input_grad[None],
         w_qkv_grad,
-        mine[B_QUERY],
-        mine[B_VALUE],
+        small[B_QUERY],
+        small[B_VALUE],
         w_attn_grad,
-        mine[B_ATTN],
-        mine[GAIN_ONE],
-        mine[SHIFT_ONE],
+        small[B_ATTN],
+        small[GAIN_ONE],
+        small[SHIFT_ONE],
         w_in_grad,
         inner_mine,
         w_out_grad,
-        mine[B_OUT],
-        mine[GAIN_TWO],
-        mine[SHIFT_TWO],
+        small[B_OUT],
+        small[GAIN_TWO],
+        small[SHIFT_TWO],
     )
 
 

time: 512 us -> 484 us (0.945)
  Pallas kernels: 311 us -> 284 us
  waiting for transfers between devices: 88.5 us -> 74.7 us
  other arithmetic: 30.4 us -> 40.6 us
    pallas_call x8 -> x4, Pallas kernels: 87.7 us -> 58.1 us  [weight_grad(): pl.pallas_call(functools.partial(weight_grad_kernel, rows=rows, groups=gr...]
    convert_element_type x15 -> x18, other arithmetic: 16.8 us -> 30.7 us  [add(): return total.astype(jnp.bfloat16)]
    ppermute x61 -> x58, waiting for transfers between devices: 88.5 us -> 74.7 us  [permute(): return lax.ppermute(array, AXES, pairs)]
    pallas_call x4, Pallas kernels: 66.5 us -> 73.1 us  [weight_call(): pl.pallas_call(body, grid_spec=pltpu.PrefetchScalarGridSpec(num_scalar_pr...]
    pallas_call x4 -> x3, Pallas kernels: 50.8 us -> 48.3 us  [plain_call(): pl.pallas_call(kernel, grid=(steps,), in_specs=in_specs, out_specs=out_sp...]
    pallas_call x4 -> x3, Pallas kernels: 39.7 us -> 37.8 us  [attention_forward(): pl.pallas_call(body, grid=(pairs,), in_specs=[pair(0), pair(1), pair(2),...]
    ppermute x61 -> x58, starting transfers between devices: 61.4 us -> 59.9 us  [permute(): return lax.ppermute(array, AXES, pairs)]
  transfers between devices with their start and end apart: 61 -> 58, of which waited for: 21 -> 21; matrix products, arithmetic and copies ran while one was open for 6% -> 8% of each run, Pallas kernels for 46% -> 43%
where the time goes in v6:
time: 484 us; the launch traced here: 476 us
  Pallas kernels  284 us (59%)
  waiting for transfers between devices  74.7 us (15%)
  starting transfers between devices  59.9 us (12%)
  other arithmetic  40.6 us (8%)
  local copies, waits for them, and re-layouts  14.5 us (3%)
    ppermute x58, waiting for transfers between devices, permute(): return lax.ppermute(array, AXES, pairs)  74.7 us
    pallas_call x4, Pallas kernels, weight_call(): pl.pallas_call(body, grid_spec=pltpu.PrefetchScalarGridSpec(num_scalar_pr...  73.1 us
    pallas_call x4, Pallas kernels, attention_backward(): pl.pallas_call(body, grid=(pairs,), in_specs=[pair(0), pair(1), pair(2),...  63.7 us
    ppermute x58, starting transfers between devices, permute(): return lax.ppermute(array, AXES, pairs)  59.9 us
    pallas_call x4, Pallas kernels, weight_grad(): pl.pallas_call(functools.partial(weight_grad_kernel, rows=rows, groups=gr...  58.1 us
    pallas_call x3, Pallas kernels, plain_call(): pl.pallas_call(kernel, grid=(steps,), in_specs=in_specs, out_specs=out_sp...  48.3 us
    pallas_call x3, Pallas kernels, attention_forward(): pl.pallas_call(body, grid=(pairs,), in_specs=[pair(0), pair(1), pair(2),...  37.8 us
    convert_element_type x18, other arithmetic, add(): return total.astype(jnp.bfloat16)  30.7 us
  transfers between devices with their start and end apart: 58, of which 21 were waited for; matrix products, arithmetic and copies ran while one was open for 8% of the time, Pallas kernels for 43%

profile of v6, /device:TPU:0, one launch (start us, length us, event | category | flops | bytes accessed | tf_op | source)
XLA Modules:
  0.0 475.8 jit_solution(15152896564144743787)
XLA Ops:
  0.7 3.1 collective-permute-start
  3.8 5.6 %collective-permute-done = bf16[128,768]{1,0:T(8,128)(2,1)S(1)} collective-permute-done((bf16[128,768]{1,0:T(8,128)(2,1)}, bf16[128,768]{1,0:T(8,128)(2,1)S(1)}, u32[]{:S(2)}, u32[]{:S(2)}) %collective-permute-start) | collective-permute-done | bytes 196640 | tf_op jit(solution)/shard_map/ppermute | solution.py:526
  10.3 2.5 collective-permute-start.1
  21.3 2.5 collective-permute-start.6
  24.8 1.6 collective-permute-start.2
  27.0 3.4 collective-permute-start.7
  31.0 3.1 collective-permute-done.7
  34.7 1.5 vectors.1
  37.0 2.2 collective-permute-start.8
  39.2 2.6 collective-permute-start.17
  42.3 6.0 %collective-permute-done.3.refs_2_ = bf16[4,128,768]{2,1,0:T(8,128)(2,1)} collective-permute-done((bf16[4,128,768]{2,1,0:T(8,128)(2,1)S(1)}, bf16[4,128,768]{2,1,0:T(8,128)(2,1)}, u32[]{:S(2)}, u32[]{:S(2)}) %collective-permute-start.3) | collective-permute-done | bytes 786464 | tf_op jit(solution)/shard_map/ppermute | solution.py:526
  48.3 8.4 %collective-permute-done.8.refs_3_ = bf16[4,128,768]{2,1,0:T(8,128)(2,1)} collective-permute-done((bf16[4,128,768]{2,1,0:T(8,128)(2,1)}, bf16[4,128,768]{2,1,0:T(8,128)(2,1)}, u32[]{:S(2)}, u32[]{:S(2)}) %collective-permute-start.8) | collective-permute-done | bytes 786464 | tf_op jit(solution)/shard_map/ppermute | solution.py:526
  60.6 12.7 %qkv.1 = (bf16[1024,3072]{1,0:T(8,128)(2,1)}, bf16[1024,3072]{1,0:T(8,128)(2,1)}) custom-call(s32[3]{0:T(128)} %pad_add_fusion.where, bf16[4,128,768]{2,1,0:T(8,128)(2,1)} %copy-done.10, bf16[4,128,768]{2,1,0:T(8,128)(2,1)} %collective-permute-done.2.refs_1_, bf16[4,128,768]{2,1,0:T(8,128)(2,1)} %collective-permute-done.3.refs_2_, ...), custom_call_target="tpu_custom_call" | custom-call | flops 6442450944 | bytes 20996096 | tf_op jit(solution)/shard_map/qkv/pallas_call | solution.py:662
  73.4 13.7 %attn_fwd.3 = (bf16[1024,1024]{1,0:T(8,128)(2,1)}, f32[8,2,1024]{2,1,0:T(2,128)}) custom-call(bf16[1024,3072]{1,0:T(8,128)(2,1)} %get-tuple-element.126.q_ref.k_ref.v_ref.refs_0_.refs_1_.refs_2_, bf16[1024,3072]{1,0:T(8,128)(2,1)} %get-tuple-element.126.q_ref.k_ref.v_ref.refs_0_.refs_1_.refs_2_, ...), custom_call_target="tpu_custom_call" | custom-call | flops 6442450944 | bytes 3145728 | tf_op jit(solution)/shard_map/attn_fwd/pallas_call | solution.py:385
  87.1 2.5 collective-permute-done.18.refs_1_
  89.6 1.7 collective-permute-start.13
  91.3 6.2 %collective-permute-done.13 = bf16[512,256]{1,0:T(8,128)(2,1)S(1)} collective-permute-done((bf16[512,256]{1,0:T(8,128)(2,1)S(1)}, bf16[512,256]{1,0:T(8,128)(2,1)S(1)}, u32[]{:S(2)}, u32[]{:S(2)}) %collective-permute-start.13) | collective-permute-done | bytes 262176 | tf_op jit(solution)/shard_map/ppermute | solution.py:526
  97.5 2.5 collective-permute-start.14
  100.0 10.3 %attn_fwd.4 = (bf16[1024,1024]{1,0:T(8,128)(2,1)}, f32[8,2,1024]{2,1,0:T(2,128)}) custom-call(bf16[1024,3072]{1,0:T(8,128)(2,1)} %get-tuple-element.126.q_ref.k_ref.v_ref.refs_0_.refs_1_.refs_2_, bf16[1024,3072]{1,0:T(8,128)(2,1)} %get-tuple-element.126.q_ref.k_ref.v_ref.refs_0_.refs_1_.refs_2_, ...), custom_call_target="tpu_custom_call", output_to_operand_aliasing={{0}: (5, {}), {1}: (6, {})} | custom-call | flops 4294967296 | bytes 2097152 | tf_op jit(solution)/shard_map/attn_fwd/pallas_call | solution.py:385
  111.0 2.4 collective-permute-done.14
  113.4 2.1 pad_maximum_fusion.2.refs_0_
  116.0 2.1 collective-permute-start.16
  118.1 13.7 %attn_fwd.5 = (bf16[1024,1024]{1,0:T(8,128)(2,1)}, f32[8,2,1024]{2,1,0:T(2,128)}) custom-call(bf16[1024,3072]{1,0:T(8,128)(2,1)} %get-tuple-element.126.q_ref.k_ref.v_ref.refs_0_.refs_1_.refs_2_, bf16[1024,3072]{1,0:T(8,128)(2,1)} %get-tuple-element.126.q_ref.k_ref.v_ref.refs_0_.refs_1_.refs_2_, ...), custom_call_target="tpu_custom_call", output_to_operand_aliasing={{0}: (5, {}), {1}: (6, {})} | custom-call | flops 6442450944 | bytes 3145728 | tf_op jit(solution)/shard_map/attn_fwd/pallas_call | solution.py:385
  131.8 9.6 %attn_out.1 = (f32[1024,1024]{1,0:T(8,128)}, f32[1024,128]{1,0:T(8,128)}, bf16[1024,1024]{1,0:T(8,128)(2,1)}, bf16[1024,1024]{1,0:T(8,128)(2,1)}) custom-call(s32[3]{0:T(128)} %pad_add_fusion.where, bf16[4,128,1280]{2,1,0:T(8,128)(2,1)} %copy-done, bf16[4,128,1280]{2,1,0:T(8,128)(2,1)} %copy-done.4, bf16[4,128,1280]{2,1,0:T(8,128)(2,1)} %collective-permute-done.19.refs_2_, ...), custom_call_target="tpu_custom_call" | custom-call | flops 2147483648 | bytes 15269888 | tf_op jit(solution)/shard_map/attn_out/pallas_call | solution.py:662
  142.3 29.1 %feed_in.1 = (bf16[1024,4096]{1,0:T(8,128)(2,1)}, bf16[1024,4096]{1,0:T(8,128)(2,1)}, bf16[1024,4096]{1,0:T(8,128)(2,1)}) custom-call(s32[3]{0:T(128)} %pad_add_fusion.where, bf16[4,128,1280]{2,1,0:T(8,128)(2,1)} %copy-done, bf16[4,128,1280]{2,1,0:T(8,128)(2,1)} %copy-done.4, bf16[4,128,1280]{2,1,0:T(8,128)(2,1)} %collective-permute-done.19.refs_2_, ...), custom_call_target="tpu_custom_call" | custom-call | flops 8589934592 | bytes 35667968 | tf_op jit(solution)/shard_map/feed_in/pallas_call | solution.py:662
  174.3 21.7 %feed_out.1 = (bf16[1024,1024]{1,0:T(8,128)(2,1)}, f32[1024,1024]{1,0:T(8,128)}, bf16[1024,1024]{1,0:T(8,128)(2,1)}, f32[8,1024]{1,0:T(8,128)}, bf16[4096,1024]{1,0:T(8,128)(2,1)}) custom-call(s32[3]{0:T(128)} %pad_add_fusion.where, bf16[4,512,256]{2,1,0:T(8,128)(2,1)} %pad_maximum_fusion.2.refs_0_, bf16[4,512,256]{2,1,0:T(8,128)(2,1)} %collective-permute-done.15.refs_1_, ...), custom_call_target="tpu_custom_call" | custom-call | flops 8589934592 | bytes 39948288 | tf_op jit(solution)/shard_map/feed_out/pallas_call | solution.py:662
  195.9 14.0 %wgrad_out.1 = (bf16[2,4,512,256]{3,2,1,0:T(8,128)(2,1)}, bf16[2,4,512,256]{3,2,1,0:T(8,128)(2,1)}, bf16[4,4,512,256]{3,2,1,0:T(8,128)(2,1)}) custom-call(s32[3]{0:T(128)} %pad_add_fusion.where, bf16[1024,4096]{1,0:T(8,128)(2,1)} %get-tuple-element.135.refs_8_.refs_0_, bf16[1024,1024]{1,0:T(8,128)(2,1)} %get-tuple-element.142.refs_1_.g_ref), custom_call_target="tpu_custom_call" | custom-call | flops 8589934592 | bytes 18874368 | tf_op jit(solution)/shard_map/wgrad_out/pallas_call | solution.py:1190
  210.3 14.9 %feed_out_back.1 = (bf16[1024,4096]{1,0:T(8,128)(2,1)}, f32[1,4096]{1,0:T(1,128)}) custom-call(bf16[1024,1024]{1,0:T(8,128)(2,1)} %get-tuple-element.142.refs_1_.g_ref, bf16[4096,1024]{1,0:T(8,128)(2,1)} %get-tuple-element.143.w_ref, bf16[1024,4096]{1,0:T(8,128)(2,1)} %get-tuple-element.144.slope_ref), custom_call_target="tpu_custom_call" | custom-call | flops 8589934592 | bytes 27279360 | tf_op jit(solution)/shard_map/feed_out_back/pallas_call | solution.py:686
  225.2 2.7 add_convert_fusion.1
  227.9 15.5 %wgrad_in.1 = (bf16[2,4,128,1024]{3,2,1,0:T(8,128)(2,1)}, bf16[2,4,128,1024]{3,2,1,0:T(8,128)(2,1)}, bf16[4,4,128,1024]{3,2,1,0:T(8,128)(2,1)}) custom-call(s32[3]{0:T(128)} %pad_add_fusion.where, bf16[1024,1024]{1,0:T(8,128)(2,1)} %get-tuple-element.148.refs_8_.refs_0_, bf16[1024,4096]{1,0:T(8,128)(2,1)} %get-tuple-element.150.refs_1_.p_ref), custom_call_target="tpu_custom_call" | custom-call | flops 8589934592 | bytes 18874368 | tf_op jit(solution)/shard_map/wgrad_in/pallas_call | solution.py:1190
  244.9 20.9 %feed_in_back.1 = (f32[1024,1024]{1,0:T(8,128)}, bf16[1024,1024]{1,0:T(8,128)(2,1)}, bf16[1024,1024]{1,0:T(8,128)(2,1)}, f32[8,1024]{1,0:T(8,128)}) custom-call(bf16[1024,4096]{1,0:T(8,128)(2,1)} %get-tuple-element.150.refs_1_.p_ref, bf16[1024,4096]{1,0:T(8,128)(2,1)} %get-tuple-element.151.w_ref, f32[1024,1024]{1,0:T(8,128)} %get-tuple-element.152.g_ref, ...), custom_call_target="tpu_custom_call" | custom-call | flops 10737418240 | bytes 36274176 | tf_op jit(solution)/shard_map/feed_in_back/pallas_call | solution.py:686
  265.8 3.9 collective-permute-done.31
  269.7 2.4 fusion.3
  272.1 1.9 collective-permute-start.32
  274.1 3.9 add_convert_fusion
  278.7 16.0 %attn_bwd.4 = (bf16[3,1024,512]{2,1,0:T(8,128)(2,1)}, f32[2,512]{1,0:T(2,128)}) custom-call(bf16[1024,3072]{1,0:T(8,128)(2,1)} %get-tuple-element.126.q_ref.k_ref.v_ref.refs_0_.refs_1_.refs_2_, bf16[1024,3072]{1,0:T(8,128)(2,1)} %get-tuple-element.126.q_ref.k_ref.v_ref.refs_0_.refs_1_.refs_2_, ...), custom_call_target="tpu_custom_call" | custom-call | flops 10737418240 | bytes 4194304 | tf_op jit(solution)/shard_map/attn_bwd/pallas_call | solution.py:480
  294.7 2.4 fusion.1
  298.3 15.8 %attn_bwd.5 = (bf16[3,1024,512]{2,1,0:T(8,128)(2,1)}, f32[2,512]{1,0:T(2,128)}) custom-call(bf16[1024,3072]{1,0:T(8,128)(2,1)} %get-tuple-element.126.q_ref.k_ref.v_ref.refs_0_.refs_1_.refs_2_, bf16[1024,3072]{1,0:T(8,128)(2,1)} %get-tuple-element.126.q_ref.k_ref.v_ref.refs_0_.refs_1_.refs_2_, ...), custom_call_target="tpu_custom_call", output_to_operand_aliasing={{0}: (8, {}), {1}: (9, {})} | custom-call | flops 10737418240 | bytes 4194304 | tf_op jit(solution)/shard_map/attn_bwd/pallas_call | solution.py:480
  314.3 3.5 fusion.4
  317.7 16.2 %wgrad_a.1 = (bf16[2,4,128,640]{3,2,1,0:T(8,128)(2,1)}, bf16[2,4,128,640]{3,2,1,0:T(8,128)(2,1)}, bf16[4,4,128,640]{3,2,1,0:T(8,128)(2,1)}) custom-call(s32[3]{0:T(128)} %pad_add_fusion.where, bf16[1024,1024]{1,0:T(8,128)(2,1)} %get-tuple-element.172.refs_8_.refs_3_.refs_0_, bf16[1024,1024]{1,0:T(8,128)(2,1)} %bitcast.150, ...), custom_call_target="tpu_custom_call" | custom-call | flops 5368709120 | bytes 12582912 | tf_op jit(solution)/shard_map/wgrad_a/pallas_call | solution.py:1190
  334.0 4.1 collective-permute-start.35
  339.4 15.9 %attn_bwd.6 = (bf16[3,1024,512]{2,1,0:T(8,128)(2,1)}, f32[2,512]{1,0:T(2,128)}) custom-call(bf16[1024,3072]{1,0:T(8,128)(2,1)} %get-tuple-element.126.q_ref.k_ref.v_ref.refs_0_.refs_1_.refs_2_, bf16[1024,3072]{1,0:T(8,128)(2,1)} %get-tuple-element.126.q_ref.k_ref.v_ref.refs_0_.refs_1_.refs_2_, ...), custom_call_target="tpu_custom_call" | custom-call | flops 10737418240 | bytes 4194304 | tf_op jit(solution)/shard_map/attn_bwd/pallas_call | solution.py:480
  355.5 2.9 fusion
  358.4 2.7 add_convert_fusion.2
  361.3 15.9 %attn_bwd.7 = (bf16[3,1024,512]{2,1,0:T(8,128)(2,1)}, f32[2,512]{1,0:T(2,128)}) custom-call(bf16[1024,3072]{1,0:T(8,128)(2,1)} %get-tuple-element.126.q_ref.k_ref.v_ref.refs_0_.refs_1_.refs_2_, bf16[1024,3072]{1,0:T(8,128)(2,1)} %get-tuple-element.126.q_ref.k_ref.v_ref.refs_0_.refs_1_.refs_2_, ...), custom_call_target="tpu_custom_call", output_to_operand_aliasing={{0}: (8, {}), {1}: (9, {})} | custom-call | flops 10737418240 | bytes 4194304 | tf_op jit(solution)/shard_map/attn_bwd/pallas_call | solution.py:480
  377.2 1.5 pack_sums.1.refs_2_
  379.8 2.4 fusion.6
  382.1 12.4 %wgrad_b.1 = (bf16[2,4,144,384]{3,2,1,0:T(8,128)(2,1)}, bf16[2,4,144,384]{3,2,1,0:T(8,128)(2,1)}, bf16[4,4,144,384]{3,2,1,0:T(8,128)(2,1)}) custom-call(s32[3]{0:T(128)} %pad_add_fusion.where, bf16[1024,1024]{1,0:T(8,128)(2,1)} %bitcast.151, bf16[3,1024,512]{2,1,0:T(8,128)(2,1)} %get-tuple-element.197.refs_1_, f32[32,1024]{1,0:T(8,128)} %pack_sums.1.refs_2_), custom_call_target="tpu_custom_call" | custom-call | flops 3221225472 | bytes 8388608 | tf_op jit(solution)/shard_map/wgrad_b/pallas_call | solution.py:1190
  396.6 8.0 %collective-permute-done.43 = bf16[128,1024]{1,0:T(8,128)(2,1)S(1)} collective-permute-done((bf16[128,1024]{1,0:T(8,128)(2,1)S(1)}, bf16[128,1024]{1,0:T(8,128)(2,1)S(1)}, u32[]{:S(2)}, u32[]{:S(2)}) %collective-permute-start.43) | collective-permute-done | bytes 262176 | tf_op jit(solution)/shard_map/ppermute | solution.py:526
  406.4 1.6 fusion.2
  410.4 1.6 collective-permute-start.45
  412.1 1.4 collective-permute-start.44
  413.5 12.6 %qkv_back.1 = f32[1024,1024]{1,0:T(8,128)} custom-call(bf16[1024,3072]{1,0:T(8,128)(2,1)} %get-tuple-element.139.w_ref, bf16[3,1024,512]{2,1,0:T(8,128)(2,1)} %get-tuple-element.167.refs_3_.refs_0_, bf16[3,1024,512]{2,1,0:T(8,128)(2,1)} %get-tuple-element.197.refs_1_, f32[1024,1024]{1,0:T(8,128)} %get-tuple-element.157.refs_2_), custom_call_target="tpu_custom_call" | custom-call | flops 6442450944 | bytes 20971520 | tf_op jit(solution)/shard_map/qkv_back/pallas_call | solution.py:686
  427.5 2.9 collective-permute-start.46
  431.1 4.4 collective-permute-done.46
  435.7 4.1 collective-permute-done.56
  439.8 2.5 collective-permute-done.47
  442.8 1.5 fusion.5
  444.4 3.1 collective-permute-start.50
  448.9 1.7 collective-permute-start.57
  451.5 4.5 collective-permute-done.51
  460.8 2.3 collective-permute-done.53
  463.1 5.5 %collective-permute-done.54 = bf16[144,384]{1,0:T(8,128)(2,1)S(1)} collective-permute-done((bf16[144,384]{1,0:T(8,128)(2,1)S(1)}, bf16[144,384]{1,0:T(8,128)(2,1)S(1)}, u32[]{:S(2)}, u32[]{:S(2)}) %collective-permute-start.54) | collective-permute-done | bytes 110624 | tf_op jit(solution)/shard_map/ppermute | solution.py:526
  473.3 1.8 pad_maximum_fusion
  (229 shorter events, 49.6 us)
Async XLA Ops:
  0.6 25.7 %copy-start.12 = (bf16[128,256]{1,0:T(8,128)(2,1)S(1)}, bf16[128,256]{1,0:T(8,128)(2,1)}, u32[]{:S(2)}) copy-start(bf16[128,256]{1,0:T(8,128)(2,1)} %param.24) | copy-start | bytes 196612
  0.7 8.7 %collective-permute-start = (bf16[128,768]{1,0:T(8,128)(2,1)}, bf16[128,768]{1,0:T(8,128)(2,1)S(1)}, u32[]{:S(2)}, u32[]{:S(2)}) collective-permute-start(bf16[128,768]{1,0:T(8,128)(2,1)} %param.21), channel_id=1, source_target_pairs={{0,2},{1,5},{2,0},{3,7},{4,6},{5,1},{6,4},{7,3},{8,10},{9,13},{10,... | collective-permute-start | bytes 589832 | tf_op jit(solution)/shard_map/ppermute | solution.py:526
  10.3 13.5 %collective-permute-start.1 = (bf16[2,128,768]{2,1,0:T(8,128)(2,1)S(1)}, bf16[2,128,768]{2,1,0:T(8,128)(2,1)S(1)}, u32[]{:S(2)}, u32[]{:S(2)}) collective-permute-start(bf16[2,128,768]{2,1,0:T(8,128)(2,1)S(1)} %pad_maximum_fusion.10), channel_id=1, source_target_pairs={{0,4},{1,3},{2,6},{3,1},{4,0},{5,7},{6,2},{7,5},{8,12},{9,11},{10,... | collective-permute-start | bytes 1179656 | tf_op jit(solution)/shard_map/ppermute | solution.py:526
  20.2 1.2 collective-permute-start.5
  21.3 5.7 %collective-permute-start.6 = (bf16[2,16,128]{2,1,0:T(8,128)(2,1)S(1)}, bf16[2,16,128]{2,1,0:T(8,128)(2,1)S(1)}, u32[]{:S(2)}, u32[]{:S(2)}) collective-permute-start(bf16[2,16,128]{2,1,0:T(8,128)(2,1)S(1)} %get-tuple-element.237), channel_id=1, source_target_pairs={{0,2},{1,5},{2,0},{3,7},{4,6},{5,1},{6,4},{7,3},{8,10},{9,13},{10,... | collective-permute-start | bytes 24584 | tf_op jit(solution)/shard_map/ppermute | solution.py:526
  24.8 33.1 %copy-start.10 = (bf16[4,128,768]{2,1,0:T(8,128)(2,1)}, bf16[4,128,768]{2,1,0:T(8,128)(2,1)S(1)}, u32[]{:S(2)}) copy-start(bf16[4,128,768]{2,1,0:T(8,128)(2,1)S(1)} %pad_maximum_fusion.4.refs_0_) | copy-start | bytes 2359300
  24.8 12.2 %collective-permute-start.2 = (bf16[4,128,768]{2,1,0:T(8,128)(2,1)S(1)}, bf16[4,128,768]{2,1,0:T(8,128)(2,1)}, u32[]{:S(2)}, u32[]{:S(2)}) collective-permute-start(bf16[4,128,768]{2,1,0:T(8,128)(2,1)S(1)} %pad_maximum_fusion.4.refs_0_), channel_id=1, source_target_pairs={{0,8},{1,17},{2,10},{3,19},{4,12},{5,21},{6,14},{7,23},{8,0},{9,25... | collective-permute-start | bytes 2359304 | tf_op jit(solution)/shard_map/ppermute | solution.py:526
  26.4 32.8 %copy-start.13 = (s32[1,1024]{1,0:T(1,128)S(1)}, s32[1,1024]{1,0:T(1,128)}, u32[]{:S(2)}) copy-start(s32[1,1024]{1,0:T(1,128)} %refs_6_.7) | copy-start | bytes 12292
  26.4 10.2 %collective-permute-start.4 = (bf16[128,1280]{1,0:T(8,128)(2,1)S(1)}, bf16[128,1280]{1,0:T(8,128)(2,1)S(1)}, u32[]{:S(2)}, u32[]{:S(2)}) collective-permute-start(bf16[128,1280]{1,0:T(8,128)(2,1)S(1)} %pad_maximum_fusion.11), channel_id=1, source_target_pairs={{0,2},{1,5},{2,0},{3,7},{4,6},{5,1},{6,4},{7,3},{8,10},{9,13},{10,... | collective-permute-start | bytes 983048 | tf_op jit(solution)/shard_map/ppermute | solution.py:526
  27.0 7.1 %collective-permute-start.7 = (bf16[2,2,16,128]{3,2,1,0:T(8,128)(2,1)S(1)}, bf16[2,2,16,128]{3,2,1,0:T(8,128)(2,1)S(1)}, u32[]{:S(2)}, u32[]{:S(2)}) collective-permute-start(bf16[2,2,16,128]{3,2,1,0:T(8,128)(2,1)S(1)} %pad_maximum_fusion.15), channel_id=1, source_target_pairs={{0,4},{1,3},{2,6},{3,1},{4,0},{5,7},{6,2},{7,5},{8,12},{9,11},{10,... | collective-permute-start | bytes 49160 | tf_op jit(solution)/shard_map/ppermute | solution.py:526
  36.2 12.1 %collective-permute-start.3 = (bf16[4,128,768]{2,1,0:T(8,128)(2,1)S(1)}, bf16[4,128,768]{2,1,0:T(8,128)(2,1)}, u32[]{:S(2)}, u32[]{:S(2)}) collective-permute-start(bf16[4,128,768]{2,1,0:T(8,128)(2,1)S(1)} %pad_maximum_fusion.4.refs_0_), channel_id=1, source_target_pairs={{0,16},{1,9},{2,18},{3,11},{4,20},{5,13},{6,22},{7,15},{8,24},{9,1... | collective-permute-start | bytes 2359304 | tf_op jit(solution)/shard_map/ppermute | solution.py:526
  37.0 19.7 %collective-permute-start.8 = (bf16[4,128,768]{2,1,0:T(8,128)(2,1)}, bf16[4,128,768]{2,1,0:T(8,128)(2,1)}, u32[]{:S(2)}, u32[]{:S(2)}) collective-permute-start(bf16[4,128,768]{2,1,0:T(8,128)(2,1)} %collective-permute-done.2.refs_1_), channel_id=1, source_target_pairs={{0,16},{1,9},{2,18},{3,11},{4,20},{5,13},{6,22},{7,15},{8,24},{9,1... | collective-permute-start | bytes 2359304 | tf_op jit(solution)/shard_map/ppermute | solution.py:526
  39.2 18.6 %collective-permute-start.17 = (bf16[2,128,1280]{2,1,0:T(8,128)(2,1)S(1)}, bf16[2,128,1280]{2,1,0:T(8,128)(2,1)S(1)}, u32[]{:S(2)}, u32[]{:S(2)}) collective-permute-start(bf16[2,128,1280]{2,1,0:T(8,128)(2,1)S(1)} %pad_maximum_fusion.5), channel_id=1, source_target_pairs={{0,4},{1,3},{2,6},{3,1},{4,0},{5,7},{6,2},{7,5},{8,12},{9,11},{10,... | collective-permute-start | bytes 1966088 | tf_op jit(solution)/shard_map/ppermute | solution.py:526
  41.8 18.5 %collective-permute-start.9 = (bf16[4,128,768]{2,1,0:T(8,128)(2,1)S(1)}, bf16[4,128,768]{2,1,0:T(8,128)(2,1)}, u32[]{:S(2)}, u32[]{:S(2)}) collective-permute-start(bf16[4,128,768]{2,1,0:T(8,128)(2,1)S(1)} %pad_maximum_fusion.4.refs_0_), channel_id=1, source_target_pairs={{0,1},{1,0},{2,3},{3,2},{4,5},{5,4},{6,7},{7,6},{8,9},{9,8},{10,11... | collective-permute-start | bytes 2359304 | tf_op jit(solution)/shard_map/ppermute | solution.py:526
  41.8 18.9 %collective-permute-start.10 = (bf16[4,128,768]{2,1,0:T(8,128)(2,1)}, bf16[4,128,768]{2,1,0:T(8,128)(2,1)}, u32[]{:S(2)}, u32[]{:S(2)}) collective-permute-start(bf16[4,128,768]{2,1,0:T(8,128)(2,1)} %collective-permute-done.2.refs_1_), channel_id=1, source_target_pairs={{0,1},{1,0},{2,3},{3,2},{4,5},{5,4},{6,7},{7,6},{8,9},{9,8},{10,11... | collective-permute-start | bytes 2359304 | tf_op jit(solution)/shard_map/ppermute | solution.py:526
  48.3 12.4 %collective-permute-start.11 = (bf16[4,128,768]{2,1,0:T(8,128)(2,1)}, bf16[4,128,768]{2,1,0:T(8,128)(2,1)}, u32[]{:S(2)}, u32[]{:S(2)}) collective-permute-start(bf16[4,128,768]{2,1,0:T(8,128)(2,1)} %collective-permute-done.3.refs_2_), channel_id=1, source_target_pairs={{0,1},{1,0},{2,3},{3,2},{4,5},{5,4},{6,7},{7,6},{8,9},{9,8},{10,11... | collective-permute-start | bytes 2359304 | tf_op jit(solution)/shard_map/ppermute | solution.py:526
  56.7 4.0 collective-permute-start.12
  57.9 33.4 %copy-start = (bf16[4,128,1280]{2,1,0:T(8,128)(2,1)}, bf16[4,128,1280]{2,1,0:T(8,128)(2,1)S(1)}, u32[]{:S(2)}) copy-start(bf16[4,128,1280]{2,1,0:T(8,128)(2,1)S(1)} %pad_maximum_fusion.1.refs_0_) | copy-start | bytes 3932164
  57.9 31.7 %collective-permute-start.18 = (bf16[4,128,1280]{2,1,0:T(8,128)(2,1)S(1)}, bf16[4,128,1280]{2,1,0:T(8,128)(2,1)S(1)}, u32[]{:S(2)}, u32[]{:S(2)}) collective-permute-start(bf16[4,128,1280]{2,1,0:T(8,128)(2,1)S(1)} %pad_maximum_fusion.1.refs_0_), channel_id=1, source_target_pairs={{0,8},{1,17},{2,10},{3,19},{4,12},{5,21},{6,14},{7,23},{8,0},{9,25... | collective-permute-start | bytes 3932168 | tf_op jit(solution)/shard_map/ppermute | solution.py:526
  60.2 39.8 %collective-permute-start.19 = (bf16[4,128,1280]{2,1,0:T(8,128)(2,1)S(1)}, bf16[4,128,1280]{2,1,0:T(8,128)(2,1)}, u32[]{:S(2)}, u32[]{:S(2)}) collective-permute-start(bf16[4,128,1280]{2,1,0:T(8,128)(2,1)S(1)} %pad_maximum_fusion.1.refs_0_), channel_id=1, source_target_pairs={{0,16},{1,9},{2,18},{3,11},{4,20},{5,13},{6,22},{7,15},{8,24},{9,1... | collective-permute-start | bytes 3932168 | tf_op jit(solution)/shard_map/ppermute | solution.py:526
  89.6 21.3 %collective-permute-start.20 = (bf16[4,128,1280]{2,1,0:T(8,128)(2,1)S(1)}, bf16[4,128,1280]{2,1,0:T(8,128)(2,1)}, u32[]{:S(2)}, u32[]{:S(2)}) collective-permute-start(bf16[4,128,1280]{2,1,0:T(8,128)(2,1)S(1)} %collective-permute-done.18.refs_1_), channel_id=1, source_target_pairs={{0,16},{1,9},{2,18},{3,11},{4,20},{5,13},{6,22},{7,15},{8,24},{9,1... | collective-permute-start | bytes 3932168 | tf_op jit(solution)/shard_map/ppermute | solution.py:526
  89.6 7.8 %collective-permute-start.13 = (bf16[512,256]{1,0:T(8,128)(2,1)S(1)}, bf16[512,256]{1,0:T(8,128)(2,1)S(1)}, u32[]{:S(2)}, u32[]{:S(2)}) collective-permute-start(bf16[512,256]{1,0:T(8,128)(2,1)S(1)} %copy-done.7), channel_id=1, source_target_pairs={{0,2},{1,5},{2,0},{3,7},{4,6},{5,1},{6,4},{7,3},{8,10},{9,13},{10,... | collective-permute-start | bytes 786440 | tf_op jit(solution)/shard_map/ppermute | solution.py:526
  91.3 24.7 %collective-permute-start.21 = (bf16[4,128,1280]{2,1,0:T(8,128)(2,1)S(1)}, bf16[4,128,1280]{2,1,0:T(8,128)(2,1)}, u32[]{:S(2)}, u32[]{:S(2)}) collective-permute-start(bf16[4,128,1280]{2,1,0:T(8,128)(2,1)S(1)} %pad_maximum_fusion.1.refs_0_), channel_id=1, source_target_pairs={{0,1},{1,0},{2,3},{3,2},{4,5},{5,4},{6,7},{7,6},{8,9},{9,8},{10,11... | collective-permute-start | bytes 3932168 | tf_op jit(solution)/shard_map/ppermute | solution.py:526
  97.5 15.9 %collective-permute-start.14 = (bf16[2,512,256]{2,1,0:T(8,128)(2,1)S(1)}, bf16[2,512,256]{2,1,0:T(8,128)(2,1)}, u32[]{:S(2)}, u32[]{:S(2)}) collective-permute-start(bf16[2,512,256]{2,1,0:T(8,128)(2,1)S(1)} %pad_maximum_fusion.6), channel_id=1, source_target_pairs={{0,4},{1,3},{2,6},{3,1},{4,0},{5,7},{6,2},{7,5},{8,12},{9,11},{10,... | collective-permute-start | bytes 1572872 | tf_op jit(solution)/shard_map/ppermute | solution.py:526
  100.0 31.8 %collective-permute-start.22 = (bf16[4,128,1280]{2,1,0:T(8,128)(2,1)S(1)}, bf16[4,128,1280]{2,1,0:T(8,128)(2,1)}, u32[]{:S(2)}, u32[]{:S(2)}) collective-permute-start(bf16[4,128,1280]{2,1,0:T(8,128)(2,1)S(1)} %collective-permute-done.18.refs_1_), channel_id=1, source_target_pairs={{0,1},{1,0},{2,3},{3,2},{4,5},{5,4},{6,7},{7,6},{8,9},{9,8},{10,11... | collective-permute-start | bytes 3932168 | tf_op jit(solution)/shard_map/ppermute | solution.py:526
  110.4 21.5 %collective-permute-start.23 = (bf16[4,128,1280]{2,1,0:T(8,128)(2,1)}, bf16[4,128,1280]{2,1,0:T(8,128)(2,1)}, u32[]{:S(2)}, u32[]{:S(2)}) collective-permute-start(bf16[4,128,1280]{2,1,0:T(8,128)(2,1)} %collective-permute-done.19.refs_2_), channel_id=1, source_target_pairs={{0,1},{1,0},{2,3},{3,2},{4,5},{5,4},{6,7},{7,6},{8,9},{9,8},{10,11... | collective-permute-start | bytes 3932168 | tf_op jit(solution)/shard_map/ppermute | solution.py:526
  110.9 20.9 %collective-permute-start.24 = (bf16[4,128,1280]{2,1,0:T(8,128)(2,1)}, bf16[4,128,1280]{2,1,0:T(8,128)(2,1)}, u32[]{:S(2)}, u32[]{:S(2)}) collective-permute-start(bf16[4,128,1280]{2,1,0:T(8,128)(2,1)} %collective-permute-done.20.refs_3_), channel_id=1, source_target_pairs={{0,1},{1,0},{2,3},{3,2},{4,5},{5,4},{6,7},{7,6},{8,9},{9,8},{10,11... | collective-permute-start | bytes 3932168 | tf_op jit(solution)/shard_map/ppermute | solution.py:526
  115.5 25.9 %collective-permute-start.15 = (bf16[4,512,256]{2,1,0:T(8,128)(2,1)}, bf16[4,512,256]{2,1,0:T(8,128)(2,1)}, u32[]{:S(2)}, u32[]{:S(2)}) collective-permute-start(bf16[4,512,256]{2,1,0:T(8,128)(2,1)} %pad_maximum_fusion.2.refs_0_), channel_id=1, source_target_pairs={{0,8},{1,17},{2,10},{3,19},{4,12},{5,21},{6,14},{7,23},{8,0},{9,25... | collective-permute-start | bytes 3145736 | tf_op jit(solution)/shard_map/ppermute | solution.py:526
  116.0 25.6 %collective-permute-start.16 = (bf16[4,512,256]{2,1,0:T(8,128)(2,1)}, bf16[4,512,256]{2,1,0:T(8,128)(2,1)S(1)}, u32[]{:S(2)}, u32[]{:S(2)}) collective-permute-start(bf16[4,512,256]{2,1,0:T(8,128)(2,1)} %pad_maximum_fusion.2.refs_0_), channel_id=1, source_target_pairs={{0,16},{1,9},{2,18},{3,11},{4,20},{5,13},{6,22},{7,15},{8,24},{9,1... | collective-permute-start | bytes 3145736 | tf_op jit(solution)/shard_map/ppermute | solution.py:526
  141.5 29.9 %collective-permute-start.25 = (bf16[4,512,256]{2,1,0:T(8,128)(2,1)}, bf16[4,512,256]{2,1,0:T(8,128)(2,1)S(1)}, u32[]{:S(2)}, u32[]{:S(2)}) collective-permute-start(bf16[4,512,256]{2,1,0:T(8,128)(2,1)} %collective-permute-done.15.refs_1_), channel_id=1, source_target_pairs={{0,16},{1,9},{2,18},{3,11},{4,20},{5,13},{6,22},{7,15},{8,24},{9,1... | collective-permute-start | bytes 3145736 | tf_op jit(solution)/shard_map/ppermute | solution.py:526
  141.6 31.3 %collective-permute-start.27 = (bf16[4,512,256]{2,1,0:T(8,128)(2,1)}, bf16[4,512,256]{2,1,0:T(8,128)(2,1)S(1)}, u32[]{:S(2)}, u32[]{:S(2)}) collective-permute-start(bf16[4,512,256]{2,1,0:T(8,128)(2,1)} %collective-permute-done.15.refs_1_), channel_id=1, source_target_pairs={{0,1},{1,0},{2,3},{3,2},{4,5},{5,4},{6,7},{7,6},{8,9},{9,8},{10,11... | collective-permute-start | bytes 3145736 | tf_op jit(solution)/shard_map/ppermute | solution.py:526
  141.7 29.7 %copy-start.17 = (bf16[4,512,256]{2,1,0:T(8,128)(2,1)}, bf16[4,512,256]{2,1,0:T(8,128)(2,1)S(1)}, u32[]{:S(2)}) copy-start(bf16[4,512,256]{2,1,0:T(8,128)(2,1)S(1)} %collective-permute-done.16.refs_2_) | copy-start | bytes 3145732
  141.7 31.2 %collective-permute-start.28 = (bf16[4,512,256]{2,1,0:T(8,128)(2,1)S(1)}, bf16[4,512,256]{2,1,0:T(8,128)(2,1)}, u32[]{:S(2)}, u32[]{:S(2)}) collective-permute-start(bf16[4,512,256]{2,1,0:T(8,128)(2,1)S(1)} %collective-permute-done.16.refs_2_), channel_id=1, source_target_pairs={{0,1},{1,0},{2,3},{3,2},{4,5},{5,4},{6,7},{7,6},{8,9},{9,8},{10,11... | collective-permute-start | bytes 3145736 | tf_op jit(solution)/shard_map/ppermute | solution.py:526
  142.2 30.8 %collective-permute-start.26 = (bf16[4,512,256]{2,1,0:T(8,128)(2,1)}, bf16[4,512,256]{2,1,0:T(8,128)(2,1)}, u32[]{:S(2)}, u32[]{:S(2)}) collective-permute-start(bf16[4,512,256]{2,1,0:T(8,128)(2,1)} %pad_maximum_fusion.2.refs_0_), channel_id=1, source_target_pairs={{0,1},{1,0},{2,3},{3,2},{4,5},{5,4},{6,7},{7,6},{8,9},{9,8},{10,11... | collective-permute-start | bytes 3145736 | tf_op jit(solution)/shard_map/ppermute | solution.py:526
  142.2 29.6 %copy-start.15 = (s32[1,1024]{1,0:T(1,128)S(1)}, s32[1,1024]{1,0:T(1,128)}, u32[]{:S(2)}) copy-start(s32[1,1024]{1,0:T(1,128)} %param.19) | copy-start | bytes 12292
  171.4 2.9 collective-permute-start.29
  210.0 15.2 %collective-permute-start.30 = (bf16[4,4,512,256]{3,2,1,0:T(8,128)(2,1)}, bf16[4,4,512,256]{3,2,1,0:T(8,128)(2,1)}, u32[]{:S(2)}, u32[]{:S(2)}) collective-permute-start(bf16[4,4,512,256]{3,2,1,0:T(8,128)(2,1)} %get-tuple-element.146), channel_id=1, source_target_pairs={{0,1},{1,0},{2,3},{3,2},{4,5},{5,4},{6,7},{7,6},{8,9},{9,8},{10,11... | collective-permute-start | bytes 12582920 | tf_op jit(solution)/shard_map/ppermute | solution.py:526
  243.4 30.7 %collective-permute-start.33 = (bf16[4,4,128,1024]{3,2,1,0:T(8,128)(2,1)}, bf16[4,4,128,1024]{3,2,1,0:T(8,128)(2,1)}, u32[]{:S(2)}, u32[]{:S(2)}) collective-permute-start(bf16[4,4,128,1024]{3,2,1,0:T(8,128)(2,1)} %get-tuple-element.159), channel_id=1, source_target_pairs={{0,1},{1,0},{2,3},{3,2},{4,5},{5,4},{6,7},{7,6},{8,9},{9,8},{10,11... | collective-permute-start | bytes 12582920 | tf_op jit(solution)/shard_map/ppermute | solution.py:526
  243.6 26.1 %collective-permute-start.31 = (bf16[2,4,512,256]{3,2,1,0:T(8,128)(2,1)S(1)}, bf16[2,4,512,256]{3,2,1,0:T(8,128)(2,1)}, u32[]{:S(2)}, u32[]{:S(2)}) collective-permute-start(bf16[2,4,512,256]{3,2,1,0:T(8,128)(2,1)S(1)} %add_convert_fusion.1), channel_id=1, source_target_pairs={{0,8},{1,17},{2,10},{3,19},{4,12},{5,21},{6,14},{7,23},{8,0},{9,25... | collective-permute-start | bytes 6291464 | tf_op jit(solution)/shard_map/ppermute | solution.py:526
  272.1 22.6 %collective-permute-start.32 = (bf16[4,512,256]{2,1,0:T(8,128)(2,1)S(1)}, bf16[4,512,256]{2,1,0:T(8,128)(2,1)S(1)}, u32[]{:S(2)}, u32[]{:S(2)}) collective-permute-start(bf16[4,512,256]{2,1,0:T(8,128)(2,1)S(1)} %fusion.3), channel_id=1, source_target_pairs={{0,16},{1,9},{2,18},{3,11},{4,20},{5,13},{6,22},{7,15},{8,24},{9,1... | collective-permute-start | bytes 3145736 | tf_op jit(solution)/shard_map/ppermute | solution.py:526
  278.0 36.3 %collective-permute-start.36 = (bf16[2,4,128,1024]{3,2,1,0:T(8,128)(2,1)}, bf16[2,4,128,1024]{3,2,1,0:T(8,128)(2,1)}, u32[]{:S(2)}, u32[]{:S(2)}) collective-permute-start(bf16[2,4,128,1024]{3,2,1,0:T(8,128)(2,1)} %add_convert_fusion), channel_id=1, source_target_pairs={{0,8},{1,17},{2,10},{3,19},{4,12},{5,21},{6,14},{7,23},{8,0},{9,25... | collective-permute-start | bytes 6291464 | tf_op jit(solution)/shard_map/ppermute | solution.py:526
  297.2 17.0 %collective-permute-start.34 = (bf16[2,512,256]{2,1,0:T(8,128)(2,1)S(1)}, bf16[2,512,256]{2,1,0:T(8,128)(2,1)S(1)}, u32[]{:S(2)}, u32[]{:S(2)}) collective-permute-start(bf16[2,512,256]{2,1,0:T(8,128)(2,1)S(1)} %pad_maximum_fusion.7), channel_id=1, source_target_pairs={{0,2},{1,5},{2,0},{3,7},{4,6},{5,1},{6,4},{7,3},{8,10},{9,13},{10,... | collective-permute-start | bytes 1572872 | tf_op jit(solution)/shard_map/ppermute | solution.py:526
  333.9 24.5 %collective-permute-start.38 = (bf16[4,4,128,640]{3,2,1,0:T(8,128)(2,1)}, bf16[4,4,128,640]{3,2,1,0:T(8,128)(2,1)}, u32[]{:S(2)}, u32[]{:S(2)}) collective-permute-start(bf16[4,4,128,640]{3,2,1,0:T(8,128)(2,1)} %get-tuple-element.179), channel_id=1, source_target_pairs={{0,1},{1,0},{2,3},{3,2},{4,5},{5,4},{6,7},{7,6},{8,9},{9,8},{10,11... | collective-permute-start | bytes 7864328 | tf_op jit(solution)/shard_map/ppermute | solution.py:526
  334.0 21.4 %collective-permute-start.35 = (bf16[512,256]{1,0:T(8,128)(2,1)S(1)}, bf16[512,256]{1,0:T(8,128)(2,1)S(1)}, u32[]{:S(2)}, u32[]{:S(2)}) collective-permute-start(bf16[512,256]{1,0:T(8,128)(2,1)S(1)} %fusion.11), channel_id=1, source_target_pairs={{0,4},{1,3},{2,6},{3,1},{4,0},{5,7},{6,2},{7,5},{8,12},{9,11},{10,... | collective-permute-start | bytes 786440 | tf_op jit(solution)/shard_map/ppermute | solution.py:526
  338.1 17.4 %collective-permute-start.37 = (bf16[4,128,1024]{2,1,0:T(8,128)(2,1)}, bf16[4,128,1024]{2,1,0:T(8,128)(2,1)S(1)}, u32[]{:S(2)}, u32[]{:S(2)}) collective-permute-start(bf16[4,128,1024]{2,1,0:T(8,128)(2,1)} %fusion.4), channel_id=1, source_target_pairs={{0,16},{1,9},{2,18},{3,11},{4,20},{5,13},{6,22},{7,15},{8,24},{9,1... | collective-permute-start | bytes 3145736 | tf_op jit(solution)/shard_map/ppermute | solution.py:526
  361.1 18.6 %collective-permute-start.39 = (bf16[2,4,128,640]{3,2,1,0:T(8,128)(2,1)}, bf16[2,4,128,640]{3,2,1,0:T(8,128)(2,1)}, u32[]{:S(2)}, u32[]{:S(2)}) collective-permute-start(bf16[2,4,128,640]{3,2,1,0:T(8,128)(2,1)} %add_convert_fusion.2), channel_id=1, source_target_pairs={{0,8},{1,17},{2,10},{3,19},{4,12},{5,21},{6,14},{7,23},{8,0},{9,25... | collective-permute-start | bytes 3932168 | tf_op jit(solution)/shard_map/ppermute | solution.py:526
  361.2 16.1 %collective-permute-start.40 = (bf16[2,128,1024]{2,1,0:T(8,128)(2,1)S(1)}, bf16[2,128,1024]{2,1,0:T(8,128)(2,1)}, u32[]{:S(2)}, u32[]{:S(2)}) collective-permute-start(bf16[2,128,1024]{2,1,0:T(8,128)(2,1)S(1)} %pad_maximum_fusion.8), channel_id=1, source_target_pairs={{0,2},{1,5},{2,0},{3,7},{4,6},{5,1},{6,4},{7,3},{8,10},{9,13},{10,... | collective-permute-start | bytes 1572872 | tf_op jit(solution)/shard_map/ppermute | solution.py:526
  394.5 13.5 %collective-permute-start.41 = (bf16[4,4,144,384]{3,2,1,0:T(8,128)(2,1)}, bf16[4,4,144,384]{3,2,1,0:T(8,128)(2,1)S(1)}, u32[]{:S(2)}, u32[]{:S(2)}) collective-permute-start(bf16[4,4,144,384]{3,2,1,0:T(8,128)(2,1)} %get-tuple-element.193), channel_id=1, source_target_pairs={{0,1},{1,0},{2,3},{3,2},{4,5},{5,4},{6,7},{7,6},{8,9},{9,8},{10,11... | collective-permute-start | bytes 5308424 | tf_op jit(solution)/shard_map/ppermute | solution.py:526
  394.5 10.1 %collective-permute-start.43 = (bf16[128,1024]{1,0:T(8,128)(2,1)S(1)}, bf16[128,1024]{1,0:T(8,128)(2,1)S(1)}, u32[]{:S(2)}, u32[]{:S(2)}) collective-permute-start(bf16[128,1024]{1,0:T(8,128)(2,1)S(1)} %fusion.12), channel_id=1, source_target_pairs={{0,4},{1,3},{2,6},{3,1},{4,0},{5,7},{6,2},{7,5},{8,12},{9,11},{10,... | collective-permute-start | bytes 786440 | tf_op jit(solution)/shard_map/ppermute | solution.py:526
  395.6 10.8 %collective-permute-start.42 = (bf16[4,128,640]{2,1,0:T(8,128)(2,1)}, bf16[4,128,640]{2,1,0:T(8,128)(2,1)S(1)}, u32[]{:S(2)}, u32[]{:S(2)}) collective-permute-start(bf16[4,128,640]{2,1,0:T(8,128)(2,1)} %fusion.6), channel_id=1, source_target_pairs={{0,16},{1,9},{2,18},{3,11},{4,20},{5,13},{6,22},{7,15},{8,24},{9,1... | collective-permute-start | bytes 1966088 | tf_op jit(solution)/shard_map/ppermute | solution.py:526
  410.4 15.7 %collective-permute-start.45 = (bf16[2,4,144,384]{3,2,1,0:T(8,128)(2,1)}, bf16[2,4,144,384]{3,2,1,0:T(8,128)(2,1)}, u32[]{:S(2)}, u32[]{:S(2)}) collective-permute-start(bf16[2,4,144,384]{3,2,1,0:T(8,128)(2,1)} %add_convert_fusion.5), channel_id=1, source_target_pairs={{0,8},{1,17},{2,10},{3,19},{4,12},{5,21},{6,14},{7,23},{8,0},{9,25... | collective-permute-start | bytes 2654216 | tf_op jit(solution)/shard_map/ppermute | solution.py:526
  412.1 15.3 %collective-permute-start.44 = (bf16[2,128,640]{2,1,0:T(8,128)(2,1)S(1)}, bf16[2,128,640]{2,1,0:T(8,128)(2,1)S(1)}, u32[]{:S(2)}, u32[]{:S(2)}) collective-permute-start(bf16[2,128,640]{2,1,0:T(8,128)(2,1)S(1)} %pad_maximum_fusion.12), channel_id=1, source_target_pairs={{0,2},{1,5},{2,0},{3,7},{4,6},{5,1},{6,4},{7,3},{8,10},{9,13},{10,... | collective-permute-start | bytes 983048 | tf_op jit(solution)/shard_map/ppermute | solution.py:526
  427.5 8.0 %collective-permute-start.46 = (bf16[128,640]{1,0:T(8,128)(2,1)S(1)}, bf16[128,640]{1,0:T(8,128)(2,1)S(1)}, u32[]{:S(2)}, u32[]{:S(2)}) collective-permute-start(bf16[128,640]{1,0:T(8,128)(2,1)S(1)} %fusion.16), channel_id=1, source_target_pairs={{0,4},{1,3},{2,6},{3,1},{4,0},{5,7},{6,2},{7,5},{8,12},{9,11},{10,... | collective-permute-start | bytes 491528 | tf_op jit(solution)/shard_map/ppermute | solution.py:526
  430.4 9.4 %collective-permute-start.56 = (bf16[1024,256]{1,0:T(8,128)(2,1)S(1)}, bf16[1024,256]{1,0:T(8,128)(2,1)S(1)}, u32[]{:S(2)}, u32[]{:S(2)}) collective-permute-start(bf16[1024,256]{1,0:T(8,128)(2,1)S(1)} %constant_dynamic-update-slice_fusion), channel_id=1, source_target_pairs={{0,8},{1,17},{2,10},{3,19},{4,12},{5,21},{6,14},{7,23},{8,0},{9,25... | collective-permute-start | bytes 1572872 | tf_op jit(solution)/shard_map/ppermute | solution.py:526
  430.4 12.4 %collective-permute-start.49 = (bf16[4,144,384]{2,1,0:T(8,128)(2,1)S(1)}, bf16[4,144,384]{2,1,0:T(8,128)(2,1)}, u32[]{:S(2)}, u32[]{:S(2)}) collective-permute-start(bf16[4,144,384]{2,1,0:T(8,128)(2,1)S(1)} %fusion.9), channel_id=1, source_target_pairs={{0,16},{1,9},{2,18},{3,11},{4,20},{5,13},{6,22},{7,15},{8,24},{9,1... | collective-permute-start | bytes 1327112 | tf_op jit(solution)/shard_map/ppermute | solution.py:526
  435.6 6.7 %collective-permute-start.47 = (bf16[128,640]{1,0:T(8,128)(2,1)S(1)}, bf16[128,640]{1,0:T(8,128)(2,1)S(1)}, u32[]{:S(2)}, u32[]{:S(2)}) collective-permute-start(bf16[128,640]{1,0:T(8,128)(2,1)S(1)} %fusion.10), channel_id=1, source_target_pairs={{0,8},{1,17},{2,10},{3,19},{4,12},{5,21},{6,14},{7,23},{8,0},{9,25... | collective-permute-start | bytes 491528 | tf_op jit(solution)/shard_map/ppermute | solution.py:526
  442.4 17.3 %collective-permute-start.48 = (bf16[2,128,640]{2,1,0:T(8,128)(2,1)S(1)}, bf16[2,128,640]{2,1,0:T(8,128)(2,1)S(1)}, u32[]{:S(2)}, u32[]{:S(2)}) collective-permute-start(bf16[2,128,640]{2,1,0:T(8,128)(2,1)S(1)} %pad_maximum_fusion.13), channel_id=1, source_target_pairs={{0,16},{1,9},{2,18},{3,11},{4,20},{5,13},{6,22},{7,15},{8,24},{9,1... | collective-permute-start | bytes 983048 | tf_op jit(solution)/shard_map/ppermute | solution.py:526
  444.4 7.1 %collective-permute-start.50 = (bf16[144,384]{1,0:T(8,128)(2,1)S(1)}, bf16[144,384]{1,0:T(8,128)(2,1)S(1)}, u32[]{:S(2)}, u32[]{:S(2)}) collective-permute-start(bf16[144,384]{1,0:T(8,128)(2,1)S(1)} %get-tuple-element.221), channel_id=1, source_target_pairs={{0,6},{1,7},{2,4},{3,5},{4,2},{5,3},{6,0},{7,1},{8,14},{9,15},{10,... | collective-permute-start | bytes 331784 | tf_op jit(solution)/shard_map/ppermute | solution.py:526
  447.4 8.6 %collective-permute-start.51 = (bf16[144,384]{1,0:T(8,128)(2,1)S(1)}, bf16[144,384]{1,0:T(8,128)(2,1)S(1)}, u32[]{:S(2)}, u32[]{:S(2)}) collective-permute-start(bf16[144,384]{1,0:T(8,128)(2,1)S(1)} %get-tuple-element.223), channel_id=1, source_target_pairs={{0,4},{1,5},{2,6},{3,7},{4,0},{5,1},{6,2},{7,3},{8,12},{9,13},{10,... | collective-permute-start | bytes 331784 | tf_op jit(solution)/shard_map/ppermute | solution.py:526
  447.4 8.6 %collective-permute-start.52 = (bf16[144,384]{1,0:T(8,128)(2,1)S(1)}, bf16[144,384]{1,0:T(8,128)(2,1)S(1)}, u32[]{:S(2)}, u32[]{:S(2)}) collective-permute-start(bf16[144,384]{1,0:T(8,128)(2,1)S(1)} %get-tuple-element.222), channel_id=1, source_target_pairs={{0,2},{1,3},{2,0},{3,1},{4,6},{5,7},{6,4},{7,5},{8,10},{9,11},{10,... | collective-permute-start | bytes 331784 | tf_op jit(solution)/shard_map/ppermute | solution.py:526
  448.9 21.6 %collective-permute-start.57 = (bf16[2,1024,256]{2,1,0:T(8,128)(2,1)S(1)}, bf16[2,1024,256]{2,1,0:T(8,128)(2,1)S(1)}, u32[]{:S(2)}, u32[]{:S(2)}) collective-permute-start(bf16[2,1024,256]{2,1,0:T(8,128)(2,1)S(1)} %pad_maximum_fusion.3), channel_id=1, source_target_pairs={{0,16},{1,9},{2,18},{3,11},{4,20},{5,13},{6,22},{7,15},{8,24},{9,1... | collective-permute-start | bytes 3145736 | tf_op jit(solution)/shard_map/ppermute | solution.py:526
  456.1 7.0 %collective-permute-start.53 = (bf16[144,384]{1,0:T(8,128)(2,1)S(1)}, bf16[144,384]{1,0:T(8,128)(2,1)S(1)}, u32[]{:S(2)}, u32[]{:S(2)}) collective-permute-start(bf16[144,384]{1,0:T(8,128)(2,1)S(1)} %fusion.15), channel_id=1, source_target_pairs={{0,24},{1,25},{2,26},{3,27},{4,28},{5,29},{6,30},{7,31},{8,16},{9,... | collective-permute-start | bytes 331784 | tf_op jit(solution)/shard_map/ppermute | solution.py:526
  457.5 11.0 %collective-permute-start.54 = (bf16[144,384]{1,0:T(8,128)(2,1)S(1)}, bf16[144,384]{1,0:T(8,128)(2,1)S(1)}, u32[]{:S(2)}, u32[]{:S(2)}) collective-permute-start(bf16[144,384]{1,0:T(8,128)(2,1)S(1)} %fusion.15), channel_id=1, source_target_pairs={{0,16},{1,17},{2,18},{3,19},{4,20},{5,21},{6,22},{7,23},{8,24},{9,... | collective-permute-start | bytes 331784 | tf_op jit(solution)/shard_map/ppermute | solution.py:526
  458.3 10.3 %collective-permute-start.55 = (bf16[144,384]{1,0:T(8,128)(2,1)S(1)}, bf16[144,384]{1,0:T(8,128)(2,1)S(1)}, u32[]{:S(2)}, u32[]{:S(2)}) collective-permute-start(bf16[144,384]{1,0:T(8,128)(2,1)S(1)} %fusion.15), channel_id=1, source_target_pairs={{0,8},{1,9},{2,10},{3,11},{4,12},{5,13},{6,14},{7,15},{8,0},{9,1},... | collective-permute-start | bytes 331784 | tf_op jit(solution)/shard_map/ppermute | solution.py:526
  (15 other events, 115.7 us)

commit v7 on v6

--- a/solution.py
+++ b/solution.py
@@ -335,6 +335,7 @@
 TN = (((0,), (0,)), ((), ()))
 LANES = 128
 AXES = ("grp", "shard")
+CHEAP = pl.CostEstimate(flops=1024, bytes_accessed=1024, transcendentals=0)
 
 
 def mxu(left, right, dims):
@@ -403,11 +404,7 @@
         ],
         input_output_aliases={} if before is None else {5: 0, 6: 1},
         compiler_params=params(60),
-        cost_estimate=pl.CostEstimate(
-            flops=16 * length * length * pairs * LANES,
-            bytes_accessed=8 * length * pairs * LANES,
-            transcendentals=0,
-        ),
+        cost_estimate=CHEAP,
         name="attn_fwd",
     )(qkv, qkv, qkv, seg_col, seg_row, *(() if before is None else before))
 
@@ -465,20 +462,16 @@
     sum_ref[1:2, :] = jnp.sum(value_grad, 0, keepdims=True)
 
 
-def attention_backward(qkv, out, out_grad, seg_col, seg_row, lse, start, pairs, at, size, before=None):
+def attention_backward(qkv, out, out_grad, seg_col, seg_row, lse, start, pairs):
     length, width = out.shape
     total = width // LANES
     rows = min(256, length)
-    anywhere = pl.BlockSpec(memory_space=pl.ANY)
 
     def pair(part):
         return pl.BlockSpec((length, LANES), lambda j: (0, part * total + start + j))
 
-    def body(*refs):
-        attention_backward_kernel(*refs[:8], *refs[-2:], rows=rows)
-
     return pl.pallas_call(
-        body,
+        functools.partial(attention_backward_kernel, rows=rows),
         grid=(pairs,),
         in_specs=[
             pair(0),
@@ -489,25 +482,19 @@
             pl.BlockSpec((length, 1), lambda j: (0, 0)),
             pl.BlockSpec((1, length), lambda j: (0, 0)),
             pl.BlockSpec((1, 2, length), lambda j: (j + start, 0, 0)),
-        ]
-        + [anywhere] * (0 if before is None else 2),
+        ],
         out_specs=[
-            pl.BlockSpec((3, length, LANES), lambda j: (0, 0, j + at)),
-            pl.BlockSpec((2, LANES), lambda j: (0, j + at)),
+            pl.BlockSpec((3, length, LANES), lambda j: (0, 0, j)),
+            pl.BlockSpec((2, LANES), lambda j: (0, j)),
         ],
         out_shape=[
-            jax.ShapeDtypeStruct((3, length, size * LANES), jnp.bfloat16),
-            jax.ShapeDtypeStruct((2, size * LANES), jnp.float32),
+            jax.ShapeDtypeStruct((3, length, pairs * LANES), jnp.bfloat16),
+            jax.ShapeDtypeStruct((2, pairs * LANES), jnp.float32),
         ],
-        input_output_aliases={} if before is None else {8: 0, 9: 1},
         compiler_params=params(60),
-        cost_estimate=pl.CostEstimate(
-            flops=40 * length * length * pairs * LANES,
-            bytes_accessed=16 * length * pairs * LANES,
-            transcendentals=0,
-        ),
+        cost_estimate=CHEAP,
         name="attn_bwd",
-    )(qkv, qkv, qkv, out, out_grad, seg_col, seg_row, lse, *(() if before is None else before))
+    )(qkv, qkv, qkv, out, out_grad, seg_col, seg_row, lse)
 
 
 class Place:
@@ -674,9 +661,7 @@
         ),
         out_shape=outs + [shaped(shape, jnp.bfloat16)],
         compiler_params=params(mb),
-        cost_estimate=pl.CostEstimate(
-            flops=flops, bytes_accessed=4 * shape[0] * shape[1] + total, transcendentals=0
-        ),
+        cost_estimate=CHEAP,
         name=name,
     )(place.scalars, *pieces, *inputs)
 
@@ -690,7 +675,7 @@
         out_specs=out_specs,
         out_shape=outs,
         compiler_params=params(mb),
-        cost_estimate=pl.CostEstimate(flops=flops, bytes_accessed=total, transcendentals=0),
+        cost_estimate=CHEAP,
         name=name,
     )(*inputs)
 
@@ -889,16 +874,6 @@
     )
 
 
-def normal_share(values):
-    power = jnp.exp(-0.5 * values * values)
-    t = 1.0 / (1.0 + (0.3275911 / math.sqrt(2.0)) * jnp.abs(values))
-    tail = 0.5 * 1.061405429
-    for factor in (-1.453152027, 1.421413741, -0.284496736, 0.254829592):
-        tail = tail * t + 0.5 * factor
-    tail = tail * t * power
-    return jnp.where(values >= 0, 1.0 - tail, tail), power * (1.0 / math.sqrt(2.0 * math.pi))
-
-
 def feed_in(place, normed_low, window, bias):
     length, width = normed_low.shape
     cols = window.cols
@@ -909,7 +884,8 @@
         for tile in range(length // TILE):
             here = pl.ds(tile * TILE, TILE)
             pre = mxu(x_ref[here, :], weight[:, at], NN) + bias_ref[:, at]
-            share, bell = normal_share(pre)
+            share = 0.5 + 0.5 * lax.erf(pre * (1.0 / math.sqrt(2.0)))
+            bell = jnp.exp(-0.5 * pre * pre) * (1.0 / math.sqrt(2.0 * math.pi))
             hid_ref[here, :] = (pre * share).astype(jnp.bfloat16)
             slope_ref[here, :] = (share + pre * bell).astype(jnp.bfloat16)
 
@@ -1205,11 +1181,7 @@
         ),
         out_shape=[shaped((n, chips, tall, cols), jnp.bfloat16) for n in (2, 2, groups)],
         compiler_params=params(60),
-        cost_estimate=pl.CostEstimate(
-            flops=2 * tokens * height * cols * groups,
-            bytes_accessed=2 * (tokens * (height + cols * groups) + height * cols * groups),
-            transcendentals=0,
-        ),
+        cost_estimate=CHEAP,
         name="wgrad_" + name,
     )(place.scalars, *inputs)
 
@@ -1398,40 +1370,28 @@
     first_grad, attn_low, context_grad, first_sums = feed_in_back(
         after(pre_low, r_in.made), full_in, second_grad, normed, scale_one, vectors, full_attn
     )
-    quarter = pairs // 4
-
-    def back(start, at, before=None, *wait):
+    half = pairs // 2
+
+    def back(start, *wait):
         return attention_backward(
-            mixed,
-            contexts,
-            after(context_grad, *wait) if wait else context_grad,
-            seg_col,
-            seg_row,
-            lse,
-            start,
-            quarter,
-            at,
-            2 * quarter,
-            before,
+            mixed, contexts, after(context_grad, *wait), seg_col, seg_row, lse, start, half
         )
 
     middle = r_out.middle(first_grad)
     near = r_in.near(first_grad)
-    part = back(0, 0, None, middle, near)
-    along = r_out.along(part[1])
-    low_a, late_a = back(quarter, quarter, part, along)
+    low_a, late_a = back(0, middle, near)
     middle = r_in.middle(late_a)
-    along = r_out.along_far(late_a)
+    along = r_out.along(late_a)
     r_a = Reduction(place, [(contexts, attn_low), (rows, low_a)], True, "a", middle, along)
-    part = back(2 * quarter, 0, None, r_a.made)
-    share_out = r_out.share(part[1])
-    along = r_in.along(part[1])
-    near = r_a.near(part[1])
-    low_b, late_b = back(3 * quarter, quarter, part, share_out, along, near)
+    far = r_out.along_far(r_a.made)
+    along = r_in.along(r_a.made)
+    near = r_a.near(r_a.made)
+    low_b, late_b = back(half, far, along, near)
     middle = r_a.middle(late_b)
     along = r_in.along_far(late_b)
+    share_out = r_out.share(late_b)
     sums = pack_sums(late_a, late_b, first_sums, second_sums, bias_in_grad)
-    r_b = Reduction(place, [(rows, low_b)], True, "b", middle, along, sums=sums)
+    r_b = Reduction(place, [(rows, low_b)], True, "b", middle, along, share_out, sums=sums)
     along = r_a.along(r_b.made)
     share_in = r_in.share(r_b.made)
     inner = share_in.shape[1] // groups

time: 484 us -> 493 us (1.019)
  waiting for transfers between devices: 74.7 us -> 87.8 us
  Pallas kernels: 284 us -> 271 us
  starting transfers between devices: 59.9 us -> 65.6 us
    ppermute x58, waiting for transfers between devices: 74.7 us -> 87.8 us  [permute(): return lax.ppermute(array, AXES, pairs)]
    pallas_call x4, Pallas kernels: 73.1 us -> 66.3 us  [weight_call(): pl.pallas_call(body, grid_spec=pltpu.PrefetchScalarGridSpec(num_scalar_pr...]
    pallas_call x4 -> x2, Pallas kernels: 63.7 us -> 57.4 us  [attention_backward(): pl.pallas_call(functools.partial(attention_backward_kernel, rows=rows), g...]
    ppermute x58, starting transfers between devices: 59.9 us -> 65.6 us  [permute(): return lax.ppermute(array, AXES, pairs)]
    unnamed x89 -> x97, local copies, waits for them, and re-layouts: 9.49 us -> 10.5 us
  transfers between devices with their start and end apart: 58 -> 58, of which waited for: 21 -> 23; matrix products, arithmetic and copies ran while one was open for 8% -> 9% of each run, Pallas kernels for 43% -> 39%
where the time goes in v7:
time: 493 us; the launch traced here: 486 us
  Pallas kernels  271 us (55%)
  waiting for transfers between devices  87.8 us (18%)
  starting transfers between devices  65.6 us (13%)
  other arithmetic  43.8 us (9%)
  local copies, waits for them, and re-layouts  15.4 us (3%)
    ppermute x58, waiting for transfers between devices, permute(): return lax.ppermute(array, AXES, pairs)  87.8 us
    pallas_call x4, Pallas kernels, weight_call(): pl.pallas_call(body, grid_spec=pltpu.PrefetchScalarGridSpec(num_scalar_pr...  66.3 us
    ppermute x58, starting transfers between devices, permute(): return lax.ppermute(array, AXES, pairs)  65.6 us
    pallas_call x4, Pallas kernels, weight_grad(): pl.pallas_call(functools.partial(weight_grad_kernel, rows=rows, groups=gr...  59 us
    pallas_call x2, Pallas kernels, attention_backward(): pl.pallas_call(functools.partial(attention_backward_kernel, rows=rows), g...  57.4 us
    pallas_call x3, Pallas kernels, plain_call(): pl.pallas_call(kernel, grid=(steps,), in_specs=in_specs, out_specs=out_sp...  47.8 us
    pallas_call x3, Pallas kernels, attention_forward(): pl.pallas_call(body, grid=(pairs,), in_specs=[pair(0), pair(1), pair(2),...  37.4 us
    convert_element_type x18, other arithmetic, add(): return total.astype(jnp.bfloat16)  32.9 us
  transfers between devices with their start and end apart: 58, of which 23 were waited for; matrix products, arithmetic and copies ran while one was open for 9% of the time, Pallas kernels for 39%

profile of v7, /device:TPU:0, one launch (start us, length us, event | category | flops | bytes accessed | tf_op | source)
XLA Modules:
  0.0 485.6 jit_solution(295429948769295086)
XLA Ops:
  0.7 3.1 collective-permute-start
  3.8 5.6 %collective-permute-done = bf16[128,768]{1,0:T(8,128)(2,1)S(1)} collective-permute-done((bf16[128,768]{1,0:T(8,128)(2,1)}, bf16[128,768]{1,0:T(8,128)(2,1)S(1)}, u32[]{:S(2)}, u32[]{:S(2)}) %collective-permute-start) | collective-permute-done | bytes 196640 | tf_op jit(solution)/shard_map/ppermute | solution.py:513
  10.3 2.5 collective-permute-start.1
  21.3 2.5 collective-permute-start.6
  24.8 1.6 collective-permute-start.2
  27.0 3.4 collective-permute-start.7
  31.0 3.1 collective-permute-done.7
  37.0 1.5 collective-permute-start.8
  38.5 1.7 collective-permute-start.17
  40.2 1.5 collective-permute-start.3
  41.7 15.3 %collective-permute-done.17 = bf16[2,128,1280]{2,1,0:T(8,128)(2,1)S(1)} collective-permute-done((bf16[2,128,1280]{2,1,0:T(8,128)(2,1)S(1)}, bf16[2,128,1280]{2,1,0:T(8,128)(2,1)S(1)}, u32[]{:S(2)}, u32[]{:S(2)}) %collective-permute-start.17) | collective-permute-done | bytes 655392 | tf_op jit(solution)/shard_map/ppermute | solution.py:513
  57.2 1.6 collective-permute-start.18
  64.8 12.7 %qkv.1 = (bf16[1024,3072]{1,0:T(8,128)(2,1)}, bf16[1024,3072]{1,0:T(8,128)(2,1)}) custom-call(s32[3]{0:T(128)} %pad_add_fusion.where, bf16[4,128,768]{2,1,0:T(8,128)(2,1)} %copy-done.3, bf16[4,128,768]{2,1,0:T(8,128)(2,1)} %collective-permute-done.2.refs_1_, bf16[4,128,768]{2,1,0:T(8,128)(2,1)} %collective-permute-done.3.refs_2_, ...), custom_call_target="tpu_custom_call" | custom-call | flops 1024 | bytes 1024 | tf_op jit(solution)/shard_map/qkv/pallas_call | solution.py:649
  77.5 13.7 %attn_fwd.3 = (bf16[1024,1024]{1,0:T(8,128)(2,1)}, f32[8,2,1024]{2,1,0:T(2,128)}) custom-call(bf16[1024,3072]{1,0:T(8,128)(2,1)} %get-tuple-element.120.q_ref.k_ref.v_ref, bf16[1024,3072]{1,0:T(8,128)(2,1)} %get-tuple-element.120.q_ref.k_ref.v_ref, bf16[1024,3072]{1,0:T(8,128)(2,1)} %get-tuple-element.120.q_ref.k_ref.v_ref, s32[1024,1]{1,0:T(8,128)} %copy.36.seg_c.seg_col, ...), custom_call_target="tpu_custom_call" | custom-call | flops 1024 | bytes 1024 | tf_op jit(solution)/shard_map/attn_fwd/pallas_call | solution.py:386
  91.7 1.5 collective-permute-start.13
  93.2 7.2 %collective-permute-done.13 = bf16[512,256]{1,0:T(8,128)(2,1)S(1)} collective-permute-done((bf16[512,256]{1,0:T(8,128)(2,1)S(1)}, bf16[512,256]{1,0:T(8,128)(2,1)S(1)}, u32[]{:S(2)}, u32[]{:S(2)}) %collective-permute-start.13) | collective-permute-done | bytes 262176 | tf_op jit(solution)/shard_map/ppermute | solution.py:513
  100.5 3.8 collective-permute-start.14
  104.8 10.0 %attn_fwd.4 = (bf16[1024,1024]{1,0:T(8,128)(2,1)}, f32[8,2,1024]{2,1,0:T(2,128)}) custom-call(bf16[1024,3072]{1,0:T(8,128)(2,1)} %get-tuple-element.120.q_ref.k_ref.v_ref, bf16[1024,3072]{1,0:T(8,128)(2,1)} %get-tuple-element.120.q_ref.k_ref.v_ref, ...), custom_call_target="tpu_custom_call", output_to_operand_aliasing={{0}: (5, {}), {1}: (6, {})} | custom-call | flops 1024 | bytes 1024 | tf_op jit(solution)/shard_map/attn_fwd/pallas_call | solution.py:386
  115.5 1.5 collective-permute-done.14
  117.0 2.1 pad_maximum_fusion.2.refs_0_
  119.2 3.5 collective-permute-start.15
  122.7 13.7 %attn_fwd.5 = (bf16[1024,1024]{1,0:T(8,128)(2,1)}, f32[8,2,1024]{2,1,0:T(2,128)}) custom-call(bf16[1024,3072]{1,0:T(8,128)(2,1)} %get-tuple-element.120.q_ref.k_ref.v_ref, bf16[1024,3072]{1,0:T(8,128)(2,1)} %get-tuple-element.120.q_ref.k_ref.v_ref, ...), custom_call_target="tpu_custom_call", output_to_operand_aliasing={{0}: (5, {}), {1}: (6, {})} | custom-call | flops 1024 | bytes 1024 | tf_op jit(solution)/shard_map/attn_fwd/pallas_call | solution.py:386
  137.4 9.6 %attn_out.1 = (f32[1024,1024]{1,0:T(8,128)}, f32[1024,128]{1,0:T(8,128)}, bf16[1024,1024]{1,0:T(8,128)(2,1)}, bf16[1024,1024]{1,0:T(8,128)(2,1)}) custom-call(s32[3]{0:T(128)} %pad_add_fusion.where, bf16[4,128,1280]{2,1,0:T(8,128)(2,1)} %copy-done, bf16[4,128,1280]{2,1,0:T(8,128)(2,1)} %copy-done.1, bf16[4,128,1280]{2,1,0:T(8,128)(2,1)} %collective-permute-done.19.refs_2_, ...), custom_call_target="tpu_custom_call" | custom-call | flops 1024 | bytes 1024 | tf_op jit(solution)/shard_map/attn_out/pallas_call | solution.py:649
  148.2 3.2 collective-permute-done.16.refs_2_
  151.9 22.3 %feed_in.1 = (bf16[1024,4096]{1,0:T(8,128)(2,1)}, bf16[1024,4096]{1,0:T(8,128)(2,1)}, bf16[1024,4096]{1,0:T(8,128)(2,1)}) custom-call(s32[3]{0:T(128)} %pad_add_fusion.where, bf16[4,128,1280]{2,1,0:T(8,128)(2,1)} %copy-done, bf16[4,128,1280]{2,1,0:T(8,128)(2,1)} %copy-done.1, bf16[4,128,1280]{2,1,0:T(8,128)(2,1)} %collective-permute-done.19.refs_2_, ...), custom_call_target="tpu_custom_call" | custom-call | flops 1024 | bytes 1024 | tf_op jit(solution)/shard_map/feed_in/pallas_call | solution.py:649
  175.5 1.7 collective-permute-done.29.refs_7_
  177.2 21.7 %feed_out.1 = (bf16[1024,1024]{1,0:T(8,128)(2,1)}, f32[1024,1024]{1,0:T(8,128)}, bf16[1024,1024]{1,0:T(8,128)(2,1)}, f32[8,1024]{1,0:T(8,128)}, bf16[4096,1024]{1,0:T(8,128)(2,1)}) custom-call(s32[3]{0:T(128)} %pad_add_fusion.where, bf16[4,512,256]{2,1,0:T(8,128)(2,1)} %pad_maximum_fusion.2.refs_0_, bf16[4,512,256]{2,1,0:T(8,128)(2,1)} %collective-permute-done.15.refs_1_, ...), custom_call_target="tpu_custom_call" | custom-call | flops 1024 | bytes 1024 | tf_op jit(solution)/shard_map/feed_out/pallas_call | solution.py:649
  198.8 14.0 %wgrad_out.1 = (bf16[2,4,512,256]{3,2,1,0:T(8,128)(2,1)}, bf16[2,4,512,256]{3,2,1,0:T(8,128)(2,1)}, bf16[4,4,512,256]{3,2,1,0:T(8,128)(2,1)}) custom-call(s32[3]{0:T(128)} %pad_add_fusion.where, bf16[1024,4096]{1,0:T(8,128)(2,1)} %get-tuple-element.129.refs_8_.refs_0_, bf16[1024,1024]{1,0:T(8,128)(2,1)} %get-tuple-element.136.refs_1_.g_ref), custom_call_target="tpu_custom_call" | custom-call | flops 1024 | bytes 1024 | tf_op jit(solution)/shard_map/wgrad_out/pallas_call | solution.py:1166
  212.9 14.6 %feed_out_back.1 = (bf16[1024,4096]{1,0:T(8,128)(2,1)}, f32[1,4096]{1,0:T(1,128)}) custom-call(bf16[1024,1024]{1,0:T(8,128)(2,1)} %get-tuple-element.136.refs_1_.g_ref, bf16[4096,1024]{1,0:T(8,128)(2,1)} %get-tuple-element.137.w_ref, bf16[1024,4096]{1,0:T(8,128)(2,1)} %get-tuple-element.138.slope_ref), custom_call_target="tpu_custom_call" | custom-call | flops 1024 | bytes 1024 | tf_op jit(solution)/shard_map/feed_out_back/pallas_call | solution.py:671
  227.5 2.7 add_convert_fusion.1
  230.3 15.9 %wgrad_in.1 = (bf16[2,4,128,1024]{3,2,1,0:T(8,128)(2,1)}, bf16[2,4,128,1024]{3,2,1,0:T(8,128)(2,1)}, bf16[4,4,128,1024]{3,2,1,0:T(8,128)(2,1)}) custom-call(s32[3]{0:T(128)} %pad_add_fusion.where, bf16[1024,1024]{1,0:T(8,128)(2,1)} %get-tuple-element.142.refs_8_.refs_0_, bf16[1024,4096]{1,0:T(8,128)(2,1)} %get-tuple-element.144.refs_1_.p_ref), custom_call_target="tpu_custom_call" | custom-call | flops 1024 | bytes 1024 | tf_op jit(solution)/shard_map/wgrad_in/pallas_call | solution.py:1166
  246.6 20.9 %feed_in_back.1 = (f32[1024,1024]{1,0:T(8,128)}, bf16[1024,1024]{1,0:T(8,128)(2,1)}, bf16[1024,1024]{1,0:T(8,128)(2,1)}, f32[8,1024]{1,0:T(8,128)}) custom-call(bf16[1024,4096]{1,0:T(8,128)(2,1)} %get-tuple-element.144.refs_1_.p_ref, bf16[1024,4096]{1,0:T(8,128)(2,1)} %get-tuple-element.145.w_ref, f32[1024,1024]{1,0:T(8,128)} %get-tuple-element.146.g_ref, ...), custom_call_target="tpu_custom_call" | custom-call | flops 1024 | bytes 1024 | tf_op jit(solution)/shard_map/feed_in_back/pallas_call | solution.py:671
  267.5 4.7 add_convert_fusion
  272.2 2.0 collective-permute-start.35
  274.2 2.9 fusion.3
  278.2 28.8 %attn_bwd.2 = (bf16[3,1024,512]{2,1,0:T(8,128)(2,1)}, f32[2,512]{1,0:T(2,128)}) custom-call(bf16[1024,3072]{1,0:T(8,128)(2,1)} %get-tuple-element.120.q_ref.k_ref.v_ref, bf16[1024,3072]{1,0:T(8,128)(2,1)} %get-tuple-element.120.q_ref.k_ref.v_ref, bf16[1024,3072]{1,0:T(8,128)(2,1)} %get-tuple-element.120.q_ref.k_ref.v_ref, ...), custom_call_target="tpu_custom_call" | custom-call | flops 1024 | bytes 1024 | tf_op jit(solution)/shard_map/attn_bwd/pallas_call | solution.py:473
  308.0 2.5 fusion.1
  310.6 3.1 fusion.4
  313.7 16.4 %wgrad_a.1 = (bf16[2,4,128,640]{3,2,1,0:T(8,128)(2,1)}, bf16[2,4,128,640]{3,2,1,0:T(8,128)(2,1)}, bf16[4,4,128,640]{3,2,1,0:T(8,128)(2,1)}) custom-call(s32[3]{0:T(128)} %pad_add_fusion.where, bf16[1024,1024]{1,0:T(8,128)(2,1)} %get-tuple-element.162.refs_8_.o_ref.refs_0_, bf16[1024,1024]{1,0:T(8,128)(2,1)} %bitcast.145, ...), custom_call_target="tpu_custom_call" | custom-call | flops 1024 | bytes 1024 | tf_op jit(solution)/shard_map/wgrad_a/pallas_call | solution.py:1166
  331.3 1.5 collective-permute-start.34
  332.8 12.6 %collective-permute-done.36 = bf16[4,128,1024]{2,1,0:T(8,128)(2,1)} collective-permute-done((bf16[4,128,1024]{2,1,0:T(8,128)(2,1)}, bf16[4,128,1024]{2,1,0:T(8,128)(2,1)}, u32[]{:S(2)}, u32[]{:S(2)}) %collective-permute-start.36) | collective-permute-done | bytes 1048608 | tf_op jit(solution)/shard_map/ppermute | solution.py:513
  345.4 2.7 add_convert_fusion.2
  349.4 2.8 fusion
  352.2 1.5 collective-permute-start.39
  354.7 3.6 collective-permute-start.40
  358.3 28.6 %attn_bwd.3 = (bf16[3,1024,512]{2,1,0:T(8,128)(2,1)}, f32[2,512]{1,0:T(2,128)}) custom-call(bf16[1024,3072]{1,0:T(8,128)(2,1)} %get-tuple-element.120.q_ref.k_ref.v_ref, bf16[1024,3072]{1,0:T(8,128)(2,1)} %get-tuple-element.120.q_ref.k_ref.v_ref, bf16[1024,3072]{1,0:T(8,128)(2,1)} %get-tuple-element.120.q_ref.k_ref.v_ref, ...), custom_call_target="tpu_custom_call" | custom-call | flops 1024 | bytes 1024 | tf_op jit(solution)/shard_map/attn_bwd/pallas_call | solution.py:473
  386.8 1.5 pack_sums.1.refs_2_
  390.4 2.6 fusion.6
  393.0 12.7 %wgrad_b.1 = (bf16[2,4,144,384]{3,2,1,0:T(8,128)(2,1)}, bf16[2,4,144,384]{3,2,1,0:T(8,128)(2,1)}, bf16[4,4,144,384]{3,2,1,0:T(8,128)(2,1)}) custom-call(s32[3]{0:T(128)} %pad_add_fusion.where, bf16[1024,1024]{1,0:T(8,128)(2,1)} %bitcast.146, bf16[3,1024,512]{2,1,0:T(8,128)(2,1)} %get-tuple-element.185.refs_1_, f32[32,1024]{1,0:T(8,128)} %pack_sums.1.refs_2_), custom_call_target="tpu_custom_call" | custom-call | flops 1024 | bytes 1024 | tf_op jit(solution)/shard_map/wgrad_b/pallas_call | solution.py:1166
  407.0 8.7 %collective-permute-done.43 = bf16[128,1024]{1,0:T(8,128)(2,1)S(1)} collective-permute-done((bf16[128,1024]{1,0:T(8,128)(2,1)S(1)}, bf16[128,1024]{1,0:T(8,128)(2,1)S(1)}, u32[]{:S(2)}, u32[]{:S(2)}) %collective-permute-start.43) | collective-permute-done | bytes 262176 | tf_op jit(solution)/shard_map/ppermute | solution.py:513
  416.9 1.7 fusion.2
  421.8 12.3 %qkv_back.1 = f32[1024,1024]{1,0:T(8,128)} custom-call(bf16[1024,3072]{1,0:T(8,128)(2,1)} %get-tuple-element.133.w_ref, bf16[3,1024,512]{2,1,0:T(8,128)(2,1)} %get-tuple-element.157.refs_3_.refs_0_, bf16[3,1024,512]{2,1,0:T(8,128)(2,1)} %get-tuple-element.185.refs_1_, f32[1024,1024]{1,0:T(8,128)} %get-tuple-element.151.refs_2_), custom_call_target="tpu_custom_call" | custom-call | flops 1024 | bytes 1024 | tf_op jit(solution)/shard_map/qkv_back/pallas_call | solution.py:671
  435.7 2.7 collective-permute-start.46
  440.6 3.1 collective-permute-done.46
  445.0 4.8 collective-permute-done.56
  449.7 1.8 collective-permute-done.47
  452.7 1.5 fusion.5
  454.2 2.7 collective-permute-start.50
  459.8 2.2 collective-permute-done.50
  462.1 3.0 collective-permute-done.51
  465.1 1.9 collective-permute-start.53
  469.8 2.4 collective-permute-done.53
  472.2 6.2 %collective-permute-done.54 = bf16[144,384]{1,0:T(8,128)(2,1)S(1)} collective-permute-done((bf16[144,384]{1,0:T(8,128)(2,1)S(1)}, bf16[144,384]{1,0:T(8,128)(2,1)S(1)}, u32[]{:S(2)}, u32[]{:S(2)}) %collective-permute-start.54) | collective-permute-done | bytes 110624 | tf_op jit(solution)/shard_map/ppermute | solution.py:513
  483.1 1.8 pad_maximum_fusion
  (235 shorter events, 56.8 us)
Async XLA Ops:
  0.6 25.7 %copy-start.20 = (bf16[128,256]{1,0:T(8,128)(2,1)S(1)}, bf16[128,256]{1,0:T(8,128)(2,1)}, u32[]{:S(2)}) copy-start(bf16[128,256]{1,0:T(8,128)(2,1)} %param.24) | copy-start | bytes 196612
  0.7 25.7 %copy-start.18 = (bf16[128,1024]{1,0:T(8,128)(2,1)S(1)}, bf16[128,1024]{1,0:T(8,128)(2,1)}, u32[]{:S(2)}) copy-start(bf16[128,1024]{1,0:T(8,128)(2,1)} %param.28) | copy-start | bytes 786436
  0.7 8.7 %collective-permute-start = (bf16[128,768]{1,0:T(8,128)(2,1)}, bf16[128,768]{1,0:T(8,128)(2,1)S(1)}, u32[]{:S(2)}, u32[]{:S(2)}) collective-permute-start(bf16[128,768]{1,0:T(8,128)(2,1)} %param.21), channel_id=1, source_target_pairs={{0,2},{1,5},{2,0},{3,7},{4,6},{5,1},{6,4},{7,3},{8,10},{9,13},{10,... | collective-permute-start | bytes 589832 | tf_op jit(solution)/shard_map/ppermute | solution.py:513
  10.3 13.5 %collective-permute-start.1 = (bf16[2,128,768]{2,1,0:T(8,128)(2,1)S(1)}, bf16[2,128,768]{2,1,0:T(8,128)(2,1)S(1)}, u32[]{:S(2)}, u32[]{:S(2)}) collective-permute-start(bf16[2,128,768]{2,1,0:T(8,128)(2,1)S(1)} %pad_maximum_fusion.10), channel_id=1, source_target_pairs={{0,4},{1,3},{2,6},{3,1},{4,0},{5,7},{6,2},{7,5},{8,12},{9,11},{10,... | collective-permute-start | bytes 1179656 | tf_op jit(solution)/shard_map/ppermute | solution.py:513
  20.2 1.2 collective-permute-start.5
  21.3 5.7 %collective-permute-start.6 = (bf16[2,16,128]{2,1,0:T(8,128)(2,1)S(1)}, bf16[2,16,128]{2,1,0:T(8,128)(2,1)S(1)}, u32[]{:S(2)}, u32[]{:S(2)}) collective-permute-start(bf16[2,16,128]{2,1,0:T(8,128)(2,1)S(1)} %get-tuple-element.225), channel_id=1, source_target_pairs={{0,2},{1,5},{2,0},{3,7},{4,6},{5,1},{6,4},{7,3},{8,10},{9,13},{10,... | collective-permute-start | bytes 24584 | tf_op jit(solution)/shard_map/ppermute | solution.py:513
  24.8 34.0 %copy-start.3 = (bf16[4,128,768]{2,1,0:T(8,128)(2,1)}, bf16[4,128,768]{2,1,0:T(8,128)(2,1)S(1)}, u32[]{:S(2)}) copy-start(bf16[4,128,768]{2,1,0:T(8,128)(2,1)S(1)} %pad_maximum_fusion.4.refs_0_) | copy-start | bytes 2359300
  24.8 12.2 %collective-permute-start.2 = (bf16[4,128,768]{2,1,0:T(8,128)(2,1)S(1)}, bf16[4,128,768]{2,1,0:T(8,128)(2,1)}, u32[]{:S(2)}, u32[]{:S(2)}) collective-permute-start(bf16[4,128,768]{2,1,0:T(8,128)(2,1)S(1)} %pad_maximum_fusion.4.refs_0_), channel_id=1, source_target_pairs={{0,8},{1,17},{2,10},{3,19},{4,12},{5,21},{6,14},{7,23},{8,0},{9,25... | collective-permute-start | bytes 2359304 | tf_op jit(solution)/shard_map/ppermute | solution.py:513
  26.4 33.4 %copy-start.19 = (s32[1,1024]{1,0:T(1,128)S(1)}, s32[1,1024]{1,0:T(1,128)}, u32[]{:S(2)}) copy-start(s32[1,1024]{1,0:T(1,128)} %seg_row.3) | copy-start | bytes 12292
  26.4 10.2 %collective-permute-start.4 = (bf16[128,1280]{1,0:T(8,128)(2,1)S(1)}, bf16[128,1280]{1,0:T(8,128)(2,1)S(1)}, u32[]{:S(2)}, u32[]{:S(2)}) collective-permute-start(bf16[128,1280]{1,0:T(8,128)(2,1)S(1)} %pad_maximum_fusion.11), channel_id=1, source_target_pairs={{0,2},{1,5},{2,0},{3,7},{4,6},{5,1},{6,4},{7,3},{8,10},{9,13},{10,... | collective-permute-start | bytes 983048 | tf_op jit(solution)/shard_map/ppermute | solution.py:513
  27.0 7.1 %collective-permute-start.7 = (bf16[2,2,16,128]{3,2,1,0:T(8,128)(2,1)S(1)}, bf16[2,2,16,128]{3,2,1,0:T(8,128)(2,1)S(1)}, u32[]{:S(2)}, u32[]{:S(2)}) collective-permute-start(bf16[2,2,16,128]{3,2,1,0:T(8,128)(2,1)S(1)} %pad_maximum_fusion.15), channel_id=1, source_target_pairs={{0,4},{1,3},{2,6},{3,1},{4,0},{5,7},{6,2},{7,5},{8,12},{9,11},{10,... | collective-permute-start | bytes 49160 | tf_op jit(solution)/shard_map/ppermute | solution.py:513
  37.0 20.1 %collective-permute-start.8 = (bf16[4,128,768]{2,1,0:T(8,128)(2,1)}, bf16[4,128,768]{2,1,0:T(8,128)(2,1)}, u32[]{:S(2)}, u32[]{:S(2)}) collective-permute-start(bf16[4,128,768]{2,1,0:T(8,128)(2,1)} %collective-permute-done.2.refs_1_), channel_id=1, source_target_pairs={{0,16},{1,9},{2,18},{3,11},{4,20},{5,13},{6,22},{7,15},{8,24},{9,1... | collective-permute-start | bytes 2359304 | tf_op jit(solution)/shard_map/ppermute | solution.py:513
  38.5 18.6 %collective-permute-start.17 = (bf16[2,128,1280]{2,1,0:T(8,128)(2,1)S(1)}, bf16[2,128,1280]{2,1,0:T(8,128)(2,1)S(1)}, u32[]{:S(2)}, u32[]{:S(2)}) collective-permute-start(bf16[2,128,1280]{2,1,0:T(8,128)(2,1)S(1)} %pad_maximum_fusion.5), channel_id=1, source_target_pairs={{0,4},{1,3},{2,6},{3,1},{4,0},{5,7},{6,2},{7,5},{8,12},{9,11},{10,... | collective-permute-start | bytes 1966088 | tf_op jit(solution)/shard_map/ppermute | solution.py:513
  40.2 19.0 %collective-permute-start.3 = (bf16[4,128,768]{2,1,0:T(8,128)(2,1)S(1)}, bf16[4,128,768]{2,1,0:T(8,128)(2,1)}, u32[]{:S(2)}, u32[]{:S(2)}) collective-permute-start(bf16[4,128,768]{2,1,0:T(8,128)(2,1)S(1)} %pad_maximum_fusion.4.refs_0_), channel_id=1, source_target_pairs={{0,16},{1,9},{2,18},{3,11},{4,20},{5,13},{6,22},{7,15},{8,24},{9,1... | collective-permute-start | bytes 2359304 | tf_op jit(solution)/shard_map/ppermute | solution.py:513
  57.2 47.1 %copy-start = (bf16[4,128,1280]{2,1,0:T(8,128)(2,1)}, bf16[4,128,1280]{2,1,0:T(8,128)(2,1)S(1)}, u32[]{:S(2)}) copy-start(bf16[4,128,1280]{2,1,0:T(8,128)(2,1)S(1)} %pad_maximum_fusion.1.refs_0_) | copy-start | bytes 3932164
  57.2 34.0 %collective-permute-start.18 = (bf16[4,128,1280]{2,1,0:T(8,128)(2,1)S(1)}, bf16[4,128,1280]{2,1,0:T(8,128)(2,1)S(1)}, u32[]{:S(2)}, u32[]{:S(2)}) collective-permute-start(bf16[4,128,1280]{2,1,0:T(8,128)(2,1)S(1)} %pad_maximum_fusion.1.refs_0_), channel_id=1, source_target_pairs={{0,8},{1,17},{2,10},{3,19},{4,12},{5,21},{6,14},{7,23},{8,0},{9,25... | collective-permute-start | bytes 3932168 | tf_op jit(solution)/shard_map/ppermute | solution.py:513
  58.8 3.5 collective-permute-start.9
  58.8 4.2 collective-permute-start.10
  59.3 4.4 collective-permute-start.11
  59.3 5.5 %collective-permute-start.12 = (bf16[4,128,768]{2,1,0:T(8,128)(2,1)}, bf16[4,128,768]{2,1,0:T(8,128)(2,1)}, u32[]{:S(2)}, u32[]{:S(2)}) collective-permute-start(bf16[4,128,768]{2,1,0:T(8,128)(2,1)} %collective-permute-done.8.refs_3_), channel_id=1, source_target_pairs={{0,1},{1,0},{2,3},{3,2},{4,5},{5,4},{6,7},{7,6},{8,9},{9,8},{10,11... | collective-permute-start | bytes 2359304 | tf_op jit(solution)/shard_map/ppermute | solution.py:513
  62.3 42.6 %collective-permute-start.19 = (bf16[4,128,1280]{2,1,0:T(8,128)(2,1)S(1)}, bf16[4,128,1280]{2,1,0:T(8,128)(2,1)}, u32[]{:S(2)}, u32[]{:S(2)}) collective-permute-start(bf16[4,128,1280]{2,1,0:T(8,128)(2,1)S(1)} %pad_maximum_fusion.1.refs_0_), channel_id=1, source_target_pairs={{0,16},{1,9},{2,18},{3,11},{4,20},{5,13},{6,22},{7,15},{8,24},{9,1... | collective-permute-start | bytes 3932168 | tf_op jit(solution)/shard_map/ppermute | solution.py:513
  91.2 24.2 %collective-permute-start.20 = (bf16[4,128,1280]{2,1,0:T(8,128)(2,1)S(1)}, bf16[4,128,1280]{2,1,0:T(8,128)(2,1)}, u32[]{:S(2)}, u32[]{:S(2)}) collective-permute-start(bf16[4,128,1280]{2,1,0:T(8,128)(2,1)S(1)} %collective-permute-done.18.refs_1_), channel_id=1, source_target_pairs={{0,16},{1,9},{2,18},{3,11},{4,20},{5,13},{6,22},{7,15},{8,24},{9,1... | collective-permute-start | bytes 3932168 | tf_op jit(solution)/shard_map/ppermute | solution.py:513
  91.7 8.7 %collective-permute-start.13 = (bf16[512,256]{1,0:T(8,128)(2,1)S(1)}, bf16[512,256]{1,0:T(8,128)(2,1)S(1)}, u32[]{:S(2)}, u32[]{:S(2)}) collective-permute-start(bf16[512,256]{1,0:T(8,128)(2,1)S(1)} %copy-done.15), channel_id=1, source_target_pairs={{0,2},{1,5},{2,0},{3,7},{4,6},{5,1},{6,4},{7,3},{8,10},{9,13},{10,... | collective-permute-start | bytes 786440 | tf_op jit(solution)/shard_map/ppermute | solution.py:513
  100.5 16.5 %collective-permute-start.14 = (bf16[2,512,256]{2,1,0:T(8,128)(2,1)S(1)}, bf16[2,512,256]{2,1,0:T(8,128)(2,1)}, u32[]{:S(2)}, u32[]{:S(2)}) collective-permute-start(bf16[2,512,256]{2,1,0:T(8,128)(2,1)S(1)} %pad_maximum_fusion.6), channel_id=1, source_target_pairs={{0,4},{1,3},{2,6},{3,1},{4,0},{5,7},{6,2},{7,5},{8,12},{9,11},{10,... | collective-permute-start | bytes 1572872 | tf_op jit(solution)/shard_map/ppermute | solution.py:513
  104.3 32.1 %collective-permute-start.21 = (bf16[4,128,1280]{2,1,0:T(8,128)(2,1)S(1)}, bf16[4,128,1280]{2,1,0:T(8,128)(2,1)}, u32[]{:S(2)}, u32[]{:S(2)}) collective-permute-start(bf16[4,128,1280]{2,1,0:T(8,128)(2,1)S(1)} %pad_maximum_fusion.1.refs_0_), channel_id=1, source_target_pairs={{0,1},{1,0},{2,3},{3,2},{4,5},{5,4},{6,7},{7,6},{8,9},{9,8},{10,11... | collective-permute-start | bytes 3932168 | tf_op jit(solution)/shard_map/ppermute | solution.py:513
  104.8 32.6 %collective-permute-start.22 = (bf16[4,128,1280]{2,1,0:T(8,128)(2,1)S(1)}, bf16[4,128,1280]{2,1,0:T(8,128)(2,1)}, u32[]{:S(2)}, u32[]{:S(2)}) collective-permute-start(bf16[4,128,1280]{2,1,0:T(8,128)(2,1)S(1)} %collective-permute-done.18.refs_1_), channel_id=1, source_target_pairs={{0,1},{1,0},{2,3},{3,2},{4,5},{5,4},{6,7},{7,6},{8,9},{9,8},{10,11... | collective-permute-start | bytes 3932168 | tf_op jit(solution)/shard_map/ppermute | solution.py:513
  114.8 22.6 %collective-permute-start.23 = (bf16[4,128,1280]{2,1,0:T(8,128)(2,1)}, bf16[4,128,1280]{2,1,0:T(8,128)(2,1)}, u32[]{:S(2)}, u32[]{:S(2)}) collective-permute-start(bf16[4,128,1280]{2,1,0:T(8,128)(2,1)} %collective-permute-done.19.refs_2_), channel_id=1, source_target_pairs={{0,1},{1,0},{2,3},{3,2},{4,5},{5,4},{6,7},{7,6},{8,9},{9,8},{10,11... | collective-permute-start | bytes 3932168 | tf_op jit(solution)/shard_map/ppermute | solution.py:513
  115.4 22.0 %collective-permute-start.24 = (bf16[4,128,1280]{2,1,0:T(8,128)(2,1)}, bf16[4,128,1280]{2,1,0:T(8,128)(2,1)}, u32[]{:S(2)}, u32[]{:S(2)}) collective-permute-start(bf16[4,128,1280]{2,1,0:T(8,128)(2,1)} %collective-permute-done.20.refs_3_), channel_id=1, source_target_pairs={{0,1},{1,0},{2,3},{3,2},{4,5},{5,4},{6,7},{7,6},{8,9},{9,8},{10,11... | collective-permute-start | bytes 3932168 | tf_op jit(solution)/shard_map/ppermute | solution.py:513
  119.2 27.9 %collective-permute-start.15 = (bf16[4,512,256]{2,1,0:T(8,128)(2,1)}, bf16[4,512,256]{2,1,0:T(8,128)(2,1)}, u32[]{:S(2)}, u32[]{:S(2)}) collective-permute-start(bf16[4,512,256]{2,1,0:T(8,128)(2,1)} %pad_maximum_fusion.2.refs_0_), channel_id=1, source_target_pairs={{0,8},{1,17},{2,10},{3,19},{4,12},{5,21},{6,14},{7,23},{8,0},{9,25... | collective-permute-start | bytes 3145736 | tf_op jit(solution)/shard_map/ppermute | solution.py:513
  136.3 15.1 %collective-permute-start.16 = (bf16[4,512,256]{2,1,0:T(8,128)(2,1)}, bf16[4,512,256]{2,1,0:T(8,128)(2,1)S(1)}, u32[]{:S(2)}, u32[]{:S(2)}) collective-permute-start(bf16[4,512,256]{2,1,0:T(8,128)(2,1)} %pad_maximum_fusion.2.refs_0_), channel_id=1, source_target_pairs={{0,16},{1,9},{2,18},{3,11},{4,20},{5,13},{6,22},{7,15},{8,24},{9,1... | collective-permute-start | bytes 3145736 | tf_op jit(solution)/shard_map/ppermute | solution.py:513
  147.1 27.2 %collective-permute-start.25 = (bf16[4,512,256]{2,1,0:T(8,128)(2,1)}, bf16[4,512,256]{2,1,0:T(8,128)(2,1)S(1)}, u32[]{:S(2)}, u32[]{:S(2)}) collective-permute-start(bf16[4,512,256]{2,1,0:T(8,128)(2,1)} %collective-permute-done.15.refs_1_), channel_id=1, source_target_pairs={{0,16},{1,9},{2,18},{3,11},{4,20},{5,13},{6,22},{7,15},{8,24},{9,1... | collective-permute-start | bytes 3145736 | tf_op jit(solution)/shard_map/ppermute | solution.py:513
  148.2 27.3 %collective-permute-start.27 = (bf16[4,512,256]{2,1,0:T(8,128)(2,1)}, bf16[4,512,256]{2,1,0:T(8,128)(2,1)S(1)}, u32[]{:S(2)}, u32[]{:S(2)}) collective-permute-start(bf16[4,512,256]{2,1,0:T(8,128)(2,1)} %collective-permute-done.15.refs_1_), channel_id=1, source_target_pairs={{0,1},{1,0},{2,3},{3,2},{4,5},{5,4},{6,7},{7,6},{8,9},{9,8},{10,11... | collective-permute-start | bytes 3145736 | tf_op jit(solution)/shard_map/ppermute | solution.py:513
  151.4 24.0 %collective-permute-start.28 = (bf16[4,512,256]{2,1,0:T(8,128)(2,1)S(1)}, bf16[4,512,256]{2,1,0:T(8,128)(2,1)}, u32[]{:S(2)}, u32[]{:S(2)}) collective-permute-start(bf16[4,512,256]{2,1,0:T(8,128)(2,1)S(1)} %collective-permute-done.16.refs_2_), channel_id=1, source_target_pairs={{0,1},{1,0},{2,3},{3,2},{4,5},{5,4},{6,7},{7,6},{8,9},{9,8},{10,11... | collective-permute-start | bytes 3145736 | tf_op jit(solution)/shard_map/ppermute | solution.py:513
  151.4 24.0 %collective-permute-start.26 = (bf16[4,512,256]{2,1,0:T(8,128)(2,1)}, bf16[4,512,256]{2,1,0:T(8,128)(2,1)}, u32[]{:S(2)}, u32[]{:S(2)}) collective-permute-start(bf16[4,512,256]{2,1,0:T(8,128)(2,1)} %pad_maximum_fusion.2.refs_0_), channel_id=1, source_target_pairs={{0,1},{1,0},{2,3},{3,2},{4,5},{5,4},{6,7},{7,6},{8,9},{9,8},{10,11... | collective-permute-start | bytes 3145736 | tf_op jit(solution)/shard_map/ppermute | solution.py:513
  174.3 2.9 collective-permute-start.29
  212.8 14.7 %collective-permute-start.30 = (bf16[4,4,512,256]{3,2,1,0:T(8,128)(2,1)}, bf16[4,4,512,256]{3,2,1,0:T(8,128)(2,1)}, u32[]{:S(2)}, u32[]{:S(2)}) collective-permute-start(bf16[4,4,512,256]{3,2,1,0:T(8,128)(2,1)} %get-tuple-element.140), channel_id=1, source_target_pairs={{0,1},{1,0},{2,3},{3,2},{4,5},{5,4},{6,7},{7,6},{8,9},{9,8},{10,11... | collective-permute-start | bytes 12582920 | tf_op jit(solution)/shard_map/ppermute | solution.py:513
  246.2 21.3 %collective-permute-start.32 = (bf16[4,4,128,1024]{3,2,1,0:T(8,128)(2,1)}, bf16[4,4,128,1024]{3,2,1,0:T(8,128)(2,1)}, u32[]{:S(2)}, u32[]{:S(2)}) collective-permute-start(bf16[4,4,128,1024]{3,2,1,0:T(8,128)(2,1)} %get-tuple-element.153), channel_id=1, source_target_pairs={{0,1},{1,0},{2,3},{3,2},{4,5},{5,4},{6,7},{7,6},{8,9},{9,8},{10,11... | collective-permute-start | bytes 12582920 | tf_op jit(solution)/shard_map/ppermute | solution.py:513
  246.6 27.6 %collective-permute-start.31 = (bf16[2,4,512,256]{3,2,1,0:T(8,128)(2,1)S(1)}, bf16[2,4,512,256]{3,2,1,0:T(8,128)(2,1)}, u32[]{:S(2)}, u32[]{:S(2)}) collective-permute-start(bf16[2,4,512,256]{3,2,1,0:T(8,128)(2,1)S(1)} %add_convert_fusion.1), channel_id=1, source_target_pairs={{0,8},{1,17},{2,10},{3,19},{4,12},{5,21},{6,14},{7,23},{8,0},{9,25... | collective-permute-start | bytes 6291464 | tf_op jit(solution)/shard_map/ppermute | solution.py:513
  272.2 38.3 %collective-permute-start.35 = (bf16[2,4,128,1024]{3,2,1,0:T(8,128)(2,1)}, bf16[2,4,128,1024]{3,2,1,0:T(8,128)(2,1)}, u32[]{:S(2)}, u32[]{:S(2)}) collective-permute-start(bf16[2,4,128,1024]{3,2,1,0:T(8,128)(2,1)} %add_convert_fusion), channel_id=1, source_target_pairs={{0,8},{1,17},{2,10},{3,19},{4,12},{5,21},{6,14},{7,23},{8,0},{9,25... | collective-permute-start | bytes 6291464 | tf_op jit(solution)/shard_map/ppermute | solution.py:513
  277.1 29.9 %collective-permute-start.33 = (bf16[4,512,256]{2,1,0:T(8,128)(2,1)}, bf16[4,512,256]{2,1,0:T(8,128)(2,1)S(1)}, u32[]{:S(2)}, u32[]{:S(2)}) collective-permute-start(bf16[4,512,256]{2,1,0:T(8,128)(2,1)} %fusion.3), channel_id=1, source_target_pairs={{0,16},{1,9},{2,18},{3,11},{4,20},{5,13},{6,22},{7,15},{8,24},{9,1... | collective-permute-start | bytes 3145736 | tf_op jit(solution)/shard_map/ppermute | solution.py:513
  278.2 29.8 %copy-start.7 = (bf16[2,4,512,256]{3,2,1,0:T(8,128)(2,1)S(1)}, bf16[2,4,512,256]{3,2,1,0:T(8,128)(2,1)}, u32[]{:S(2)}) copy-start(bf16[2,4,512,256]{3,2,1,0:T(8,128)(2,1)} %get-tuple-element.150) | copy-start | bytes 6291460
  330.1 15.3 %collective-permute-start.37 = (bf16[4,4,128,640]{3,2,1,0:T(8,128)(2,1)}, bf16[4,4,128,640]{3,2,1,0:T(8,128)(2,1)}, u32[]{:S(2)}, u32[]{:S(2)}) collective-permute-start(bf16[4,4,128,640]{3,2,1,0:T(8,128)(2,1)} %get-tuple-element.167), channel_id=1, source_target_pairs={{0,1},{1,0},{2,3},{3,2},{4,5},{5,4},{6,7},{7,6},{8,9},{9,8},{10,11... | collective-permute-start | bytes 7864328 | tf_op jit(solution)/shard_map/ppermute | solution.py:513
  330.2 15.2 %collective-permute-start.36 = (bf16[4,128,1024]{2,1,0:T(8,128)(2,1)}, bf16[4,128,1024]{2,1,0:T(8,128)(2,1)}, u32[]{:S(2)}, u32[]{:S(2)}) collective-permute-start(bf16[4,128,1024]{2,1,0:T(8,128)(2,1)} %fusion.4), channel_id=1, source_target_pairs={{0,16},{1,9},{2,18},{3,11},{4,20},{5,13},{6,22},{7,15},{8,24},{9,1... | collective-permute-start | bytes 3145736 | tf_op jit(solution)/shard_map/ppermute | solution.py:513
  331.3 22.4 %collective-permute-start.34 = (bf16[2,512,256]{2,1,0:T(8,128)(2,1)S(1)}, bf16[2,512,256]{2,1,0:T(8,128)(2,1)}, u32[]{:S(2)}, u32[]{:S(2)}) collective-permute-start(bf16[2,512,256]{2,1,0:T(8,128)(2,1)S(1)} %pad_maximum_fusion.7), channel_id=1, source_target_pairs={{0,2},{1,5},{2,0},{3,7},{4,6},{5,1},{6,4},{7,3},{8,10},{9,13},{10,... | collective-permute-start | bytes 1572872 | tf_op jit(solution)/shard_map/ppermute | solution.py:513
  348.1 42.3 %collective-permute-start.38 = (bf16[2,4,128,640]{3,2,1,0:T(8,128)(2,1)}, bf16[2,4,128,640]{3,2,1,0:T(8,128)(2,1)}, u32[]{:S(2)}, u32[]{:S(2)}) collective-permute-start(bf16[2,4,128,640]{3,2,1,0:T(8,128)(2,1)} %add_convert_fusion.2), channel_id=1, source_target_pairs={{0,8},{1,17},{2,10},{3,19},{4,12},{5,21},{6,14},{7,23},{8,0},{9,25... | collective-permute-start | bytes 3932168 | tf_op jit(solution)/shard_map/ppermute | solution.py:513
  352.2 34.6 %collective-permute-start.39 = (bf16[2,128,1024]{2,1,0:T(8,128)(2,1)S(1)}, bf16[2,128,1024]{2,1,0:T(8,128)(2,1)}, u32[]{:S(2)}, u32[]{:S(2)}) collective-permute-start(bf16[2,128,1024]{2,1,0:T(8,128)(2,1)S(1)} %pad_maximum_fusion.8), channel_id=1, source_target_pairs={{0,2},{1,5},{2,0},{3,7},{4,6},{5,1},{6,4},{7,3},{8,10},{9,13},{10,... | collective-permute-start | bytes 1572872 | tf_op jit(solution)/shard_map/ppermute | solution.py:513
  354.7 32.1 %collective-permute-start.40 = (bf16[512,256]{1,0:T(8,128)(2,1)S(1)}, bf16[512,256]{1,0:T(8,128)(2,1)S(1)}, u32[]{:S(2)}, u32[]{:S(2)}) collective-permute-start(bf16[512,256]{1,0:T(8,128)(2,1)S(1)} %fusion.11), channel_id=1, source_target_pairs={{0,4},{1,3},{2,6},{3,1},{4,0},{5,7},{6,2},{7,5},{8,12},{9,11},{10,... | collective-permute-start | bytes 786440 | tf_op jit(solution)/shard_map/ppermute | solution.py:513
  405.7 12.9 %collective-permute-start.41 = (bf16[4,4,144,384]{3,2,1,0:T(8,128)(2,1)}, bf16[4,4,144,384]{3,2,1,0:T(8,128)(2,1)S(1)}, u32[]{:S(2)}, u32[]{:S(2)}) collective-permute-start(bf16[4,4,144,384]{3,2,1,0:T(8,128)(2,1)} %get-tuple-element.181), channel_id=1, source_target_pairs={{0,1},{1,0},{2,3},{3,2},{4,5},{5,4},{6,7},{7,6},{8,9},{9,8},{10,11... | collective-permute-start | bytes 5308424 | tf_op jit(solution)/shard_map/ppermute | solution.py:513
  405.8 9.9 %collective-permute-start.43 = (bf16[128,1024]{1,0:T(8,128)(2,1)S(1)}, bf16[128,1024]{1,0:T(8,128)(2,1)S(1)}, u32[]{:S(2)}, u32[]{:S(2)}) collective-permute-start(bf16[128,1024]{1,0:T(8,128)(2,1)S(1)} %fusion.12), channel_id=1, source_target_pairs={{0,4},{1,3},{2,6},{3,1},{4,0},{5,7},{6,2},{7,5},{8,12},{9,11},{10,... | collective-permute-start | bytes 786440 | tf_op jit(solution)/shard_map/ppermute | solution.py:513
  405.9 11.0 %collective-permute-start.42 = (bf16[4,128,640]{2,1,0:T(8,128)(2,1)}, bf16[4,128,640]{2,1,0:T(8,128)(2,1)S(1)}, u32[]{:S(2)}, u32[]{:S(2)}) collective-permute-start(bf16[4,128,640]{2,1,0:T(8,128)(2,1)} %fusion.6), channel_id=1, source_target_pairs={{0,16},{1,9},{2,18},{3,11},{4,20},{5,13},{6,22},{7,15},{8,24},{9,1... | collective-permute-start | bytes 1966088 | tf_op jit(solution)/shard_map/ppermute | solution.py:513
  420.9 13.4 %collective-permute-start.45 = (bf16[2,4,144,384]{3,2,1,0:T(8,128)(2,1)}, bf16[2,4,144,384]{3,2,1,0:T(8,128)(2,1)}, u32[]{:S(2)}, u32[]{:S(2)}) collective-permute-start(bf16[2,4,144,384]{3,2,1,0:T(8,128)(2,1)} %add_convert_fusion.5), channel_id=1, source_target_pairs={{0,8},{1,17},{2,10},{3,19},{4,12},{5,21},{6,14},{7,23},{8,0},{9,25... | collective-permute-start | bytes 2654216 | tf_op jit(solution)/shard_map/ppermute | solution.py:513
  421.8 13.9 %collective-permute-start.44 = (bf16[2,128,640]{2,1,0:T(8,128)(2,1)S(1)}, bf16[2,128,640]{2,1,0:T(8,128)(2,1)S(1)}, u32[]{:S(2)}, u32[]{:S(2)}) collective-permute-start(bf16[2,128,640]{2,1,0:T(8,128)(2,1)S(1)} %pad_maximum_fusion.12), channel_id=1, source_target_pairs={{0,2},{1,5},{2,0},{3,7},{4,6},{5,1},{6,4},{7,3},{8,10},{9,13},{10,... | collective-permute-start | bytes 983048 | tf_op jit(solution)/shard_map/ppermute | solution.py:513
  435.7 8.0 %collective-permute-start.46 = (bf16[128,640]{1,0:T(8,128)(2,1)S(1)}, bf16[128,640]{1,0:T(8,128)(2,1)S(1)}, u32[]{:S(2)}, u32[]{:S(2)}) collective-permute-start(bf16[128,640]{1,0:T(8,128)(2,1)S(1)} %fusion.16), channel_id=1, source_target_pairs={{0,4},{1,3},{2,6},{3,1},{4,0},{5,7},{6,2},{7,5},{8,12},{9,11},{10,... | collective-permute-start | bytes 491528 | tf_op jit(solution)/shard_map/ppermute | solution.py:513
  438.4 11.4 %collective-permute-start.56 = (bf16[1024,256]{1,0:T(8,128)(2,1)S(1)}, bf16[1024,256]{1,0:T(8,128)(2,1)S(1)}, u32[]{:S(2)}, u32[]{:S(2)}) collective-permute-start(bf16[1024,256]{1,0:T(8,128)(2,1)S(1)} %constant_dynamic-update-slice_fusion), channel_id=1, source_target_pairs={{0,8},{1,17},{2,10},{3,19},{4,12},{5,21},{6,14},{7,23},{8,0},{9,25... | collective-permute-start | bytes 1572872 | tf_op jit(solution)/shard_map/ppermute | solution.py:513
  439.5 13.2 %collective-permute-start.49 = (bf16[4,144,384]{2,1,0:T(8,128)(2,1)S(1)}, bf16[4,144,384]{2,1,0:T(8,128)(2,1)}, u32[]{:S(2)}, u32[]{:S(2)}) collective-permute-start(bf16[4,144,384]{2,1,0:T(8,128)(2,1)S(1)} %fusion.9), channel_id=1, source_target_pairs={{0,16},{1,9},{2,18},{3,11},{4,20},{5,13},{6,22},{7,15},{8,24},{9,1... | collective-permute-start | bytes 1327112 | tf_op jit(solution)/shard_map/ppermute | solution.py:513
  443.8 7.7 %collective-permute-start.47 = (bf16[128,640]{1,0:T(8,128)(2,1)S(1)}, bf16[128,640]{1,0:T(8,128)(2,1)S(1)}, u32[]{:S(2)}, u32[]{:S(2)}) collective-permute-start(bf16[128,640]{1,0:T(8,128)(2,1)S(1)} %fusion.10), channel_id=1, source_target_pairs={{0,8},{1,17},{2,10},{3,19},{4,12},{5,21},{6,14},{7,23},{8,0},{9,25... | collective-permute-start | bytes 491528 | tf_op jit(solution)/shard_map/ppermute | solution.py:513
  451.5 17.1 %collective-permute-start.48 = (bf16[2,128,640]{2,1,0:T(8,128)(2,1)S(1)}, bf16[2,128,640]{2,1,0:T(8,128)(2,1)S(1)}, u32[]{:S(2)}, u32[]{:S(2)}) collective-permute-start(bf16[2,128,640]{2,1,0:T(8,128)(2,1)S(1)} %pad_maximum_fusion.13), channel_id=1, source_target_pairs={{0,16},{1,9},{2,18},{3,11},{4,20},{5,13},{6,22},{7,15},{8,24},{9,1... | collective-permute-start | bytes 983048 | tf_op jit(solution)/shard_map/ppermute | solution.py:513
  454.2 7.8 %collective-permute-start.50 = (bf16[144,384]{1,0:T(8,128)(2,1)S(1)}, bf16[144,384]{1,0:T(8,128)(2,1)S(1)}, u32[]{:S(2)}, u32[]{:S(2)}) collective-permute-start(bf16[144,384]{1,0:T(8,128)(2,1)S(1)} %get-tuple-element.209), channel_id=1, source_target_pairs={{0,6},{1,7},{2,4},{3,5},{4,2},{5,3},{6,0},{7,1},{8,14},{9,15},{10,... | collective-permute-start | bytes 331784 | tf_op jit(solution)/shard_map/ppermute | solution.py:513
  456.9 8.1 %collective-permute-start.51 = (bf16[144,384]{1,0:T(8,128)(2,1)S(1)}, bf16[144,384]{1,0:T(8,128)(2,1)S(1)}, u32[]{:S(2)}, u32[]{:S(2)}) collective-permute-start(bf16[144,384]{1,0:T(8,128)(2,1)S(1)} %get-tuple-element.211), channel_id=1, source_target_pairs={{0,4},{1,5},{2,6},{3,7},{4,0},{5,1},{6,2},{7,3},{8,12},{9,13},{10,... | collective-permute-start | bytes 331784 | tf_op jit(solution)/shard_map/ppermute | solution.py:513
  457.5 7.6 %collective-permute-start.52 = (bf16[144,384]{1,0:T(8,128)(2,1)S(1)}, bf16[144,384]{1,0:T(8,128)(2,1)S(1)}, u32[]{:S(2)}, u32[]{:S(2)}) collective-permute-start(bf16[144,384]{1,0:T(8,128)(2,1)S(1)} %get-tuple-element.210), channel_id=1, source_target_pairs={{0,2},{1,3},{2,0},{3,1},{4,6},{5,7},{6,4},{7,5},{8,10},{9,11},{10,... | collective-permute-start | bytes 331784 | tf_op jit(solution)/shard_map/ppermute | solution.py:513
  458.8 21.6 %collective-permute-start.57 = (bf16[2,1024,256]{2,1,0:T(8,128)(2,1)S(1)}, bf16[2,1024,256]{2,1,0:T(8,128)(2,1)S(1)}, u32[]{:S(2)}, u32[]{:S(2)}) collective-permute-start(bf16[2,1024,256]{2,1,0:T(8,128)(2,1)S(1)} %pad_maximum_fusion.3), channel_id=1, source_target_pairs={{0,16},{1,9},{2,18},{3,11},{4,20},{5,13},{6,22},{7,15},{8,24},{9,1... | collective-permute-start | bytes 3145736 | tf_op jit(solution)/shard_map/ppermute | solution.py:513
  465.1 7.1 %collective-permute-start.53 = (bf16[144,384]{1,0:T(8,128)(2,1)S(1)}, bf16[144,384]{1,0:T(8,128)(2,1)S(1)}, u32[]{:S(2)}, u32[]{:S(2)}) collective-permute-start(bf16[144,384]{1,0:T(8,128)(2,1)S(1)} %fusion.15), channel_id=1, source_target_pairs={{0,24},{1,25},{2,26},{3,27},{4,28},{5,29},{6,30},{7,31},{8,16},{9,... | collective-permute-start | bytes 331784 | tf_op jit(solution)/shard_map/ppermute | solution.py:513
  467.0 11.4 %collective-permute-start.54 = (bf16[144,384]{1,0:T(8,128)(2,1)S(1)}, bf16[144,384]{1,0:T(8,128)(2,1)S(1)}, u32[]{:S(2)}, u32[]{:S(2)}) collective-permute-start(bf16[144,384]{1,0:T(8,128)(2,1)S(1)} %fusion.15), channel_id=1, source_target_pairs={{0,16},{1,17},{2,18},{3,19},{4,20},{5,21},{6,22},{7,23},{8,24},{9,... | collective-permute-start | bytes 331784 | tf_op jit(solution)/shard_map/ppermute | solution.py:513
  468.2 10.2 %collective-permute-start.55 = (bf16[144,384]{1,0:T(8,128)(2,1)S(1)}, bf16[144,384]{1,0:T(8,128)(2,1)S(1)}, u32[]{:S(2)}, u32[]{:S(2)}) collective-permute-start(bf16[144,384]{1,0:T(8,128)(2,1)S(1)} %fusion.15), channel_id=1, source_target_pairs={{0,8},{1,9},{2,10},{3,11},{4,12},{5,13},{6,14},{7,15},{8,0},{9,1},... | collective-permute-start | bytes 331784 | tf_op jit(solution)/shard_map/ppermute | solution.py:513
  (19 other events, 177.5 us)

commit v8 on v7

--- a/solution.py
+++ b/solution.py
@@ -335,11 +335,14 @@
 TN = (((0,), (0,)), ((), ()))
 LANES = 128
 AXES = ("grp", "shard")
-CHEAP = pl.CostEstimate(flops=1024, bytes_accessed=1024, transcendentals=0)
 
 
 def mxu(left, right, dims):
     return lax.dot_general(left, right, dims, preferred_element_type=jnp.float32)
+
+
+def cost(flops):
+    return pl.CostEstimate(flops=2 * flops, bytes_accessed=0, transcendentals=0)
 
 
 def params(megabytes=60):
@@ -404,7 +407,7 @@
         ],
         input_output_aliases={} if before is None else {5: 0, 6: 1},
         compiler_params=params(60),
-        cost_estimate=CHEAP,
+        cost_estimate=cost(16 * length * length * pairs * LANES),
         name="attn_fwd",
     )(qkv, qkv, qkv, seg_col, seg_row, *(() if before is None else before))
 
@@ -462,16 +465,20 @@
     sum_ref[1:2, :] = jnp.sum(value_grad, 0, keepdims=True)
 
 
-def attention_backward(qkv, out, out_grad, seg_col, seg_row, lse, start, pairs):
+def attention_backward(qkv, out, out_grad, seg_col, seg_row, lse, start, pairs, at, size, before=None):
     length, width = out.shape
     total = width // LANES
     rows = min(256, length)
+    more = () if before is None else before
 
     def pair(part):
         return pl.BlockSpec((length, LANES), lambda j: (0, part * total + start + j))
 
+    def body(*refs):
+        attention_backward_kernel(*refs[:8], *refs[-2:], rows=rows)
+
     return pl.pallas_call(
-        functools.partial(attention_backward_kernel, rows=rows),
+        body,
         grid=(pairs,),
         in_specs=[
             pair(0),
@@ -482,19 +489,21 @@
             pl.BlockSpec((length, 1), lambda j: (0, 0)),
             pl.BlockSpec((1, length), lambda j: (0, 0)),
             pl.BlockSpec((1, 2, length), lambda j: (j + start, 0, 0)),
-        ],
+        ]
+        + [pl.BlockSpec(memory_space=pl.ANY)] * len(more),
         out_specs=[
-            pl.BlockSpec((3, length, LANES), lambda j: (0, 0, j)),
-            pl.BlockSpec((2, LANES), lambda j: (0, j)),
+            pl.BlockSpec((3, length, LANES), lambda j: (0, 0, j + at)),
+            pl.BlockSpec((2, LANES), lambda j: (0, j + at)),
         ],
         out_shape=[
-            jax.ShapeDtypeStruct((3, length, pairs * LANES), jnp.bfloat16),
-            jax.ShapeDtypeStruct((2, pairs * LANES), jnp.float32),
+            jax.ShapeDtypeStruct((3, length, size * LANES), jnp.bfloat16),
+            jax.ShapeDtypeStruct((2, size * LANES), jnp.float32),
         ],
+        input_output_aliases={} if before is None else {8: 0, 9: 1},
         compiler_params=params(60),
-        cost_estimate=CHEAP,
+        cost_estimate=cost(40 * length * length * pairs * LANES),
         name="attn_bwd",
-    )(qkv, qkv, qkv, out, out_grad, seg_col, seg_row, lse)
+    )(qkv, qkv, qkv, out, out_grad, seg_col, seg_row, lse, *more)
 
 
 class Place:
@@ -540,6 +549,13 @@
     return lax.optimization_barrier((value, *others))[0]
 
 
+def meet(anchor, *flights):
+    arrays = [f.flying for f in flights]
+    _, *arrays = lax.optimization_barrier((anchor, *arrays))
+    for f, array in zip(flights, arrays):
+        f.flying = array
+
+
 class Gather:
     def __init__(self, place, piece):
         self.place = place
@@ -548,34 +564,31 @@
         self.crossed = [None] * 4
 
     def chips_near(self, *wait):
-        piece = after(self.piece, *wait) if wait else self.piece
-        self.pair = [piece, self.place.swap_chip(piece, 0)]
-        return self.pair[1]
-
-    def chips_far(self, *wait):
-        pair = jnp.stack([self.pair[0], after(self.pair[1], *wait)])
-        self.rest = [pair, self.place.swap_chip(pair, 1)]
-        return self.rest[1]
-
-    def join(self, *wait):
-        rest = after(self.rest[1], *wait) if wait else self.rest[1]
-        self.held[0] = jnp.concatenate([self.rest[0], rest])
+        self.piece = after(self.piece, *wait)
+        self.flying = self.place.swap_chip(self.piece, 0)
+
+    def chips_far(self):
+        self.pair = jnp.stack([self.piece, self.flying])
+        self.flying = self.place.swap_chip(self.pair, 1)
+        return self.pair
+
+    def near(self, *wait):
+        joined = jnp.concatenate([self.pair, self.flying])
+        self.held[0] = after(joined, *wait)
+        self.flying = (self.place.swap_grp(self.held[0], 0), self.place.swap_grp(self.held[0], 1))
         return self.held[0]
 
-    def near(self):
-        self.held[1] = self.place.swap_grp(self.held[0], 0)
-        self.held[2] = self.place.swap_grp(self.held[0], 1)
-        return self.held[2]
-
     def far(self, *wait):
-        first = after(self.held[1], *wait) if wait else self.held[1]
-        self.held[3] = self.place.swap_grp(first, 1)
-        return self.held[3]
+        self.held[1:3] = self.flying
+        first = after(self.held[1], *wait)
+        self.flying = self.place.swap_grp(first, 1)
+
+    def landed(self):
+        self.held[3] = self.flying
 
     def cross(self, *which, wait=()):
         for n in which:
-            piece = after(self.held[n], *wait) if wait else self.held[n]
-            self.crossed[n] = self.place.swap_core(piece)
+            self.crossed[n] = self.place.swap_core(after(self.held[n], *wait))
 
     def pieces(self):
         return self.held + self.crossed
@@ -661,7 +674,7 @@
         ),
         out_shape=outs + [shaped(shape, jnp.bfloat16)],
         compiler_params=params(mb),
-        cost_estimate=CHEAP,
+        cost_estimate=cost(flops),
         name=name,
     )(place.scalars, *pieces, *inputs)
 
@@ -675,7 +688,7 @@
         out_specs=out_specs,
         out_shape=outs,
         compiler_params=params(mb),
-        cost_estimate=CHEAP,
+        cost_estimate=cost(flops),
         name=name,
     )(*inputs)
 
@@ -708,8 +721,9 @@
 
 class Vectors:
     def __init__(self, place, vectors, *wait):
-        flat = jnp.concatenate([after(vectors[0], *wait), *vectors[1:]])
-        own = jnp.pad(flat.reshape(-1, LANES), ((0, -(flat.shape[0] // LANES) % 16), (0, 0)))
+        lines = [v.reshape(-1, LANES) for v in (after(vectors[0], *wait), *vectors[1:])]
+        blank = jnp.zeros((-sum(x.shape[0] for x in lines) % 16, LANES), jnp.bfloat16)
+        own = jnp.concatenate([*lines, blank])
         own = jnp.stack([own, place.swap_core(own)])
         pair = jnp.stack([own, place.swap_chip(own, 0)])
         self.slots = jnp.concatenate([pair, place.swap_chip(pair, 1)])
@@ -1009,12 +1023,12 @@
     )
 
 
-def project_qkv_back(grads, weight, first_grad):
+def project_qkv_back(grads, weight, first_grad, start, tiles, before=None):
     length, width = first_grad.shape
     part = width // len(grads)
 
     def kernel(w_ref, *refs):
-        *grad_refs, first_ref, out_ref = refs
+        grad_refs, first_ref, out_ref = refs[: len(grads)], refs[len(grads)], refs[-1]
         total = first_ref[...]
         for n in range(3):
             for m, grad_ref in enumerate(grad_refs):
@@ -1022,18 +1036,22 @@
                 total = total + mxu(grad_ref[n], w_ref[:, at : at + part], NT)
         out_ref[...] = total
 
-    return plain_call(
+    tile = pl.BlockSpec((TILE, width), lambda i: (start + i, 0))
+    more = () if before is None else (before,)
+    return pl.pallas_call(
         kernel,
-        (weight, *grads, first_grad),
-        [whole_once(weight.shape)]
-        + [pl.BlockSpec((3, TILE, part), lambda i: (0, i, 0))] * len(grads)
-        + [row_tiles(width)],
-        [shaped((length, width), jnp.float32)],
-        [row_tiles(width)],
-        length // TILE,
-        "qkv_back",
-        6 * length * width * width,
-    )[0]
+        grid=(tiles,),
+        in_specs=[whole_once(weight.shape)]
+        + [pl.BlockSpec((3, TILE, part), lambda i: (0, start + i, 0))] * len(grads)
+        + [tile]
+        + [pl.BlockSpec(memory_space=pl.ANY)] * len(more),
+        out_specs=tile,
+        out_shape=shaped((length, width), jnp.float32),
+        input_output_aliases={} if before is None else {len(grads) + 2: 0},
+        compiler_params=params(60),
+        cost_estimate=cost(6 * tiles * TILE * width * width),
+        name="qkv_back",
+    )(weight, *grads, first_grad, *more)
 
 
 ORDER = (1, 3, 0, 2)
@@ -1181,7 +1199,7 @@
         ),
         out_shape=[shaped((n, chips, tall, cols), jnp.bfloat16) for n in (2, 2, groups)],
         compiler_params=params(60),
-        cost_estimate=CHEAP,
+        cost_estimate=cost(2 * tokens * height * cols * groups),
         name="wgrad_" + name,
     )(place.scalars, *inputs)
 
@@ -1196,49 +1214,47 @@
 class Reduction:
     def __init__(self, place, pairs, split, name, *wait, sums=None):
         self.place = place
-        if wait:
-            pairs = [(after(pairs[0][0], *wait), pairs[0][1])] + pairs[1:]
+        pairs = [(after(pairs[0][0], *wait), pairs[0][1])] + pairs[1:]
         self.leave, self.keep, sent = weight_grad(place, pairs, split, name, sums)
         self.made = self.leave
-        self.core = place.swap_core(sent)
-
-    def near(self, *wait):
-        self.core = after(self.core, *wait) if wait else self.core
+        self.flying = place.swap_core(sent)
+
+    def near(self):
+        self.core = self.flying
         leave = add(self.leave, self.core[:2])
-        self.first = self.place.swap_grp(leave, 0)
+        self.flying = self.place.swap_grp(leave, 0)
         return leave
 
-    def middle(self, *wait):
-        self.first = after(self.first, *wait) if wait else self.first
+    def middle(self):
+        self.first = self.flying
         second = add(self.keep[1], self.core[3], self.first[1])
-        self.second = self.place.swap_grp(second, 1)
+        self.flying = self.place.swap_grp(second, 1)
         return second
 
-    def column(self, *wait):
-        second = after(self.second, *wait) if wait else self.second
-        mine = add(self.keep[0], self.core[2], self.first[0], second)
+    def column(self):
+        mine = add(self.keep[0], self.core[2], self.first[0], self.flying)
         return mine, lambda chip: lax.dynamic_index_in_dim(mine, chip, 0, False)
 
-    def along(self, *wait):
+    def along(self):
         place = self.place
-        mine, at = self.column(*wait)
+        mine, at = self.column()
         self.mine = [at(place.slot_chip(slot)) for slot in range(4)]
-        self.first = place.swap_chip(jnp.stack([self.mine[1], self.mine[3]]), 0)
-        return mine
-
-    def along_far(self, *wait):
-        self.first = after(self.first, *wait) if wait else self.first
+        both = jnp.stack([self.mine[1], self.mine[3]])
+        self.flying = place.swap_chip(both, 0)
+        return both
+
+    def along_far(self):
+        self.first = self.flying
         second = add(self.mine[2], self.first[1])
-        self.second = self.place.swap_chip(second, 1)
+        self.flying = self.place.swap_chip(second, 1)
         return second
 
-    def share(self, *wait):
-        second = after(self.second, *wait) if wait else self.second
-        return add(self.mine[0], self.first[0], second)
-
-    def share_direct(self, *wait):
+    def share(self):
+        return add(self.mine[0], self.first[0], self.flying)
+
+    def share_direct(self):
         place = self.place
-        mine, at = self.column(*wait)
+        mine, at = self.column()
         terms = [
             place.permute(at(place.chip ^ k), (2 * k, 2 * k)) for k in range(place.chips - 1, 0, -1)
         ]
@@ -1248,28 +1264,31 @@
 class Replication:
     def __init__(self, place, share, direct=False):
         self.place = place
+        self.blocks = [share] + [None] * 3
         if direct:
             size = place.shards
-            self.blocks = [share] + [None] * 3
             for mask in (3, 1, 2):
                 self.blocks[mask] = place.permute(share, (mask * size, mask * size))
             self.owner = lambda n: place.grp ^ n
         else:
-            self.blocks = [share, place.swap_grp(share, 0), None, None]
+            self.flying = place.swap_grp(share, 0)
             self.owner = place.slot_grp
 
-    def far(self, *wait):
-        pair = jnp.stack([self.blocks[0], after(self.blocks[1], *wait)])
-        rest = self.place.swap_grp(pair, 1)
-        self.blocks[2:] = [rest[0], rest[1]]
-        return rest
+    def far(self):
+        pair = jnp.stack([self.blocks[0], self.flying])
+        self.blocks[1] = self.flying
+        self.flying = self.place.swap_grp(pair, 1)
+        return pair
 
     def result(self):
+        blocks = self.blocks
+        if blocks[2] is None:
+            blocks = [*blocks[:2], self.flying[0], self.flying[1]]
         ordered = []
         for g in range(self.place.groups):
-            block = self.blocks[0]
+            block = blocks[0]
             for n in range(1, self.place.groups):
-                block = jnp.where(self.owner(n) == g, self.blocks[n], block)
+                block = jnp.where(self.owner(n) == g, blocks[n], block)
             ordered.append(block.astype(jnp.float32))
         return ordered
 
@@ -1309,21 +1328,21 @@
     c3 = Gather(place, w_out)
     c1.chips_near()
     c1.chips_far()
-    joined = c1.join()
-    c1.near()
+    joined = c1.near()
     small = Vectors(
         place,
         (b_query, b_value, b_attn_out, norm1_gain, norm1_bias, b_out, norm2_gain, norm2_bias, b_in),
-        c1.pair[1],
-    )
+        joined,
+    )
+    c2.chips_near(joined)
+    pair = c2.chips_far()
+    c1.flying = lax.optimization_barrier(c1.flying)
+    c1.far(pair)
+    c1.cross(0, 1, 2)
     vectors, bias_in, qkv_bias = small.unpack()
-    c2.chips_near(joined)
-    c1.cross(0)
-    c2.chips_far()
-    far = c1.far(c2.rest[0], vectors)
-    c1.cross(1, 2)
+    meet(vectors, c1, c2)
+    c1.landed()
     c1.cross(3)
-    c2.join(far)
     c2.near()
     blank = jnp.ones((1, width), jnp.float32)
     qkv_scale = jnp.concatenate([blank / math.sqrt(HD), blank, blank], 1)
@@ -1331,81 +1350,98 @@
     mixed, full_qkv = project_qkv(place, rows, Window(c1, 0, w_qkv.shape[1]), qkv_bias, qkv_scale)
     c3.chips_near(mixed)
     c2.cross(0, wait=(mixed,))
-    share_of = (pairs // 2 - pairs // 8, pairs // 4, pairs // 2 - pairs // 8)
-    forward = None
-    start = 0
-    for n, count in enumerate(share_of):
-        wait = (c2.held[3],) if n == 2 else ()
-        forward = attention_forward(
-            after(mixed, *wait) if wait else mixed, seg_col, seg_row, start, count, forward
-        )
-        start += count
-        done = forward[1]
-        if n == 0:
-            c2.far(done)
-            c3.chips_far(done)
-            c2.cross(1, 2, wait=(done,))
-        if n == 1:
-            c3.join(done)
-            c3.near()
-            c2.cross(3, wait=(done,))
-    contexts, lse = forward
+    first, second = pairs * 3 // 8, pairs * 3 // 4
+    forward = attention_forward(mixed, seg_col, seg_row, 0, first)
+    meet(forward[1], c2, c3)
+    c2.far()
+    pair = c3.chips_far()
+    c2.cross(1, 2)
+    forward = attention_forward(after(mixed, pair), seg_col, seg_row, first, second - first, forward)
+    meet(forward[1], c2, c3)
+    c2.landed()
+    c2.cross(3)
+    joined = c3.near()
+    contexts, lse = attention_forward(
+        after(mixed, joined), seg_col, seg_row, second, pairs - second, forward
+    )
     normed, scale_one, normed_low, full_attn = project_out(
         place, contexts, Window(c2, w_in.shape[1], w_attn_out.shape[1]), rows, vectors
     )
-    c3.far(normed_low)
-    c3.cross(0, 1, 2, wait=(normed_low,))
+    meet(normed_low, c3)
+    c3.far()
+    c3.cross(0, 1, 2)
     hidden, slope, full_in = feed_in(
         place, after(normed_low, c3.held[1]), Window(c2, 0, w_in.shape[1]), bias_in
     )
-    c3.cross(3, wait=(hidden,))
+    meet(hidden, c3)
+    c3.landed()
+    c3.cross(3)
     layer_out, second_grad, out_low, second_sums, full_out = feed_out(
         place, hidden, Window(c3, 0, w_out.shape[1]), normed, cotangent[0], keep, vectors
     )
 
     r_out = Reduction(place, [(hidden, out_low)], False, "out")
     pre_low, bias_in_grad = feed_out_back(after(out_low, r_out.made), full_out, slope)
-    near = r_out.near(pre_low)
-    r_in = Reduction(place, [(normed_low, pre_low)], True, "in", near)
+    meet(pre_low, r_out)
+    step = r_out.near()
+    r_in = Reduction(place, [(normed_low, pre_low)], True, "in", step)
     first_grad, attn_low, context_grad, first_sums = feed_in_back(
         after(pre_low, r_in.made), full_in, second_grad, normed, scale_one, vectors, full_attn
     )
-    half = pairs // 2
-
-    def back(start, *wait):
+    meet(attn_low, r_out, r_in)
+    steps = (r_out.middle(), r_in.near())
+    half, quarter = pairs // 2, pairs // 4
+
+    def back(wait, start, count, at, before=None):
         return attention_backward(
-            mixed, contexts, after(context_grad, *wait), seg_col, seg_row, lse, start, half
+            mixed,
+            contexts,
+            after(context_grad, *wait),
+            seg_col,
+            seg_row,
+            lse,
+            start,
+            count,
+            at,
+            half,
+            before,
         )
 
-    middle = r_out.middle(first_grad)
-    near = r_in.near(first_grad)
-    low_a, late_a = back(0, middle, near)
-    middle = r_in.middle(late_a)
-    along = r_out.along(late_a)
-    r_a = Reduction(place, [(contexts, attn_low), (rows, low_a)], True, "a", middle, along)
-    far = r_out.along_far(r_a.made)
-    along = r_in.along(r_a.made)
-    near = r_a.near(r_a.made)
-    low_b, late_b = back(half, far, along, near)
-    middle = r_a.middle(late_b)
-    along = r_in.along_far(late_b)
-    share_out = r_out.share(late_b)
-    sums = pack_sums(late_a, late_b, first_sums, second_sums, bias_in_grad)
-    r_b = Reduction(place, [(rows, low_b)], True, "b", middle, along, share_out, sums=sums)
-    along = r_a.along(r_b.made)
-    share_in = r_in.share(r_b.made)
+    low_a, late_a = back(steps, 0, half, 0)
+    meet(late_a, r_out, r_in)
+    steps = (r_out.along(), r_in.middle())
+    r_a = Reduction(place, [(contexts, attn_low), (rows, low_a)], True, "a", *steps)
+    meet(r_a.made, r_out, r_in)
+    steps = (r_out.along_far(), r_in.along())
+    part = back((r_a.made, *steps), half, quarter, 0)
+    meet(part[1], r_out, r_in, r_a)
+    steps = (r_out.share(), r_in.along_far(), r_a.near())
+    share_out = steps[0]
+    low_b, late_b = back(steps, half + quarter, quarter, quarter, part)
+    meet(late_b, r_in, r_a)
+    share_in = r_in.share()
     inner = share_in.shape[1] // groups
     joined = jnp.concatenate(
         [share_out] + [share_in[:, n * inner : (n + 1) * inner] for n in range(groups)]
     )
     all_ffn = Replication(place, joined)
-    near = r_b.near(along, joined)
-    input_grad = project_qkv_back((low_a, after(low_b, near)), full_qkv, first_grad)
-    middle = r_b.middle(input_grad)
-    along = r_a.along_far(middle)
-    all_ffn.far(middle)
+    sums = pack_sums(late_a, late_b, first_sums, second_sums, bias_in_grad)
+    r_b = Reduction(place, [(rows, low_b)], True, "b", joined, r_a.middle(), sums=sums)
+    meet(r_b.made, r_a, all_ffn)
+    steps = (r_a.along(), all_ffn.far())
+    grads = (low_a, after(low_b, r_b.made, *steps))
+    tiles = length // TILE // 2
+    input_grad = project_qkv_back(grads, full_qkv, first_grad, 0, tiles)
+    meet(input_grad, r_b)
+    step = r_b.near()
+    input_grad = project_qkv_back(
+        grads, full_qkv, after(first_grad, step), tiles, tiles, input_grad
+    )
+    meet(input_grad, r_b, r_a)
+    r_b.middle()
+    r_a.along_far()
     share_b = r_b.share_direct()
-    all_a = Replication(place, r_a.share(along))
+    all_a = Replication(place, r_a.share())
     all_b = Replication(place, share_b, direct=True)
     all_a.far()
 

time: 493 us -> 490 us (level)
  waiting for transfers between devices: 87.8 us -> 75.1 us
  Pallas kernels: 271 us -> 278 us
    pallas_call x2 -> x5, Pallas kernels: 57.4 us -> 76.9 us  [the longest x3 60.1 us: attention_backward(): pl.pallas_call(body, grid=(pairs,), in_specs=[pair(0), pair(1), pair(2),...]
    ppermute x58, waiting for transfers between devices: 87.8 us -> 75.1 us  [permute(): return lax.ppermute(array, AXES, pairs)]
    pallas_call x3 -> x2, Pallas kernels: 47.8 us -> 36.2 us  [plain_call(): pl.pallas_call(kernel, grid=(steps,), in_specs=in_specs, out_specs=out_sp...]
    unnamed x97 -> x119, local copies, waits for them, and re-layouts: 10.5 us -> 12.8 us
  transfers between devices with their start and end apart: 58 -> 58, of which waited for: 23 -> 24; matrix products, arithmetic and copies ran while one was open for 9% -> 7% of each run, Pallas kernels for 39% -> 47%
where the time goes in v8:
time: 490 us; the launch traced here: 480 us
  Pallas kernels  278 us (57%)
  waiting for transfers between devices  75.1 us (15%)
  starting transfers between devices  62.3 us (13%)
  other arithmetic  44.7 us (9%)
  local copies, waits for them, and re-layouts  17.7 us (4%)
    ppermute x58, waiting for transfers between devices, permute(): return lax.ppermute(array, AXES, pairs)  75.1 us
    pallas_call x4, Pallas kernels, weight_call(): pl.pallas_call(body, grid_spec=pltpu.PrefetchScalarGridSpec(num_scalar_pr...  66.3 us
    ppermute x58, starting transfers between devices, permute(): return lax.ppermute(array, AXES, pairs)  62.3 us
    pallas_call x3, Pallas kernels, attention_backward(): pl.pallas_call(body, grid=(pairs,), in_specs=[pair(0), pair(1), pair(2),...  60.1 us
    pallas_call x4, Pallas kernels, weight_grad(): pl.pallas_call(functools.partial(weight_grad_kernel, rows=rows, groups=gr...  58.6 us
    pallas_call x3, Pallas kernels, attention_forward(): pl.pallas_call(body, grid=(pairs,), in_specs=[pair(0), pair(1), pair(2),...  37.3 us
    pallas_call x2, Pallas kernels, plain_call(): pl.pallas_call(kernel, grid=(steps,), in_specs=in_specs, out_specs=out_sp...  36.2 us
    convert_element_type x18, other arithmetic, add(): return total.astype(jnp.bfloat16)  35 us
  transfers between devices with their start and end apart: 58, of which 24 were waited for; matrix products, arithmetic and copies ran while one was open for 7% of the time, Pallas kernels for 47%

profile of v8, /device:TPU:0, one launch (start us, length us, event | category | flops | bytes accessed | tf_op | source)
XLA Modules:
  0.0 480.0 jit_solution(2627510005400622058)
XLA Ops:
  0.7 3.1 collective-permute-start
  3.8 5.6 %collective-permute-done = bf16[128,768]{1,0:T(8,128)(2,1)S(1)} collective-permute-done((bf16[128,768]{1,0:T(8,128)(2,1)}, bf16[128,768]{1,0:T(8,128)(2,1)S(1)}, u32[]{:S(2)}, u32[]{:S(2)}) %collective-permute-start) | collective-permute-done | bytes 196640 | tf_op jit(solution)/shard_map/ppermute | solution.py:522
  10.5 2.5 collective-permute-start.1
  13.0 8.8 %collective-permute-done.1 = bf16[2,128,768]{2,1,0:T(8,128)(2,1)S(1)} collective-permute-done((bf16[2,128,768]{2,1,0:T(8,128)(2,1)S(1)}, bf16[2,128,768]{2,1,0:T(8,128)(2,1)S(1)}, u32[]{:S(2)}, u32[]{:S(2)}) %collective-permute-start.1) | collective-permute-done | bytes 393248 | tf_op jit(solution)/shard_map/ppermute | solution.py:522
  22.8 2.3 collective-permute-start.2
  25.1 1.5 collective-permute-start.3
  26.7 1.9 collective-permute-start.7
  28.6 8.6 %collective-permute-done.7 = bf16[128,1280]{1,0:T(8,128)(2,1)S(1)} collective-permute-done((bf16[128,1280]{1,0:T(8,128)(2,1)S(1)}, bf16[128,1280]{1,0:T(8,128)(2,1)S(1)}, u32[]{:S(2)}, u32[]{:S(2)}) %collective-permute-start.7) | collective-permute-done | bytes 327712 | tf_op jit(solution)/shard_map/ppermute | solution.py:522
  37.3 6.0 %collective-permute-done.2.refs_1_ = bf16[4,128,768]{2,1,0:T(8,128)(2,1)} collective-permute-done((bf16[4,128,768]{2,1,0:T(8,128)(2,1)S(1)}, bf16[4,128,768]{2,1,0:T(8,128)(2,1)}, u32[]{:S(2)}, u32[]{:S(2)}) %collective-permute-start.2) | collective-permute-done | bytes 786464 | tf_op jit(solution)/shard_map/ppermute | solution.py:522
  47.0 2.3 collective-permute-start.5
  49.3 9.2 %collective-permute-done.5 = bf16[2,16,128]{2,1,0:T(8,128)(2,1)S(1)} collective-permute-done((bf16[2,16,128]{2,1,0:T(8,128)(2,1)S(1)}, bf16[2,16,128]{2,1,0:T(8,128)(2,1)S(1)}, u32[]{:S(2)}, u32[]{:S(2)}) %collective-permute-start.5) | collective-permute-done | bytes 8224 | tf_op jit(solution)/shard_map/ppermute | solution.py:522
  58.5 4.5 collective-permute-start.6
  71.6 12.9 %qkv.1 = (bf16[1024,3072]{1,0:T(8,128)(2,1)}, bf16[1024,3072]{1,0:T(8,128)(2,1)}) custom-call(s32[3]{0:T(128)} %pad_add_fusion.where, bf16[4,128,768]{2,1,0:T(8,128)(2,1)} %copy-done.17, bf16[4,128,768]{2,1,0:T(8,128)(2,1)} %collective-permute-done.2.refs_1_, bf16[4,128,768]{2,1,0:T(8,128)(2,1)} %copy-done.38, ...), custom_call_target="tpu_custom_call" | custom-call | flops 12884901888 | tf_op jit(solution)/shard_map/qkv/pallas_call | solution.py:662
  85.6 13.7 %attn_fwd.3 = (bf16[1024,1024]{1,0:T(8,128)(2,1)}, f32[8,2,1024]{2,1,0:T(2,128)}) custom-call(bf16[1024,3072]{1,0:T(8,128)(2,1)} %get-tuple-element.130.q_ref.k_ref.v_ref.refs_0_.refs_1_.refs_2_, bf16[1024,3072]{1,0:T(8,128)(2,1)} %get-tuple-element.130.q_ref.k_ref.v_ref.refs_0_.refs_1_.refs_2_, ...), custom_call_target="tpu_custom_call" | custom-call | flops 12884901888 | tf_op jit(solution)/shard_map/attn_fwd/pallas_call | solution.py:389
  99.2 1.9 collective-permute-start.19
  102.3 1.8 collective-permute-start.18
  104.5 13.7 %attn_fwd.4 = (bf16[1024,1024]{1,0:T(8,128)(2,1)}, f32[8,2,1024]{2,1,0:T(2,128)}) custom-call(bf16[1024,3072]{1,0:T(8,128)(2,1)} %get-tuple-element.130.q_ref.k_ref.v_ref.refs_0_.refs_1_.refs_2_, bf16[1024,3072]{1,0:T(8,128)(2,1)} %get-tuple-element.130.q_ref.k_ref.v_ref.refs_0_.refs_1_.refs_2_, ...), custom_call_target="tpu_custom_call", output_to_operand_aliasing={{0}: (5, {}), {1}: (6, {})} | custom-call | flops 12884901888 | tf_op jit(solution)/shard_map/attn_fwd/pallas_call | solution.py:389
  120.0 10.0 %attn_fwd.5 = (bf16[1024,1024]{1,0:T(8,128)(2,1)}, f32[8,2,1024]{2,1,0:T(2,128)}) custom-call(bf16[1024,3072]{1,0:T(8,128)(2,1)} %get-tuple-element.130.q_ref.k_ref.v_ref.refs_0_.refs_1_.refs_2_, bf16[1024,3072]{1,0:T(8,128)(2,1)} %get-tuple-element.130.q_ref.k_ref.v_ref.refs_0_.refs_1_.refs_2_, ...), custom_call_target="tpu_custom_call", output_to_operand_aliasing={{0}: (5, {}), {1}: (6, {})} | custom-call | flops 8589934592 | tf_op jit(solution)/shard_map/attn_fwd/pallas_call | solution.py:389
  130.2 9.6 %attn_out.1 = (f32[1024,1024]{1,0:T(8,128)}, f32[1024,128]{1,0:T(8,128)}, bf16[1024,1024]{1,0:T(8,128)(2,1)}, bf16[1024,1024]{1,0:T(8,128)(2,1)}) custom-call(s32[3]{0:T(128)} %pad_add_fusion.where, bf16[4,128,1280]{2,1,0:T(8,128)(2,1)} %copy-done.8, bf16[4,128,1280]{2,1,0:T(8,128)(2,1)} %collective-permute-done.14.refs_1_, ...), custom_call_target="tpu_custom_call" | custom-call | flops 4294967296 | tf_op jit(solution)/shard_map/attn_out/pallas_call | solution.py:662
  139.9 5.2 %collective-permute-done.23.refs_1_ = bf16[4,512,256]{2,1,0:T(8,128)(2,1)} collective-permute-done((bf16[4,512,256]{2,1,0:T(8,128)(2,1)S(1)}, bf16[4,512,256]{2,1,0:T(8,128)(2,1)}, u32[]{:S(2)}, u32[]{:S(2)}) %collective-permute-start.23) | collective-permute-done | bytes 1048608 | tf_op jit(solution)/shard_map/ppermute | solution.py:522
  145.7 22.1 %feed_in.1 = (bf16[1024,4096]{1,0:T(8,128)(2,1)}, bf16[1024,4096]{1,0:T(8,128)(2,1)}, bf16[1024,4096]{1,0:T(8,128)(2,1)}) custom-call(s32[3]{0:T(128)} %pad_add_fusion.where, bf16[4,128,1280]{2,1,0:T(8,128)(2,1)} %copy-done.8, bf16[4,128,1280]{2,1,0:T(8,128)(2,1)} %collective-permute-done.14.refs_1_, bf16[4,128,1280]{2,1,0:T(8,128)(2,1)} %copy-done.36, ...), custom_call_target="tpu_custom_call" | custom-call | flops 17179869184 | tf_op jit(solution)/shard_map/feed_in/pallas_call | solution.py:662
  169.0 1.9 collective-permute-done.29.refs_7_
  170.9 21.6 %feed_out.1 = (bf16[1024,1024]{1,0:T(8,128)(2,1)}, f32[1024,1024]{1,0:T(8,128)}, bf16[1024,1024]{1,0:T(8,128)(2,1)}, f32[8,1024]{1,0:T(8,128)}, bf16[4096,1024]{1,0:T(8,128)(2,1)}) custom-call(s32[3]{0:T(128)} %pad_add_fusion.where, bf16[4,512,256]{2,1,0:T(8,128)(2,1)} %copy-done.12, bf16[4,512,256]{2,1,0:T(8,128)(2,1)} %collective-permute-done.23.refs_1_, ...), custom_call_target="tpu_custom_call" | custom-call | flops 17179869184 | tf_op jit(solution)/shard_map/feed_out/pallas_call | solution.py:662
  192.5 14.2 %wgrad_out.1 = (bf16[2,4,512,256]{3,2,1,0:T(8,128)(2,1)}, bf16[2,4,512,256]{3,2,1,0:T(8,128)(2,1)}, bf16[4,4,512,256]{3,2,1,0:T(8,128)(2,1)}) custom-call(s32[3]{0:T(128)} %pad_add_fusion.where, bf16[1024,4096]{1,0:T(8,128)(2,1)} %get-tuple-element.138.refs_8_.refs_0_, bf16[1024,1024]{1,0:T(8,128)(2,1)} %get-tuple-element.145.refs_1_.g_ref), custom_call_target="tpu_custom_call" | custom-call | flops 17179869184 | tf_op jit(solution)/shard_map/wgrad_out/pallas_call | solution.py:1184
  206.9 14.8 %feed_out_back.1 = (bf16[1024,4096]{1,0:T(8,128)(2,1)}, f32[1,4096]{1,0:T(1,128)}) custom-call(bf16[1024,1024]{1,0:T(8,128)(2,1)} %get-tuple-element.145.refs_1_.g_ref, bf16[4096,1024]{1,0:T(8,128)(2,1)} %get-tuple-element.146.w_ref, bf16[1024,4096]{1,0:T(8,128)(2,1)} %get-tuple-element.147.slope_ref), custom_call_target="tpu_custom_call" | custom-call | flops 17179869184 | tf_op jit(solution)/shard_map/feed_out_back/pallas_call | solution.py:684
  221.7 3.5 add_convert_fusion.1
  225.2 15.6 %wgrad_in.1 = (bf16[2,4,128,1024]{3,2,1,0:T(8,128)(2,1)}, bf16[2,4,128,1024]{3,2,1,0:T(8,128)(2,1)}, bf16[4,4,128,1024]{3,2,1,0:T(8,128)(2,1)}) custom-call(s32[3]{0:T(128)} %pad_add_fusion.where, bf16[1024,1024]{1,0:T(8,128)(2,1)} %get-tuple-element.151.refs_8_.refs_0_, bf16[1024,4096]{1,0:T(8,128)(2,1)} %get-tuple-element.153.refs_1_.p_ref), custom_call_target="tpu_custom_call" | custom-call | flops 17179869184 | tf_op jit(solution)/shard_map/wgrad_in/pallas_call | solution.py:1184
  242.2 21.4 %feed_in_back.1 = (f32[1024,1024]{1,0:T(8,128)}, bf16[1024,1024]{1,0:T(8,128)(2,1)}, bf16[1024,1024]{1,0:T(8,128)(2,1)}, f32[8,1024]{1,0:T(8,128)}) custom-call(bf16[1024,4096]{1,0:T(8,128)(2,1)} %get-tuple-element.153.refs_1_.p_ref, bf16[1024,4096]{1,0:T(8,128)(2,1)} %get-tuple-element.154.w_ref, f32[1024,1024]{1,0:T(8,128)} %get-tuple-element.155.g_ref, ...), custom_call_target="tpu_custom_call" | custom-call | flops 21474836480 | tf_op jit(solution)/shard_map/feed_in_back/pallas_call | solution.py:684
  263.6 3.9 collective-permute-done.31
  267.5 4.1 add_convert_fusion
  272.7 2.9 fusion.3
  276.9 28.7 %attn_bwd.3 = (bf16[3,1024,512]{2,1,0:T(8,128)(2,1)}, f32[2,512]{1,0:T(2,128)}) custom-call(bf16[1024,3072]{1,0:T(8,128)(2,1)} %get-tuple-element.130.q_ref.k_ref.v_ref.refs_0_.refs_1_.refs_2_, bf16[1024,3072]{1,0:T(8,128)(2,1)} %get-tuple-element.130.q_ref.k_ref.v_ref.refs_0_.refs_1_.refs_2_, ...), custom_call_target="tpu_custom_call" | custom-call | flops 42949672960 | tf_op jit(solution)/shard_map/attn_bwd/pallas_call | solution.py:480
  305.6 3.6 collective-permute-done.34
  309.2 2.5 fusion.1
  311.7 3.2 fusion.4
  314.9 2.0 collective-permute-start.36
  317.0 16.4 %wgrad_a.1 = (bf16[2,4,128,640]{3,2,1,0:T(8,128)(2,1)}, bf16[2,4,128,640]{3,2,1,0:T(8,128)(2,1)}, bf16[4,4,128,640]{3,2,1,0:T(8,128)(2,1)}) custom-call(s32[3]{0:T(128)} %pad_add_fusion.where, bf16[1024,1024]{1,0:T(8,128)(2,1)} %get-tuple-element.171.refs_8_.refs_3_.refs_0_, bf16[1024,1024]{1,0:T(8,128)(2,1)} %bitcast.184, ...), custom_call_target="tpu_custom_call" | custom-call | flops 10737418240 | tf_op jit(solution)/shard_map/wgrad_a/pallas_call | solution.py:1184
  333.5 2.8 fusion
  336.3 2.1 collective-permute-start.38
  339.2 1.6 collective-permute-start.37
  340.8 15.7 %attn_bwd.4 = (bf16[3,1024,512]{2,1,0:T(8,128)(2,1)}, f32[2,512]{1,0:T(2,128)}) custom-call(bf16[1024,3072]{1,0:T(8,128)(2,1)} %get-tuple-element.130.q_ref.k_ref.v_ref.refs_0_.refs_1_.refs_2_, bf16[1024,3072]{1,0:T(8,128)(2,1)} %get-tuple-element.130.q_ref.k_ref.v_ref.refs_0_.refs_1_.refs_2_, ...), custom_call_target="tpu_custom_call" | custom-call | flops 21474836480 | tf_op jit(solution)/shard_map/attn_bwd/pallas_call | solution.py:480
  356.8 3.3 add_convert_fusion.2
  361.6 2.4 collective-permute-start.40
  364.1 15.8 %attn_bwd.5 = (bf16[3,1024,512]{2,1,0:T(8,128)(2,1)}, f32[2,512]{1,0:T(2,128)}) custom-call(bf16[1024,3072]{1,0:T(8,128)(2,1)} %get-tuple-element.130.q_ref.k_ref.v_ref.refs_0_.refs_1_.refs_2_, bf16[1024,3072]{1,0:T(8,128)(2,1)} %get-tuple-element.130.q_ref.k_ref.v_ref.refs_0_.refs_1_.refs_2_, ...), custom_call_target="tpu_custom_call", output_to_operand_aliasing={{0}: (8, {}), {1}: (9, {})} | custom-call | flops 21474836480 | tf_op jit(solution)/shard_map/attn_bwd/pallas_call | solution.py:480
  379.9 1.6 pack_sums.1.refs_2_
  382.6 1.5 fusion.6
  385.9 12.4 %wgrad_b.1 = (bf16[2,4,144,384]{3,2,1,0:T(8,128)(2,1)}, bf16[2,4,144,384]{3,2,1,0:T(8,128)(2,1)}, bf16[4,4,144,384]{3,2,1,0:T(8,128)(2,1)}) custom-call(s32[3]{0:T(128)} %pad_add_fusion.where, bf16[1024,1024]{1,0:T(8,128)(2,1)} %bitcast.185, bf16[3,1024,512]{2,1,0:T(8,128)(2,1)} %get-tuple-element.195.refs_1_, f32[32,1024]{1,0:T(8,128)} %pack_sums.1.refs_2_), custom_call_target="tpu_custom_call" | custom-call | flops 6442450944 | tf_op jit(solution)/shard_map/wgrad_b/pallas_call | solution.py:1184
  399.2 2.0 collective-permute-start.57
  401.3 1.6 fusion.2
  404.6 8.5 %qkv_back.2.refs_3_ = f32[1024,1024]{1,0:T(8,128)} custom-call(bf16[1024,3072]{1,0:T(8,128)(2,1)} %get-tuple-element.142.w_ref, bf16[3,1024,512]{2,1,0:T(8,128)(2,1)} %get-tuple-element.166.refs_3_.refs_0_, bf16[3,1024,512]{2,1,0:T(8,128)(2,1)} %get-tuple-element.195.refs_1_, f32[1024,1024]{1,0:T(8,128)} %get-tuple-element.199.refs_2_), custom_call_target="tpu_custom_call" | custom-call | flops 6442450944 | tf_op jit(solution)/shard_map/qkv_back/pallas_call | solution.py:1041
  417.0 1.5 select_convert_fusion
  424.5 2.3 add_convert_fusion.5
  430.2 8.3 %qkv_back.3 = f32[1024,1024]{1,0:T(8,128)} custom-call(bf16[1024,3072]{1,0:T(8,128)(2,1)} %get-tuple-element.142.w_ref, bf16[3,1024,512]{2,1,0:T(8,128)(2,1)} %get-tuple-element.166.refs_3_.refs_0_, bf16[3,1024,512]{2,1,0:T(8,128)(2,1)} %get-tuple-element.195.refs_1_, f32[1024,1024]{1,0:T(8,128)} %get-tuple-element.199.refs_2_, ...), custom_call_target="tpu_custom_call", output_to_operand_aliasing={{}: (4, {})} | custom-call | flops 6442450944 | tf_op jit(solution)/shard_map/qkv_back/pallas_call | solution.py:1041
  438.5 1.7 collective-permute-done.45
  441.1 2.1 collective-permute-start.47
  444.6 1.5 collective-permute-start.50
  446.0 3.1 collective-permute-done.47
  452.0 5.0 %collective-permute-done.48 = bf16[128,640]{1,0:T(8,128)(2,1)S(1)} collective-permute-done((bf16[128,640]{1,0:T(8,128)(2,1)S(1)}, bf16[128,640]{1,0:T(8,128)(2,1)S(1)}, u32[]{:S(2)}, u32[]{:S(2)}) %collective-permute-start.48) | collective-permute-done | bytes 163872 | tf_op jit(solution)/shard_map/ppermute | solution.py:522
  457.0 2.0 collective-permute-start.49
  460.5 1.7 collective-permute-start.51
  462.2 2.7 collective-permute-start.53
  464.9 1.6 pad_maximum_fusion
  467.2 2.3 collective-permute-done.52
  470.5 1.7 collective-permute-start.55
  (258 shorter events, 62.1 us)
Async XLA Ops:
  0.7 8.7 %collective-permute-start = (bf16[128,768]{1,0:T(8,128)(2,1)}, bf16[128,768]{1,0:T(8,128)(2,1)S(1)}, u32[]{:S(2)}, u32[]{:S(2)}) collective-permute-start(bf16[128,768]{1,0:T(8,128)(2,1)} %param.21), channel_id=1, source_target_pairs={{0,2},{1,5},{2,0},{3,7},{4,6},{5,1},{6,4},{7,3},{8,10},{9,13},{10,... | collective-permute-start | bytes 589832 | tf_op jit(solution)/shard_map/ppermute | solution.py:522
  9.4 36.3 %copy-start.31 = (bf16[128]{0:T(256)(128)(2,1)S(1)}, bf16[128]{0:T(256)(128)(2,1)}, u32[]{:S(2)}) copy-start(bf16[128]{0:T(256)(128)(2,1)} %param.26) | copy-start | bytes 772
  9.4 36.3 %copy-start.32 = (bf16[128]{0:T(256)(128)(2,1)S(1)}, bf16[128]{0:T(256)(128)(2,1)}, u32[]{:S(2)}) copy-start(bf16[128]{0:T(256)(128)(2,1)} %param.27) | copy-start | bytes 772
  9.4 36.3 %copy-start.33 = (bf16[128]{0:T(256)(128)(2,1)S(1)}, bf16[128]{0:T(256)(128)(2,1)}, u32[]{:S(2)}) copy-start(bf16[128]{0:T(256)(128)(2,1)} %param.31) | copy-start | bytes 772
  9.4 36.3 %copy-start.34 = (bf16[128]{0:T(256)(128)(2,1)S(1)}, bf16[128]{0:T(256)(128)(2,1)}, u32[]{:S(2)}) copy-start(bf16[128]{0:T(256)(128)(2,1)} %param.32) | copy-start | bytes 772
  9.4 57.9 %copy-start.24 = (s32[1,1024]{1,0:T(1,128)S(1)}, s32[1,1024]{1,0:T(1,128)}, u32[]{:S(2)}) copy-start(s32[1,1024]{1,0:T(1,128)} %refs_6_.5) | copy-start | bytes 12292
  10.5 11.3 %collective-permute-start.1 = (bf16[2,128,768]{2,1,0:T(8,128)(2,1)S(1)}, bf16[2,128,768]{2,1,0:T(8,128)(2,1)S(1)}, u32[]{:S(2)}, u32[]{:S(2)}) collective-permute-start(bf16[2,128,768]{2,1,0:T(8,128)(2,1)S(1)} %pad_maximum_fusion.10), channel_id=1, source_target_pairs={{0,4},{1,3},{2,6},{3,1},{4,0},{5,7},{6,2},{7,5},{8,12},{9,11},{10,... | collective-permute-start | bytes 1179656 | tf_op jit(solution)/shard_map/ppermute | solution.py:522
  22.8 45.7 %copy-start.17 = (bf16[4,128,768]{2,1,0:T(8,128)(2,1)}, bf16[4,128,768]{2,1,0:T(8,128)(2,1)S(1)}, u32[]{:S(2)}) copy-start(bf16[4,128,768]{2,1,0:T(8,128)(2,1)S(1)} %pad_maximum_fusion.4.refs_0_) | copy-start | bytes 2359300
  22.8 20.5 %collective-permute-start.2 = (bf16[4,128,768]{2,1,0:T(8,128)(2,1)S(1)}, bf16[4,128,768]{2,1,0:T(8,128)(2,1)}, u32[]{:S(2)}, u32[]{:S(2)}) collective-permute-start(bf16[4,128,768]{2,1,0:T(8,128)(2,1)S(1)} %pad_maximum_fusion.4.refs_0_), channel_id=1, source_target_pairs={{0,8},{1,17},{2,10},{3,19},{4,12},{5,21},{6,14},{7,23},{8,0},{9,25... | collective-permute-start | bytes 2359304 | tf_op jit(solution)/shard_map/ppermute | solution.py:522
  25.1 18.2 %collective-permute-start.3 = (bf16[4,128,768]{2,1,0:T(8,128)(2,1)S(1)}, bf16[4,128,768]{2,1,0:T(8,128)(2,1)S(1)}, u32[]{:S(2)}, u32[]{:S(2)}) collective-permute-start(bf16[4,128,768]{2,1,0:T(8,128)(2,1)S(1)} %pad_maximum_fusion.4.refs_0_), channel_id=1, source_target_pairs={{0,16},{1,9},{2,18},{3,11},{4,20},{5,13},{6,22},{7,15},{8,24},{9,1... | collective-permute-start | bytes 2359304 | tf_op jit(solution)/shard_map/ppermute | solution.py:522
  26.7 10.6 %collective-permute-start.7 = (bf16[128,1280]{1,0:T(8,128)(2,1)S(1)}, bf16[128,1280]{1,0:T(8,128)(2,1)S(1)}, u32[]{:S(2)}, u32[]{:S(2)}) collective-permute-start(bf16[128,1280]{1,0:T(8,128)(2,1)S(1)} %pad_maximum_fusion.11), channel_id=1, source_target_pairs={{0,2},{1,5},{2,0},{3,7},{4,6},{5,1},{6,4},{7,3},{8,10},{9,13},{10,... | collective-permute-start | bytes 983048 | tf_op jit(solution)/shard_map/ppermute | solution.py:522
  43.3 23.9 %collective-permute-start.8 = (bf16[4,128,768]{2,1,0:T(8,128)(2,1)}, bf16[4,128,768]{2,1,0:T(8,128)(2,1)}, u32[]{:S(2)}, u32[]{:S(2)}) collective-permute-start(bf16[4,128,768]{2,1,0:T(8,128)(2,1)} %collective-permute-done.2.refs_1_), channel_id=1, source_target_pairs={{0,16},{1,9},{2,18},{3,11},{4,20},{5,13},{6,22},{7,15},{8,24},{9,1... | collective-permute-start | bytes 2359304 | tf_op jit(solution)/shard_map/ppermute | solution.py:522
  44.3 23.0 %collective-permute-start.9 = (bf16[2,128,1280]{2,1,0:T(8,128)(2,1)S(1)}, bf16[2,128,1280]{2,1,0:T(8,128)(2,1)S(1)}, u32[]{:S(2)}, u32[]{:S(2)}) collective-permute-start(bf16[2,128,1280]{2,1,0:T(8,128)(2,1)S(1)} %pad_maximum_fusion.5), channel_id=1, source_target_pairs={{0,4},{1,3},{2,6},{3,1},{4,0},{5,7},{6,2},{7,5},{8,12},{9,11},{10,... | collective-permute-start | bytes 1966088 | tf_op jit(solution)/shard_map/ppermute | solution.py:522
  45.8 1.2 collective-permute-start.4
  47.0 11.5 %collective-permute-start.5 = (bf16[2,16,128]{2,1,0:T(8,128)(2,1)S(1)}, bf16[2,16,128]{2,1,0:T(8,128)(2,1)S(1)}, u32[]{:S(2)}, u32[]{:S(2)}) collective-permute-start(bf16[2,16,128]{2,1,0:T(8,128)(2,1)S(1)} %get-tuple-element.237), channel_id=1, source_target_pairs={{0,2},{1,5},{2,0},{3,7},{4,6},{5,1},{6,4},{7,3},{8,10},{9,13},{10,... | collective-permute-start | bytes 24584 | tf_op jit(solution)/shard_map/ppermute | solution.py:522
  58.5 6.2 %collective-permute-start.6 = (bf16[2,2,16,128]{3,2,1,0:T(8,128)(2,1)S(1)}, bf16[2,2,16,128]{3,2,1,0:T(8,128)(2,1)S(1)}, u32[]{:S(2)}, u32[]{:S(2)}) collective-permute-start(bf16[2,2,16,128]{3,2,1,0:T(8,128)(2,1)S(1)} %pad_maximum_fusion.15), channel_id=1, source_target_pairs={{0,4},{1,3},{2,6},{3,1},{4,0},{5,7},{6,2},{7,5},{8,12},{9,11},{10,... | collective-permute-start | bytes 49160 | tf_op jit(solution)/shard_map/ppermute | solution.py:522
  63.6 5.6 %collective-permute-start.10 = (bf16[4,128,768]{2,1,0:T(8,128)(2,1)S(1)}, bf16[4,128,768]{2,1,0:T(8,128)(2,1)}, u32[]{:S(2)}, u32[]{:S(2)}) collective-permute-start(bf16[4,128,768]{2,1,0:T(8,128)(2,1)S(1)} %pad_maximum_fusion.4.refs_0_), channel_id=1, source_target_pairs={{0,1},{1,0},{2,3},{3,2},{4,5},{5,4},{6,7},{7,6},{8,9},{9,8},{10,11... | collective-permute-start | bytes 2359304 | tf_op jit(solution)/shard_map/ppermute | solution.py:522
  66.8 2.7 collective-permute-start.11
  66.8 3.7 collective-permute-start.12
  67.3 4.4 collective-permute-start.13
  68.5 32.6 %collective-permute-start.14 = (bf16[4,128,1280]{2,1,0:T(8,128)(2,1)S(1)}, bf16[4,128,1280]{2,1,0:T(8,128)(2,1)}, u32[]{:S(2)}, u32[]{:S(2)}) collective-permute-start(bf16[4,128,1280]{2,1,0:T(8,128)(2,1)S(1)} %pad_maximum_fusion.1.refs_0_), channel_id=1, source_target_pairs={{0,8},{1,17},{2,10},{3,19},{4,12},{5,21},{6,14},{7,23},{8,0},{9,25... | collective-permute-start | bytes 3932168 | tf_op jit(solution)/shard_map/ppermute | solution.py:522
  69.2 32.0 %collective-permute-start.15 = (bf16[4,128,1280]{2,1,0:T(8,128)(2,1)S(1)}, bf16[4,128,1280]{2,1,0:T(8,128)(2,1)S(1)}, u32[]{:S(2)}, u32[]{:S(2)}) collective-permute-start(bf16[4,128,1280]{2,1,0:T(8,128)(2,1)S(1)} %pad_maximum_fusion.1.refs_0_), channel_id=1, source_target_pairs={{0,16},{1,9},{2,18},{3,11},{4,20},{5,13},{6,22},{7,15},{8,24},{9,1... | collective-permute-start | bytes 3932168 | tf_op jit(solution)/shard_map/ppermute | solution.py:522
  84.5 16.6 %collective-permute-start.16 = (bf16[512,256]{1,0:T(8,128)(2,1)S(1)}, bf16[512,256]{1,0:T(8,128)(2,1)S(1)}, u32[]{:S(2)}, u32[]{:S(2)}) collective-permute-start(bf16[512,256]{1,0:T(8,128)(2,1)S(1)} %copy-done.13), channel_id=1, source_target_pairs={{0,2},{1,5},{2,0},{3,7},{4,6},{5,1},{6,4},{7,3},{8,10},{9,13},{10,... | collective-permute-start | bytes 786440 | tf_op jit(solution)/shard_map/ppermute | solution.py:522
  99.2 20.6 %collective-permute-start.19 = (bf16[4,128,1280]{2,1,0:T(8,128)(2,1)S(1)}, bf16[4,128,1280]{2,1,0:T(8,128)(2,1)}, u32[]{:S(2)}, u32[]{:S(2)}) collective-permute-start(bf16[4,128,1280]{2,1,0:T(8,128)(2,1)S(1)} %pad_maximum_fusion.1.refs_0_), channel_id=1, source_target_pairs={{0,1},{1,0},{2,3},{3,2},{4,5},{5,4},{6,7},{7,6},{8,9},{9,8},{10,11... | collective-permute-start | bytes 3932168 | tf_op jit(solution)/shard_map/ppermute | solution.py:522
  101.2 18.0 %collective-permute-start.17 = (bf16[4,128,1280]{2,1,0:T(8,128)(2,1)}, bf16[4,128,1280]{2,1,0:T(8,128)(2,1)}, u32[]{:S(2)}, u32[]{:S(2)}) collective-permute-start(bf16[4,128,1280]{2,1,0:T(8,128)(2,1)} %collective-permute-done.14.refs_1_), channel_id=1, source_target_pairs={{0,16},{1,9},{2,18},{3,11},{4,20},{5,13},{6,22},{7,15},{8,24},{9,1... | collective-permute-start | bytes 3932168 | tf_op jit(solution)/shard_map/ppermute | solution.py:522
  102.3 15.9 %collective-permute-start.18 = (bf16[2,512,256]{2,1,0:T(8,128)(2,1)S(1)}, bf16[2,512,256]{2,1,0:T(8,128)(2,1)S(1)}, u32[]{:S(2)}, u32[]{:S(2)}) collective-permute-start(bf16[2,512,256]{2,1,0:T(8,128)(2,1)S(1)} %pad_maximum_fusion.6), channel_id=1, source_target_pairs={{0,4},{1,3},{2,6},{3,1},{4,0},{5,7},{6,2},{7,5},{8,12},{9,11},{10,... | collective-permute-start | bytes 1572872 | tf_op jit(solution)/shard_map/ppermute | solution.py:522
  104.0 26.0 %collective-permute-start.20 = (bf16[4,128,1280]{2,1,0:T(8,128)(2,1)}, bf16[4,128,1280]{2,1,0:T(8,128)(2,1)}, u32[]{:S(2)}, u32[]{:S(2)}) collective-permute-start(bf16[4,128,1280]{2,1,0:T(8,128)(2,1)} %collective-permute-done.14.refs_1_), channel_id=1, source_target_pairs={{0,1},{1,0},{2,3},{3,2},{4,5},{5,4},{6,7},{7,6},{8,9},{9,8},{10,11... | collective-permute-start | bytes 3932168 | tf_op jit(solution)/shard_map/ppermute | solution.py:522
  104.0 26.2 %collective-permute-start.21 = (bf16[4,128,1280]{2,1,0:T(8,128)(2,1)}, bf16[4,128,1280]{2,1,0:T(8,128)(2,1)}, u32[]{:S(2)}, u32[]{:S(2)}) collective-permute-start(bf16[4,128,1280]{2,1,0:T(8,128)(2,1)} %copy-done.36), channel_id=1, source_target_pairs={{0,1},{1,0},{2,3},{3,2},{4,5},{5,4},{6,7},{7,6},{8,9},{9,8},{10,11... | collective-permute-start | bytes 3932168 | tf_op jit(solution)/shard_map/ppermute | solution.py:522
  119.1 11.1 %collective-permute-start.22 = (bf16[4,128,1280]{2,1,0:T(8,128)(2,1)}, bf16[4,128,1280]{2,1,0:T(8,128)(2,1)}, u32[]{:S(2)}, u32[]{:S(2)}) collective-permute-start(bf16[4,128,1280]{2,1,0:T(8,128)(2,1)} %collective-permute-done.17.refs_3_), channel_id=1, source_target_pairs={{0,1},{1,0},{2,3},{3,2},{4,5},{5,4},{6,7},{7,6},{8,9},{9,8},{10,11... | collective-permute-start | bytes 3932168 | tf_op jit(solution)/shard_map/ppermute | solution.py:522
  119.3 25.8 %collective-permute-start.23 = (bf16[4,512,256]{2,1,0:T(8,128)(2,1)S(1)}, bf16[4,512,256]{2,1,0:T(8,128)(2,1)}, u32[]{:S(2)}, u32[]{:S(2)}) collective-permute-start(bf16[4,512,256]{2,1,0:T(8,128)(2,1)S(1)} %pad_maximum_fusion.2.refs_0_), channel_id=1, source_target_pairs={{0,8},{1,17},{2,10},{3,19},{4,12},{5,21},{6,14},{7,23},{8,0},{9,25... | collective-permute-start | bytes 3145736 | tf_op jit(solution)/shard_map/ppermute | solution.py:522
  119.8 25.3 %collective-permute-start.24 = (bf16[4,512,256]{2,1,0:T(8,128)(2,1)S(1)}, bf16[4,512,256]{2,1,0:T(8,128)(2,1)S(1)}, u32[]{:S(2)}, u32[]{:S(2)}) collective-permute-start(bf16[4,512,256]{2,1,0:T(8,128)(2,1)S(1)} %pad_maximum_fusion.2.refs_0_), channel_id=1, source_target_pairs={{0,16},{1,9},{2,18},{3,11},{4,20},{5,13},{6,22},{7,15},{8,24},{9,1... | collective-permute-start | bytes 3145736 | tf_op jit(solution)/shard_map/ppermute | solution.py:522
  130.0 39.0 %collective-permute-start.26 = (bf16[4,512,256]{2,1,0:T(8,128)(2,1)S(1)}, bf16[4,512,256]{2,1,0:T(8,128)(2,1)}, u32[]{:S(2)}, u32[]{:S(2)}) collective-permute-start(bf16[4,512,256]{2,1,0:T(8,128)(2,1)S(1)} %pad_maximum_fusion.2.refs_0_), channel_id=1, source_target_pairs={{0,1},{1,0},{2,3},{3,2},{4,5},{5,4},{6,7},{7,6},{8,9},{9,8},{10,11... | collective-permute-start | bytes 3145736 | tf_op jit(solution)/shard_map/ppermute | solution.py:522
  145.1 22.7 %collective-permute-start.25 = (bf16[4,512,256]{2,1,0:T(8,128)(2,1)}, bf16[4,512,256]{2,1,0:T(8,128)(2,1)}, u32[]{:S(2)}, u32[]{:S(2)}) collective-permute-start(bf16[4,512,256]{2,1,0:T(8,128)(2,1)} %collective-permute-done.23.refs_1_), channel_id=1, source_target_pairs={{0,16},{1,9},{2,18},{3,11},{4,20},{5,13},{6,22},{7,15},{8,24},{9,1... | collective-permute-start | bytes 3145736 | tf_op jit(solution)/shard_map/ppermute | solution.py:522
  145.2 23.8 %collective-permute-start.27 = (bf16[4,512,256]{2,1,0:T(8,128)(2,1)}, bf16[4,512,256]{2,1,0:T(8,128)(2,1)}, u32[]{:S(2)}, u32[]{:S(2)}) collective-permute-start(bf16[4,512,256]{2,1,0:T(8,128)(2,1)} %collective-permute-done.23.refs_1_), channel_id=1, source_target_pairs={{0,1},{1,0},{2,3},{3,2},{4,5},{5,4},{6,7},{7,6},{8,9},{9,8},{10,11... | collective-permute-start | bytes 3145736 | tf_op jit(solution)/shard_map/ppermute | solution.py:522
  145.2 23.8 %collective-permute-start.28 = (bf16[4,512,256]{2,1,0:T(8,128)(2,1)S(1)}, bf16[4,512,256]{2,1,0:T(8,128)(2,1)}, u32[]{:S(2)}, u32[]{:S(2)}) collective-permute-start(bf16[4,512,256]{2,1,0:T(8,128)(2,1)S(1)} %collective-permute-done.24.refs_2_), channel_id=1, source_target_pairs={{0,1},{1,0},{2,3},{3,2},{4,5},{5,4},{6,7},{7,6},{8,9},{9,8},{10,11... | collective-permute-start | bytes 3145736 | tf_op jit(solution)/shard_map/ppermute | solution.py:522
  167.8 3.1 collective-permute-start.29
  206.8 14.9 %collective-permute-start.30 = (bf16[4,4,512,256]{3,2,1,0:T(8,128)(2,1)}, bf16[4,4,512,256]{3,2,1,0:T(8,128)(2,1)}, u32[]{:S(2)}, u32[]{:S(2)}) collective-permute-start(bf16[4,4,512,256]{3,2,1,0:T(8,128)(2,1)} %get-tuple-element.149), channel_id=1, source_target_pairs={{0,1},{1,0},{2,3},{3,2},{4,5},{5,4},{6,7},{7,6},{8,9},{9,8},{10,11... | collective-permute-start | bytes 12582920 | tf_op jit(solution)/shard_map/ppermute | solution.py:522
  240.7 26.8 %collective-permute-start.32 = (bf16[4,4,128,1024]{3,2,1,0:T(8,128)(2,1)}, bf16[4,4,128,1024]{3,2,1,0:T(8,128)(2,1)}, u32[]{:S(2)}, u32[]{:S(2)}) collective-permute-start(bf16[4,4,128,1024]{3,2,1,0:T(8,128)(2,1)} %get-tuple-element.161), channel_id=1, source_target_pairs={{0,1},{1,0},{2,3},{3,2},{4,5},{5,4},{6,7},{7,6},{8,9},{9,8},{10,11... | collective-permute-start | bytes 12582920 | tf_op jit(solution)/shard_map/ppermute | solution.py:522
  241.1 26.4 %collective-permute-start.31 = (bf16[2,4,512,256]{3,2,1,0:T(8,128)(2,1)}, bf16[2,4,512,256]{3,2,1,0:T(8,128)(2,1)}, u32[]{:S(2)}, u32[]{:S(2)}) collective-permute-start(bf16[2,4,512,256]{3,2,1,0:T(8,128)(2,1)} %add_convert_fusion.1), channel_id=1, source_target_pairs={{0,8},{1,17},{2,10},{3,19},{4,12},{5,21},{6,14},{7,23},{8,0},{9,25... | collective-permute-start | bytes 6291464 | tf_op jit(solution)/shard_map/ppermute | solution.py:522
  271.6 37.6 %collective-permute-start.34 = (bf16[2,4,128,1024]{3,2,1,0:T(8,128)(2,1)}, bf16[2,4,128,1024]{3,2,1,0:T(8,128)(2,1)}, u32[]{:S(2)}, u32[]{:S(2)}) collective-permute-start(bf16[2,4,128,1024]{3,2,1,0:T(8,128)(2,1)} %add_convert_fusion), channel_id=1, source_target_pairs={{0,8},{1,17},{2,10},{3,19},{4,12},{5,21},{6,14},{7,23},{8,0},{9,25... | collective-permute-start | bytes 6291464 | tf_op jit(solution)/shard_map/ppermute | solution.py:522
  275.6 30.0 %collective-permute-start.33 = (bf16[4,512,256]{2,1,0:T(8,128)(2,1)}, bf16[4,512,256]{2,1,0:T(8,128)(2,1)S(1)}, u32[]{:S(2)}, u32[]{:S(2)}) collective-permute-start(bf16[4,512,256]{2,1,0:T(8,128)(2,1)} %fusion.3), channel_id=1, source_target_pairs={{0,16},{1,9},{2,18},{3,11},{4,20},{5,13},{6,22},{7,15},{8,24},{9,1... | collective-permute-start | bytes 3145736 | tf_op jit(solution)/shard_map/ppermute | solution.py:522
  314.9 18.6 %collective-permute-start.36 = (bf16[4,128,1024]{2,1,0:T(8,128)(2,1)}, bf16[4,128,1024]{2,1,0:T(8,128)(2,1)S(1)}, u32[]{:S(2)}, u32[]{:S(2)}) collective-permute-start(bf16[4,128,1024]{2,1,0:T(8,128)(2,1)} %fusion.4), channel_id=1, source_target_pairs={{0,16},{1,9},{2,18},{3,11},{4,20},{5,13},{6,22},{7,15},{8,24},{9,1... | collective-permute-start | bytes 3145736 | tf_op jit(solution)/shard_map/ppermute | solution.py:522
  317.0 16.5 %collective-permute-start.35 = (bf16[2,512,256]{2,1,0:T(8,128)(2,1)S(1)}, bf16[2,512,256]{2,1,0:T(8,128)(2,1)S(1)}, u32[]{:S(2)}, u32[]{:S(2)}) collective-permute-start(bf16[2,512,256]{2,1,0:T(8,128)(2,1)S(1)} %pad_maximum_fusion.7), channel_id=1, source_target_pairs={{0,2},{1,5},{2,0},{3,7},{4,6},{5,1},{6,4},{7,3},{8,10},{9,13},{10,... | collective-permute-start | bytes 1572872 | tf_op jit(solution)/shard_map/ppermute | solution.py:522
  333.4 23.4 %collective-permute-start.39 = (bf16[4,4,128,640]{3,2,1,0:T(8,128)(2,1)}, bf16[4,4,128,640]{3,2,1,0:T(8,128)(2,1)}, u32[]{:S(2)}, u32[]{:S(2)}) collective-permute-start(bf16[4,4,128,640]{3,2,1,0:T(8,128)(2,1)} %get-tuple-element.177), channel_id=1, source_target_pairs={{0,1},{1,0},{2,3},{3,2},{4,5},{5,4},{6,7},{7,6},{8,9},{9,8},{10,11... | collective-permute-start | bytes 7864328 | tf_op jit(solution)/shard_map/ppermute | solution.py:522
  336.3 20.5 %collective-permute-start.38 = (bf16[2,128,1024]{2,1,0:T(8,128)(2,1)S(1)}, bf16[2,128,1024]{2,1,0:T(8,128)(2,1)S(1)}, u32[]{:S(2)}, u32[]{:S(2)}) collective-permute-start(bf16[2,128,1024]{2,1,0:T(8,128)(2,1)S(1)} %pad_maximum_fusion.8), channel_id=1, source_target_pairs={{0,2},{1,5},{2,0},{3,7},{4,6},{5,1},{6,4},{7,3},{8,10},{9,13},{10,... | collective-permute-start | bytes 1572872 | tf_op jit(solution)/shard_map/ppermute | solution.py:522
  339.2 17.3 %collective-permute-start.37 = (bf16[512,256]{1,0:T(8,128)(2,1)}, bf16[512,256]{1,0:T(8,128)(2,1)S(1)}, u32[]{:S(2)}, u32[]{:S(2)}) collective-permute-start(bf16[512,256]{1,0:T(8,128)(2,1)} %fusion.11), channel_id=1, source_target_pairs={{0,4},{1,3},{2,6},{3,1},{4,0},{5,7},{6,2},{7,5},{8,12},{9,11},{10,... | collective-permute-start | bytes 786440 | tf_op jit(solution)/shard_map/ppermute | solution.py:522
  360.9 20.6 %collective-permute-start.41 = (bf16[2,4,128,640]{3,2,1,0:T(8,128)(2,1)}, bf16[2,4,128,640]{3,2,1,0:T(8,128)(2,1)}, u32[]{:S(2)}, u32[]{:S(2)}) collective-permute-start(bf16[2,4,128,640]{3,2,1,0:T(8,128)(2,1)} %add_convert_fusion.2), channel_id=1, source_target_pairs={{0,8},{1,17},{2,10},{3,19},{4,12},{5,21},{6,14},{7,23},{8,0},{9,25... | collective-permute-start | bytes 3932168 | tf_op jit(solution)/shard_map/ppermute | solution.py:522
  361.6 19.8 %collective-permute-start.40 = (bf16[128,1024]{1,0:T(8,128)(2,1)}, bf16[128,1024]{1,0:T(8,128)(2,1)}, u32[]{:S(2)}, u32[]{:S(2)}) collective-permute-start(bf16[128,1024]{1,0:T(8,128)(2,1)} %fusion.12), channel_id=1, source_target_pairs={{0,4},{1,3},{2,6},{3,1},{4,0},{5,7},{6,2},{7,5},{8,12},{9,11},{10,... | collective-permute-start | bytes 786440 | tf_op jit(solution)/shard_map/ppermute | solution.py:522
  384.2 14.1 %collective-permute-start.42 = (bf16[4,128,640]{2,1,0:T(8,128)(2,1)S(1)}, bf16[4,128,640]{2,1,0:T(8,128)(2,1)S(1)}, u32[]{:S(2)}, u32[]{:S(2)}) collective-permute-start(bf16[4,128,640]{2,1,0:T(8,128)(2,1)S(1)} %fusion.6), channel_id=1, source_target_pairs={{0,16},{1,9},{2,18},{3,11},{4,20},{5,13},{6,22},{7,15},{8,24},{9,1... | collective-permute-start | bytes 1966088 | tf_op jit(solution)/shard_map/ppermute | solution.py:522
  384.9 13.3 %collective-permute-start.43 = (bf16[1024,256]{1,0:T(8,128)(2,1)S(1)}, bf16[1024,256]{1,0:T(8,128)(2,1)S(1)}, u32[]{:S(2)}, u32[]{:S(2)}) collective-permute-start(bf16[1024,256]{1,0:T(8,128)(2,1)S(1)} %constant_dynamic-update-slice_fusion), channel_id=1, source_target_pairs={{0,8},{1,17},{2,10},{3,19},{4,12},{5,21},{6,14},{7,23},{8,0},{9,25... | collective-permute-start | bytes 1572872 | tf_op jit(solution)/shard_map/ppermute | solution.py:522
  398.3 26.3 %collective-permute-start.44 = (bf16[4,4,144,384]{3,2,1,0:T(8,128)(2,1)}, bf16[4,4,144,384]{3,2,1,0:T(8,128)(2,1)}, u32[]{:S(2)}, u32[]{:S(2)}) collective-permute-start(bf16[4,4,144,384]{3,2,1,0:T(8,128)(2,1)} %get-tuple-element.197), channel_id=1, source_target_pairs={{0,1},{1,0},{2,3},{3,2},{4,5},{5,4},{6,7},{7,6},{8,9},{9,8},{10,11... | collective-permute-start | bytes 5308424 | tf_op jit(solution)/shard_map/ppermute | solution.py:522
  399.2 14.9 %collective-permute-start.57 = (bf16[2,1024,256]{2,1,0:T(8,128)(2,1)S(1)}, bf16[2,1024,256]{2,1,0:T(8,128)(2,1)S(1)}, u32[]{:S(2)}, u32[]{:S(2)}) collective-permute-start(bf16[2,1024,256]{2,1,0:T(8,128)(2,1)S(1)} %pad_maximum_fusion.3), channel_id=1, source_target_pairs={{0,16},{1,9},{2,18},{3,11},{4,20},{5,13},{6,22},{7,15},{8,24},{9,1... | collective-permute-start | bytes 3145736 | tf_op jit(solution)/shard_map/ppermute | solution.py:522
  403.7 34.8 %collective-permute-start.46 = (bf16[2,128,640]{2,1,0:T(8,128)(2,1)}, bf16[2,128,640]{2,1,0:T(8,128)(2,1)}, u32[]{:S(2)}, u32[]{:S(2)}) collective-permute-start(bf16[2,128,640]{2,1,0:T(8,128)(2,1)} %pad_maximum_fusion.12), channel_id=1, source_target_pairs={{0,2},{1,5},{2,0},{3,7},{4,6},{5,1},{6,4},{7,3},{8,10},{9,13},{10,... | collective-permute-start | bytes 983048 | tf_op jit(solution)/shard_map/ppermute | solution.py:522
  426.8 13.4 %collective-permute-start.45 = (bf16[2,4,144,384]{3,2,1,0:T(8,128)(2,1)}, bf16[2,4,144,384]{3,2,1,0:T(8,128)(2,1)}, u32[]{:S(2)}, u32[]{:S(2)}) collective-permute-start(bf16[2,4,144,384]{3,2,1,0:T(8,128)(2,1)} %add_convert_fusion.5), channel_id=1, source_target_pairs={{0,8},{1,17},{2,10},{3,19},{4,12},{5,21},{6,14},{7,23},{8,0},{9,25... | collective-permute-start | bytes 2654216 | tf_op jit(solution)/shard_map/ppermute | solution.py:522
  441.1 8.0 %collective-permute-start.47 = (bf16[128,640]{1,0:T(8,128)(2,1)S(1)}, bf16[128,640]{1,0:T(8,128)(2,1)S(1)}, u32[]{:S(2)}, u32[]{:S(2)}) collective-permute-start(bf16[128,640]{1,0:T(8,128)(2,1)S(1)} %fusion.16), channel_id=1, source_target_pairs={{0,4},{1,3},{2,6},{3,1},{4,0},{5,7},{6,2},{7,5},{8,12},{9,11},{10,... | collective-permute-start | bytes 491528 | tf_op jit(solution)/shard_map/ppermute | solution.py:522
  444.6 14.5 %collective-permute-start.50 = (bf16[4,144,384]{2,1,0:T(8,128)(2,1)S(1)}, bf16[4,144,384]{2,1,0:T(8,128)(2,1)S(1)}, u32[]{:S(2)}, u32[]{:S(2)}) collective-permute-start(bf16[4,144,384]{2,1,0:T(8,128)(2,1)S(1)} %fusion.9), channel_id=1, source_target_pairs={{0,16},{1,9},{2,18},{3,11},{4,20},{5,13},{6,22},{7,15},{8,24},{9,1... | collective-permute-start | bytes 1327112 | tf_op jit(solution)/shard_map/ppermute | solution.py:522
  450.2 6.8 %collective-permute-start.48 = (bf16[128,640]{1,0:T(8,128)(2,1)S(1)}, bf16[128,640]{1,0:T(8,128)(2,1)S(1)}, u32[]{:S(2)}, u32[]{:S(2)}) collective-permute-start(bf16[128,640]{1,0:T(8,128)(2,1)S(1)} %fusion.10), channel_id=1, source_target_pairs={{0,8},{1,17},{2,10},{3,19},{4,12},{5,21},{6,14},{7,23},{8,0},{9,25... | collective-permute-start | bytes 491528 | tf_op jit(solution)/shard_map/ppermute | solution.py:522
  457.0 16.1 %collective-permute-start.49 = (bf16[2,128,640]{2,1,0:T(8,128)(2,1)S(1)}, bf16[2,128,640]{2,1,0:T(8,128)(2,1)S(1)}, u32[]{:S(2)}, u32[]{:S(2)}) collective-permute-start(bf16[2,128,640]{2,1,0:T(8,128)(2,1)S(1)} %pad_maximum_fusion.13), channel_id=1, source_target_pairs={{0,16},{1,9},{2,18},{3,11},{4,20},{5,13},{6,22},{7,15},{8,24},{9,1... | collective-permute-start | bytes 983048 | tf_op jit(solution)/shard_map/ppermute | solution.py:522
  460.5 6.7 %collective-permute-start.51 = (bf16[144,384]{1,0:T(8,128)(2,1)S(1)}, bf16[144,384]{1,0:T(8,128)(2,1)S(1)}, u32[]{:S(2)}, u32[]{:S(2)}) collective-permute-start(bf16[144,384]{1,0:T(8,128)(2,1)S(1)} %get-tuple-element.221), channel_id=1, source_target_pairs={{0,6},{1,7},{2,4},{3,5},{4,2},{5,3},{6,0},{7,1},{8,14},{9,15},{10,... | collective-permute-start | bytes 331784 | tf_op jit(solution)/shard_map/ppermute | solution.py:522
  462.2 7.2 %collective-permute-start.52 = (bf16[144,384]{1,0:T(8,128)(2,1)S(1)}, bf16[144,384]{1,0:T(8,128)(2,1)S(1)}, u32[]{:S(2)}, u32[]{:S(2)}) collective-permute-start(bf16[144,384]{1,0:T(8,128)(2,1)S(1)} %get-tuple-element.223), channel_id=1, source_target_pairs={{0,4},{1,5},{2,6},{3,7},{4,0},{5,1},{6,2},{7,3},{8,12},{9,13},{10,... | collective-permute-start | bytes 331784 | tf_op jit(solution)/shard_map/ppermute | solution.py:522
  462.2 7.2 %collective-permute-start.53 = (bf16[144,384]{1,0:T(8,128)(2,1)S(1)}, bf16[144,384]{1,0:T(8,128)(2,1)S(1)}, u32[]{:S(2)}, u32[]{:S(2)}) collective-permute-start(bf16[144,384]{1,0:T(8,128)(2,1)S(1)} %get-tuple-element.222), channel_id=1, source_target_pairs={{0,2},{1,3},{2,0},{3,1},{4,6},{5,7},{6,4},{7,5},{8,10},{9,11},{10,... | collective-permute-start | bytes 331784 | tf_op jit(solution)/shard_map/ppermute | solution.py:522
  469.5 5.8 %collective-permute-start.54 = (bf16[144,384]{1,0:T(8,128)(2,1)S(1)}, bf16[144,384]{1,0:T(8,128)(2,1)S(1)}, u32[]{:S(2)}, u32[]{:S(2)}) collective-permute-start(bf16[144,384]{1,0:T(8,128)(2,1)S(1)} %fusion.15), channel_id=1, source_target_pairs={{0,24},{1,25},{2,26},{3,27},{4,28},{5,29},{6,30},{7,31},{8,16},{9,... | collective-permute-start | bytes 331784 | tf_op jit(solution)/shard_map/ppermute | solution.py:522
  470.5 5.9 %collective-permute-start.55 = (bf16[144,384]{1,0:T(8,128)(2,1)S(1)}, bf16[144,384]{1,0:T(8,128)(2,1)S(1)}, u32[]{:S(2)}, u32[]{:S(2)}) collective-permute-start(bf16[144,384]{1,0:T(8,128)(2,1)S(1)} %fusion.15), channel_id=1, source_target_pairs={{0,16},{1,17},{2,18},{3,19},{4,20},{5,21},{6,22},{7,23},{8,24},{9,... | collective-permute-start | bytes 331784 | tf_op jit(solution)/shard_map/ppermute | solution.py:522
  472.2 4.7 collective-permute-start.56
  (34 other events, 549.1 us)
